TPU v7x, 128 devices: a whole 4x4x4 slice. The times are simulated.
128 devices in a mesh: blk: 32 (over x, y, core), chain: 4 (over z).
Axes of the slice: x: 4, y: 4, z: 4, core: 2. Of those that a mesh axis runs over, the one named last changes fastest.
Arguments:
- rhs: float32 [4, 2, 32, 256, 256], P('chain', None, 'blk'), may hold values from -6 to 6
- inverses: bfloat16 [4, 2, 32, 256, 256], P('chain', None, 'blk'), as said below
- blocks: bfloat16 [4, 2, 32, 8, 256, 256], P('chain', None, 'blk'), may hold values from -0.125 to 0.125
- pattern: int32 [4, 2, 32, 8], P('chain', None, 'blk'), may hold values from 0 to 63
Outputs:
- forward_solution: float32 [4, 2, 32, 256, 256], P('chain', None, 'blk')
- solution: float32 [4, 2, 32, 256, 256], P('chain', None, 'blk')
Inputs may be any that keep to these rules, and one draw needn't show every extreme that they name: `pattern`: every entry names a supernode of the next level. `inverses`: each block is the identity plus entries of standard deviation about 0.5 / sqrt(256).
All inputs are finite; a program needn't handle non-finite values.
Results may differ from a plain program's by a relative error of at most 0.025.
Values may be sent and summed in bfloat16 or wider, within the bound.
No kernel may reach another device: no remote copies, remote signals or barrier semaphores. Data moves between devices by JAX's collectives and lax.ppermute only.
A program may use at most 128 MiB of HBM per device.

v0:
```python
import jax
import jax.numpy as jnp
from jax import lax
from jax.sharding import PartitionSpec as P


def from_behind(value, axis, by):
    length = lax.axis_size(axis)
    pairs = [(i, i + by) for i in range(length) if 0 <= i + by < length]
    return lax.ppermute(value, axis, pairs)


def fan_in_level(terms, targets, per_dev, groups, blk_at):
    all_nodes = per_dev * groups
    nodes = jnp.arange(all_nodes, dtype=jnp.int32)
    onehot = (targets[:, None] == nodes[None, :]).astype(jnp.float32)
    dense = jnp.dot(onehot.T, terms, precision=lax.Precision.HIGHEST)
    summed = lax.psum(dense.astype(jnp.bfloat16), "blk").astype(jnp.float32)
    summed = summed.reshape(per_dev, groups, terms.shape[1])
    owned = lax.dynamic_slice_in_dim(summed, blk_at, 1, 1).reshape(per_dev, terms.shape[1])
    return owned


def on_device(rhs, inverses, blocks, pattern):
    levels = lax.axis_size("chain")
    groups = lax.axis_size("blk")
    chain_at = lax.axis_index("chain")
    blk_at = lax.axis_index("blk")
    per_dev = rhs.shape[1]
    width = rhs.shape[3]
    columns = rhs.shape[4]
    fanout = blocks.shape[3]
    all_nodes = per_dev * groups
    right = rhs.reshape(per_dev, width, columns)
    inverse = inverses.reshape(per_dev, width, width)
    factor = blocks.reshape(per_dev, fanout, width, width)
    targets = pattern.reshape(per_dev * fanout)
    inflow = jnp.zeros((per_dev, width, columns), jnp.float32)
    forward = jnp.zeros((per_dev, width, columns), jnp.float32)

    def solve_down(operand):
        part, income, kept = operand
        resid = (part - income).astype(jnp.bfloat16)
        return jnp.einsum("sij,sjr->sir", inverse, resid, preferred_element_type=jnp.float32)

    def keep_last(operand):
        return operand[2]

    def make_terms(solved):
        terms = jnp.einsum("spij,sjr->spir", factor, solved, preferred_element_type=jnp.float32)
        return terms.reshape(per_dev * fanout, width * columns)

    def no_terms(solved):
        return jnp.zeros((per_dev * fanout, width * columns), jnp.float32)

    for level in range(levels):
        active = chain_at == level
        forward = lax.cond(active, solve_down, keep_last, (right, inflow, forward))
        if level < levels - 1:
            terms = lax.cond(active, make_terms, no_terms, forward.astype(jnp.bfloat16))
            owned = fan_in_level(terms, targets, per_dev, groups, blk_at)
            inflow = (
                from_behind(owned.astype(jnp.bfloat16), "chain", 1)
                .astype(owned.dtype)
                .reshape(per_dev, width, columns)
            )
    result = jnp.zeros((per_dev, width, columns), jnp.float32)
    parents = jnp.zeros((per_dev, groups, width * columns), jnp.bfloat16)

    def solve_up(operand):
        above, kept = operand
        flat = above.reshape(all_nodes, width, columns)
        picked = jnp.take(flat, targets, axis=0).reshape(per_dev, fanout, width, columns)
        back = jnp.einsum("spji,spjr->sir", factor, picked, preferred_element_type=jnp.float32)
        upper = (forward - back).astype(jnp.bfloat16)
        return jnp.einsum("sji,sjr->sir", inverse, upper, preferred_element_type=jnp.float32)

    def solve_top(operand):
        upper = forward.astype(jnp.bfloat16)
        return jnp.einsum("sji,sjr->sir", inverse, upper, preferred_element_type=jnp.float32)

    def keep_result(operand):
        return operand[1]

    for level in reversed(range(levels)):
        active = chain_at == level
        if level == levels - 1:
            result = lax.cond(active, solve_top, keep_result, (parents, result))
        else:
            result = lax.cond(active, solve_up, keep_result, (parents, result))
        if level > 0:
            own_solved = result.astype(jnp.bfloat16).reshape(per_dev, 1, width * columns)
            near = from_behind(own_solved, "chain", -1)
            parents = lax.all_gather(near, "blk", axis=1, tiled=True)
    shape = (1, per_dev, 1, width, columns)
    return (forward.reshape(shape), result.reshape(shape))


def solution(mesh):
    placed = (
        P("chain", None, "blk", None, None),
        P("chain", None, "blk", None, None),
        P("chain", None, "blk", None, None, None),
        P("chain", None, "blk", None),
    )
    return jax.shard_map(
        on_device,
        mesh=mesh,
        in_specs=placed,
        out_specs=(P("chain", None, "blk", None, None), P("chain", None, "blk", None, None)),
        check_vma=False,
    )
```

profile of v0, /device:TPU:0, one launch (start us, length us, event | category | flops | bytes accessed | tf_op | source)
XLA Modules:
  0.0 808.9 jit_solution(14134128192458965840)
XLA Ops:
  7.7 1.3 reduce.3
  9.2 1.3 conditional.11
  9.2 1.3 fusion
  10.5 6.7 conditional.12
  10.5 2.3 convolution_bitcast_fusion
  12.8 4.4 copy.82
  17.2 8.7 %convolution_convert_fusion.2 = bf16[64,65536]{1,0:T(8,128)(2,1)S(1)} fusion(f32[16,65536]{1,0:T(8,128)} %get-tuple-element.239, s32[16]{0:T(128)S(1)} %eq.20), kind=kOutput, calls=%fused_computation.51 | convolution fusion | flops 809501696 | bytes 12582976 | tf_op jit(solution)/shard_map/dot_general | solution.py:17
  26.0 15.7 %copy.50 = bf16[2,32,65536]{2,0,1:T(2,128)(2,1)} copy(bf16[2,32,65536]{2,1,0:T(8,128)(2,1)S(1)} %bitcast.147) | data formatting | bytes 16777216 | tf_op jit(solution)/shard_map/reshape | solution.py:19
  41.7 119.7 %all-reduce.4.cloned.1.call-done = bf16[2,32,65536]{2,0,1:T(2,128)(2,1)} async-done(((bf16[2,32,65536]{2,0,1:T(2,128)(2,1)}), bf16[2,32,65536]{2,0,1:T(2,128)(2,1)}) %all-reduce.4.cloned.1.call-update) | async-done | bytes 8388624 | tf_op jit(solution)/shard_map/psum | solution.py:18
  161.4 1.1 fusion.19
  162.5 3.5 collective-permute-start
  166.0 5.3 collective-permute-done
  172.1 1.0 conditional.13
  172.1 1.0 copy.76
  173.8 2.7 conditional.14
  173.8 2.2 broadcast.22
  176.5 8.7 %convolution_convert_fusion.1 = bf16[64,65536]{1,0:T(8,128)(2,1)S(1)} fusion(f32[16,65536]{1,0:T(8,128)} %get-tuple-element.241, s32[16]{0:T(128)S(1)} %eq.20), kind=kOutput, calls=%fused_computation.50 | convolution fusion | flops 809501696 | bytes 12582976 | tf_op jit(solution)/shard_map/dot_general | solution.py:17
  185.3 15.7 %copy.54 = bf16[2,32,65536]{2,0,1:T(2,128)(2,1)} copy(bf16[2,32,65536]{2,1,0:T(8,128)(2,1)S(1)} %bitcast.148) | data formatting | bytes 16777216 | tf_op jit(solution)/shard_map/reshape | solution.py:19
  201.0 128.3 %all-reduce.6.cloned.1.call-done = bf16[2,32,65536]{2,0,1:T(2,128)(2,1)} async-done(((bf16[2,32,65536]{2,0,1:T(2,128)(2,1)}), bf16[2,32,65536]{2,0,1:T(2,128)(2,1)}) %all-reduce.6.cloned.1.call-update) | async-done | bytes 8388624 | tf_op jit(solution)/shard_map/psum | solution.py:18
  329.3 1.1 fusion.20
  330.4 3.5 collective-permute-start.1
  333.9 5.3 collective-permute-done.1
  339.2 2.4 conditional.16
  339.2 2.2 broadcast.23
  341.6 8.7 %convolution_convert_fusion = bf16[64,65536]{1,0:T(8,128)(2,1)S(1)} fusion(f32[16,65536]{1,0:T(8,128)} %get-tuple-element.243, s32[16]{0:T(128)S(1)} %eq.20), kind=kOutput, calls=%fused_computation.49 | convolution fusion | flops 809501696 | bytes 12582976 | tf_op jit(solution)/shard_map/dot_general | solution.py:17
  350.4 15.7 %copy.57 = bf16[2,32,65536]{2,0,1:T(2,128)(2,1)} copy(bf16[2,32,65536]{2,1,0:T(8,128)(2,1)S(1)} %bitcast.149) | data formatting | bytes 16777216 | tf_op jit(solution)/shard_map/reshape | solution.py:19
  366.1 132.2 %all-reduce.8.cloned.1.call-done = bf16[2,32,65536]{2,0,1:T(2,128)(2,1)} async-done(((bf16[2,32,65536]{2,0,1:T(2,128)(2,1)}), bf16[2,32,65536]{2,0,1:T(2,128)(2,1)}) %all-reduce.8.cloned.1.call-update) | async-done | bytes 8388624 | tf_op jit(solution)/shard_map/psum | solution.py:18
  498.3 1.1 fusion.21
  499.4 4.2 collective-permute-start.2
  503.6 4.7 collective-permute-done.2
  508.2 1.1 convert_element_type.115
  509.3 1.3 conditional.17
  509.4 1.2 copy.77
  511.6 1.3 collective-permute-start.3
  512.9 8.4 %collective-permute-done.3 = bf16[2,1,65536]{2,0,1:T(2,128)(2,1)S(1)} collective-permute-done((bf16[2,1,65536]{2,0,1:T(2,128)(2,1)S(1)}, bf16[2,1,65536]{2,0,1:T(2,128)(2,1)S(1)}, u32[]{:S(2)}, u32[]{:S(2)}) %collective-permute-start.3) | collective-permute-done | bytes 262176 | tf_op jit(solution)/shard_map/ppermute | solution.py:10
  522.1 55.5 %all-gather.4.cloned.1.call-done = bf16[2,32,65536]{2,0,1:T(2,128)(2,1)} async-done(((bf16[2,1,65536]{2,0,1:T(2,128)(2,1)}), bf16[2,32,65536]{2,0,1:T(2,128)(2,1)}) %all-gather.4.cloned.1.call-update) | async-done | bytes 8388624 | tf_op jit(solution)/shard_map/all_gather | solution.py:94
  578.9 1.3 collective-permute-start.4
  580.2 9.3 %collective-permute-done.4 = bf16[2,1,65536]{2,0,1:T(2,128)(2,1)S(1)} collective-permute-done((bf16[2,1,65536]{2,0,1:T(2,128)(2,1)}, bf16[2,1,65536]{2,0,1:T(2,128)(2,1)S(1)}, u32[]{:S(2)}, u32[]{:S(2)}) %collective-permute-start.4) | collective-permute-done | bytes 262176 | tf_op jit(solution)/shard_map/ppermute | solution.py:10
  590.3 83.7 %all-gather.6.cloned.1.call-done = bf16[2,32,65536]{2,0,1:T(2,128)(2,1)} async-done(((bf16[2,1,65536]{2,0,1:T(2,128)(2,1)}), bf16[2,32,65536]{2,0,1:T(2,128)(2,1)}) %all-gather.6.cloned.1.call-update) | async-done | bytes 8388624 | tf_op jit(solution)/shard_map/all_gather | solution.py:94
  675.1 1.3 collective-permute-start.5
  676.4 40.5 %collective-permute-done.5 = bf16[2,1,65536]{2,0,1:T(2,128)(2,1)S(1)} collective-permute-done((bf16[2,1,65536]{2,0,1:T(2,128)(2,1)}, bf16[2,1,65536]{2,0,1:T(2,128)(2,1)S(1)}, u32[]{:S(2)}, u32[]{:S(2)}) %collective-permute-start.5) | collective-permute-done | bytes 262176 | tf_op jit(solution)/shard_map/ppermute | solution.py:10
  717.7 51.1 %all-gather.8.cloned.1.call-done = bf16[2,32,65536]{2,0,1:T(2,128)(2,1)} async-done(((bf16[2,1,65536]{2,0,1:T(2,128)(2,1)}), bf16[2,32,65536]{2,0,1:T(2,128)(2,1)}) %all-gather.8.cloned.1.call-update) | async-done | bytes 8388624 | tf_op jit(solution)/shard_map/all_gather | solution.py:94
  768.8 31.9 %conditional.21 = (f32[1,2,1,256,256]{4,3,2,1,0:T(8,128)S(1)}) conditional(s32[]{:T(128)} %convert_element_type.105, f32[2,256,256]{1,2,0:T(8,128)S(1)} %get-tuple-element.246, (bf16[2,32,65536]{2,0,1:T(2,128)(2,1)}, s32[16]{0:T(128)S(1)}, bf16[2,8,256,256]{3,2,1,0:T(8,128)(2,1)S(1)}, f32[2,256,256]{1,2,0:T(8,128)}, ...), branch_computations={%region_23.25_spmd, %region_24.26_spmd} | conditional | flops 605291648 | bytes 48501096 | solution.py:90
  769.1 11.3 %copy.65 = bf16[2,32,65536]{2,1,0:T(8,128)(2,1)} copy(bf16[2,32,65536]{2,0,1:T(2,128)(2,1)} %get-tuple-element.219) | data formatting | bytes 16777216 | tf_op jit(solution)/shard_map
  780.4 8.9 %copy.90 = bf16[8,8,256,256]{3,2,1,0:T(8,128)(2,1)} copy(bf16[8,8,256,256]{3,1,2,0:T(8,128)(2,1)} %bitcast.152) | data formatting | bytes 16777216 | tf_op jit(solution)/shard_map/cond
  789.3 5.4 gather_fusion.2
  794.7 3.2 broadcast_select_fusion.2
  797.9 2.7 convolution_bitcast_fusion.10
  (50 shorter events, 9.2 us)
Async XLA Ops:
  7.2 154.2 %all-reduce.4.cloned.1.call-start = ((), (), s32[]{:S(2)}) async-start(), calls=%async_computation | async-start | bytes 16777216 | tf_op jit(solution)/shard_map/psum | solution.py:18
  41.6 130.5 %copy-start.1 = (bf16[1,2,1,256,256]{4,3,2,1,0:T(8,128)(2,1)S(1)}, bf16[1,2,1,256,256]{4,3,2,1,0:T(8,128)(2,1)}, u32[]{:S(2)}) copy-start(bf16[1,2,1,256,256]{4,3,2,1,0:T(8,128)(2,1)} %param.29) | copy-start | bytes 786436
  41.6 130.5 %copy-start.2 = (f32[1,2,1,256,256]{4,3,2,1,0:T(8,128)S(1)}, f32[1,2,1,256,256]{4,3,2,1,0:T(8,128)}, u32[]{:S(2)}) copy-start(f32[1,2,1,256,256]{4,3,2,1,0:T(8,128)} %param.28) | copy-start | bytes 1572868
  41.6 287.7 %all-reduce.6.cloned.1.call-start = ((), (), s32[]{:S(2)}) async-start(), calls=%async_computation.1 | async-start | bytes 16777216 | tf_op jit(solution)/shard_map/psum | solution.py:18
  162.5 8.8 %collective-permute-start = (bf16[2,65536]{1,0:T(2,128)(2,1)S(1)}, bf16[2,65536]{1,0:T(2,128)(2,1)S(1)}, u32[]{:S(2)}, u32[]{:S(2)}) collective-permute-start(bf16[2,65536]{1,0:T(2,128)(2,1)S(1)} %fusion.19), channel_id=1, source_target_pairs={{0,1},{1,2},{2,3},{4,5},{5,6},{6,7},{8,9},{9,10},{10,11},{12,13},{... | collective-permute-start | bytes 786440 | tf_op jit(solution)/shard_map/ppermute | solution.py:10
  171.4 0.7 copy-start.5
  172.1 1.8 copy-start
  200.9 297.3 %all-reduce.8.cloned.1.call-start = ((), (), s32[]{:S(2)}) async-start(), calls=%async_computation.2 | async-start | bytes 16777216 | tf_op jit(solution)/shard_map/psum | solution.py:18
  330.4 8.8 %collective-permute-start.1 = (bf16[2,65536]{1,0:T(2,128)(2,1)S(1)}, bf16[2,65536]{1,0:T(2,128)(2,1)S(1)}, u32[]{:S(2)}, u32[]{:S(2)}) collective-permute-start(bf16[2,65536]{1,0:T(2,128)(2,1)S(1)} %fusion.20), channel_id=1, source_target_pairs={{0,1},{1,2},{2,3},{4,5},{5,6},{6,7},{8,9},{9,10},{10,11},{12,13},{... | collective-permute-start | bytes 786440 | tf_op jit(solution)/shard_map/ppermute | solution.py:10
  366.0 211.5 %all-gather.4.cloned.1.call-start = ((), (), s32[]{:S(2)}) async-start(), calls=%async_computation.3 | async-start | bytes 8650752 | tf_op jit(solution)/shard_map/all_gather | solution.py:94
  499.4 8.8 %collective-permute-start.2 = (bf16[2,65536]{1,0:T(2,128)(2,1)S(1)}, bf16[2,65536]{1,0:T(2,128)(2,1)}, u32[]{:S(2)}, u32[]{:S(2)}) collective-permute-start(bf16[2,65536]{1,0:T(2,128)(2,1)S(1)} %fusion.21), channel_id=1, source_target_pairs={{0,1},{1,2},{2,3},{4,5},{5,6},{6,7},{8,9},{9,10},{10,11},{12,13},{... | collective-permute-start | bytes 786440 | tf_op jit(solution)/shard_map/ppermute | solution.py:10
  510.6 0.8 copy-start.3
  511.6 9.7 %collective-permute-start.3 = (bf16[2,1,65536]{2,0,1:T(2,128)(2,1)S(1)}, bf16[2,1,65536]{2,0,1:T(2,128)(2,1)S(1)}, u32[]{:S(2)}, u32[]{:S(2)}) collective-permute-start(bf16[2,1,65536]{2,0,1:T(2,128)(2,1)S(1)} %reshape.123), channel_id=1, source_target_pairs={{1,0},{2,1},{3,2},{5,4},{6,5},{7,6},{9,8},{10,9},{11,10},{13,12},{... | collective-permute-start | bytes 786440 | tf_op jit(solution)/shard_map/ppermute | solution.py:10
  521.3 0.7 copy-start.7
  522.0 152.0 %all-gather.6.cloned.1.call-start = ((), (), s32[]{:S(2)}) async-start(), calls=%async_computation.4 | async-start | bytes 8650752 | tf_op jit(solution)/shard_map/all_gather | solution.py:94
  578.9 10.6 %collective-permute-start.4 = (bf16[2,1,65536]{2,0,1:T(2,128)(2,1)}, bf16[2,1,65536]{2,0,1:T(2,128)(2,1)S(1)}, u32[]{:S(2)}, u32[]{:S(2)}) collective-permute-start(bf16[2,1,65536]{2,0,1:T(2,128)(2,1)} %reshape.124), channel_id=1, source_target_pairs={{1,0},{2,1},{3,2},{5,4},{6,5},{7,6},{9,8},{10,9},{11,10},{13,12},{... | collective-permute-start | bytes 786440 | tf_op jit(solution)/shard_map/ppermute | solution.py:10
  589.5 0.7 copy-start.8
  590.2 178.6 %all-gather.8.cloned.1.call-start = ((), (), s32[]{:S(2)}) async-start(), calls=%async_computation.5 | async-start | bytes 8650752 | tf_op jit(solution)/shard_map/all_gather | solution.py:94
  675.1 41.8 %collective-permute-start.5 = (bf16[2,1,65536]{2,0,1:T(2,128)(2,1)}, bf16[2,1,65536]{2,0,1:T(2,128)(2,1)S(1)}, u32[]{:S(2)}, u32[]{:S(2)}) collective-permute-start(bf16[2,1,65536]{2,0,1:T(2,128)(2,1)} %reshape.125), channel_id=1, source_target_pairs={{1,0},{2,1},{3,2},{5,4},{6,5},{7,6},{9,8},{10,9},{11,10},{13,12},{... | collective-permute-start | bytes 786440 | tf_op jit(solution)/shard_map/ppermute | solution.py:10
  717.0 0.7 copy-start.9
  800.8 0.8 copy-start.4
Sparse Core Ops, SparseCore 0:
  41.8 119.6 all-reduce.3
  201.1 128.1 all-reduce.5
  366.2 132.0 all-reduce.7
  522.1 55.3 all-gather.3
  590.3 83.5 all-gather.5
  717.8 50.9 all-gather.7
where the time goes:
time: 818 us; the launch traced here: 809 us
  waiting for transfers between devices  644 us (79%)
  local copies, waits for them, and re-layouts  91.7 us (11%)
  matrix products  32.4 us (4%)
  starting transfers between devices  15.2 us (2%)
  between operations  14.8 us (2%)
  other arithmetic  9.18 us (1%)
    psum x3, waiting for transfers between devices, fan_in_level(): summed = lax.psum(dense.astype(jnp.bfloat16), 'blk').astype(jnp.float32)  380 us
    all_gather x3, waiting for transfers between devices, on_device(): parents = lax.all_gather(near, 'blk', axis=1, tiled=True)  190 us
    ppermute x6, waiting for transfers between devices, from_behind(): return lax.ppermute(value, axis, pairs)  73.5 us
    reshape x3, local copies, waits for them, and re-layouts, fan_in_level(): summed = summed.reshape(per_dev, groups, terms.shape[1])  47 us
    dot_general x3, matrix products, fan_in_level(): dense = jnp.dot(onehot.T, terms, precision=lax.Precision.HIGHEST)  26.1 us
  transfers between devices with their start and end apart: 12, of which 12 were waited for; matrix products, arithmetic and copies ran while one was open for 0% of the time, Pallas kernels for 0%

commit v1 on v0

v1 whole, which is shorter than its diff:
```python
import functools

import jax
import jax.numpy as jnp
from jax import lax
from jax.experimental import pallas as pl
from jax.experimental.pallas import tpu as pltpu
from jax.sharding import Mesh, PartitionSpec as P


BF = jnp.bfloat16
F32 = jnp.float32
VMEM = 56 * 1024 * 1024
NODES = 64
CHIPS = 16
WIDTH = 256
FAN = 8
HALF = 128
COLS = 32


def dot_t(a, b):
    return lax.dot_general(a, b, (((1,), (1,)), ((), ())), preferred_element_type=F32)


def dot_n(a, b):
    return lax.dot_general(a, b, (((1,), (0,)), ((), ())), preferred_element_type=F32)


def first_kernel(core_ref, rhs_ref, inv_ref, f_ref, solved_ref, rows_ref):
    core = core_ref[0]
    for j in range(2):
        right = rhs_ref[j]
        f = dot_n(inv_ref[j], right.astype(BF))
        f_ref[j] = f
        ft = jnp.transpose(f).astype(BF)
        rt = jnp.transpose(right).astype(BF)
        for half in range(2):
            rel = jnp.bitwise_xor(core, half)
            solved_ref[rel, j] = ft[half * HALF : (half + 1) * HALF]
            for z in range(4):
                at = half * HALF + z * COLS
                rows_ref[rel, z, j] = rt[at : at + COLS]


def first_step(core, rhs, inverse):
    vm = pl.BlockSpec(memory_space=pltpu.VMEM)
    return pl.pallas_call(
        first_kernel,
        out_shape=(
            jax.ShapeDtypeStruct((2, WIDTH, WIDTH), F32),
            jax.ShapeDtypeStruct((2, 2, HALF, WIDTH), BF),
            jax.ShapeDtypeStruct((2, 4, 2, COLS, WIDTH), BF),
        ),
        in_specs=[pl.BlockSpec(memory_space=pltpu.SMEM), vm, vm],
        out_specs=(vm, vm, vm),
        compiler_params=pltpu.CompilerParams(vmem_limit_bytes=VMEM),
        cost_estimate=pl.CostEstimate(flops=2 * 2 * WIDTH**3, bytes_accessed=2 * 2**20, transcendentals=0),
    )(core, rhs, inverse)


def scatter_terms(step, at_ref, solved, own_ref, other_ref, acc_ref):
    def add(block_ref):
        for p in range(FAN):
            t = at_ref[step, p]
            acc_ref[t] += dot_t(solved, block_ref[0, 0, p])

    @pl.when(step < 2)
    def _():
        add(own_ref)

    @pl.when(step >= 2)
    def _():
        add(other_ref)


def zero_kernel(at_ref, solved_ref, own_ref, other_ref, share_ref, acc_ref):
    step = pl.program_id(0)

    @pl.when(step == 0)
    def _():
        acc_ref[...] = jnp.zeros_like(acc_ref)

    scatter_terms(step, at_ref, solved_ref[0], own_ref, other_ref, acc_ref)

    @pl.when(step == 3)
    def _():
        share_ref[...] = acc_ref[...].astype(BF)


def pair_specs(level, fan):
    own = pl.BlockSpec((1, 1, fan, WIDTH, WIDTH), lambda n, *_: (level, jnp.minimum(n, 1), 0, 0, 0))
    other = pl.BlockSpec((1, 1, fan, WIDTH, WIDTH), lambda n, *_: (level, jnp.maximum(n - 2, 0), 0, 0, 0))
    return [own, other]


def zero_level(at, solved, own, other):
    return pl.pallas_call(
        zero_kernel,
        grid_spec=pltpu.PrefetchScalarGridSpec(
            num_scalar_prefetch=1,
            grid=(4,),
            in_specs=[pl.BlockSpec((1, HALF, WIDTH), lambda n, *_: (n, 0, 0))] + pair_specs(0, FAN),
            out_specs=pl.BlockSpec((NODES, HALF, WIDTH), lambda n, *_: (0, 0, 0)),
            scratch_shapes=[pltpu.VMEM((NODES, HALF, WIDTH), F32)],
        ),
        out_shape=jax.ShapeDtypeStruct((NODES, HALF, WIDTH), BF),
        compiler_params=pltpu.CompilerParams(vmem_limit_bytes=VMEM, dimension_semantics=("arbitrary",)),
        cost_estimate=pl.CostEstimate(flops=2 * 32 * HALF * WIDTH**2, bytes_accessed=8 * 2**20, transcendentals=0),
    )(at, solved, own, other)


def solve_node(step, inflow, rhs_ref, own_inv_ref, other_inv_ref):
    resid = (rhs_ref[0].astype(F32) - inflow).astype(BF)
    inv = jnp.where(step < 2, own_inv_ref[0, 0, 0], other_inv_ref[0, 0, 0])
    return dot_t(resid, inv), inv


def forward_kernel(at_ref, got_ref, rhs_ref, own_inv_ref, other_inv_ref, own_ref, other_ref, f_ref, share_ref, acc_ref):
    step = pl.program_id(0)

    @pl.when(step == 0)
    def _():
        acc_ref[...] = jnp.zeros_like(acc_ref)

    inflow = jnp.sum(got_ref[:, 0].astype(F32), axis=0)
    f, _ = solve_node(step, inflow, rhs_ref, own_inv_ref, other_inv_ref)
    f_ref[0] = f
    scatter_terms(step, at_ref, f.astype(BF), own_ref, other_ref, acc_ref)

    @pl.when(step == 3)
    def _():
        share_ref[...] = acc_ref[...].astype(BF)


def got_spec(got):
    return pl.BlockSpec((got.shape[0], 1, COLS, WIDTH), lambda n, *_: (0, n, 0, 0))


NODE = pl.BlockSpec((1, COLS, WIDTH), lambda n, *_: (n, 0, 0))


def forward_level(level, at, got, rhs, own_inv, other_inv, own, other):
    return pl.pallas_call(
        forward_kernel,
        grid_spec=pltpu.PrefetchScalarGridSpec(
            num_scalar_prefetch=1,
            grid=(4,),
            in_specs=[got_spec(got), NODE] + pair_specs(level, 1) + pair_specs(level, FAN),
            out_specs=(NODE, pl.BlockSpec((NODES, COLS, WIDTH), lambda n, *_: (0, 0, 0))),
            scratch_shapes=[pltpu.VMEM((NODES, COLS, WIDTH), F32)],
        ),
        out_shape=(
            jax.ShapeDtypeStruct((4, COLS, WIDTH), F32),
            jax.ShapeDtypeStruct((NODES, COLS, WIDTH), BF),
        ),
        compiler_params=pltpu.CompilerParams(vmem_limit_bytes=VMEM, dimension_semantics=("arbitrary",)),
        cost_estimate=pl.CostEstimate(flops=2 * 36 * COLS * WIDTH**2, bytes_accessed=6 * 2**20, transcendentals=0),
    )(at, got, rhs, own_inv, other_inv, own, other)


def top_kernel(got_ref, rhs_ref, own_inv_ref, other_inv_ref, f_ref, sol_ref, copies_ref):
    step = pl.program_id(0)
    inflow = jnp.sum(got_ref[:, 0].astype(F32), axis=0)
    f, inv = solve_node(step, inflow, rhs_ref, own_inv_ref, other_inv_ref)
    f_ref[0] = f
    sol = dot_n(f.astype(BF), inv).astype(BF)
    sol_ref[0] = sol
    for k in range(CHIPS):
        copies_ref[k, 0] = sol


COPIES = pl.BlockSpec((CHIPS, 1, COLS, WIDTH), lambda n, *_: (0, n, 0, 0))


def top_level(got, rhs, own_inv, other_inv):
    return pl.pallas_call(
        top_kernel,
        grid=(4,),
        in_specs=[got_spec(got), NODE] + pair_specs(3, 1),
        out_specs=(NODE, NODE, COPIES),
        out_shape=(
            jax.ShapeDtypeStruct((4, COLS, WIDTH), F32),
            jax.ShapeDtypeStruct((4, COLS, WIDTH), BF),
            jax.ShapeDtypeStruct((CHIPS, 4, COLS, WIDTH), BF),
        ),
        compiler_params=pltpu.CompilerParams(vmem_limit_bytes=VMEM, dimension_semantics=("arbitrary",)),
        cost_estimate=pl.CostEstimate(flops=2 * 8 * COLS * WIDTH**2, bytes_accessed=3 * 2**20, transcendentals=0),
    )(got, rhs, own_inv, other_inv)


def backward_kernel(copies, at_ref, above_ref, f_ref, own_inv_ref, other_inv_ref, own_ref, other_ref, sol_ref, *rest):
    step = pl.program_id(0)

    def solve(block_ref, inv_ref):
        picked = jnp.concatenate([above_ref[at_ref[step, p]] for p in range(FAN)], axis=1)
        back = dot_n(picked, block_ref[0, 0].reshape(FAN * WIDTH, WIDTH))
        upper = (f_ref[0] - back).astype(BF)
        sol = dot_n(upper, inv_ref[0, 0, 0]).astype(BF)
        sol_ref[0] = sol
        if copies:
            for k in range(CHIPS):
                rest[0][k, 0] = sol

    @pl.when(step < 2)
    def _():
        solve(own_ref, own_inv_ref)

    @pl.when(step >= 2)
    def _():
        solve(other_ref, other_inv_ref)


def backward_level(level, at, above, f, own_inv, other_inv, own, other):
    copies = level > 0
    out_specs = (NODE, COPIES) if copies else (NODE,)
    out_shape = (jax.ShapeDtypeStruct((4, COLS, WIDTH), BF),)
    if copies:
        out_shape += (jax.ShapeDtypeStruct((CHIPS, 4, COLS, WIDTH), BF),)
    return pl.pallas_call(
        functools.partial(backward_kernel, copies),
        grid_spec=pltpu.PrefetchScalarGridSpec(
            num_scalar_prefetch=1,
            grid=(4,),
            in_specs=[pl.BlockSpec((NODES, COLS, WIDTH), lambda n, *_: (0, 0, 0)), NODE]
            + pair_specs(level, 1)
            + pair_specs(level, FAN),
            out_specs=out_specs,
        ),
        out_shape=out_shape,
        compiler_params=pltpu.CompilerParams(vmem_limit_bytes=VMEM, dimension_semantics=("arbitrary",)),
        cost_estimate=pl.CostEstimate(flops=2 * 36 * COLS * WIDTH**2, bytes_accessed=6 * 2**20, transcendentals=0),
    )(at, above, f, own_inv, other_inv, own, other)


def last_kernel(core_ref, plane_ref, first_ref, f_ref, x_ref, forward_ref, result_ref):
    core = core_ref[0]

    def gather(ref, j):
        halves = []
        for half in range(2):
            rel = jnp.bitwise_xor(core, half)
            halves += [ref[z, rel, j] for z in range(4)]
        return jnp.transpose(jnp.concatenate(halves, axis=0).astype(F32))

    for j in range(2):
        result_ref[j] = gather(x_ref, j)

    @pl.when(plane_ref[0] == 0)
    def _():
        forward_ref[...] = first_ref[...]

    @pl.when(plane_ref[0] != 0)
    def _():
        for j in range(2):
            forward_ref[j] = gather(f_ref, j)


def last_step(core, plane, first, f, x):
    vm = pl.BlockSpec(memory_space=pltpu.VMEM)
    sm = pl.BlockSpec(memory_space=pltpu.SMEM)
    return pl.pallas_call(
        last_kernel,
        out_shape=(jax.ShapeDtypeStruct((2, WIDTH, WIDTH), F32),) * 2,
        in_specs=[sm, sm, vm, vm, vm],
        out_specs=(vm, vm),
        compiler_params=pltpu.CompilerParams(vmem_limit_bytes=VMEM),
        cost_estimate=pl.CostEstimate(flops=0, bytes_accessed=2 * 2**20, transcendentals=0),
    )(core, plane, first, f, x)


def swap(value):
    return lax.ppermute(value, "c", [(0, 1), (1, 0)])


def on_device(rhs, inverses, blocks, pattern):
    core = lax.axis_index("c").astype(jnp.int32)
    plane = lax.axis_index("z").astype(jnp.int32)
    core1, plane1 = core.reshape(1), plane.reshape(1)
    right = rhs.reshape(2, WIDTH, WIDTH)
    inverse = inverses.reshape(2, WIDTH, WIDTH)
    factor = blocks.reshape(2, FAN, WIDTH, WIDTH)
    targets = jnp.clip(pattern.reshape(2, FAN), 0, NODES - 1)

    with jax.named_scope("patterns"):
        pair = jnp.concatenate([targets, swap(targets)], axis=0)
        place = (pair % 32) // 2 * 4 + jnp.bitwise_xor(pair % 2, core) * 2 + pair // 32
        places = lax.all_gather(place, "z", axis=0)

    with jax.named_scope("factor_everywhere"):
        own = lax.all_gather(factor, "z", axis=0)
        other = swap(own)
        own_inv = lax.all_gather(inverse.reshape(2, 1, WIDTH, WIDTH), "z", axis=0)
        other_inv = swap(own_inv)

    with jax.named_scope("level_0"):
        first, solved, rows = first_step(core1, right, inverse)
        solved_pair = jnp.concatenate([solved[0], swap(solved[1])], axis=0)
        near = swap(factor)
        share = zero_level(place, solved_pair, factor[None], near[None])
        got = lax.all_to_all(share.reshape(CHIPS, 4, HALF, WIDTH), ("x", "y"), 0, 0, tiled=True)
        summed = jnp.sum(got.astype(F32), axis=0).astype(BF)
        parts = [summed[:, z * COLS : (z + 1) * COLS] for z in range(4)]
        inflow = jnp.where(plane == 0, parts[0], jnp.zeros_like(parts[0]))
        for z in range(1, 4):
            inflow = inflow + lax.ppermute(parts[z], "z", [(0, z)])

    with jax.named_scope("rhs_by_columns"):
        both = jnp.stack([rows[0], swap(rows[1])], axis=1)
        right_at = lax.all_to_all(both, "z", 0, 0, tiled=True).reshape(4, 4, COLS, WIDTH)

    got = inflow[None]
    forward = [None] * 4
    for level in (1, 2):
        with jax.named_scope(f"forward_{level}"):
            forward[level], share = forward_level(
                level, places[level], got, right_at[level], own_inv, other_inv, own, other
            )
            got = lax.all_to_all(share.reshape(CHIPS, 4, COLS, WIDTH), ("x", "y"), 0, 0, tiled=True)
    result = [None] * 4
    with jax.named_scope("top"):
        forward[3], result[3], copies = top_level(got, right_at[3], own_inv, other_inv)

    with jax.named_scope("forward_0_by_columns"):
        by_plane = solved.reshape(2, 2, 4, COLS, WIDTH)
        halves = jnp.concatenate([by_plane[0], swap(by_plane[1])], axis=0)
        mine = jnp.where(plane == 0, halves[:, 0], jnp.zeros_like(halves[:, 0]))
        for z in range(1, 4):
            mine = mine + lax.ppermute(halves[:, z], "z", [(0, z)])
        forward[0] = mine.astype(F32)

    for level in (2, 1, 0):
        with jax.named_scope(f"backward_{level}"):
            above = lax.all_to_all(copies, ("x", "y"), 0, 0, tiled=True).reshape(NODES, COLS, WIDTH)
            out = backward_level(
                level, places[level], above, forward[level], own_inv, other_inv, own, other
            )
            result[level] = out[0]
            if level > 0:
                copies = out[1]

    with jax.named_scope("to_planes"):
        forward[0] = jnp.zeros_like(forward[1])
        f = jnp.stack(forward).astype(BF).reshape(4, 2, 2, COLS, WIDTH)
        x = jnp.stack(result).reshape(4, 2, 2, COLS, WIDTH)
        fx = jnp.stack([f, x], axis=1)
        fx = jnp.stack([fx[:, :, 0], swap(fx[:, :, 1])], axis=2)
        fx = lax.all_to_all(fx, "z", 0, 0, tiled=True)
        forward_out, result_out = last_step(core1, plane1, first, fx[:, 0], fx[:, 1])
    shape = (1, 2, 1, WIDTH, WIDTH)
    return forward_out.reshape(shape), result_out.reshape(shape)


def solution(mesh):
    wide = Mesh(mesh.devices.reshape(4, 4, 2, 4), ("x", "y", "c", "z"))
    blk = ("x", "y", "c")
    return jax.shard_map(
        on_device,
        mesh=wide,
        in_specs=(
            P("z", None, blk, None, None),
            P("z", None, blk, None, None),
            P("z", None, blk, None, None, None),
            P("z", None, blk, None),
        ),
        out_specs=(P("z", None, blk, None, None), P("z", None, blk, None, None)),
        check_vma=False,
    )
```

time: 818 us -> 365 us (0.45)
  waiting for transfers between devices: 644 us -> 147 us
  blocking collectives: 0 us -> 106 us
  local copies, waits for them, and re-layouts: 91.7 us -> 7.36 us
  Pallas kernels: 0 us -> 51 us
  matrix products: 32.4 us -> 0 us
  starting transfers between devices: 15.2 us -> 30.1 us
    psum x3 -> x0, waiting for transfers between devices: 380 us -> none  [fan_in_level(): summed = lax.psum(dense.astype(jnp.bfloat16), 'blk').astype(jnp.float32)]
    all_to_all x0 -> x5, blocking collectives: none -> 95.5 us  [the longest x2 46.6 us: on_device(): lax.all_to_all(share.reshape(CHIPS, 4, COLS, WIDTH), ('x', 'y'), 0, 0, ti...]
    all_gather x3 -> x2, waiting for transfers between devices: 190 us -> 115 us  [the longest x1 87.6 us: on_device(): own = lax.all_gather(factor, 'z', axis=0)]
    ppermute x6 -> x14, waiting for transfers between devices: 73.5 us -> 13 us  [the longest x8 10 us: swap(): return lax.ppermute(value, 'c', [(0, 1), (1, 0)])]
    pallas_call x0 -> x9, Pallas kernels: none -> 51 us  [the longest x3 20.3 us: backward_level(): pl.pallas_call(functools.partial(backward_kernel, copies), grid_spec=pltp...]
    reshape x6 -> x0, local copies, waits for them, and re-layouts: 48.6 us -> none  [the longest x3 47 us: fan_in_level(): summed = summed.reshape(per_dev, groups, terms.shape[1])]
    dot_general x6 -> x0, matrix products: 32.4 us -> none  [the longest x3 26.1 us: fan_in_level(): dense = jnp.dot(onehot.T, terms, precision=lax.Precision.HIGHEST)]
    all_to_all x0 -> x3, waiting for transfers between devices: none -> 17.8 us  [the longest x1 15.9 us: on_device(): lax.all_to_all(share.reshape(CHIPS, 4, HALF, WIDTH), ('x', 'y'), 0, 0, ti...]
  transfers between devices with their start and end apart: 12 -> 19, of which waited for: 12 -> 9; matrix products, arithmetic and copies ran while one was open for 0% -> 3% of each run, Pallas kernels for 0% -> 3%
where the time goes in v1:
time: 365 us; the launch traced here: 363 us
  waiting for transfers between devices  147 us (40%)
  blocking collectives  106 us (29%)
  Pallas kernels  51 us (14%)
  starting transfers between devices  30.1 us (8%)
  between operations  14.3 us (4%)
  other arithmetic  7.43 us (2%)
  local copies, waits for them, and re-layouts  7.36 us (2%)
    all_gather x1, waiting for transfers between devices, on_device(): own = lax.all_gather(factor, 'z', axis=0)  87.6 us
    all_to_all x2, blocking collectives, on_device(): lax.all_to_all(share.reshape(CHIPS, 4, COLS, WIDTH), ('x', 'y'), 0, 0, ti...  46.6 us
    all_to_all x2, blocking collectives, on_device(): lax.all_to_all(copies, ('x', 'y'), 0, 0, tiled=True)  34.5 us
    all_gather x1, waiting for transfers between devices, on_device(): own_inv = lax.all_gather(inverse.reshape(2, 1, WIDTH, WIDTH), 'z', axis=0)  26.9 us
    pallas_call x3, Pallas kernels, backward_level(): pl.pallas_call(functools.partial(backward_kernel, copies), grid_spec=pltp...  20.3 us
    all_to_all x1, waiting for transfers between devices, on_device(): lax.all_to_all(share.reshape(CHIPS, 4, HALF, WIDTH), ('x', 'y'), 0, 0, ti...  15.9 us
    all_to_all x1, blocking collectives, on_device(): fx = lax.all_to_all(fx, 'z', 0, 0, tiled=True)  14.5 us
    pallas_call x2, Pallas kernels, forward_level(): pl.pallas_call(forward_kernel, grid_spec=pltpu.PrefetchScalarGridSpec(num...  13.8 us
  transfers between devices with their start and end apart: 19, of which 9 were waited for; matrix products, arithmetic and copies ran while one was open for 3% of the time, Pallas kernels for 3%

profile of v1, /device:TPU:0, one launch (start us, length us, event | category | flops | bytes accessed | tf_op | source)
XLA Modules:
  0.0 362.8 jit_solution(8028809565886785730)
XLA Ops:
  7.2 0.7 all-gather.6.cloned.1.call-update
  7.9 87.6 %all-gather.6.cloned.1.call-done = bf16[4,2,1,8,256,256]{5,4,3,2,1,0:T(8,128)(2,1)} async-done(((bf16[1,2,1,8,256,256]{5,4,3,2,1,0:T(8,128)(2,1)}), bf16[4,2,1,8,256,256]{5,4,3,2,1,0:T(8,128)(2,1)}) %all-gather.6.cloned.1.call-update) | async-done | bytes 8388624 | tf_op jit(solution)/shard_map/factor_everywhere/all_gather | solution.py:291
  96.0 2.3 level_0.2
  98.3 1.0 fusion.27
  99.4 0.7 broadcast_clamp_fusion
  100.6 7.1 %collective-permute-done = s32[2,8]{1,0:T(2,128)S(1)} collective-permute-done((s32[2,8]{1,0:T(2,128)S(1)}, s32[2,8]{1,0:T(2,128)S(1)}, u32[]{:S(2)}, u32[]{:S(2)}) %collective-permute-start) | collective-permute-done | bytes 96 | tf_op jit(solution)/shard_map/patterns/ppermute | solution.py:273
  108.4 0.7 pad_maximum_fusion.1.solved_ref
  109.1 1.4 copy-done.2
  110.5 8.0 %level_0.3 = bf16[64,128,256]{2,1,0:T(8,128)(2,1)} custom-call(s32[4,8]{1,0:T(4,128)} %fusion.18.at_ref, bf16[4,128,256]{2,1,0:T(8,128)(2,1)} %pad_maximum_fusion.1.solved_ref, bf16[1,2,8,256,256]{4,3,2,1,0:T(8,128)(2,1)} %bitcast.104, bf16[1,2,8,256,256]{4,3,2,1,0:T(8,128)(2,1)} %bitcast.108), custom_call_target="tpu_custom_call" | custom-call | flops 536870912 | bytes 8388608 | tf_op jit(solution)/shard_map/level_0/pallas_call | solution.py:98
  118.5 7.0 %all-to-all-start = ((bf16[16,4,128,256]{3,2,1,0:T(8,128)(2,1)}), bf16[16,4,128,256]{3,2,1,0:T(8,128)(2,1)}, u32[]{:S(2)}, u32[]{:S(2)}) async-start(bf16[16,4,128,256]{3,2,1,0:T(8,128)(2,1)} %bitcast.102), calls=%async_computation | async-start | bytes 8388608 | tf_op jit(solution)/shard_map/level_0/all_to_all | solution.py:301
  125.5 0.7 all-gather.4.cloned.1.call-update
  126.5 26.9 %all-gather.4.cloned.1.call-done.own_inv_ref = bf16[4,2,1,256,256]{4,3,2,1,0:T(8,128)(2,1)} async-done(((bf16[1,2,1,256,256]{4,3,2,1,0:T(8,128)(2,1)}), bf16[4,2,1,256,256]{4,3,2,1,0:T(8,128)(2,1)}) %all-gather.4.cloned.1.call-update) | async-done | bytes 1048592 | tf_op jit(solution)/shard_map/factor_everywhere/all_gather | solution.py:293
  153.4 10.4 %all_gather.10 = s32[4,4,8]{2,1,0:T(4,128)S(1)} all-gather(s32[1,4,8]{2,1,0:T(4,128)S(1)} %fusion.12), channel_id=1, replica_groups=mesh['x'=4,'y'=4,'c'=2,'z'=4] {'z'}, dimensions={0}, use_global_device_ids=true | all-gather | bytes 640 | tf_op jit(solution)/shard_map/patterns/all_gather | solution.py:288
  164.4 0.7 copy.16
  165.1 15.9 %all-to-all-done = bf16[16,4,128,256]{3,2,1,0:T(8,128)(2,1)} async-done(((bf16[16,4,128,256]{3,2,1,0:T(8,128)(2,1)}), bf16[16,4,128,256]{3,2,1,0:T(8,128)(2,1)}, u32[]{:S(2)}, u32[]{:S(2)}) %all-to-all-start) | async-done | bytes 4194336 | tf_op jit(solution)/shard_map/level_0/all_to_all | solution.py:301
  181.0 4.0 %all-to-all-start.1 = ((bf16[4,2,2,32,256]{4,3,2,1,0:T(8,128)(2,1)}), bf16[4,2,2,32,256]{4,3,2,1,0:T(8,128)(2,1)S(1)}, u32[]{:S(2)}, u32[]{:S(2)}) async-start(bf16[4,2,2,32,256]{4,3,2,1,0:T(8,128)(2,1)} %copy.16), calls=%async_computation.1 | async-start | bytes 524288 | tf_op jit(solution)/shard_map/rhs_by_columns/all_to_all | solution.py:310
  185.0 3.0 reduce_sum.12
  188.0 3.9 %collective-permute-start.3 = (bf16[4,32,256]{2,1,0:T(8,128)(2,1)S(1)}, bf16[4,32,256]{2,1,0:T(8,128)(2,1)S(1)}, u32[]{:S(2)}, u32[]{:S(2)}) collective-permute-start(bf16[4,32,256]{2,1,0:T(8,128)(2,1)S(1)} %get-tuple-element.56), channel_id=1, source_target_pairs={{0,1},{4,5},{8,9},{12,13},{16,17},{20,21},{24,25},{28,29},{32,33},... | collective-permute-start | bytes 196616 | tf_op jit(solution)/shard_map/level_0/ppermute | solution.py:306
  192.0 1.9 collective-permute-start.5
  193.8 1.3 collective-permute-start.4
  195.2 0.7 fusion.28
  195.8 1.2 collective-permute-done.4
  197.0 0.6 fusion.8.got_ref
  197.7 1.0 copy-done
  198.7 6.8 %forward_1.1 = (f32[4,32,256]{2,1,0:T(8,128)}, bf16[64,32,256]{2,1,0:T(8,128)(2,1)}) custom-call(s32[4,8]{1,0:T(4,128)} %get-tuple-element.61.at_ref, bf16[1,4,32,256]{3,2,1,0:T(8,128)(2,1)} %fusion.8.got_ref, bf16[4,32,256]{2,1,0:T(8,128)(2,1)} %bitcast.117, bf16[4,2,1,256,256]{4,3,2,1,0:T(8,128)(2,1)} %all-gather.4.cloned.1.call-done.own_inv_ref, ...), custom_call_target="tpu_custom_call" | custom-call | flops 150994944 | bytes 6291456 | tf_op jit(solution)/shard_map/forward_1/pallas_call | solution.py:144
  205.5 29.1 %all_to_all.40.got_ref = bf16[16,4,32,256]{3,2,1,0:T(8,128)(2,1)} all-to-all(bf16[16,4,32,256]{3,2,1,0:T(8,128)(2,1)} %bitcast.109), channel_id=1, replica_groups=mesh['x'=4,'y'=4,'c'=2,'z'=4] {'x','y'}, dimensions={0} | all-to-all | bytes 2097152 | tf_op jit(solution)/shard_map/forward_1/all_to_all | solution.py:319
  234.5 7.0 %forward_2.1 = (f32[4,32,256]{2,1,0:T(8,128)}, bf16[64,32,256]{2,1,0:T(8,128)(2,1)}) custom-call(s32[4,8]{1,0:T(4,128)} %get-tuple-element.60.at_ref, bf16[16,4,32,256]{3,2,1,0:T(8,128)(2,1)} %all_to_all.40.got_ref, bf16[4,32,256]{2,1,0:T(8,128)(2,1)} %bitcast.116, bf16[4,2,1,256,256]{4,3,2,1,0:T(8,128)(2,1)} %all-gather.4.cloned.1.call-done.own_inv_ref, ...), custom_call_target="tpu_custom_call" | custom-call | flops 150994944 | bytes 6291456 | tf_op jit(solution)/shard_map/forward_2/pallas_call | solution.py:144
  241.5 17.5 %all_to_all.41.got_ref = bf16[16,4,32,256]{3,2,1,0:T(8,128)(2,1)} all-to-all(bf16[16,4,32,256]{3,2,1,0:T(8,128)(2,1)} %bitcast.110), channel_id=1, replica_groups=mesh['x'=4,'y'=4,'c'=2,'z'=4] {'x','y'}, dimensions={0} | all-to-all | bytes 2097152 | tf_op jit(solution)/shard_map/forward_2/all_to_all | solution.py:319
  259.0 4.2 %top.1 = (f32[4,32,256]{2,1,0:T(8,128)}, bf16[4,32,256]{2,1,0:T(8,128)(2,1)}, bf16[16,4,32,256]{3,2,1,0:T(8,128)(2,1)}) custom-call(bf16[16,4,32,256]{3,2,1,0:T(8,128)(2,1)} %all_to_all.41.got_ref, bf16[4,32,256]{2,1,0:T(8,128)(2,1)} %bitcast.121, bf16[4,2,1,256,256]{4,3,2,1,0:T(8,128)(2,1)} %all-gather.4.cloned.1.call-done.own_inv_ref, ...), custom_call_target="tpu_custom_call" | custom-call | flops 33554432 | bytes 3145728 | tf_op jit(solution)/shard_map/top/pallas_call | solution.py:177
  263.3 17.2 %all_to_all.42 = bf16[16,4,32,256]{3,2,1,0:T(8,128)(2,1)} all-to-all(bf16[16,4,32,256]{3,2,1,0:T(8,128)(2,1)} %get-tuple-element.26), channel_id=1, replica_groups=mesh['x'=4,'y'=4,'c'=2,'z'=4] {'x','y'}, dimensions={0} | all-to-all | bytes 2097152 | tf_op jit(solution)/shard_map/backward_2/all_to_all | solution.py:334
  280.5 6.8 %backward_2.1 = (bf16[4,32,256]{2,1,0:T(8,128)(2,1)}, bf16[16,4,32,256]{3,2,1,0:T(8,128)(2,1)}) custom-call(s32[4,8]{1,0:T(4,128)} %get-tuple-element.60.at_ref, bf16[64,32,256]{2,1,0:T(8,128)(2,1)} %bitcast.106, f32[4,32,256]{2,1,0:T(8,128)} %get-tuple-element.23.f_ref, bf16[4,2,1,256,256]{4,3,2,1,0:T(8,128)(2,1)} %all-gather.4.cloned.1.call-done.own_inv_ref, ...), custom_call_target="tpu_custom_call" | custom-call | flops 150994944 | bytes 6291456 | tf_op jit(solution)/shard_map/backward_2/pallas_call | solution.py:220
  287.3 17.2 %all_to_all.43 = bf16[16,4,32,256]{3,2,1,0:T(8,128)(2,1)} all-to-all(bf16[16,4,32,256]{3,2,1,0:T(8,128)(2,1)} %get-tuple-element.27), channel_id=1, replica_groups=mesh['x'=4,'y'=4,'c'=2,'z'=4] {'x','y'}, dimensions={0} | all-to-all | bytes 2097152 | tf_op jit(solution)/shard_map/backward_1/all_to_all | solution.py:334
  304.6 6.9 %backward_1.1 = (bf16[4,32,256]{2,1,0:T(8,128)(2,1)}, bf16[16,4,32,256]{3,2,1,0:T(8,128)(2,1)}) custom-call(s32[4,8]{1,0:T(4,128)} %get-tuple-element.61.at_ref, bf16[64,32,256]{2,1,0:T(8,128)(2,1)} %bitcast.107, f32[4,32,256]{2,1,0:T(8,128)} %get-tuple-element.21.f_ref, bf16[4,2,1,256,256]{4,3,2,1,0:T(8,128)(2,1)} %all-gather.4.cloned.1.call-done.own_inv_ref, ...), custom_call_target="tpu_custom_call" | custom-call | flops 150994944 | bytes 6291456 | tf_op jit(solution)/shard_map/backward_1/pallas_call | solution.py:220
  311.5 3.7 %all-to-all-start.6 = ((bf16[16,4,32,256]{3,2,1,0:T(8,128)(2,1)}), bf16[16,4,32,256]{3,2,1,0:T(8,128)(2,1)S(1)}, u32[]{:S(2)}, u32[]{:S(2)}) async-start(bf16[16,4,32,256]{3,2,1,0:T(8,128)(2,1)} %get-tuple-element.28), calls=%async_computation.6 | async-start | bytes 2097152 | tf_op jit(solution)/shard_map/backward_0/all_to_all | solution.py:334
  315.3 1.3 collective-permute-done.9
  316.6 1.3 collective-permute-start.10
  317.9 3.3 collective-permute-start.12
  321.2 2.3 collective-permute-start.11
  323.5 1.9 collective-permute-done.11
  325.4 0.7 fusion.4.f_ref
  326.1 1.9 all-to-all-done.6
  328.0 1.0 copy-done.1
  329.0 6.6 %backward_0.1 = bf16[4,32,256]{2,1,0:T(8,128)(2,1)} custom-call(s32[4,8]{1,0:T(4,128)} %get-tuple-element.59.at_ref, bf16[64,32,256]{2,1,0:T(8,128)(2,1)} %bitcast.105, f32[4,32,256]{2,1,0:T(8,128)} %fusion.4.f_ref, bf16[4,2,1,256,256]{4,3,2,1,0:T(8,128)(2,1)} %all-gather.4.cloned.1.call-done.own_inv_ref, bf16[4,2,1,256,256]{4,3,2,1,0:T(8,128)(2,1)} %copy-done, ...), custom_call_target="tpu_custom_call" | custom-call | flops 150994944 | bytes 6291456 | tf_op jit(solution)/shard_map/backward_0/pallas_call | solution.py:220
  335.6 1.0 maximum_maximum_fusion
  336.7 1.5 collective-permute-done.13
  338.3 14.5 %all_to_all.44 = bf16[4,2,2,2,32,256]{5,4,3,2,1,0:T(8,128)(2,1)S(1)} all-to-all(bf16[4,2,2,2,32,256]{5,4,3,2,1,0:T(8,128)(2,1)S(1)} %pad_maximum_fusion), channel_id=1, replica_groups=mesh['x'=4,'y'=4,'c'=2,'z'=4] {'z'}, dimensions={0} | all-to-all | bytes 1048576 | tf_op jit(solution)/shard_map/to_planes/all_to_all | solution.py:348
  352.8 0.8 slice_bitcast_fusion
  353.6 2.3 to_planes.1
  (53 shorter events, 3.0 us)
Async XLA Ops:
  7.2 88.4 %all-gather.6.cloned.1.call-start = ((), (), s32[]{:S(2)}) async-start(), calls=%async_computation.9 | async-start | bytes 10485760 | tf_op jit(solution)/shard_map/factor_everywhere/all_gather | solution.py:291
  95.5 102.2 %collective-permute-start.8 = (bf16[4,2,8,256,256]{4,3,2,1,0:T(8,128)(2,1)}, bf16[4,2,8,256,256]{4,3,2,1,0:T(8,128)(2,1)}, u32[]{:S(2)}, u32[]{:S(2)}) collective-permute-start(bf16[4,2,8,256,256]{4,3,2,1,0:T(8,128)(2,1)} %bitcast.96), channel_id=1, source_target_pairs={{0,4},{4,0},{1,5},{5,1},{2,6},{6,2},{3,7},{7,3},{8,12},{12,8},{9,1... | collective-permute-start | bytes 25165832 | tf_op jit(solution)/shard_map/factor_everywhere/ppermute | solution.py:273
  95.5 13.6 %collective-permute-start.2 = (bf16[2,8,256,256]{3,2,1,0:T(8,128)(2,1)}, bf16[2,8,256,256]{3,2,1,0:T(8,128)(2,1)S(1)}, u32[]{:S(2)}, u32[]{:S(2)}) collective-permute-start(bf16[2,8,256,256]{3,2,1,0:T(8,128)(2,1)} %bitcast.103), channel_id=1, source_target_pairs={{0,4},{4,0},{1,5},{5,1},{2,6},{6,2},{3,7},{7,3},{8,12},{12,8},{9,1... | collective-permute-start | bytes 6291464 | tf_op jit(solution)/shard_map/level_0/ppermute | solution.py:273
  99.3 9.0 %collective-permute-start.1 = (bf16[2,128,256]{2,1,0:T(8,128)(2,1)S(1)}, bf16[2,128,256]{2,1,0:T(8,128)(2,1)S(1)}, u32[]{:S(2)}, u32[]{:S(2)}) collective-permute-start(bf16[2,128,256]{2,1,0:T(8,128)(2,1)S(1)} %get-tuple-element.49), channel_id=1, source_target_pairs={{0,4},{4,0},{1,5},{5,1},{2,6},{6,2},{3,7},{7,3},{8,12},{12,8},{9,1... | collective-permute-start | bytes 393224 | tf_op jit(solution)/shard_map/level_0/ppermute | solution.py:273
  100.1 7.6 %collective-permute-start = (s32[2,8]{1,0:T(2,128)S(1)}, s32[2,8]{1,0:T(2,128)S(1)}, u32[]{:S(2)}, u32[]{:S(2)}) collective-permute-start(s32[2,8]{1,0:T(2,128)S(1)} %bitcast.127), channel_id=1, source_target_pairs={{0,4},{4,0},{1,5},{5,1},{2,6},{6,2},{3,7},{7,3},{8,12},{12,8},{9,1... | collective-permute-start | bytes 200 | tf_op jit(solution)/shard_map/patterns/ppermute | solution.py:273
  109.1 1.4 copy-start.2
  118.5 7.8 %copy-start.5 = (bf16[2,4,2,32,256]{4,3,2,1,0:T(8,128)(2,1)S(1)}, bf16[2,4,2,32,256]{4,3,2,1,0:T(8,128)(2,1)}, u32[]{:S(2)}) copy-start(bf16[2,4,2,32,256]{4,3,2,1,0:T(8,128)(2,1)} %get-tuple-element.20) | copy-start | bytes 786436
  118.5 62.6 %all-to-all-start = ((bf16[16,4,128,256]{3,2,1,0:T(8,128)(2,1)}), bf16[16,4,128,256]{3,2,1,0:T(8,128)(2,1)}, u32[]{:S(2)}, u32[]{:S(2)}) async-start(bf16[16,4,128,256]{3,2,1,0:T(8,128)(2,1)} %bitcast.102), calls=%async_computation | async-start | bytes 8388608 | tf_op jit(solution)/shard_map/level_0/all_to_all | solution.py:301
  125.5 27.9 %all-gather.4.cloned.1.call-start = ((), (), s32[]{:S(2)}) async-start(), calls=%async_computation.8 | async-start | bytes 1310720 | tf_op jit(solution)/shard_map/factor_everywhere/all_gather | solution.py:293
  126.3 38.1 %collective-permute-start.6 = (bf16[4,2,32,256]{3,2,1,0:T(8,128)(2,1)S(1)}, bf16[4,2,32,256]{3,2,1,0:T(8,128)(2,1)S(1)}, u32[]{:S(2)}, u32[]{:S(2)}) collective-permute-start(bf16[4,2,32,256]{3,2,1,0:T(8,128)(2,1)S(1)} %get-tuple-element.55), channel_id=1, source_target_pairs={{0,4},{4,0},{1,5},{5,1},{2,6},{6,2},{3,7},{7,3},{8,12},{12,8},{9,1... | collective-permute-start | bytes 393224 | tf_op jit(solution)/shard_map/rhs_by_columns/ppermute | solution.py:273
  153.4 44.3 %collective-permute-start.7 = (bf16[4,2,1,256,256]{4,3,2,1,0:T(8,128)(2,1)}, bf16[4,2,1,256,256]{4,3,2,1,0:T(8,128)(2,1)S(1)}, u32[]{:S(2)}, u32[]{:S(2)}) collective-permute-start(bf16[4,2,1,256,256]{4,3,2,1,0:T(8,128)(2,1)} %all-gather.4.cloned.1.call-done.own_inv_ref), channel_id=1, source_target_pairs={{0,4},{4,0},{1,5},{5,1},{2,6},{6,2},{3,7},{7,3},{8,12},{12,8},{9,1... | collective-permute-start | bytes 3145736 | tf_op jit(solution)/shard_map/factor_everywhere/ppermute | solution.py:273
  181.0 14.1 %all-to-all-start.1 = ((bf16[4,2,2,32,256]{4,3,2,1,0:T(8,128)(2,1)}), bf16[4,2,2,32,256]{4,3,2,1,0:T(8,128)(2,1)S(1)}, u32[]{:S(2)}, u32[]{:S(2)}) async-start(bf16[4,2,2,32,256]{4,3,2,1,0:T(8,128)(2,1)} %copy.16), calls=%async_computation.1 | async-start | bytes 524288 | tf_op jit(solution)/shard_map/rhs_by_columns/all_to_all | solution.py:310
  188.0 7.8 %collective-permute-start.3 = (bf16[4,32,256]{2,1,0:T(8,128)(2,1)S(1)}, bf16[4,32,256]{2,1,0:T(8,128)(2,1)S(1)}, u32[]{:S(2)}, u32[]{:S(2)}) collective-permute-start(bf16[4,32,256]{2,1,0:T(8,128)(2,1)S(1)} %get-tuple-element.56), channel_id=1, source_target_pairs={{0,1},{4,5},{8,9},{12,13},{16,17},{20,21},{24,25},{28,29},{32,33},... | collective-permute-start | bytes 196616 | tf_op jit(solution)/shard_map/level_0/ppermute | solution.py:306
  192.0 3.9 %collective-permute-start.5 = (bf16[4,32,256]{2,1,0:T(8,128)(2,1)S(1)}, bf16[4,32,256]{2,1,0:T(8,128)(2,1)S(1)}, u32[]{:S(2)}, u32[]{:S(2)}) collective-permute-start(bf16[4,32,256]{2,1,0:T(8,128)(2,1)S(1)} %get-tuple-element.57), channel_id=1, source_target_pairs={{0,3},{4,7},{8,11},{12,15},{16,19},{20,23},{24,27},{28,31},{32,35}... | collective-permute-start | bytes 196616 | tf_op jit(solution)/shard_map/level_0/ppermute | solution.py:306
  193.8 3.2 collective-permute-start.4
  197.7 1.0 copy-start
  304.6 21.5 %copy-start.3 = (f32[4,32,256]{2,1,0:T(8,128)S(1)}, f32[4,32,256]{2,1,0:T(8,128)}, u32[]{:S(2)}) copy-start(f32[4,32,256]{2,1,0:T(8,128)} %get-tuple-element.21.f_ref) | copy-start | bytes 393220
  304.6 21.5 %copy-start.4 = (f32[4,32,256]{2,1,0:T(8,128)S(1)}, f32[4,32,256]{2,1,0:T(8,128)}, u32[]{:S(2)}) copy-start(f32[4,32,256]{2,1,0:T(8,128)} %get-tuple-element.23.f_ref) | copy-start | bytes 393220
  304.6 21.5 %copy-start.6 = (f32[4,32,256]{2,1,0:T(8,128)S(1)}, f32[4,32,256]{2,1,0:T(8,128)}, u32[]{:S(2)}) copy-start(f32[4,32,256]{2,1,0:T(8,128)} %get-tuple-element.25) | copy-start | bytes 393220
  311.5 16.5 %all-to-all-start.6 = ((bf16[16,4,32,256]{3,2,1,0:T(8,128)(2,1)}), bf16[16,4,32,256]{3,2,1,0:T(8,128)(2,1)S(1)}, u32[]{:S(2)}, u32[]{:S(2)}) async-start(bf16[16,4,32,256]{3,2,1,0:T(8,128)(2,1)} %get-tuple-element.28), calls=%async_computation.6 | async-start | bytes 2097152 | tf_op jit(solution)/shard_map/backward_0/all_to_all | solution.py:334
  315.1 1.4 collective-permute-start.9
  316.6 6.9 %collective-permute-start.10 = (bf16[4,32,256]{2,1,0:T(8,128)(2,1)S(1)}, bf16[4,32,256]{2,1,0:T(8,128)(2,1)S(1)}, u32[]{:S(2)}, u32[]{:S(2)}) collective-permute-start(bf16[4,32,256]{2,1,0:T(8,128)(2,1)S(1)} %get-tuple-element.44), channel_id=1, source_target_pairs={{0,1},{4,5},{8,9},{12,13},{16,17},{20,21},{24,25},{28,29},{32,33},... | collective-permute-start | bytes 196616 | tf_op jit(solution)/shard_map/forward_0_by_columns/ppermute | solution.py:329
  317.9 5.6 %collective-permute-start.12 = (bf16[4,32,256]{2,1,0:T(8,128)(2,1)S(1)}, bf16[4,32,256]{2,1,0:T(8,128)(2,1)S(1)}, u32[]{:S(2)}, u32[]{:S(2)}) collective-permute-start(bf16[4,32,256]{2,1,0:T(8,128)(2,1)S(1)} %get-tuple-element.45), channel_id=1, source_target_pairs={{0,3},{4,7},{8,11},{12,15},{16,19},{20,23},{24,27},{28,31},{32,35}... | collective-permute-start | bytes 196616 | tf_op jit(solution)/shard_map/forward_0_by_columns/ppermute | solution.py:329
  321.2 4.1 %collective-permute-start.11 = (bf16[4,32,256]{2,1,0:T(8,128)(2,1)S(1)}, bf16[4,32,256]{2,1,0:T(8,128)(2,1)S(1)}, u32[]{:S(2)}, u32[]{:S(2)}) collective-permute-start(bf16[4,32,256]{2,1,0:T(8,128)(2,1)S(1)} %get-tuple-element.46), channel_id=1, source_target_pairs={{0,2},{4,6},{8,10},{12,14},{16,18},{20,22},{24,26},{28,30},{32,34}... | collective-permute-start | bytes 196616 | tf_op jit(solution)/shard_map/forward_0_by_columns/ppermute | solution.py:329
  328.0 1.0 copy-start.1
  329.0 6.6 %copy-start.7 = (bf16[4,32,256]{2,1,0:T(8,128)(2,1)S(1)}, bf16[4,32,256]{2,1,0:T(8,128)(2,1)}, u32[]{:S(2)}) copy-start(bf16[4,32,256]{2,1,0:T(8,128)(2,1)} %get-tuple-element.31) | copy-start | bytes 196612
  329.0 6.6 %copy-start.8 = (bf16[4,32,256]{2,1,0:T(8,128)(2,1)S(1)}, bf16[4,32,256]{2,1,0:T(8,128)(2,1)}, u32[]{:S(2)}) copy-start(bf16[4,32,256]{2,1,0:T(8,128)(2,1)} %get-tuple-element.30) | copy-start | bytes 196612
  329.0 6.6 %copy-start.9 = (bf16[4,32,256]{2,1,0:T(8,128)(2,1)S(1)}, bf16[4,32,256]{2,1,0:T(8,128)(2,1)}, u32[]{:S(2)}) copy-start(bf16[4,32,256]{2,1,0:T(8,128)(2,1)} %get-tuple-element.29) | copy-start | bytes 196612
  336.6 1.6 collective-permute-start.13
Sparse Core Ops, SparseCore 0:
  9.7 85.8 all-gather.5
  128.0 25.3 all-gather.3

commit v2 on v1

v2 whole, which is shorter than its diff:
```python
import functools

import jax
import jax.numpy as jnp
from jax import lax
from jax.experimental import pallas as pl
from jax.experimental.pallas import tpu as pltpu
from jax.sharding import Mesh, PartitionSpec as P


BF = jnp.bfloat16
F32 = jnp.float32
VMEM = 56 * 1024 * 1024
NODES = 64
CHIPS = 16
WIDTH = 256
FAN = 8
HALF = 128
COLS = 32
UP_1 = [(0, 1), (1, 2), (2, 3)]
DOWN_1 = [(0, 3), (1, 0), (2, 1)]
UP = [(z, (z + 1) % 4) for z in range(4)]
DOWN = [(z, (z + 3) % 4) for z in range(4)]


def dot_t(a, b):
    return lax.dot_general(a, b, (((1,), (1,)), ((), ())), preferred_element_type=F32)


def dot_n(a, b):
    return lax.dot_general(a, b, (((1,), (0,)), ((), ())), preferred_element_type=F32)


def first_kernel(core_ref, rhs_ref, inv_ref, f_ref, solved_ref, rows_ref):
    core = core_ref[0]
    for j in range(2):
        right = rhs_ref[j]
        f = dot_n(inv_ref[j], right.astype(BF))
        f_ref[j] = f
        ft = jnp.transpose(f).astype(BF)
        rt = jnp.transpose(right).astype(BF)
        for half in range(2):
            rel = jnp.bitwise_xor(core, half)
            solved_ref[rel, j] = ft[half * HALF : (half + 1) * HALF]
            for z in range(4):
                at = half * HALF + z * COLS
                rows_ref[rel, z, j] = rt[at : at + COLS]


def first_step(core, rhs, inverse):
    vm = pl.BlockSpec(memory_space=pltpu.VMEM)
    return pl.pallas_call(
        first_kernel,
        out_shape=(
            jax.ShapeDtypeStruct((2, WIDTH, WIDTH), F32),
            jax.ShapeDtypeStruct((2, 2, HALF, WIDTH), BF),
            jax.ShapeDtypeStruct((2, 4, 2, COLS, WIDTH), BF),
        ),
        in_specs=[pl.BlockSpec(memory_space=pltpu.SMEM), vm, vm],
        out_specs=(vm, vm, vm),
        compiler_params=pltpu.CompilerParams(vmem_limit_bytes=VMEM),
        cost_estimate=pl.CostEstimate(flops=2 * 2 * WIDTH**3, bytes_accessed=2 * 2**20, transcendentals=0),
    )(core, rhs, inverse)


def any_specs(count):
    return [pl.BlockSpec(memory_space=pl.ANY)] * count


SMEM = pl.BlockSpec(memory_space=pltpu.SMEM)
VM = pl.BlockSpec(memory_space=pltpu.VMEM)


def fetch(plane, choices, dst, sem):
    for z, src in enumerate(choices):

        @pl.when(plane == z)
        def _():
            pltpu.make_async_copy(src, dst, sem).start()

    return pltpu.make_async_copy(choices[0], dst, sem)


def factor_copies(plane, refs, buf, sems):
    return [fetch(plane, refs[4 * n : 4 * n + 4], buf.at[n], sems.at[n]) for n in range(4)]


def add_terms(n, at_ref, solved, buf, acc_ref):
    rows = buf.shape[1] * WIDTH
    terms = dot_t(solved, buf[n].reshape(rows, WIDTH))
    for p in range(FAN):
        acc_ref[at_ref[n, p]] += terms[:, p * WIDTH : (p + 1) * WIDTH]


def zero_kernel(at_ref, solved_ref, own_ref, other_ref, share_ref, buf, sems, acc_ref):
    copies = []
    for n in range(4):
        src = (own_ref if n < 2 else other_ref).at[n % 2]
        copies.append(pltpu.make_async_copy(src, buf.at[n], sems.at[n]))
        copies[n].start()
    acc_ref[...] = jnp.zeros_like(acc_ref)
    for n in range(4):
        copies[n].wait()
        add_terms(n, at_ref, solved_ref[n], buf, acc_ref)
    share_ref[...] = acc_ref[...].astype(BF)


def zero_level(at, solved, own, other):
    return pl.pallas_call(
        zero_kernel,
        in_specs=[SMEM, VM] + any_specs(2),
        out_specs=VM,
        scratch_shapes=[
            pltpu.VMEM((4, FAN, WIDTH, WIDTH), BF),
            pltpu.SemaphoreType.DMA((4,)),
            pltpu.VMEM((NODES, HALF, WIDTH), F32),
        ],
        out_shape=jax.ShapeDtypeStruct((NODES, HALF, WIDTH), BF),
        compiler_params=pltpu.CompilerParams(vmem_limit_bytes=VMEM),
        cost_estimate=pl.CostEstimate(flops=2 * 32 * HALF * WIDTH**2, bytes_accessed=8 * 2**20, transcendentals=0),
    )(at, solved, own, other)


def solve_node(n, got_ref, rhs_ref, inv_ref):
    inflow = jnp.sum(got_ref[:, n].astype(F32), axis=0)
    resid = (rhs_ref[n].astype(F32) - inflow).astype(BF)
    return dot_t(resid, inv_ref[n])


def forward_kernel(plane_ref, at_ref, got_ref, rhs_ref, inv_ref, *rest):
    refs, (f_ref, share_ref, buf, sems, acc_ref) = rest[:16], rest[16:]
    copies = factor_copies(plane_ref[0], refs, buf, sems)
    acc_ref[...] = jnp.zeros_like(acc_ref)
    for n in range(4):
        f = solve_node(n, got_ref, rhs_ref, inv_ref)
        f_ref[n] = f
        copies[n].wait()
        add_terms(n, at_ref, f.astype(BF), buf, acc_ref)
    share_ref[...] = acc_ref[...].astype(BF)


def forward_level(plane, at, got, rhs, inv, choices):
    return pl.pallas_call(
        forward_kernel,
        in_specs=[SMEM, SMEM, VM, VM, VM] + any_specs(16),
        out_specs=(VM, VM),
        scratch_shapes=[
            pltpu.VMEM((4, FAN, WIDTH, WIDTH), BF),
            pltpu.SemaphoreType.DMA((4,)),
            pltpu.VMEM((NODES, COLS, WIDTH), F32),
        ],
        out_shape=(
            jax.ShapeDtypeStruct((4, COLS, WIDTH), F32),
            jax.ShapeDtypeStruct((NODES, COLS, WIDTH), BF),
        ),
        compiler_params=pltpu.CompilerParams(vmem_limit_bytes=VMEM),
        cost_estimate=pl.CostEstimate(flops=2 * 36 * COLS * WIDTH**2, bytes_accessed=6 * 2**20, transcendentals=0),
    )(plane, at, got, rhs, inv, *choices)


def top_kernel(got_ref, rhs_ref, inv_ref, f_ref, sol_ref, copies_ref):
    for n in range(4):
        f = solve_node(n, got_ref, rhs_ref, inv_ref)
        f_ref[n] = f
        sol = dot_n(f.astype(BF), inv_ref[n]).astype(BF)
        sol_ref[n] = sol
        for k in range(CHIPS):
            copies_ref[k, n] = sol


def top_level(got, rhs, inv):
    return pl.pallas_call(
        top_kernel,
        in_specs=[VM] * 3,
        out_specs=(VM, VM, VM),
        out_shape=(
            jax.ShapeDtypeStruct((4, COLS, WIDTH), F32),
            jax.ShapeDtypeStruct((4, COLS, WIDTH), BF),
            jax.ShapeDtypeStruct((CHIPS, 4, COLS, WIDTH), BF),
        ),
        compiler_params=pltpu.CompilerParams(vmem_limit_bytes=VMEM),
        cost_estimate=pl.CostEstimate(flops=2 * 8 * COLS * WIDTH**2, bytes_accessed=3 * 2**20, transcendentals=0),
    )(got, rhs, inv)


def backward_kernel(plane_ref, at_ref, above_ref, f_ref, inv_ref, *rest):
    refs, outs, (buf, sems) = rest[:16], rest[16:-2], rest[-2:]
    copies = factor_copies(plane_ref[0], refs, buf, sems)
    for n in range(4):
        picked = jnp.concatenate([above_ref[at_ref[n, p]] for p in range(FAN)], axis=1)
        copies[n].wait()
        back = dot_n(picked, buf[n].reshape(FAN * WIDTH, WIDTH))
        upper = (f_ref[n] - back).astype(BF)
        sol = dot_n(upper, inv_ref[n]).astype(BF)
        outs[0][n] = sol
        if len(outs) > 1:
            for k in range(CHIPS):
                outs[1][k, n] = sol


def backward_level(level, plane, at, above, f, inv, choices):
    out_shape = (jax.ShapeDtypeStruct((4, COLS, WIDTH), BF),)
    if level > 0:
        out_shape += (jax.ShapeDtypeStruct((CHIPS, 4, COLS, WIDTH), BF),)
    return pl.pallas_call(
        backward_kernel,
        in_specs=[SMEM, SMEM, VM, VM, VM] + any_specs(16),
        out_specs=(VM,) * len(out_shape),
        scratch_shapes=[
            pltpu.VMEM((4, FAN, WIDTH, WIDTH), BF),
            pltpu.SemaphoreType.DMA((4,)),
        ],
        out_shape=out_shape,
        compiler_params=pltpu.CompilerParams(vmem_limit_bytes=VMEM),
        cost_estimate=pl.CostEstimate(flops=2 * 36 * COLS * WIDTH**2, bytes_accessed=6 * 2**20, transcendentals=0),
    )(plane, at, above, f, inv, *choices)


def last_kernel(core_ref, plane_ref, first_ref, f_ref, x_ref, forward_ref, result_ref):
    core = core_ref[0]

    def gather(ref, j):
        halves = []
        for half in range(2):
            rel = jnp.bitwise_xor(core, half)
            halves += [ref[z, rel, j] for z in range(4)]
        return jnp.transpose(jnp.concatenate(halves, axis=0).astype(F32))

    for j in range(2):
        result_ref[j] = gather(x_ref, j)

    @pl.when(plane_ref[0] == 0)
    def _():
        forward_ref[...] = first_ref[...]

    @pl.when(plane_ref[0] != 0)
    def _():
        for j in range(2):
            forward_ref[j] = gather(f_ref, j)


def last_step(core, plane, first, f, x):
    vm = pl.BlockSpec(memory_space=pltpu.VMEM)
    sm = pl.BlockSpec(memory_space=pltpu.SMEM)
    return pl.pallas_call(
        last_kernel,
        out_shape=(jax.ShapeDtypeStruct((2, WIDTH, WIDTH), F32),) * 2,
        in_specs=[sm, sm, vm, vm, vm],
        out_specs=(vm, vm),
        compiler_params=pltpu.CompilerParams(vmem_limit_bytes=VMEM),
        cost_estimate=pl.CostEstimate(flops=0, bytes_accessed=2 * 2**20, transcendentals=0),
    )(core, plane, first, f, x)


def swap(value):
    return lax.ppermute(value, "c", [(0, 1), (1, 0)])


def on_device(rhs, inverses, blocks, pattern):
    core = lax.axis_index("c").astype(jnp.int32)
    plane = lax.axis_index("z").astype(jnp.int32)
    core1, plane1 = core.reshape(1), plane.reshape(1)
    right = rhs.reshape(2, WIDTH, WIDTH)
    inverse = inverses.reshape(2, WIDTH, WIDTH)
    factor = blocks.reshape(2, FAN, WIDTH, WIDTH)
    targets = jnp.clip(pattern.reshape(2, FAN), 0, NODES - 1)

    def places_of(pair):
        return (pair % 32) // 2 * 4 + jnp.bitwise_xor(pair % 2, core) * 2 + pair // 32

    with jax.named_scope("factor_step_1"):
        own_a, own_b = factor[0], factor[1]
        up_1 = lax.ppermute(own_a, "z", UP_1)
        down_1 = lax.ppermute(own_b, "z", DOWN_1)
        near = swap(factor)

    with jax.named_scope("inverses_and_patterns"):
        tail = jnp.pad(targets.astype(BF)[:, None], ((0, 0), (0, 15), (0, WIDTH - FAN)))
        small = lax.all_gather(jnp.concatenate([inverse, tail], axis=1), "z", axis=0)
        small = jnp.concatenate([small, swap(small)], axis=1)
        inv_at = small[:, :, :WIDTH]
        places = places_of(small[:, :, WIDTH, :FAN].astype(jnp.int32))

    with jax.named_scope("level_0"):
        first, solved, rows = first_step(core1, right, inverse)
        solved_pair = jnp.concatenate([solved[0], swap(solved[1])], axis=0)
        place = places_of(jnp.concatenate([targets, swap(targets)], axis=0))
        share = zero_level(place, solved_pair, factor, near)
        got = lax.all_to_all(share.reshape(CHIPS, 4, HALF, WIDTH), ("x", "y"), 0, 0, tiled=True)

    with jax.named_scope("factor_step_2"):
        up_2 = lax.ppermute(jnp.where(plane <= 1, own_b, up_1), "z", UP)
        down_2 = lax.ppermute(jnp.where((plane == 1) | (plane == 2), own_a, down_1), "z", DOWN)
        up_1o, down_1o = swap(up_1), swap(down_1)
    with jax.named_scope("factor_step_3"):
        up_3 = lax.ppermute(jnp.where(plane == 1, up_1, own_b), "z", [(1, 2), (2, 3)])
        down_3 = lax.ppermute(jnp.where(plane == 0, own_a, down_1), "z", [(0, 3), (1, 0)])
        up_2o, down_2o = swap(up_2), swap(down_2)
        up_3o, down_3o = swap(up_3), swap(down_3)

    def choices_of(a, b, u1, d1, u2, d2, u3, d3):
        return {
            0: ([a, u1, u3, d3], [b, u2, d2, d1]),
            1: ([d2, a, u1, u2], [d1, b, u2, d2]),
            2: ([u2, d2, a, u1], [d3, d1, b, u3]),
        }

    mine = choices_of(own_a, own_b, up_1, down_1, up_2, down_2, up_3, down_3)
    theirs = choices_of(near[0], near[1], up_1o, down_1o, up_2o, down_2o, up_3o, down_3o)
    choices = {k: mine[k][0] + mine[k][1] + theirs[k][0] + theirs[k][1] for k in mine}

    with jax.named_scope("level_0_to_columns"):
        summed = jnp.sum(got.astype(F32), axis=0).astype(BF)
        parts = [summed[:, z * COLS : (z + 1) * COLS] for z in range(4)]
        inflow = jnp.where(plane == 0, parts[0], jnp.zeros_like(parts[0]))
        for z in range(1, 4):
            inflow = inflow + lax.ppermute(parts[z], "z", [(0, z)])

    with jax.named_scope("rhs_by_columns"):
        both = jnp.stack([rows[0], swap(rows[1])], axis=1)
        right_at = lax.all_to_all(both, "z", 0, 0, tiled=True).reshape(4, 4, COLS, WIDTH)

    got = inflow[None]
    forward = [None] * 4
    for level in (1, 2):
        with jax.named_scope(f"forward_{level}"):
            forward[level], share = forward_level(
                plane1, places[level], got, right_at[level], inv_at[level], choices[level]
            )
            got = lax.all_to_all(share.reshape(CHIPS, 4, COLS, WIDTH), ("x", "y"), 0, 0, tiled=True)
    result = [None] * 4
    with jax.named_scope("top"):
        forward[3], result[3], copies = top_level(got, right_at[3], inv_at[3])

    with jax.named_scope("forward_0_by_columns"):
        by_plane = solved.reshape(2, 2, 4, COLS, WIDTH)
        halves = jnp.concatenate([by_plane[0], swap(by_plane[1])], axis=0)
        mine = jnp.where(plane == 0, halves[:, 0], jnp.zeros_like(halves[:, 0]))
        for z in range(1, 4):
            mine = mine + lax.ppermute(halves[:, z], "z", [(0, z)])
        forward[0] = mine.astype(F32)

    for level in (2, 1, 0):
        with jax.named_scope(f"backward_{level}"):
            above = lax.all_to_all(copies, ("x", "y"), 0, 0, tiled=True).reshape(NODES, COLS, WIDTH)
            out = backward_level(
                level, plane1, places[level], above, forward[level], inv_at[level], choices[level]
            )
            result[level] = out[0]
            if level > 0:
                copies = out[1]

    with jax.named_scope("to_planes"):
        forward[0] = jnp.zeros_like(forward[1])
        f = jnp.stack(forward).astype(BF).reshape(4, 2, 2, COLS, WIDTH)
        x = jnp.stack(result).reshape(4, 2, 2, COLS, WIDTH)
        fx = jnp.stack([f, x], axis=1)
        fx = jnp.stack([fx[:, :, 0], swap(fx[:, :, 1])], axis=2)
        fx = lax.all_to_all(fx, "z", 0, 0, tiled=True)
        forward_out, result_out = last_step(core1, plane1, first, fx[:, 0], fx[:, 1])
    shape = (1, 2, 1, WIDTH, WIDTH)
    return forward_out.reshape(shape), result_out.reshape(shape)


def solution(mesh):
    wide = Mesh(mesh.devices.reshape(4, 4, 2, 4), ("x", "y", "c", "z"))
    blk = ("x", "y", "c")
    return jax.shard_map(
        on_device,
        mesh=wide,
        in_specs=(
            P("z", None, blk, None, None),
            P("z", None, blk, None, None),
            P("z", None, blk, None, None, None),
            P("z", None, blk, None),
        ),
        out_specs=(P("z", None, blk, None, None), P("z", None, blk, None, None)),
        check_vma=False,
    )
```

time: 365 us -> 300 us (0.82)
  waiting for transfers between devices: 147 us -> 72.2 us
  starting transfers between devices: 30.1 us -> 69.6 us
  blocking collectives: 106 us -> 70.5 us
  Pallas kernels: 51 us -> 42.6 us
  other arithmetic: 7.43 us -> 15.7 us
  local copies, waits for them, and re-layouts: 7.36 us -> 13.2 us
    all_gather x2 -> x1, waiting for transfers between devices: 115 us -> 26.9 us  [on_device(): lax.all_gather(jnp.concatenate([inverse, tail], axis=1), 'z', axis=0)]
    all_to_all x2 -> x1, blocking collectives: 46.6 us -> 19.4 us  [on_device(): lax.all_to_all(share.reshape(CHIPS, 4, COLS, WIDTH), ('x', 'y'), 0, 0, ti...]
    ppermute x0 -> x6, waiting for transfers between devices: none -> 22.5 us  [the longest x1 13.8 us: on_device(): up_2 = lax.ppermute(jnp.where(plane <= 1, own_b, up_1), 'z', UP)]
    all_to_all x0 -> x1, waiting for transfers between devices: none -> 18 us  [on_device(): lax.all_to_all(share.reshape(CHIPS, 4, COLS, WIDTH), ('x', 'y'), 0, 0, ti...]
    all_to_all x1, waiting for transfers between devices: 15.9 us -> 0.01 us  [on_device(): lax.all_to_all(share.reshape(CHIPS, 4, HALF, WIDTH), ('x', 'y'), 0, 0, ti...]
    ppermute x3, starting transfers between devices: 7.1 us -> 21.4 us  [on_device(): inflow = inflow + lax.ppermute(parts[z], 'z', [(0, z)])]
    ppermute x0 -> x6, starting transfers between devices: none -> 13.9 us  [the longest x1 3.99 us: on_device(): up_1 = lax.ppermute(own_a, 'z', UP_1)]
    all_gather x1 -> x0, blocking collectives: 10.4 us -> none  [on_device(): places = lax.all_gather(place, 'z', axis=0)]
  transfers between devices with their start and end apart: 19 -> 30, of which waited for: 9 -> 9; matrix products, arithmetic and copies ran while one was open for 3% -> 8% of each run, Pallas kernels for 3% -> 5%
where the time goes in v2:
time: 300 us; the launch traced here: 298 us
  waiting for transfers between devices  72.2 us (24%)
  blocking collectives  70.5 us (24%)
  starting transfers between devices  69.6 us (23%)
  Pallas kernels  42.6 us (14%)
  other arithmetic  15.7 us (5%)
  between operations  14.6 us (5%)
  local copies, waits for them, and re-layouts  13.2 us (4%)
    all_to_all x2, blocking collectives, on_device(): lax.all_to_all(copies, ('x', 'y'), 0, 0, tiled=True)  34.8 us
    all_gather x1, waiting for transfers between devices, on_device(): lax.all_gather(jnp.concatenate([inverse, tail], axis=1), 'z', axis=0)  26.9 us
    ppermute x3, starting transfers between devices, on_device(): inflow = inflow + lax.ppermute(parts[z], 'z', [(0, z)])  21.4 us
    all_to_all x1, blocking collectives, on_device(): lax.all_to_all(share.reshape(CHIPS, 4, COLS, WIDTH), ('x', 'y'), 0, 0, ti...  19.4 us
    all_to_all x1, waiting for transfers between devices, on_device(): lax.all_to_all(share.reshape(CHIPS, 4, COLS, WIDTH), ('x', 'y'), 0, 0, ti...  18 us
    pallas_call x3, Pallas kernels, backward_level(): pl.pallas_call(backward_kernel, in_specs=[SMEM, SMEM, VM, VM, VM] + any_s...  17.1 us
    all_to_all x1, blocking collectives, on_device(): fx = lax.all_to_all(fx, 'z', 0, 0, tiled=True)  16.3 us
    ppermute x1, waiting for transfers between devices, on_device(): up_2 = lax.ppermute(jnp.where(plane <= 1, own_b, up_1), 'z', UP)  13.8 us
  transfers between devices with their start and end apart: 30, of which 9 were waited for; matrix products, arithmetic and copies ran while one was open for 8% of the time, Pallas kernels for 5%

profile of v2, /device:TPU:0, one launch (start us, length us, event | category | flops | bytes accessed | tf_op | source)
XLA Modules:
  0.0 298.5 jit_solution(2689795813919997207)
XLA Ops:
  8.4 2.3 level_0.2
  10.7 1.0 slice_bitcast_fusion.9
  11.8 1.7 fusion.30
  14.7 5.4 %all-to-all-start.1 = ((bf16[4,2,2,32,256]{4,3,2,1,0:T(8,128)(2,1)}), bf16[4,2,2,32,256]{4,3,2,1,0:T(8,128)(2,1)S(1)}, u32[]{:S(2)}, u32[]{:S(2)}) async-start(bf16[4,2,2,32,256]{4,3,2,1,0:T(8,128)(2,1)} %copy.17), calls=%async_computation.1 | async-start | bytes 524288 | tf_op jit(solution)/shard_map/rhs_by_columns/all_to_all | solution.py:321
  21.5 1.3 copy-done.7
  22.8 6.6 %level_0.3 = bf16[64,128,256]{2,1,0:T(8,128)(2,1)} custom-call(s32[4,8]{1,0:T(4,128)} %fusion.24.at_ref, bf16[4,128,256]{2,1,0:T(8,128)(2,1)} %pad_maximum_fusion.2.solved_ref, bf16[2,8,256,256]{3,2,1,0:T(8,128)(2,1)} %bitcast.120, bf16[2,8,256,256]{3,2,1,0:T(8,128)(2,1)} %copy-done.7), custom_call_target="tpu_custom_call" | custom-call | flops 536870912 | bytes 8388608 | tf_op jit(solution)/shard_map/level_0/pallas_call | solution.py:109
  29.4 7.2 %all-to-all-start = ((bf16[16,4,128,256]{3,2,1,0:T(8,128)(2,1)}), bf16[16,4,128,256]{3,2,1,0:T(8,128)(2,1)}, u32[]{:S(2)}, u32[]{:S(2)}) async-start(bf16[16,4,128,256]{3,2,1,0:T(8,128)(2,1)} %bitcast.121), calls=%async_computation | async-start | bytes 8388608 | tf_op jit(solution)/shard_map/level_0/all_to_all | solution.py:289
  37.4 1.7 slice_bitcast_fusion.3
  39.1 4.0 %collective-permute-start.10 = (bf16[8,256,256]{2,1,0:T(8,128)(2,1)S(1)}, bf16[8,256,256]{2,1,0:T(8,128)(2,1)S(1)}, u32[]{:S(2)}, u32[]{:S(2)}) collective-permute-start(bf16[8,256,256]{2,1,0:T(8,128)(2,1)S(1)} %get-tuple-element.52.rest_1_.rest_2_.rest_0_), channel_id=1, source_target_pairs={{0,1},{1,2},{2,3},{4,5},{5,6},{6,7},{8,9},{9,10},{10,11},{12,13},{... | collective-permute-start | bytes 3145736 | tf_op jit(solution)/shard_map/factor_step_1/ppermute | solution.py:273
  43.1 2.4 collective-permute-start.8
  45.6 26.9 %all-gather.3.cloned.1.call-done = bf16[8,272,256]{2,1,0:T(8,128)(2,1)} async-done(((bf16[2,272,256]{2,1,0:T(8,128)(2,1)}), bf16[8,272,256]{2,1,0:T(8,128)(2,1)}) %all-gather.3.cloned.1.call-update) | async-done | bytes 1114128 | tf_op jit(solution)/shard_map/inverses_and_patterns/all_gather | solution.py:279
  72.6 1.2 collective-permute-done.10.rest_2_.rest_3_.rest_1_
  73.8 4.3 %collective-permute-done.8.rest_4_.rest_5_.rest_7_ = bf16[8,256,256]{2,1,0:T(8,128)(2,1)} collective-permute-done((bf16[8,256,256]{2,1,0:T(8,128)(2,1)S(1)}, bf16[8,256,256]{2,1,0:T(8,128)(2,1)}, u32[]{:S(2)}, u32[]{:S(2)}) %collective-permute-start.8) | collective-permute-done | bytes 1048608 | tf_op jit(solution)/shard_map/factor_step_1/ppermute | solution.py:274
  78.0 3.5 %broadcast_select_fusion = (bf16[8,256,256]{2,1,0:T(8,128)(2,1)}, bf16[8,256,256]{2,1,0:T(8,128)(2,1)S(1)}, bf16[8,256,256]{2,1,0:T(8,128)(2,1)S(1)}, bf16[8,256,256]{2,1,0:T(8,128)(2,1)}) fusion(bf16[8,256,256]{2,1,0:T(8,128)(2,1)S(1)} %collective-permute-done.10.rest_2_.rest_3_.rest_1_, pred[]{:T(512)S(6)} %eq.19, ...), kind=kLoop, calls=%fused_computation.4 | loop fusion | flops 2097152 | bytes 8388612 | tf_op jit(solution)/shard_map/factor_step_3/jit(_where)/select_n | solution.py:296
  81.6 1.5 collective-permute-start.11
  83.1 1.8 collective-permute-start.9
  84.9 1.7 collective-permute-start.17
  87.2 2.5 collective-permute-start.16
  89.7 1.5 slice_bitcast_fusion
  92.1 13.8 %collective-permute-done.11.rest_3_.rest_6_.rest_0_.rest_5_ = bf16[8,256,256]{2,1,0:T(8,128)(2,1)S(1)} collective-permute-done((bf16[8,256,256]{2,1,0:T(8,128)(2,1)S(1)}, bf16[8,256,256]{2,1,0:T(8,128)(2,1)S(1)}, u32[]{:S(2)}, u32[]{:S(2)}) %collective-permute-start.11) | collective-permute-done | bytes 1048608 | tf_op jit(solution)/shard_map/factor_step_2/ppermute | solution.py:292
  105.9 3.2 %collective-permute-done.9.rest_0_.rest_7_.rest_1_.rest_6_ = bf16[8,256,256]{2,1,0:T(8,128)(2,1)S(1)} collective-permute-done((bf16[8,256,256]{2,1,0:T(8,128)(2,1)S(1)}, bf16[8,256,256]{2,1,0:T(8,128)(2,1)S(1)}, u32[]{:S(2)}, u32[]{:S(2)}) %collective-permute-start.9) | collective-permute-done | bytes 1048608 | tf_op jit(solution)/shard_map/factor_step_2/ppermute | solution.py:293
  109.2 3.3 %reduce_sum.12 = bf16[4,128,256]{2,1,0:T(8,128)(2,1)S(1)} reduce(bf16[16,4,128,256]{3,2,1,0:T(8,128)(2,1)} %all-to-all-done, bf16[]{:T(256)} %constant.90.clone.1), dimensions={0}, to_apply=%region_0.1 | reduce | flops 1966080 | bytes 4456450 | tf_op jit(solution)/shard_map/level_0_to_columns/reduce_sum | solution.py:313
  112.6 16.3 %collective-permute-start.4 = (bf16[4,32,256]{2,1,0:T(8,128)(2,1)S(1)}, bf16[4,32,256]{2,1,0:T(8,128)(2,1)S(1)}, u32[]{:S(2)}, u32[]{:S(2)}) collective-permute-start(bf16[4,32,256]{2,1,0:T(8,128)(2,1)S(1)} %get-tuple-element.70), channel_id=1, source_target_pairs={{0,1},{4,5},{8,9},{12,13},{16,17},{20,21},{24,25},{28,29},{32,33},... | collective-permute-start | bytes 196616 | tf_op jit(solution)/shard_map/level_0_to_columns/ppermute | solution.py:317
  129.5 3.8 %collective-permute-start.6 = (bf16[4,32,256]{2,1,0:T(8,128)(2,1)S(1)}, bf16[4,32,256]{2,1,0:T(8,128)(2,1)S(1)}, u32[]{:S(2)}, u32[]{:S(2)}) collective-permute-start(bf16[4,32,256]{2,1,0:T(8,128)(2,1)S(1)} %get-tuple-element.71), channel_id=1, source_target_pairs={{0,3},{4,7},{8,11},{12,15},{16,19},{20,23},{24,27},{28,31},{32,35}... | collective-permute-start | bytes 196616 | tf_op jit(solution)/shard_map/level_0_to_columns/ppermute | solution.py:317
  133.4 1.3 collective-permute-start.5
  134.7 2.9 fusion.1
  138.8 1.0 copy-done.2
  139.8 5.4 %forward_1.1 = (f32[4,32,256]{2,1,0:T(8,128)}, bf16[64,32,256]{2,1,0:T(8,128)(2,1)}) custom-call(s32[1]{0:T(128)} %bitcast.1.plane_ref, s32[4,8]{1,0:T(4,128)} %get-tuple-element.75.at_ref, bf16[1,4,32,256]{3,2,1,0:T(8,128)(2,1)} %fusion.11.got_ref, bf16[4,32,256]{2,1,0:T(8,128)(2,1)} %bitcast.137, bf16[4,256,256]{2,1,0:T(8,128)(2,1)} %get-tuple-element.47.inv_ref, ...), custom_call_target="tpu_custom_call" | custom-call | flops 150994944 | bytes 6291456 | tf_op jit(solution)/shard_map/forward_1/pallas_call | solution.py:143
  145.2 6.6 %all-to-all-start.2 = ((bf16[16,4,32,256]{3,2,1,0:T(8,128)(2,1)}), bf16[16,4,32,256]{3,2,1,0:T(8,128)(2,1)S(1)}, u32[]{:S(2)}, u32[]{:S(2)}) async-start(bf16[16,4,32,256]{3,2,1,0:T(8,128)(2,1)} %bitcast.128), calls=%async_computation.2 | async-start | bytes 2097152 | tf_op jit(solution)/shard_map/forward_1/all_to_all | solution.py:330
  151.8 18.0 %all-to-all-done.2.got_ref = bf16[16,4,32,256]{3,2,1,0:T(8,128)(2,1)S(1)} async-done(((bf16[16,4,32,256]{3,2,1,0:T(8,128)(2,1)}), bf16[16,4,32,256]{3,2,1,0:T(8,128)(2,1)S(1)}, u32[]{:S(2)}, u32[]{:S(2)}) %all-to-all-start.2) | async-done | bytes 1048608 | tf_op jit(solution)/shard_map/forward_1/all_to_all | solution.py:330
  169.8 1.0 copy-done.11
  170.8 5.7 %forward_2.1 = (f32[4,32,256]{2,1,0:T(8,128)}, bf16[64,32,256]{2,1,0:T(8,128)(2,1)}) custom-call(s32[1]{0:T(128)} %bitcast.1.plane_ref, s32[4,8]{1,0:T(4,128)} %get-tuple-element.74.at_ref, bf16[16,4,32,256]{3,2,1,0:T(8,128)(2,1)} %copy-done.11, bf16[4,32,256]{2,1,0:T(8,128)(2,1)} %bitcast.136, bf16[4,256,256]{2,1,0:T(8,128)(2,1)} %get-tuple-element.46.inv_ref, ...), custom_call_target="tpu_custom_call" | custom-call | flops 150994944 | bytes 6291456 | tf_op jit(solution)/shard_map/forward_2/pallas_call | solution.py:143
  176.5 19.4 %all_to_all.40.got_ref = bf16[16,4,32,256]{3,2,1,0:T(8,128)(2,1)} all-to-all(bf16[16,4,32,256]{3,2,1,0:T(8,128)(2,1)} %bitcast.129), channel_id=1, replica_groups=mesh['x'=4,'y'=4,'c'=2,'z'=4] {'x','y'}, dimensions={0} | all-to-all | bytes 2097152 | tf_op jit(solution)/shard_map/forward_2/all_to_all | solution.py:330
  195.9 3.3 %top.1 = (f32[4,32,256]{2,1,0:T(8,128)}, bf16[4,32,256]{2,1,0:T(8,128)(2,1)}, bf16[16,4,32,256]{3,2,1,0:T(8,128)(2,1)}) custom-call(bf16[16,4,32,256]{3,2,1,0:T(8,128)(2,1)} %all_to_all.40.got_ref, bf16[4,32,256]{2,1,0:T(8,128)(2,1)} %bitcast.141, bf16[4,256,256]{2,1,0:T(8,128)(2,1)} %get-tuple-element.45.inv_ref), custom_call_target="tpu_custom_call" | custom-call | flops 33554432 | bytes 3145728 | tf_op jit(solution)/shard_map/top/pallas_call | solution.py:172
  199.2 17.5 %all_to_all.41 = bf16[16,4,32,256]{3,2,1,0:T(8,128)(2,1)} all-to-all(bf16[16,4,32,256]{3,2,1,0:T(8,128)(2,1)} %get-tuple-element.26), channel_id=1, replica_groups=mesh['x'=4,'y'=4,'c'=2,'z'=4] {'x','y'}, dimensions={0} | all-to-all | bytes 2097152 | tf_op jit(solution)/shard_map/backward_2/all_to_all | solution.py:345
  216.7 5.9 %backward_2.1 = (bf16[4,32,256]{2,1,0:T(8,128)(2,1)}, bf16[16,4,32,256]{3,2,1,0:T(8,128)(2,1)}) custom-call(s32[1]{0:T(128)} %bitcast.1.plane_ref, s32[4,8]{1,0:T(4,128)} %get-tuple-element.74.at_ref, bf16[64,32,256]{2,1,0:T(8,128)(2,1)} %bitcast.126, f32[4,32,256]{2,1,0:T(8,128)} %get-tuple-element.23.f_ref, ...), custom_call_target="tpu_custom_call" | custom-call | flops 150994944 | bytes 6291456 | tf_op jit(solution)/shard_map/backward_2/pallas_call | solution.py:205
  222.6 17.2 %all_to_all.42 = bf16[16,4,32,256]{3,2,1,0:T(8,128)(2,1)} all-to-all(bf16[16,4,32,256]{3,2,1,0:T(8,128)(2,1)} %get-tuple-element.27), channel_id=1, replica_groups=mesh['x'=4,'y'=4,'c'=2,'z'=4] {'x','y'}, dimensions={0} | all-to-all | bytes 2097152 | tf_op jit(solution)/shard_map/backward_1/all_to_all | solution.py:345
  239.8 5.8 %backward_1.1 = (bf16[4,32,256]{2,1,0:T(8,128)(2,1)}, bf16[16,4,32,256]{3,2,1,0:T(8,128)(2,1)}) custom-call(s32[1]{0:T(128)} %bitcast.1.plane_ref, s32[4,8]{1,0:T(4,128)} %get-tuple-element.75.at_ref, bf16[64,32,256]{2,1,0:T(8,128)(2,1)} %bitcast.127, f32[4,32,256]{2,1,0:T(8,128)} %get-tuple-element.21.f_ref, ...), custom_call_target="tpu_custom_call" | custom-call | flops 150994944 | bytes 6291456 | tf_op jit(solution)/shard_map/backward_1/pallas_call | solution.py:205
  245.7 3.8 %all-to-all-start.6 = ((bf16[16,4,32,256]{3,2,1,0:T(8,128)(2,1)}), bf16[16,4,32,256]{3,2,1,0:T(8,128)(2,1)S(1)}, u32[]{:S(2)}, u32[]{:S(2)}) async-start(bf16[16,4,32,256]{3,2,1,0:T(8,128)(2,1)} %get-tuple-element.28), calls=%async_computation.6 | async-start | bytes 2097152 | tf_op jit(solution)/shard_map/backward_0/all_to_all | solution.py:345
  249.7 1.3 collective-permute-done.20
  251.0 1.4 collective-permute-start.21
  252.4 2.2 collective-permute-start.23
  254.6 5.8 %collective-permute-start.22 = (bf16[4,32,256]{2,1,0:T(8,128)(2,1)S(1)}, bf16[4,32,256]{2,1,0:T(8,128)(2,1)S(1)}, u32[]{:S(2)}, u32[]{:S(2)}) collective-permute-start(bf16[4,32,256]{2,1,0:T(8,128)(2,1)S(1)} %get-tuple-element.60), channel_id=1, source_target_pairs={{0,2},{4,6},{8,10},{12,14},{16,18},{20,22},{24,26},{28,30},{32,34}... | collective-permute-start | bytes 196616 | tf_op jit(solution)/shard_map/forward_0_by_columns/ppermute | solution.py:340
  260.4 1.9 collective-permute-done.22
  264.0 5.4 %backward_0.1 = bf16[4,32,256]{2,1,0:T(8,128)(2,1)} custom-call(s32[1]{0:T(128)} %bitcast.1.plane_ref, s32[4,8]{1,0:T(4,128)} %get-tuple-element.73.at_ref, bf16[64,32,256]{2,1,0:T(8,128)(2,1)} %bitcast.125, f32[4,32,256]{2,1,0:T(8,128)} %fusion.7.f_ref, bf16[4,256,256]{2,1,0:T(8,128)(2,1)} %get-tuple-element.44.inv_ref, bf16[8,256,256]{2,1,0:T(8,128)(2,1)} %copy-done.4, ...), custom_call_target="tpu_custom_call" | custom-call | flops 150994944 | bytes 6291456 | tf_op jit(solution)/shard_map/backward_0/pallas_call | solution.py:205
  270.5 1.5 collective-permute-done.24
  272.1 16.3 %all_to_all.43 = bf16[4,2,2,2,32,256]{5,4,3,2,1,0:T(8,128)(2,1)S(1)} all-to-all(bf16[4,2,2,2,32,256]{5,4,3,2,1,0:T(8,128)(2,1)S(1)} %pad_maximum_fusion.1), channel_id=1, replica_groups=mesh['x'=4,'y'=4,'c'=2,'z'=4] {'z'}, dimensions={0} | all-to-all | bytes 1048576 | tf_op jit(solution)/shard_map/to_planes/all_to_all | solution.py:359
  289.3 2.3 to_planes.1
  (98 shorter events, 12.0 us)
Async XLA Ops:
  7.2 14.3 %collective-permute-start.3 = (bf16[2,8,256,256]{3,2,1,0:T(8,128)(2,1)}, bf16[2,8,256,256]{3,2,1,0:T(8,128)(2,1)S(1)}, u32[]{:S(2)}, u32[]{:S(2)}) collective-permute-start(bf16[2,8,256,256]{3,2,1,0:T(8,128)(2,1)} %bitcast.119), channel_id=1, source_target_pairs={{0,4},{4,0},{1,5},{5,1},{2,6},{6,2},{3,7},{7,3},{8,12},{12,8},{9,1... | collective-permute-start | bytes 6291464 | tf_op jit(solution)/shard_map/factor_step_1/ppermute | solution.py:256
  7.9 12.2 %collective-permute-start.1 = (s32[2,8]{1,0:T(2,128)S(1)}, s32[2,8]{1,0:T(2,128)S(1)}, u32[]{:S(2)}, u32[]{:S(2)}) collective-permute-start(s32[2,8]{1,0:T(2,128)S(1)} %bitcast.148), channel_id=1, source_target_pairs={{0,4},{4,0},{1,5},{5,1},{2,6},{6,2},{3,7},{7,3},{8,12},{12,8},{9,1... | collective-permute-start | bytes 200 | tf_op jit(solution)/shard_map/level_0/ppermute | solution.py:256
  11.7 2.2 collective-permute-start.7
  13.5 7.3 %collective-permute-start.2 = (bf16[2,128,256]{2,1,0:T(8,128)(2,1)S(1)}, bf16[2,128,256]{2,1,0:T(8,128)(2,1)S(1)}, u32[]{:S(2)}, u32[]{:S(2)}) collective-permute-start(bf16[2,128,256]{2,1,0:T(8,128)(2,1)S(1)} %get-tuple-element.63), channel_id=1, source_target_pairs={{0,4},{4,0},{1,5},{5,1},{2,6},{6,2},{3,7},{7,3},{8,12},{12,8},{9,1... | collective-permute-start | bytes 393224 | tf_op jit(solution)/shard_map/level_0/ppermute | solution.py:256
  14.7 14.6 %all-to-all-start.1 = ((bf16[4,2,2,32,256]{4,3,2,1,0:T(8,128)(2,1)}), bf16[4,2,2,32,256]{4,3,2,1,0:T(8,128)(2,1)S(1)}, u32[]{:S(2)}, u32[]{:S(2)}) async-start(bf16[4,2,2,32,256]{4,3,2,1,0:T(8,128)(2,1)} %copy.17), calls=%async_computation.1 | async-start | bytes 524288 | tf_op jit(solution)/shard_map/rhs_by_columns/all_to_all | solution.py:321
  21.5 1.3 copy-start.7
  29.4 7.3 %copy-start.12 = (bf16[1,2,1,256,256]{4,3,2,1,0:T(8,128)(2,1)S(1)}, bf16[1,2,1,256,256]{4,3,2,1,0:T(8,128)(2,1)}, u32[]{:S(2)}) copy-start(bf16[1,2,1,256,256]{4,3,2,1,0:T(8,128)(2,1)} %param.5) | copy-start | bytes 786436
  29.4 79.8 %all-to-all-start = ((bf16[16,4,128,256]{3,2,1,0:T(8,128)(2,1)}), bf16[16,4,128,256]{3,2,1,0:T(8,128)(2,1)}, u32[]{:S(2)}, u32[]{:S(2)}) async-start(bf16[16,4,128,256]{3,2,1,0:T(8,128)(2,1)} %bitcast.121), calls=%async_computation | async-start | bytes 8388608 | tf_op jit(solution)/shard_map/level_0/all_to_all | solution.py:289
  36.6 35.9 %all-gather.3.cloned.1.call-start = ((), (), s32[]{:S(2)}) async-start(), calls=%async_computation.8 | async-start | bytes 1392640 | tf_op jit(solution)/shard_map/inverses_and_patterns/all_gather | solution.py:279
  39.1 42.5 %copy-start.4 = (bf16[8,256,256]{2,1,0:T(8,128)(2,1)}, bf16[8,256,256]{2,1,0:T(8,128)(2,1)S(1)}, u32[]{:S(2)}) copy-start(bf16[8,256,256]{2,1,0:T(8,128)(2,1)S(1)} %get-tuple-element.52.rest_1_.rest_2_.rest_0_) | copy-start | bytes 3145732
  39.1 42.5 %copy-start.5 = (bf16[8,256,256]{2,1,0:T(8,128)(2,1)}, bf16[8,256,256]{2,1,0:T(8,128)(2,1)S(1)}, u32[]{:S(2)}) copy-start(bf16[8,256,256]{2,1,0:T(8,128)(2,1)S(1)} %get-tuple-element.53.rest_5_.rest_6_.rest_4_) | copy-start | bytes 3145732
  39.1 34.6 %collective-permute-start.10 = (bf16[8,256,256]{2,1,0:T(8,128)(2,1)S(1)}, bf16[8,256,256]{2,1,0:T(8,128)(2,1)S(1)}, u32[]{:S(2)}, u32[]{:S(2)}) collective-permute-start(bf16[8,256,256]{2,1,0:T(8,128)(2,1)S(1)} %get-tuple-element.52.rest_1_.rest_2_.rest_0_), channel_id=1, source_target_pairs={{0,1},{1,2},{2,3},{4,5},{5,6},{6,7},{8,9},{9,10},{10,11},{12,13},{... | collective-permute-start | bytes 3145736 | tf_op jit(solution)/shard_map/factor_step_1/ppermute | solution.py:273
  43.1 34.9 %collective-permute-start.8 = (bf16[8,256,256]{2,1,0:T(8,128)(2,1)S(1)}, bf16[8,256,256]{2,1,0:T(8,128)(2,1)}, u32[]{:S(2)}, u32[]{:S(2)}) collective-permute-start(bf16[8,256,256]{2,1,0:T(8,128)(2,1)S(1)} %get-tuple-element.53.rest_5_.rest_6_.rest_4_), channel_id=1, source_target_pairs={{0,3},{1,0},{2,1},{4,7},{5,4},{6,5},{8,11},{9,8},{10,9},{12,15},{1... | collective-permute-start | bytes 3145736 | tf_op jit(solution)/shard_map/factor_step_1/ppermute | solution.py:274
  72.5 14.7 %collective-permute-start = (bf16[4,2,272,256]{3,2,1,0:T(8,128)(2,1)}, bf16[4,2,272,256]{3,2,1,0:T(8,128)(2,1)}, u32[]{:S(2)}, u32[]{:S(2)}) collective-permute-start(bf16[4,2,272,256]{3,2,1,0:T(8,128)(2,1)} %bitcast.122), channel_id=1, source_target_pairs={{0,4},{4,0},{1,5},{5,1},{2,6},{6,2},{3,7},{7,3},{8,12},{12,8},{9,1... | collective-permute-start | bytes 3342344 | tf_op jit(solution)/shard_map/inverses_and_patterns/ppermute | solution.py:256
  72.6 17.2 %copy-start.8 = (bf16[2,8,256,256]{3,2,1,0:T(8,128)(2,1)S(1)}, bf16[2,8,256,256]{3,2,1,0:T(8,128)(2,1)}, u32[]{:S(2)}) copy-start(bf16[2,8,256,256]{3,2,1,0:T(8,128)(2,1)} %copy-done.7) | copy-start | bytes 6291460
  73.8 7.8 %copy-start.3 = (bf16[8,256,256]{2,1,0:T(8,128)(2,1)}, bf16[8,256,256]{2,1,0:T(8,128)(2,1)S(1)}, u32[]{:S(2)}) copy-start(bf16[8,256,256]{2,1,0:T(8,128)(2,1)S(1)} %collective-permute-done.10.rest_2_.rest_3_.rest_1_) | copy-start | bytes 3145732
  73.8 18.2 %collective-permute-start.13 = (bf16[8,256,256]{2,1,0:T(8,128)(2,1)S(1)}, bf16[8,256,256]{2,1,0:T(8,128)(2,1)S(1)}, u32[]{:S(2)}, u32[]{:S(2)}) collective-permute-start(bf16[8,256,256]{2,1,0:T(8,128)(2,1)S(1)} %collective-permute-done.10.rest_2_.rest_3_.rest_1_), channel_id=1, source_target_pairs={{0,4},{4,0},{1,5},{5,1},{2,6},{6,2},{3,7},{7,3},{8,12},{12,8},{9,1... | collective-permute-start | bytes 3145736 | tf_op jit(solution)/shard_map/factor_step_2/ppermute | solution.py:256
  81.6 24.3 %collective-permute-start.11 = (bf16[8,256,256]{2,1,0:T(8,128)(2,1)S(1)}, bf16[8,256,256]{2,1,0:T(8,128)(2,1)S(1)}, u32[]{:S(2)}, u32[]{:S(2)}) collective-permute-start(bf16[8,256,256]{2,1,0:T(8,128)(2,1)S(1)} %get-tuple-element.41), channel_id=1, source_target_pairs={{0,1},{1,2},{2,3},{3,0},{4,5},{5,6},{6,7},{7,4},{8,9},{9,10},{10,1... | collective-permute-start | bytes 3145736 | tf_op jit(solution)/shard_map/factor_step_2/ppermute | solution.py:292
  83.1 26.1 %collective-permute-start.9 = (bf16[8,256,256]{2,1,0:T(8,128)(2,1)S(1)}, bf16[8,256,256]{2,1,0:T(8,128)(2,1)S(1)}, u32[]{:S(2)}, u32[]{:S(2)}) collective-permute-start(bf16[8,256,256]{2,1,0:T(8,128)(2,1)S(1)} %get-tuple-element.48), channel_id=1, source_target_pairs={{0,3},{1,0},{2,1},{3,2},{4,7},{5,4},{6,5},{7,6},{8,11},{9,8},{10,9... | collective-permute-start | bytes 3145736 | tf_op jit(solution)/shard_map/factor_step_2/ppermute | solution.py:293
  84.9 27.7 %collective-permute-start.17 = (bf16[8,256,256]{2,1,0:T(8,128)(2,1)}, bf16[8,256,256]{2,1,0:T(8,128)(2,1)}, u32[]{:S(2)}, u32[]{:S(2)}) collective-permute-start(bf16[8,256,256]{2,1,0:T(8,128)(2,1)} %get-tuple-element.40), channel_id=1, source_target_pairs={{1,2},{2,3},{5,6},{6,7},{9,10},{10,11},{13,14},{14,15},{17,18},{18... | collective-permute-start | bytes 3145736 | tf_op jit(solution)/shard_map/factor_step_3/ppermute | solution.py:296
  87.2 4.0 %copy-start.9 = (bf16[8,272,256]{2,1,0:T(8,128)(2,1)S(1)}, bf16[8,272,256]{2,1,0:T(8,128)(2,1)}, u32[]{:S(2)}) copy-start(bf16[8,272,256]{2,1,0:T(8,128)(2,1)} %all-gather.3.cloned.1.call-done) | copy-start | bytes 3342340
  87.2 42.2 %collective-permute-start.16 = (bf16[8,256,256]{2,1,0:T(8,128)(2,1)}, bf16[8,256,256]{2,1,0:T(8,128)(2,1)}, u32[]{:S(2)}, u32[]{:S(2)}) collective-permute-start(bf16[8,256,256]{2,1,0:T(8,128)(2,1)} %get-tuple-element.49), channel_id=1, source_target_pairs={{0,3},{1,0},{4,7},{5,4},{8,11},{9,8},{12,15},{13,12},{16,19},{17,1... | collective-permute-start | bytes 3145736 | tf_op jit(solution)/shard_map/factor_step_3/ppermute | solution.py:297
  92.0 17.1 %copy-start.6 = (bf16[8,256,256]{2,1,0:T(8,128)(2,1)}, bf16[8,256,256]{2,1,0:T(8,128)(2,1)S(1)}, u32[]{:S(2)}) copy-start(bf16[8,256,256]{2,1,0:T(8,128)(2,1)S(1)} %collective-permute-done.13.rest_10_.rest_11_.rest_9_) | copy-start | bytes 3145732
  92.0 46.7 %collective-permute-start.15 = (bf16[8,256,256]{2,1,0:T(8,128)(2,1)}, bf16[8,256,256]{2,1,0:T(8,128)(2,1)}, u32[]{:S(2)}, u32[]{:S(2)}) collective-permute-start(bf16[8,256,256]{2,1,0:T(8,128)(2,1)} %collective-permute-done.8.rest_4_.rest_5_.rest_7_), channel_id=1, source_target_pairs={{0,4},{4,0},{1,5},{5,1},{2,6},{6,2},{3,7},{7,3},{8,12},{12,8},{9,1... | collective-permute-start | bytes 3145736 | tf_op jit(solution)/shard_map/factor_step_2/ppermute | solution.py:256
  105.9 6.6 %copy-start = (bf16[8,256,256]{2,1,0:T(8,128)(2,1)}, bf16[8,256,256]{2,1,0:T(8,128)(2,1)S(1)}, u32[]{:S(2)}) copy-start(bf16[8,256,256]{2,1,0:T(8,128)(2,1)S(1)} %collective-permute-done.11.rest_3_.rest_6_.rest_0_.rest_5_) | copy-start | bytes 3145732
  105.9 32.8 %collective-permute-start.14 = (bf16[8,256,256]{2,1,0:T(8,128)(2,1)S(1)}, bf16[8,256,256]{2,1,0:T(8,128)(2,1)S(1)}, u32[]{:S(2)}, u32[]{:S(2)}) collective-permute-start(bf16[8,256,256]{2,1,0:T(8,128)(2,1)S(1)} %collective-permute-done.11.rest_3_.rest_6_.rest_0_.rest_5_), channel_id=1, source_target_pairs={{0,4},{4,0},{1,5},{5,1},{2,6},{6,2},{3,7},{7,3},{8,12},{12,8},{9,1... | collective-permute-start | bytes 3145736 | tf_op jit(solution)/shard_map/factor_step_3/ppermute | solution.py:256
  109.2 3.4 %copy-start.1 = (bf16[8,256,256]{2,1,0:T(8,128)(2,1)}, bf16[8,256,256]{2,1,0:T(8,128)(2,1)S(1)}, u32[]{:S(2)}) copy-start(bf16[8,256,256]{2,1,0:T(8,128)(2,1)S(1)} %collective-permute-done.9.rest_0_.rest_7_.rest_1_.rest_6_) | copy-start | bytes 3145732
  109.2 29.6 %collective-permute-start.12 = (bf16[8,256,256]{2,1,0:T(8,128)(2,1)S(1)}, bf16[8,256,256]{2,1,0:T(8,128)(2,1)}, u32[]{:S(2)}, u32[]{:S(2)}) collective-permute-start(bf16[8,256,256]{2,1,0:T(8,128)(2,1)S(1)} %collective-permute-done.9.rest_0_.rest_7_.rest_1_.rest_6_), channel_id=1, source_target_pairs={{0,4},{4,0},{1,5},{5,1},{2,6},{6,2},{3,7},{7,3},{8,12},{12,8},{9,1... | collective-permute-start | bytes 3145736 | tf_op jit(solution)/shard_map/factor_step_3/ppermute | solution.py:256
  112.6 20.7 %collective-permute-start.4 = (bf16[4,32,256]{2,1,0:T(8,128)(2,1)S(1)}, bf16[4,32,256]{2,1,0:T(8,128)(2,1)S(1)}, u32[]{:S(2)}, u32[]{:S(2)}) collective-permute-start(bf16[4,32,256]{2,1,0:T(8,128)(2,1)S(1)} %get-tuple-element.70), channel_id=1, source_target_pairs={{0,1},{4,5},{8,9},{12,13},{16,17},{20,21},{24,25},{28,29},{32,33},... | collective-permute-start | bytes 196616 | tf_op jit(solution)/shard_map/level_0_to_columns/ppermute | solution.py:317
  129.5 8.1 %collective-permute-start.6 = (bf16[4,32,256]{2,1,0:T(8,128)(2,1)S(1)}, bf16[4,32,256]{2,1,0:T(8,128)(2,1)S(1)}, u32[]{:S(2)}, u32[]{:S(2)}) collective-permute-start(bf16[4,32,256]{2,1,0:T(8,128)(2,1)S(1)} %get-tuple-element.71), channel_id=1, source_target_pairs={{0,3},{4,7},{8,11},{12,15},{16,19},{20,23},{24,27},{28,31},{32,35}... | collective-permute-start | bytes 196616 | tf_op jit(solution)/shard_map/level_0_to_columns/ppermute | solution.py:317
  133.4 4.2 %collective-permute-start.5 = (bf16[4,32,256]{2,1,0:T(8,128)(2,1)S(1)}, bf16[4,32,256]{2,1,0:T(8,128)(2,1)S(1)}, u32[]{:S(2)}, u32[]{:S(2)}) collective-permute-start(bf16[4,32,256]{2,1,0:T(8,128)(2,1)S(1)} %get-tuple-element.72), channel_id=1, source_target_pairs={{0,2},{4,6},{8,10},{12,14},{16,18},{20,22},{24,26},{28,30},{32,34}... | collective-permute-start | bytes 196616 | tf_op jit(solution)/shard_map/level_0_to_columns/ppermute | solution.py:317
  137.6 14.2 %collective-permute-start.19 = (bf16[8,256,256]{2,1,0:T(8,128)(2,1)}, bf16[8,256,256]{2,1,0:T(8,128)(2,1)}, u32[]{:S(2)}, u32[]{:S(2)}) collective-permute-start(bf16[8,256,256]{2,1,0:T(8,128)(2,1)} %collective-permute-done.17.rest_7_.rest_2_), channel_id=1, source_target_pairs={{0,4},{4,0},{1,5},{5,1},{2,6},{6,2},{3,7},{7,3},{8,12},{12,8},{9,1... | collective-permute-start | bytes 3145736 | tf_op jit(solution)/shard_map/factor_step_3/ppermute | solution.py:256
  137.6 14.2 %collective-permute-start.18 = (bf16[8,256,256]{2,1,0:T(8,128)(2,1)}, bf16[8,256,256]{2,1,0:T(8,128)(2,1)}, u32[]{:S(2)}, u32[]{:S(2)}) collective-permute-start(bf16[8,256,256]{2,1,0:T(8,128)(2,1)} %collective-permute-done.16.rest_4_.rest_3_), channel_id=1, source_target_pairs={{0,4},{4,0},{1,5},{5,1},{2,6},{6,2},{3,7},{7,3},{8,12},{12,8},{9,1... | collective-permute-start | bytes 3145736 | tf_op jit(solution)/shard_map/factor_step_3/ppermute | solution.py:256
  138.7 1.0 copy-start.2
  145.2 24.7 %all-to-all-start.2 = ((bf16[16,4,32,256]{3,2,1,0:T(8,128)(2,1)}), bf16[16,4,32,256]{3,2,1,0:T(8,128)(2,1)S(1)}, u32[]{:S(2)}, u32[]{:S(2)}) async-start(bf16[16,4,32,256]{3,2,1,0:T(8,128)(2,1)} %bitcast.128), calls=%async_computation.2 | async-start | bytes 2097152 | tf_op jit(solution)/shard_map/forward_1/all_to_all | solution.py:330
  245.7 3.8 %copy-start.15 = (bf16[1,2,128,256]{3,2,1,0:T(8,128)(2,1)S(1)}, bf16[1,2,128,256]{3,2,1,0:T(8,128)(2,1)}, u32[]{:S(2)}) copy-start(bf16[1,2,128,256]{3,2,1,0:T(8,128)(2,1)} %get-tuple-element.61) | copy-start | bytes 393220
  245.7 17.2 %copy-start.13 = (f32[4,32,256]{2,1,0:T(8,128)S(1)}, f32[4,32,256]{2,1,0:T(8,128)}, u32[]{:S(2)}) copy-start(f32[4,32,256]{2,1,0:T(8,128)} %get-tuple-element.21.f_ref) | copy-start | bytes 393220
  245.7 17.2 %copy-start.14 = (f32[4,32,256]{2,1,0:T(8,128)S(1)}, f32[4,32,256]{2,1,0:T(8,128)}, u32[]{:S(2)}) copy-start(f32[4,32,256]{2,1,0:T(8,128)} %get-tuple-element.23.f_ref) | copy-start | bytes 393220
  245.7 17.2 %copy-start.16 = (f32[4,32,256]{2,1,0:T(8,128)S(1)}, f32[4,32,256]{2,1,0:T(8,128)}, u32[]{:S(2)}) copy-start(f32[4,32,256]{2,1,0:T(8,128)} %get-tuple-element.25) | copy-start | bytes 393220
  245.7 17.3 %all-to-all-start.6 = ((bf16[16,4,32,256]{3,2,1,0:T(8,128)(2,1)}), bf16[16,4,32,256]{3,2,1,0:T(8,128)(2,1)S(1)}, u32[]{:S(2)}, u32[]{:S(2)}) async-start(bf16[16,4,32,256]{3,2,1,0:T(8,128)(2,1)} %get-tuple-element.28), calls=%async_computation.6 | async-start | bytes 2097152 | tf_op jit(solution)/shard_map/backward_0/all_to_all | solution.py:345
  249.6 1.4 collective-permute-start.20
  251.0 9.3 %collective-permute-start.21 = (bf16[4,32,256]{2,1,0:T(8,128)(2,1)S(1)}, bf16[4,32,256]{2,1,0:T(8,128)(2,1)S(1)}, u32[]{:S(2)}, u32[]{:S(2)}) collective-permute-start(bf16[4,32,256]{2,1,0:T(8,128)(2,1)S(1)} %get-tuple-element.58), channel_id=1, source_target_pairs={{0,1},{4,5},{8,9},{12,13},{16,17},{20,21},{24,25},{28,29},{32,33},... | collective-permute-start | bytes 196616 | tf_op jit(solution)/shard_map/forward_0_by_columns/ppermute | solution.py:340
  252.4 8.0 %collective-permute-start.23 = (bf16[4,32,256]{2,1,0:T(8,128)(2,1)S(1)}, bf16[4,32,256]{2,1,0:T(8,128)(2,1)S(1)}, u32[]{:S(2)}, u32[]{:S(2)}) collective-permute-start(bf16[4,32,256]{2,1,0:T(8,128)(2,1)S(1)} %get-tuple-element.59), channel_id=1, source_target_pairs={{0,3},{4,7},{8,11},{12,15},{16,19},{20,23},{24,27},{28,31},{32,35}... | collective-permute-start | bytes 196616 | tf_op jit(solution)/shard_map/forward_0_by_columns/ppermute | solution.py:340
  254.6 7.7 %collective-permute-start.22 = (bf16[4,32,256]{2,1,0:T(8,128)(2,1)S(1)}, bf16[4,32,256]{2,1,0:T(8,128)(2,1)S(1)}, u32[]{:S(2)}, u32[]{:S(2)}) collective-permute-start(bf16[4,32,256]{2,1,0:T(8,128)(2,1)S(1)} %get-tuple-element.60), channel_id=1, source_target_pairs={{0,2},{4,6},{8,10},{12,14},{16,18},{20,22},{24,26},{28,30},{32,34}... | collective-permute-start | bytes 196616 | tf_op jit(solution)/shard_map/forward_0_by_columns/ppermute | solution.py:340
  264.0 5.4 %copy-start.17 = (bf16[4,32,256]{2,1,0:T(8,128)(2,1)S(1)}, bf16[4,32,256]{2,1,0:T(8,128)(2,1)}, u32[]{:S(2)}) copy-start(bf16[4,32,256]{2,1,0:T(8,128)(2,1)} %get-tuple-element.31) | copy-start | bytes 196612
  264.0 5.4 %copy-start.18 = (bf16[4,32,256]{2,1,0:T(8,128)(2,1)S(1)}, bf16[4,32,256]{2,1,0:T(8,128)(2,1)}, u32[]{:S(2)}) copy-start(bf16[4,32,256]{2,1,0:T(8,128)(2,1)} %get-tuple-element.30) | copy-start | bytes 196612
  264.0 5.4 %copy-start.19 = (bf16[4,32,256]{2,1,0:T(8,128)(2,1)S(1)}, bf16[4,32,256]{2,1,0:T(8,128)(2,1)}, u32[]{:S(2)}) copy-start(bf16[4,32,256]{2,1,0:T(8,128)(2,1)} %get-tuple-element.29) | copy-start | bytes 196612
  270.4 1.6 collective-permute-start.24
  (2 other events, 2.0 us)
Sparse Core Ops, SparseCore 0:
  39.7 32.7 all-gather.2

commit v3 on v0

v3 whole, which is shorter than its diff:
```python
import functools

import jax
import jax.numpy as jnp
from jax import lax
from jax.experimental import pallas as pl
from jax.experimental.pallas import tpu as pltpu
from jax.sharding import Mesh, PartitionSpec as P


BF = jnp.bfloat16
F32 = jnp.float32
MIB = 1024 * 1024
LIMIT = 14 * MIB
NODES = 64
CHIPS = 16
WIDTH = 256
FAN = 8
HALF = 128
COLS = 32
UP_1 = [(0, 1), (1, 2), (2, 3)]
DOWN_1 = [(0, 3), (1, 0), (2, 1)]
UP = [(z, (z + 1) % 4) for z in range(4)]
DOWN = [(z, (z + 3) % 4) for z in range(4)]


SMEM = pl.BlockSpec(memory_space=pltpu.SMEM)
VM = pl.BlockSpec(memory_space=pltpu.VMEM)


def dot_t(a, b):
    return lax.dot_general(a, b, (((1,), (1,)), ((), ())), preferred_element_type=F32)


def dot_n(a, b):
    return lax.dot_general(a, b, (((1,), (0,)), ((), ())), preferred_element_type=F32)


KEEP, SEND, INV, PAT, ROWS = 0, 64, 128, 640, 656


def pack_kernel(core_ref, rhs_ref, inv_ref, pat_ref, out_ref):
    core = core_ref[0]
    for z in range(4):
        for j in range(2):
            out_ref[z, INV + j * WIDTH : INV + (j + 1) * WIDTH] = inv_ref[j]
        out_ref[z, PAT:ROWS] = pat_ref[...]
    for j in range(2):
        rt = jnp.transpose(rhs_ref[j]).astype(BF)
        for half in range(2):
            at = pl.multiple_of(jnp.where(core == half, KEEP, SEND) + j * COLS, COLS)
            for z in range(4):
                first = half * HALF + z * COLS
                out_ref[z, pl.ds(at, COLS)] = rt[first : first + COLS]


def pack(core, rhs, inverse, pat):
    return pl.pallas_call(
        pack_kernel,
        out_shape=jax.ShapeDtypeStruct((4, ROWS, WIDTH), BF),
        in_specs=[SMEM, VM, VM, VM],
        out_specs=VM,
        compiler_params=pltpu.CompilerParams(vmem_limit_bytes=8 * MIB),
        cost_estimate=pl.CostEstimate(flops=0, bytes_accessed=2 * 2**20, transcendentals=0),
    )(core, rhs, inverse, pat)


def any_specs(count):
    return [pl.BlockSpec(memory_space=pl.ANY)] * count


def fetch(plane, choices, dst, sem):
    choices = [ref if at is None else ref.at[at] for ref, at in choices]
    for z, src in enumerate(choices):

        @pl.when(plane == z)
        def _():
            pltpu.make_async_copy(src, dst, sem).start()

    return pltpu.make_async_copy(choices[0], dst, sem)


A, B = "A", "B"
WHERE = {
    0: ([A, 0, 2, 3], [B, 2, 3, 1]),
    1: ([3, A, 0, 2], [1, B, 4, 5]),
    2: ([2, 3, A, 0], [5, 1, B, 4]),
}


def factor_copies(level, plane, refs, buf, sems):
    copies = []
    for n in range(4):
        base = refs[7 * (n // 2) : 7 * (n // 2) + 7]
        choices = [(base[0], "AB".index(k)) if k in (A, B) else (base[1 + k], None) for k in WHERE[level][n % 2]]
        copies.append(fetch(plane, choices, buf.at[n], sems.at[n]))
    return copies


def add_terms(n, at_ref, solved, buf, acc_ref):
    rows = buf.shape[1] * WIDTH
    terms = dot_t(solved, buf[n].reshape(rows, WIDTH))
    for p in range(FAN):
        acc_ref[at_ref[n, p]] += terms[:, p * WIDTH : (p + 1) * WIDTH]


def message_copies(level, refs, bufs, sems, parts):
    copies = []
    for r in range(2):
        for k in parts:
            at, size = ((KEEP, SEND)[r], 2 * COLS) if k == 0 else (INV, 2 * WIDTH)
            src = refs[r].at[level, pl.ds(at, size)]
            copies.append(pltpu.make_async_copy(src, bufs[k].at[pl.ds(r * size, size)], sems.at[r, k]))
            copies[-1].start()
    return copies


def rows_of(buf, n, size):
    return buf[n * size : (n + 1) * size]


def forward_kernel(level, plane_ref, at_ref, *rest):
    gots, rest = (rest[:1], rest[1:]) if level else ((), rest)
    told, refs, (f_ref, fb_ref, share_ref, rows, inv, msems, buf, sems, acc_ref) = rest[:2], rest[2:16], rest[16:]
    copies_m = message_copies(level, told, (rows, inv), msems, (0, 1))
    copies = factor_copies(level, plane_ref[0], refs, buf, sems)
    acc_ref[...] = jnp.zeros_like(acc_ref)
    for copy in copies_m:
        copy.wait()
    for n in range(4):
        resid = rows_of(rows, n, COLS)
        if level:
            resid = (resid.astype(F32) - jnp.sum(gots[0][:, n].astype(F32), axis=0)).astype(BF)
        f = dot_t(resid, rows_of(inv, n, WIDTH))
        solved = f.astype(BF)
        f_ref[n] = f
        fb_ref[n] = solved
        copies[n].wait()
        add_terms(n, at_ref, solved, buf, acc_ref)
    share_ref[...] = acc_ref[...].astype(BF)


SMALL = [
    pltpu.VMEM((4 * COLS, WIDTH), BF),
    pltpu.VMEM((4 * WIDTH, WIDTH), BF),
    pltpu.SemaphoreType.DMA((2, 2)),
]
LARGE = [
    pltpu.VMEM((4, FAN, WIDTH, WIDTH), BF),
    pltpu.SemaphoreType.DMA((4,)),
]
NODE_F32 = jax.ShapeDtypeStruct((4, COLS, WIDTH), F32)
NODE_BF = jax.ShapeDtypeStruct((4, COLS, WIDTH), BF)
COPIES = jax.ShapeDtypeStruct((CHIPS, 4, COLS, WIDTH), BF)


def forward_level(level, plane, at, gots, told, factors):
    return pl.pallas_call(
        functools.partial(forward_kernel, level),
        in_specs=[SMEM, SMEM] + [VM] * len(gots) + any_specs(16),
        out_specs=(VM, VM, VM),
        scratch_shapes=SMALL + LARGE + [pltpu.VMEM((NODES, COLS, WIDTH), F32)],
        out_shape=(NODE_F32, NODE_BF, jax.ShapeDtypeStruct((NODES, COLS, WIDTH), BF)),
        compiler_params=pltpu.CompilerParams(vmem_limit_bytes=LIMIT),
        cost_estimate=pl.CostEstimate(flops=2 * 36 * COLS * WIDTH**2, bytes_accessed=6 * 2**20, transcendentals=0),
    )(plane, at, *gots, *told, *factors)


def top_kernel(got_ref, own_told, other_told, fb_ref, sol_ref, copies_ref, rows, inv, msems):
    for copy in message_copies(3, (own_told, other_told), (rows, inv), msems, (0, 1)):
        copy.wait()
    for n in range(4):
        inflow = jnp.sum(got_ref[:, n].astype(F32), axis=0)
        resid = (rows_of(rows, n, COLS).astype(F32) - inflow).astype(BF)
        fb = dot_t(resid, rows_of(inv, n, WIDTH)).astype(BF)
        fb_ref[n] = fb
        sol = dot_n(fb, rows_of(inv, n, WIDTH)).astype(BF)
        sol_ref[n] = sol
        for k in range(CHIPS):
            copies_ref[k, n] = sol


def top_level(got, told):
    return pl.pallas_call(
        top_kernel,
        in_specs=[VM] + any_specs(2),
        out_specs=(VM, VM, VM),
        scratch_shapes=SMALL,
        out_shape=(NODE_BF, NODE_BF, COPIES),
        compiler_params=pltpu.CompilerParams(vmem_limit_bytes=8 * MIB),
        cost_estimate=pl.CostEstimate(flops=2 * 8 * COLS * WIDTH**2, bytes_accessed=3 * 2**20, transcendentals=0),
    )(got, *told)


def backward_kernel(level, plane_ref, at_ref, above_ref, f_ref, *rest):
    told, refs, outs, (rows, inv, msems, buf, sems) = rest[:2], rest[2:16], rest[16:-5], rest[-5:]
    copies_m = message_copies(level, told, (rows, inv), msems, (1,))
    copies = factor_copies(level, plane_ref[0], refs, buf, sems)
    for copy in copies_m:
        copy.wait()
    for n in range(4):
        picked = jnp.concatenate([above_ref[at_ref[n, p]] for p in range(FAN)], axis=1)
        copies[n].wait()
        back = dot_n(picked, buf[n].reshape(FAN * WIDTH, WIDTH))
        upper = (f_ref[n] - back).astype(BF)
        sol = dot_n(upper, rows_of(inv, n, WIDTH)).astype(BF)
        outs[0][n] = sol
        if level:
            for k in range(CHIPS):
                outs[1][k, n] = sol


def backward_level(level, plane, at, above, f, told, factors):
    out_shape = (NODE_BF, COPIES) if level else (NODE_BF,)
    return pl.pallas_call(
        functools.partial(backward_kernel, level),
        in_specs=[SMEM, SMEM, VM, VM] + any_specs(16),
        out_specs=(VM,) * len(out_shape),
        scratch_shapes=SMALL + LARGE,
        out_shape=out_shape,
        compiler_params=pltpu.CompilerParams(vmem_limit_bytes=LIMIT),
        cost_estimate=pl.CostEstimate(flops=2 * 36 * COLS * WIDTH**2, bytes_accessed=6 * 2**20, transcendentals=0),
    )(plane, at, above, f, *told, *factors)


def last_kernel(core_ref, fx_ref, forward_ref, result_ref):
    core = core_ref[0]
    for k, out_ref in enumerate((forward_ref, result_ref)):
        for j in range(2):
            halves = []
            for half in range(2):
                rel = jnp.bitwise_xor(core, half)
                halves += [fx_ref[z, rel, k, j] for z in range(4)]
            out_ref[j] = jnp.transpose(jnp.concatenate(halves, axis=0).astype(F32))


def last_step(core, fx):
    return pl.pallas_call(
        last_kernel,
        out_shape=(jax.ShapeDtypeStruct((2, WIDTH, WIDTH), F32),) * 2,
        in_specs=[SMEM, VM],
        out_specs=(VM, VM),
        compiler_params=pltpu.CompilerParams(vmem_limit_bytes=8 * MIB),
        cost_estimate=pl.CostEstimate(flops=0, bytes_accessed=2 * 2**20, transcendentals=0),
    )(core, fx)


def swap(value):
    return lax.ppermute(value, "c", [(0, 1), (1, 0)])


def exchange(value):
    return lax.all_to_all(value.reshape(CHIPS, 4, COLS, WIDTH), ("x", "y"), 0, 0, tiled=True)


def on_device(rhs, inverses, blocks, pattern):
    core = lax.axis_index("c").astype(jnp.int32)
    plane = lax.axis_index("z").astype(jnp.int32)
    core1, plane1 = core.reshape(1), plane.reshape(1)
    factor = blocks.reshape(2, FAN, WIDTH, WIDTH)

    with jax.named_scope("factor_step_1"):
        own_a, own_b = factor[0], factor[1]
        up_1 = lax.ppermute(own_a, "z", UP_1)
        down_1 = lax.ppermute(own_b, "z", DOWN_1)
        near = swap(factor)

    with jax.named_scope("tell_planes"):
        pat = jnp.pad(pattern.reshape(2, FAN).astype(BF), ((0, ROWS - PAT - 2), (0, WIDTH - FAN)))
        message = pack(core1, rhs.reshape(2, WIDTH, WIDTH), inverses.reshape(2, WIDTH, WIDTH), pat)
        told = lax.all_to_all(message, "z", 0, 0, tiled=True)
        told = (told, swap(told))
        targets = jnp.concatenate([t[:, PAT : PAT + 2, :FAN] for t in told], axis=1).astype(jnp.int32)
        targets = jnp.clip(targets, 0, NODES - 1)
        places = (targets % 32) // 2 * 4 + jnp.bitwise_xor(targets % 2, core) * 2 + targets // 32
        places = [places[k] for k in range(4)]

    with jax.named_scope("factor_step_2"):
        up_2 = lax.ppermute(jnp.where(plane == 0, own_b, up_1), "z", UP)
        down_2 = lax.ppermute(jnp.where(plane == 3, down_1, own_a), "z", DOWN)
        up_1o, down_1o = swap(up_1), swap(down_1)
        up_2, down_2, own_3, down_1 = lax.optimization_barrier((up_2, down_2, own_b, down_1))
        up_2o, down_2o = swap(up_2), swap(down_2)
    with jax.named_scope("factor_step_3"):
        up_3 = lax.ppermute(own_3, "z", [(1, 2), (2, 3)])
        down_3 = lax.ppermute(down_1, "z", [(0, 3), (1, 0)])

    factors = [factor, up_1, down_1, up_2, down_2, factor, factor]
    factors += [near, up_1o, down_1o, up_2o, down_2o, near, near]
    forward = [None] * 3
    solved = [None] * 4
    gots = ()
    for level in range(3):
        with jax.named_scope(f"forward_{level}"):
            forward[level], solved[level], share = forward_level(level, plane1, places[level], gots, told, factors)
            got = exchange(share)
            gots = (got,)
        if level == 0:
            with jax.named_scope("factor_step_3"):
                up_3, down_3, got = lax.optimization_barrier((up_3, down_3, got))
                gots = (got,)
                factors[5:7] = [up_3, down_3]
                factors[12:14] = [swap(up_3), swap(down_3)]
    result = [None] * 4
    with jax.named_scope("top"):
        solved[3], result[3], copies = top_level(got, told)

    for level in (2, 1, 0):
        with jax.named_scope(f"backward_{level}"):
            above = exchange(copies).reshape(NODES, COLS, WIDTH)
            out = backward_level(level, plane1, places[level], above, forward[level], told, factors)
            result[level] = out[0]
            if level > 0:
                copies = out[1]

    with jax.named_scope("to_planes"):
        fx = jnp.stack([jnp.stack(solved), jnp.stack(result)], axis=1).reshape(4, 2, 2, 2, COLS, WIDTH)
        fx = jnp.stack([fx[:, :, 0], swap(fx[:, :, 1])], axis=1)
        fx = lax.all_to_all(fx, "z", 0, 0, tiled=True)
        forward_out, result_out = last_step(core1, fx)
    shape = (1, 2, 1, WIDTH, WIDTH)
    return forward_out.reshape(shape), result_out.reshape(shape)


def solution(mesh):
    wide = Mesh(mesh.devices.reshape(4, 4, 2, 4), ("x", "y", "c", "z"))
    blk = ("x", "y", "c")
    return jax.shard_map(
        on_device,
        mesh=wide,
        in_specs=(
            P("z", None, blk, None, None),
            P("z", None, blk, None, None),
            P("z", None, blk, None, None, None),
            P("z", None, blk, None),
        ),
        out_specs=(P("z", None, blk, None, None), P("z", None, blk, None, None)),
        check_vma=False,
    )
```

time: 818 us -> 260 us (0.32)
  waiting for transfers between devices: 644 us -> 80.7 us
  blocking collectives: 0 us -> 105 us
  local copies, waits for them, and re-layouts: 91.7 us -> 16.2 us
  matrix products: 32.4 us -> 0 us
  Pallas kernels: 0 us -> 24.3 us
  starting transfers between devices: 15.2 us -> 31 us
  between operations: 14.8 us -> 1.08 us
  other arithmetic: 9.18 us -> 0.4 us
    psum x3 -> x0, waiting for transfers between devices: 380 us -> none  [fan_in_level(): summed = lax.psum(dense.astype(jnp.bfloat16), 'blk').astype(jnp.float32)]
    all_gather x3 -> x0, waiting for transfers between devices: 190 us -> none  [on_device(): parents = lax.all_gather(near, 'blk', axis=1, tiled=True)]
    all_to_all x0 -> x6, blocking collectives: none -> 105 us  [the longest x5 91.7 us: exchange(): lax.all_to_all(value.reshape(CHIPS, 4, COLS, WIDTH), ('x', 'y'), 0, 0, ti...]
    reshape x6 -> x0, local copies, waits for them, and re-layouts: 48.6 us -> none  [the longest x3 47 us: fan_in_level(): summed = summed.reshape(per_dev, groups, terms.shape[1])]
    all_to_all x0 -> x2, waiting for transfers between devices: none -> 37.6 us  [the longest x1 31.5 us: on_device(): told = lax.all_to_all(message, 'z', 0, 0, tiled=True)]
    dot_general x6 -> x0, matrix products: 32.4 us -> none  [the longest x3 26.1 us: fan_in_level(): dense = jnp.dot(onehot.T, terms, precision=lax.Precision.HIGHEST)]
    ppermute x6 -> x15, waiting for transfers between devices: 73.5 us -> 43.1 us  [the longest x1 22.6 us: on_device(): down_2 = lax.ppermute(jnp.where(plane == 3, down_1, own_a), 'z', DOWN)]
    pallas_call x0 -> x9, Pallas kernels: none -> 24.3 us  [the longest x3 11.4 us: forward_level(): pl.pallas_call(functools.partial(forward_kernel, level), in_specs=[SMEM,...]
  transfers between devices with their start and end apart: 12 -> 17, of which waited for: 12 -> 8; matrix products, arithmetic and copies ran while one was open for 0% -> 0% of each run, Pallas kernels for 0% -> 1%
where the time goes in v3:
time: 260 us; the launch traced here: 259 us
  blocking collectives  105 us (40%)
  waiting for transfers between devices  80.7 us (31%)
  starting transfers between devices  31 us (12%)
  Pallas kernels  24.3 us (9%)
  local copies, waits for them, and re-layouts  16.2 us (6%)
    all_to_all x5, blocking collectives, exchange(): lax.all_to_all(value.reshape(CHIPS, 4, COLS, WIDTH), ('x', 'y'), 0, 0, ti...  91.7 us
    all_to_all x1, waiting for transfers between devices, on_device(): told = lax.all_to_all(message, 'z', 0, 0, tiled=True)  31.5 us
    ppermute x1, waiting for transfers between devices, on_device(): down_2 = lax.ppermute(jnp.where(plane == 3, down_1, own_a), 'z', DOWN)  22.6 us
    all_to_all x1, blocking collectives, on_device(): fx = lax.all_to_all(fx, 'z', 0, 0, tiled=True)  13.5 us
    unnamed x57, local copies, waits for them, and re-layouts  13.1 us
    ppermute x1, waiting for transfers between devices, on_device(): down_3 = lax.ppermute(down_1, 'z', [(0, 3), (1, 0)])  11.7 us
    pallas_call x3, Pallas kernels, forward_level(): pl.pallas_call(functools.partial(forward_kernel, level), in_specs=[SMEM,...  11.4 us
    pallas_call x3, Pallas kernels, backward_level(): pl.pallas_call(functools.partial(backward_kernel, level), in_specs=[SMEM,...  10.6 us
  transfers between devices with their start and end apart: 17, of which 8 were waited for; matrix products, arithmetic and copies ran while one was open for 0% of the time, Pallas kernels for 1%

profile of v3, /device:TPU:0, one launch (start us, length us, event | category | flops | bytes accessed | tf_op | source)
XLA Modules:
  0.0 258.9 jit_solution(18440695880536660123)
XLA Ops:
  0.7 3.1 %slice_bitcast_fusion = (bf16[8,256,256]{2,1,0:T(8,128)(2,1)}, bf16[8,256,256]{2,1,0:T(8,128)(2,1)}) fusion(bf16[1,2,1,8,256,256]{5,4,3,2,1,0:T(8,128)(2,1)} %param.6), kind=kLoop, calls=%fused_computation | loop fusion | bytes 4194304 | tf_op jit(solution)/shard_map/factor_step_1/squeeze | solution.py:263
  3.8 4.9 %collective-permute-start.1 = (bf16[8,256,256]{2,1,0:T(8,128)(2,1)}, bf16[8,256,256]{2,1,0:T(8,128)(2,1)}, u32[]{:S(2)}, u32[]{:S(2)}) collective-permute-start(bf16[8,256,256]{2,1,0:T(8,128)(2,1)} %get-tuple-element.57), channel_id=1, source_target_pairs={{0,1},{1,2},{2,3},{4,5},{5,6},{6,7},{8,9},{9,10},{10,11},{12,13},{... | collective-permute-start | bytes 3145736 | tf_op jit(solution)/shard_map/factor_step_1/ppermute | solution.py:264
  8.7 2.4 collective-permute-start.3
  11.2 0.2 tell_planes.1
  11.4 1.1 copy-done.21
  12.5 4.7 %all-to-all-start = ((bf16[4,656,256]{2,1,0:T(8,128)(2,1)}), bf16[4,656,256]{2,1,0:T(8,128)(2,1)S(1)}, u32[]{:S(2)}, u32[]{:S(2)}) async-start(bf16[4,656,256]{2,1,0:T(8,128)(2,1)} %copy-done.21), calls=%async_computation | async-start | bytes 2686976 | tf_op jit(solution)/shard_map/tell_planes/all_to_all | solution.py:271
  17.2 31.5 %all-to-all-done.rest_0_.rest_1_.own_told = bf16[4,656,256]{2,1,0:T(8,128)(2,1)S(1)} async-done(((bf16[4,656,256]{2,1,0:T(8,128)(2,1)}), bf16[4,656,256]{2,1,0:T(8,128)(2,1)S(1)}, u32[]{:S(2)}, u32[]{:S(2)}) %all-to-all-start) | async-done | bytes 1343520 | tf_op jit(solution)/shard_map/tell_planes/all_to_all | solution.py:271
  48.7 0.2 broadcast_select_fusion
  49.0 5.3 %collective-permute-start.4 = (bf16[8,256,256]{2,1,0:T(8,128)(2,1)S(1)}, bf16[8,256,256]{2,1,0:T(8,128)(2,1)S(1)}, u32[]{:S(2)}, u32[]{:S(2)}) collective-permute-start(bf16[8,256,256]{2,1,0:T(8,128)(2,1)S(1)} %get-tuple-element.54), channel_id=1, source_target_pairs={{0,3},{1,0},{2,1},{3,2},{4,7},{5,4},{6,5},{7,6},{8,11},{9,8},{10,9... | collective-permute-start | bytes 3145736 | tf_op jit(solution)/shard_map/factor_step_2/ppermute | solution.py:280
  54.3 0.2 collective-permute-start.5
  54.5 0.3 collective-permute-start.6
  54.8 22.6 %collective-permute-done.4.rest_6_.rest_7_ = bf16[8,256,256]{2,1,0:T(8,128)(2,1)S(1)} collective-permute-done((bf16[8,256,256]{2,1,0:T(8,128)(2,1)S(1)}, bf16[8,256,256]{2,1,0:T(8,128)(2,1)S(1)}, u32[]{:S(2)}, u32[]{:S(2)}) %collective-permute-start.4) | collective-permute-done | bytes 1048608 | tf_op jit(solution)/shard_map/factor_step_2/ppermute | solution.py:280
  77.4 3.4 %collective-permute-done.2.rest_5_.rest_6_ = bf16[8,256,256]{2,1,0:T(8,128)(2,1)S(1)} collective-permute-done((bf16[8,256,256]{2,1,0:T(8,128)(2,1)S(1)}, bf16[8,256,256]{2,1,0:T(8,128)(2,1)S(1)}, u32[]{:S(2)}, u32[]{:S(2)}) %collective-permute-start.2) | collective-permute-done | bytes 1048608 | tf_op jit(solution)/shard_map/factor_step_2/ppermute | solution.py:279
  80.8 0.5 collective-permute-start.9
  81.4 1.7 collective-permute-start.10
  83.1 3.3 %collective-permute-start.11 = (bf16[8,256,256]{2,1,0:T(8,128)(2,1)}, bf16[8,256,256]{2,1,0:T(8,128)(2,1)}, u32[]{:S(2)}, u32[]{:S(2)}) collective-permute-start(bf16[8,256,256]{2,1,0:T(8,128)(2,1)} %collective-permute-done.3.rest_4_.rest_5_), channel_id=1, source_target_pairs={{0,3},{1,0},{4,7},{5,4},{8,11},{9,8},{12,15},{13,12},{16,19},{17,1... | collective-permute-start | bytes 3145736 | tf_op jit(solution)/shard_map/factor_step_3/ppermute | solution.py:286
  86.4 3.5 %forward_0.1 = (f32[4,32,256]{2,1,0:T(8,128)S(1)}, bf16[4,32,256]{2,1,0:T(8,128)(2,1)S(1)}, bf16[64,32,256]{2,1,0:T(8,128)(2,1)S(1)}) custom-call(s32[1]{0:T(128)} %bitcast.1.plane_ref, s32[4,8]{1,0:T(4,128)S(1)} %get-tuple-element.60.at_ref, bf16[4,656,256]{2,1,0:T(8,128)(2,1)S(1)} %all-to-all-done.rest_0_.rest_1_.own_told, ...), custom_call_target="tpu_custom_call" | custom-call | flops 150994944 | bytes 6291456 | tf_op jit(solution)/shard_map/forward_0/pallas_call | solution.py:158
  90.0 1.0 copy-done.22
  91.0 0.7 copy-done.25
  91.6 7.1 %all-to-all-start.1 = ((bf16[16,4,32,256]{3,2,1,0:T(8,128)(2,1)}), bf16[16,4,32,256]{3,2,1,0:T(8,128)(2,1)}, u32[]{:S(2)}, u32[]{:S(2)}) async-start(bf16[16,4,32,256]{3,2,1,0:T(8,128)(2,1)} %bitcast.61), calls=%async_computation.1 | async-start | bytes 2097152 | tf_op jit(solution)/shard_map/forward_0/all_to_all | solution.py:253
  98.7 11.7 %collective-permute-done.11.rest_9_.rest_8_ = bf16[8,256,256]{2,1,0:T(8,128)(2,1)} collective-permute-done((bf16[8,256,256]{2,1,0:T(8,128)(2,1)}, bf16[8,256,256]{2,1,0:T(8,128)(2,1)}, u32[]{:S(2)}, u32[]{:S(2)}) %collective-permute-start.11) | collective-permute-done | bytes 1048608 | tf_op jit(solution)/shard_map/factor_step_3/ppermute | solution.py:286
  110.4 6.1 %all-to-all-done.1.rest_0_ = bf16[16,4,32,256]{3,2,1,0:T(8,128)(2,1)} async-done(((bf16[16,4,32,256]{3,2,1,0:T(8,128)(2,1)}), bf16[16,4,32,256]{3,2,1,0:T(8,128)(2,1)}, u32[]{:S(2)}, u32[]{:S(2)}) %all-to-all-start.1) | async-done | bytes 1048608 | tf_op jit(solution)/shard_map/forward_0/all_to_all | solution.py:253
  116.5 0.5 collective-permute-start.13
  117.0 2.4 collective-permute-done.12.rest_15_.rest_14_
  119.4 1.5 collective-permute-done.13.rest_16_.rest_15_
  120.9 1.6 copy-done.2
  122.5 1.3 copy-done.5
  123.8 1.2 copy-done.8
  125.0 1.2 copy-done.11
  126.2 1.2 copy-done.14
  127.5 1.2 copy-done.16
  128.7 1.2 copy-done.18
  129.9 1.2 copy-done.20
  131.1 4.3 %forward_1.1 = (f32[4,32,256]{2,1,0:T(8,128)S(1)}, bf16[4,32,256]{2,1,0:T(8,128)(2,1)S(1)}, bf16[64,32,256]{2,1,0:T(8,128)(2,1)S(1)}) custom-call(s32[1]{0:T(128)} %bitcast.1.plane_ref, s32[4,8]{1,0:T(4,128)S(1)} %get-tuple-element.62.at_ref, bf16[16,4,32,256]{3,2,1,0:T(8,128)(2,1)} %all-to-all-done.1.rest_0_, ...), custom_call_target="tpu_custom_call" | custom-call | flops 150994944 | bytes 6291456 | tf_op jit(solution)/shard_map/forward_1/pallas_call | solution.py:158
  135.4 20.5 %all_to_all.40.rest_0_ = bf16[16,4,32,256]{3,2,1,0:T(8,128)(2,1)S(1)} all-to-all(bf16[16,4,32,256]{3,2,1,0:T(8,128)(2,1)S(1)} %bitcast.62), channel_id=1, replica_groups=mesh['x'=4,'y'=4,'c'=2,'z'=4] {'x','y'}, dimensions={0} | all-to-all | bytes 2097152 | tf_op jit(solution)/shard_map/forward_1/all_to_all | solution.py:253
  155.9 3.6 %forward_2.1 = (f32[4,32,256]{2,1,0:T(8,128)S(1)}, bf16[4,32,256]{2,1,0:T(8,128)(2,1)S(1)}, bf16[64,32,256]{2,1,0:T(8,128)(2,1)S(1)}) custom-call(s32[1]{0:T(128)} %bitcast.1.plane_ref, s32[4,8]{1,0:T(4,128)S(1)} %get-tuple-element.61.at_ref, bf16[16,4,32,256]{3,2,1,0:T(8,128)(2,1)S(1)} %all_to_all.40.rest_0_, ...), custom_call_target="tpu_custom_call" | custom-call | flops 150994944 | bytes 6291456 | tf_op jit(solution)/shard_map/forward_2/pallas_call | solution.py:158
  159.5 19.5 %all_to_all.41.got_ref = bf16[16,4,32,256]{3,2,1,0:T(8,128)(2,1)S(1)} all-to-all(bf16[16,4,32,256]{3,2,1,0:T(8,128)(2,1)S(1)} %bitcast.63), channel_id=1, replica_groups=mesh['x'=4,'y'=4,'c'=2,'z'=4] {'x','y'}, dimensions={0} | all-to-all | bytes 2097152 | tf_op jit(solution)/shard_map/forward_2/all_to_all | solution.py:253
  179.0 1.0 top.1
  180.1 18.3 %all_to_all.42 = bf16[16,4,32,256]{3,2,1,0:T(8,128)(2,1)S(1)} all-to-all(bf16[16,4,32,256]{3,2,1,0:T(8,128)(2,1)S(1)} %get-tuple-element.41), channel_id=1, replica_groups=mesh['x'=4,'y'=4,'c'=2,'z'=4] {'x','y'}, dimensions={0} | all-to-all | bytes 2097152 | tf_op jit(solution)/shard_map/backward_2/all_to_all | solution.py:253
  198.4 3.6 %backward_2.1 = (bf16[4,32,256]{2,1,0:T(8,128)(2,1)S(1)}, bf16[16,4,32,256]{3,2,1,0:T(8,128)(2,1)S(1)}) custom-call(s32[1]{0:T(128)} %bitcast.1.plane_ref, s32[4,8]{1,0:T(4,128)S(1)} %get-tuple-element.61.at_ref, bf16[64,32,256]{2,1,0:T(8,128)(2,1)S(1)} %bitcast.59, f32[4,32,256]{2,1,0:T(8,128)S(1)} %get-tuple-element.42.f_ref, ...), custom_call_target="tpu_custom_call" | custom-call | flops 150994944 | bytes 6291456 | tf_op jit(solution)/shard_map/backward_2/pallas_call | solution.py:215
  202.0 17.1 %all_to_all.43 = bf16[16,4,32,256]{3,2,1,0:T(8,128)(2,1)S(1)} all-to-all(bf16[16,4,32,256]{3,2,1,0:T(8,128)(2,1)S(1)} %get-tuple-element.43), channel_id=1, replica_groups=mesh['x'=4,'y'=4,'c'=2,'z'=4] {'x','y'}, dimensions={0} | all-to-all | bytes 2097152 | tf_op jit(solution)/shard_map/backward_1/all_to_all | solution.py:253
  219.1 4.0 %backward_1.1 = (bf16[4,32,256]{2,1,0:T(8,128)(2,1)S(1)}, bf16[16,4,32,256]{3,2,1,0:T(8,128)(2,1)S(1)}) custom-call(s32[1]{0:T(128)} %bitcast.1.plane_ref, s32[4,8]{1,0:T(4,128)S(1)} %get-tuple-element.62.at_ref, bf16[64,32,256]{2,1,0:T(8,128)(2,1)S(1)} %bitcast.60, f32[4,32,256]{2,1,0:T(8,128)S(1)} %get-tuple-element.44.f_ref, ...), custom_call_target="tpu_custom_call" | custom-call | flops 150994944 | bytes 6291456 | tf_op jit(solution)/shard_map/backward_1/pallas_call | solution.py:215
  223.1 16.3 %all_to_all.44 = bf16[16,4,32,256]{3,2,1,0:T(8,128)(2,1)S(1)} all-to-all(bf16[16,4,32,256]{3,2,1,0:T(8,128)(2,1)S(1)} %get-tuple-element.45), channel_id=1, replica_groups=mesh['x'=4,'y'=4,'c'=2,'z'=4] {'x','y'}, dimensions={0} | all-to-all | bytes 2097152 | tf_op jit(solution)/shard_map/backward_0/all_to_all | solution.py:253
  239.4 3.1 %backward_0.1 = bf16[4,32,256]{2,1,0:T(8,128)(2,1)S(1)} custom-call(s32[1]{0:T(128)} %bitcast.1.plane_ref, s32[4,8]{1,0:T(4,128)S(1)} %get-tuple-element.60.at_ref, bf16[64,32,256]{2,1,0:T(8,128)(2,1)S(1)} %bitcast.58, f32[4,32,256]{2,1,0:T(8,128)S(1)} %copy-done.26, bf16[4,656,256]{2,1,0:T(8,128)(2,1)S(1)} %all-to-all-done.rest_0_.rest_1_.own_told, ...), custom_call_target="tpu_custom_call" | custom-call | flops 150994944 | bytes 6291456 | tf_op jit(solution)/shard_map/backward_0/pallas_call | solution.py:215
  242.6 0.1 collective-permute-start.14
  242.7 1.5 collective-permute-done.14
  244.3 13.5 %all_to_all.45.fx_ref = bf16[4,2,2,2,32,256]{5,4,3,2,1,0:T(8,128)(2,1)S(1)} all-to-all(bf16[4,2,2,2,32,256]{5,4,3,2,1,0:T(8,128)(2,1)S(1)} %pad_maximum_fusion), channel_id=1, replica_groups=mesh['x'=4,'y'=4,'c'=2,'z'=4] {'z'}, dimensions={0} | all-to-all | bytes 1048576 | tf_op jit(solution)/shard_map/to_planes/all_to_all | solution.py:319
  257.8 1.1 to_planes.1
  (69 shorter events, 0.4 us)
Async XLA Ops:
  0.6 10.5 %copy-start.27 = (s32[1,2,1,8]{3,2,1,0:T(1,128)S(1)}, s32[1,2,1,8]{3,2,1,0:T(1,128)}, u32[]{:S(2)}) copy-start(s32[1,2,1,8]{3,2,1,0:T(1,128)} %param.7) | copy-start | bytes 196
  0.6 10.5 %copy-start.24 = (bf16[1,2,1,256,256]{4,3,2,1,0:T(8,128)(2,1)S(1)}, bf16[1,2,1,256,256]{4,3,2,1,0:T(8,128)(2,1)}, u32[]{:S(2)}) copy-start(bf16[1,2,1,256,256]{4,3,2,1,0:T(8,128)(2,1)} %param.5) | copy-start | bytes 786436
  0.6 10.5 %copy-start.23 = (f32[1,2,1,256,256]{4,3,2,1,0:T(8,128)S(1)}, f32[1,2,1,256,256]{4,3,2,1,0:T(8,128)}, u32[]{:S(2)}) copy-start(f32[1,2,1,256,256]{4,3,2,1,0:T(8,128)} %param.4) | copy-start | bytes 1572868
  3.8 45.0 %collective-permute-start.1 = (bf16[8,256,256]{2,1,0:T(8,128)(2,1)}, bf16[8,256,256]{2,1,0:T(8,128)(2,1)}, u32[]{:S(2)}, u32[]{:S(2)}) collective-permute-start(bf16[8,256,256]{2,1,0:T(8,128)(2,1)} %get-tuple-element.57), channel_id=1, source_target_pairs={{0,1},{1,2},{2,3},{4,5},{5,6},{6,7},{8,9},{9,10},{10,11},{12,13},{... | collective-permute-start | bytes 3145736 | tf_op jit(solution)/shard_map/factor_step_1/ppermute | solution.py:264
  8.7 40.1 %collective-permute-start.3 = (bf16[8,256,256]{2,1,0:T(8,128)(2,1)}, bf16[8,256,256]{2,1,0:T(8,128)(2,1)}, u32[]{:S(2)}, u32[]{:S(2)}) collective-permute-start(bf16[8,256,256]{2,1,0:T(8,128)(2,1)} %get-tuple-element.31), channel_id=1, source_target_pairs={{0,3},{1,0},{2,1},{4,7},{5,4},{6,5},{8,11},{9,8},{10,9},{12,15},{1... | collective-permute-start | bytes 3145736 | tf_op jit(solution)/shard_map/factor_step_1/ppermute | solution.py:265
  11.2 37.6 %copy-start = (bf16[1,2,1,8,256,256]{5,4,3,2,1,0:T(8,128)(2,1)S(1)}, bf16[1,2,1,8,256,256]{5,4,3,2,1,0:T(8,128)(2,1)}, u32[]{:S(2)}) copy-start(bf16[1,2,1,8,256,256]{5,4,3,2,1,0:T(8,128)(2,1)} %param.6) | copy-start | bytes 6291460
  11.4 1.1 copy-start.21
  12.5 36.2 %all-to-all-start = ((bf16[4,656,256]{2,1,0:T(8,128)(2,1)}), bf16[4,656,256]{2,1,0:T(8,128)(2,1)S(1)}, u32[]{:S(2)}, u32[]{:S(2)}) async-start(bf16[4,656,256]{2,1,0:T(8,128)(2,1)} %copy-done.21), calls=%async_computation | async-start | bytes 2686976 | tf_op jit(solution)/shard_map/tell_planes/all_to_all | solution.py:271
  48.7 32.1 %collective-permute-start = (bf16[4,656,256]{2,1,0:T(8,128)(2,1)S(1)}, bf16[4,656,256]{2,1,0:T(8,128)(2,1)S(1)}, u32[]{:S(2)}, u32[]{:S(2)}) collective-permute-start(bf16[4,656,256]{2,1,0:T(8,128)(2,1)S(1)} %all-to-all-done.rest_0_.rest_1_.own_told), channel_id=1, source_target_pairs={{0,4},{4,0},{1,5},{5,1},{2,6},{6,2},{3,7},{7,3},{8,12},{12,8},{9,1... | collective-permute-start | bytes 4030472 | tf_op jit(solution)/shard_map/tell_planes/ppermute | solution.py:249
  49.0 28.4 %collective-permute-start.4 = (bf16[8,256,256]{2,1,0:T(8,128)(2,1)S(1)}, bf16[8,256,256]{2,1,0:T(8,128)(2,1)S(1)}, u32[]{:S(2)}, u32[]{:S(2)}) collective-permute-start(bf16[8,256,256]{2,1,0:T(8,128)(2,1)S(1)} %get-tuple-element.54), channel_id=1, source_target_pairs={{0,3},{1,0},{2,1},{3,2},{4,7},{5,4},{6,5},{7,6},{8,11},{9,8},{10,9... | collective-permute-start | bytes 3145736 | tf_op jit(solution)/shard_map/factor_step_2/ppermute | solution.py:280
  54.3 26.5 %collective-permute-start.2 = (bf16[8,256,256]{2,1,0:T(8,128)(2,1)S(1)}, bf16[8,256,256]{2,1,0:T(8,128)(2,1)S(1)}, u32[]{:S(2)}, u32[]{:S(2)}) collective-permute-start(bf16[8,256,256]{2,1,0:T(8,128)(2,1)S(1)} %get-tuple-element.55), channel_id=1, source_target_pairs={{0,1},{1,2},{2,3},{3,0},{4,5},{5,6},{6,7},{7,4},{8,9},{9,10},{10,1... | collective-permute-start | bytes 3145736 | tf_op jit(solution)/shard_map/factor_step_2/ppermute | solution.py:279
  54.3 32.1 %collective-permute-start.5 = (bf16[2,8,256,256]{3,2,1,0:T(8,128)(2,1)S(1)}, bf16[2,8,256,256]{3,2,1,0:T(8,128)(2,1)S(1)}, u32[]{:S(2)}, u32[]{:S(2)}) collective-permute-start(bf16[2,8,256,256]{3,2,1,0:T(8,128)(2,1)S(1)} %bitcast.49), channel_id=1, source_target_pairs={{0,4},{4,0},{1,5},{5,1},{2,6},{6,2},{3,7},{7,3},{8,12},{12,8},{9,1... | collective-permute-start | bytes 6291464 | tf_op jit(solution)/shard_map/factor_step_1/ppermute | solution.py:249
  54.5 26.9 %collective-permute-start.6 = (bf16[8,256,256]{2,1,0:T(8,128)(2,1)}, bf16[8,256,256]{2,1,0:T(8,128)(2,1)S(1)}, u32[]{:S(2)}, u32[]{:S(2)}) collective-permute-start(bf16[8,256,256]{2,1,0:T(8,128)(2,1)} %collective-permute-done.1.rest_3_.rest_4_), channel_id=1, source_target_pairs={{0,4},{4,0},{1,5},{5,1},{2,6},{6,2},{3,7},{7,3},{8,12},{12,8},{9,1... | collective-permute-start | bytes 3145736 | tf_op jit(solution)/shard_map/factor_step_2/ppermute | solution.py:249
  77.4 12.5 %copy-start.7 = (bf16[8,256,256]{2,1,0:T(8,128)(2,1)}, bf16[8,256,256]{2,1,0:T(8,128)(2,1)S(1)}, u32[]{:S(2)}) copy-start(bf16[8,256,256]{2,1,0:T(8,128)(2,1)S(1)} %collective-permute-done.4.rest_6_.rest_7_) | copy-start | bytes 3145732
  77.4 5.7 %collective-permute-start.7 = (bf16[8,256,256]{2,1,0:T(8,128)(2,1)}, bf16[8,256,256]{2,1,0:T(8,128)(2,1)S(1)}, u32[]{:S(2)}, u32[]{:S(2)}) collective-permute-start(bf16[8,256,256]{2,1,0:T(8,128)(2,1)} %collective-permute-done.3.rest_4_.rest_5_), channel_id=1, source_target_pairs={{0,4},{4,0},{1,5},{5,1},{2,6},{6,2},{3,7},{7,3},{8,12},{12,8},{9,1... | collective-permute-start | bytes 3145736 | tf_op jit(solution)/shard_map/factor_step_2/ppermute | solution.py:249
  80.8 9.1 %copy-start.10 = (bf16[8,256,256]{2,1,0:T(8,128)(2,1)}, bf16[8,256,256]{2,1,0:T(8,128)(2,1)S(1)}, u32[]{:S(2)}) copy-start(bf16[8,256,256]{2,1,0:T(8,128)(2,1)S(1)} %collective-permute-done.2.rest_5_.rest_6_) | copy-start | bytes 3145732
  80.8 5.6 %collective-permute-start.8 = (bf16[8,256,256]{2,1,0:T(8,128)(2,1)S(1)}, bf16[8,256,256]{2,1,0:T(8,128)(2,1)S(1)}, u32[]{:S(2)}, u32[]{:S(2)}) collective-permute-start(bf16[8,256,256]{2,1,0:T(8,128)(2,1)S(1)} %collective-permute-done.2.rest_5_.rest_6_), channel_id=1, source_target_pairs={{0,4},{4,0},{1,5},{5,1},{2,6},{6,2},{3,7},{7,3},{8,12},{12,8},{9,1... | collective-permute-start | bytes 3145736 | tf_op jit(solution)/shard_map/factor_step_2/ppermute | solution.py:249
  80.8 9.1 %copy-start.4 = (bf16[4,656,256]{2,1,0:T(8,128)(2,1)}, bf16[4,656,256]{2,1,0:T(8,128)(2,1)S(1)}, u32[]{:S(2)}) copy-start(bf16[4,656,256]{2,1,0:T(8,128)(2,1)S(1)} %collective-permute-done.rest_1_.rest_2_.other_told) | copy-start | bytes 4030468
  80.8 5.6 %collective-permute-start.9 = (bf16[8,256,256]{2,1,0:T(8,128)(2,1)S(1)}, bf16[8,256,256]{2,1,0:T(8,128)(2,1)S(1)}, u32[]{:S(2)}, u32[]{:S(2)}) collective-permute-start(bf16[8,256,256]{2,1,0:T(8,128)(2,1)S(1)} %collective-permute-done.4.rest_6_.rest_7_), channel_id=1, source_target_pairs={{0,4},{4,0},{1,5},{5,1},{2,6},{6,2},{3,7},{7,3},{8,12},{12,8},{9,1... | collective-permute-start | bytes 3145736 | tf_op jit(solution)/shard_map/factor_step_2/ppermute | solution.py:249
  81.4 8.6 %copy-start.13 = (bf16[8,256,256]{2,1,0:T(8,128)(2,1)}, bf16[8,256,256]{2,1,0:T(8,128)(2,1)S(1)}, u32[]{:S(2)}) copy-start(bf16[8,256,256]{2,1,0:T(8,128)(2,1)S(1)} %collective-permute-done.6.rest_10_.rest_11_) | copy-start | bytes 3145732
  81.4 17.3 %collective-permute-start.10 = (bf16[8,256,256]{2,1,0:T(8,128)(2,1)}, bf16[8,256,256]{2,1,0:T(8,128)(2,1)}, u32[]{:S(2)}, u32[]{:S(2)}) collective-permute-start(bf16[8,256,256]{2,1,0:T(8,128)(2,1)} %get-tuple-element.31), channel_id=1, source_target_pairs={{1,2},{2,3},{5,6},{6,7},{9,10},{10,11},{13,14},{14,15},{17,18},{18... | collective-permute-start | bytes 3145736 | tf_op jit(solution)/shard_map/factor_step_3/ppermute | solution.py:285
  83.1 6.9 %copy-start.15 = (bf16[8,256,256]{2,1,0:T(8,128)(2,1)}, bf16[8,256,256]{2,1,0:T(8,128)(2,1)S(1)}, u32[]{:S(2)}) copy-start(bf16[8,256,256]{2,1,0:T(8,128)(2,1)S(1)} %collective-permute-done.7.rest_11_.rest_12_) | copy-start | bytes 3145732
  83.1 27.4 %collective-permute-start.11 = (bf16[8,256,256]{2,1,0:T(8,128)(2,1)}, bf16[8,256,256]{2,1,0:T(8,128)(2,1)}, u32[]{:S(2)}, u32[]{:S(2)}) collective-permute-start(bf16[8,256,256]{2,1,0:T(8,128)(2,1)} %collective-permute-done.3.rest_4_.rest_5_), channel_id=1, source_target_pairs={{0,3},{1,0},{4,7},{5,4},{8,11},{9,8},{12,15},{13,12},{16,19},{17,1... | collective-permute-start | bytes 3145736 | tf_op jit(solution)/shard_map/factor_step_3/ppermute | solution.py:286
  86.4 3.6 %copy-start.1 = (bf16[2,8,256,256]{3,2,1,0:T(8,128)(2,1)}, bf16[2,8,256,256]{3,2,1,0:T(8,128)(2,1)S(1)}, u32[]{:S(2)}) copy-start(bf16[2,8,256,256]{3,2,1,0:T(8,128)(2,1)S(1)} %collective-permute-done.5.rest_9_.rest_14_.rest_15_.rest_10_) | copy-start | bytes 6291460
  86.4 3.6 %copy-start.17 = (bf16[8,256,256]{2,1,0:T(8,128)(2,1)}, bf16[8,256,256]{2,1,0:T(8,128)(2,1)S(1)}, u32[]{:S(2)}) copy-start(bf16[8,256,256]{2,1,0:T(8,128)(2,1)S(1)} %collective-permute-done.8.rest_12_.rest_13_) | copy-start | bytes 3145732
  86.4 3.6 %copy-start.19 = (bf16[8,256,256]{2,1,0:T(8,128)(2,1)}, bf16[8,256,256]{2,1,0:T(8,128)(2,1)S(1)}, u32[]{:S(2)}) copy-start(bf16[8,256,256]{2,1,0:T(8,128)(2,1)S(1)} %collective-permute-done.9.rest_13_.rest_14_) | copy-start | bytes 3145732
  90.0 1.0 copy-start.22
  91.0 0.7 copy-start.25
  91.6 24.9 %all-to-all-start.1 = ((bf16[16,4,32,256]{3,2,1,0:T(8,128)(2,1)}), bf16[16,4,32,256]{3,2,1,0:T(8,128)(2,1)}, u32[]{:S(2)}, u32[]{:S(2)}) async-start(bf16[16,4,32,256]{3,2,1,0:T(8,128)(2,1)} %bitcast.61), calls=%async_computation.1 | async-start | bytes 2097152 | tf_op jit(solution)/shard_map/forward_0/all_to_all | solution.py:253
  116.5 2.9 %collective-permute-start.12 = (bf16[8,256,256]{2,1,0:T(8,128)(2,1)}, bf16[8,256,256]{2,1,0:T(8,128)(2,1)S(1)}, u32[]{:S(2)}, u32[]{:S(2)}) collective-permute-start(bf16[8,256,256]{2,1,0:T(8,128)(2,1)} %collective-permute-done.10.rest_8_.rest_7_), channel_id=1, source_target_pairs={{0,4},{4,0},{1,5},{5,1},{2,6},{6,2},{3,7},{7,3},{8,12},{12,8},{9,1... | collective-permute-start | bytes 3145736 | tf_op jit(solution)/shard_map/factor_step_3/ppermute | solution.py:249
  116.5 4.4 %collective-permute-start.13 = (bf16[8,256,256]{2,1,0:T(8,128)(2,1)}, bf16[8,256,256]{2,1,0:T(8,128)(2,1)S(1)}, u32[]{:S(2)}, u32[]{:S(2)}) collective-permute-start(bf16[8,256,256]{2,1,0:T(8,128)(2,1)} %collective-permute-done.11.rest_9_.rest_8_), channel_id=1, source_target_pairs={{0,4},{4,0},{1,5},{5,1},{2,6},{6,2},{3,7},{7,3},{8,12},{12,8},{9,1... | collective-permute-start | bytes 3145736 | tf_op jit(solution)/shard_map/factor_step_3/ppermute | solution.py:249
  120.9 1.6 copy-start.2
  122.5 1.3 copy-start.5
  123.8 1.2 copy-start.8
  125.0 1.2 copy-start.11
  126.2 1.2 copy-start.14
  127.5 1.2 copy-start.16
  128.7 1.2 copy-start.18
  129.9 1.2 copy-start.20
  219.1 20.3 %copy-start.6 = (bf16[4,656,256]{2,1,0:T(8,128)(2,1)S(1)}, bf16[4,656,256]{2,1,0:T(8,128)(2,1)}, u32[]{:S(2)}) copy-start(bf16[4,656,256]{2,1,0:T(8,128)(2,1)} %copy-done.4) | copy-start | bytes 4030468
  219.1 20.3 %copy-start.9 = (bf16[8,256,256]{2,1,0:T(8,128)(2,1)S(1)}, bf16[8,256,256]{2,1,0:T(8,128)(2,1)}, u32[]{:S(2)}) copy-start(bf16[8,256,256]{2,1,0:T(8,128)(2,1)} %copy-done.7) | copy-start | bytes 3145732
  219.1 20.3 %copy-start.12 = (bf16[8,256,256]{2,1,0:T(8,128)(2,1)S(1)}, bf16[8,256,256]{2,1,0:T(8,128)(2,1)}, u32[]{:S(2)}) copy-start(bf16[8,256,256]{2,1,0:T(8,128)(2,1)} %copy-done.10) | copy-start | bytes 3145732
  219.1 20.3 %copy-start.26 = (f32[4,32,256]{2,1,0:T(8,128)S(1)}, f32[4,32,256]{2,1,0:T(8,128)}, u32[]{:S(2)}) copy-start(f32[4,32,256]{2,1,0:T(8,128)} %copy-done.25) | copy-start | bytes 393220
  223.1 16.3 %copy-start.3 = (bf16[2,8,256,256]{3,2,1,0:T(8,128)(2,1)S(1)}, bf16[2,8,256,256]{3,2,1,0:T(8,128)(2,1)}, u32[]{:S(2)}) copy-start(bf16[2,8,256,256]{3,2,1,0:T(8,128)(2,1)} %copy-done.1) | copy-start | bytes 6291460
  242.6 1.6 collective-permute-start.14

commit v4 on v3

v4 whole, which is shorter than its diff:
```python
import functools

import jax
import jax.numpy as jnp
from jax import lax
from jax.experimental import pallas as pl
from jax.experimental.pallas import tpu as pltpu
from jax.sharding import Mesh, PartitionSpec as P


BF = jnp.bfloat16
F32 = jnp.float32
MIB = 1024 * 1024
LIMIT = 14 * MIB
NODES = 64
CHIPS = 16
WIDTH = 256
FAN = 8
HALF = 128
COLS = 32
UP = [(z, (z + 1) % 4) for z in range(4)]
DOWN = [(z, (z + 3) % 4) for z in range(4)]


SMEM = pl.BlockSpec(memory_space=pltpu.SMEM)
VM = pl.BlockSpec(memory_space=pltpu.VMEM)


def dot_t(a, b):
    return lax.dot_general(a, b, (((1,), (1,)), ((), ())), preferred_element_type=F32)


def dot_n(a, b):
    return lax.dot_general(a, b, (((1,), (0,)), ((), ())), preferred_element_type=F32)


KEEP, SEND, PAT, ROWS = 0, 64, 128, 144


def pack_kernel(core_ref, plane_ref, rhs_ref, pat_ref, out_ref):
    core, plane = core_ref[0], plane_ref[0]
    for k in range(4):
        out_ref[k, PAT:ROWS] = pat_ref[...]
    for j in range(2):
        rt = jnp.transpose(rhs_ref[j]).astype(BF)
        for half in range(2):
            at = pl.multiple_of(jnp.where(core == half, KEEP, SEND) + j * COLS, COLS)
            for z in range(4):
                first = half * HALF + z * COLS
                out_ref[jnp.bitwise_and(z - plane + 4, 3), pl.ds(at, COLS)] = rt[first : first + COLS]


def pack(core, plane, rhs, pat):
    return pl.pallas_call(
        pack_kernel,
        out_shape=jax.ShapeDtypeStruct((4, ROWS, WIDTH), BF),
        in_specs=[SMEM, SMEM, VM, VM],
        out_specs=VM,
        compiler_params=pltpu.CompilerParams(vmem_limit_bytes=8 * MIB),
        cost_estimate=pl.CostEstimate(flops=0, bytes_accessed=2 * MIB, transcendentals=0),
    )(core, plane, rhs, pat)


ANY = pl.BlockSpec(memory_space=pl.ANY)


def any_specs(count):
    return [ANY] * count


PACKED = FAN + 1


def join_kernel(j, blocks_ref, inv_ref, out_ref, sems):
    copies = [pltpu.make_async_copy(inv_ref.at[j], out_ref.at[FAN], sems.at[0])]
    for k in range(4):
        part = pl.ds(2 * k, 2)
        copies.append(pltpu.make_async_copy(blocks_ref.at[j, part], out_ref.at[part], sems.at[1 + k]))
    for copy in copies:
        copy.start()
    for copy in copies:
        copy.wait()


def join(j, blocks, inverse):
    return pl.pallas_call(
        functools.partial(join_kernel, j),
        in_specs=[ANY, ANY],
        out_specs=VM,
        out_shape=jax.ShapeDtypeStruct((PACKED, WIDTH, WIDTH), BF),
        scratch_shapes=[pltpu.SemaphoreType.DMA((5,))],
        compiler_params=pltpu.CompilerParams(vmem_limit_bytes=3 * MIB),
        cost_estimate=pl.CostEstimate(flops=0, bytes_accessed=3 * MIB, transcendentals=0),
    )(blocks, inverse)


def choose_kernel(chosen, plane_ref, here_ref, else_ref, out_ref, sems):
    for k in range(3):
        part = pl.ds(3 * k, 3)

        @pl.when(plane_ref[0] == chosen)
        def _():
            pltpu.make_async_copy(here_ref.at[part], out_ref.at[part], sems.at[k]).start()

        @pl.when(plane_ref[0] != chosen)
        def _():
            pltpu.make_async_copy(else_ref.at[part], out_ref.at[part], sems.at[k]).start()

    for k in range(3):
        part = pl.ds(3 * k, 3)
        pltpu.make_async_copy(else_ref.at[part], out_ref.at[part], sems.at[k]).wait()


def choose(plane, chosen, here, otherwise):
    return pl.pallas_call(
        functools.partial(choose_kernel, chosen),
        in_specs=[SMEM, ANY, ANY],
        out_specs=VM,
        out_shape=jax.ShapeDtypeStruct((PACKED, WIDTH, WIDTH), BF),
        scratch_shapes=[pltpu.SemaphoreType.DMA((3,))],
        compiler_params=pltpu.CompilerParams(vmem_limit_bytes=3 * MIB),
        cost_estimate=pl.CostEstimate(flops=0, bytes_accessed=3 * MIB, transcendentals=0),
    )(plane, here, otherwise)


def fetch(plane, choices, dst, sem):
    for z, src in enumerate(choices):

        @pl.when(plane == z)
        def _():
            pltpu.make_async_copy(src, dst, sem).start()

    return pltpu.make_async_copy(choices[0], dst, sem)


WHERE = {
    0: ([0, 2, 4, 5], [1, 4, 5, 3]),
    1: ([5, 0, 2, 4], [3, 1, 6, 7]),
    2: ([4, 5, 0, 2], [7, 3, 1, 6]),
    3: ([2, 6, 7, 0], [6, 7, 3, 1]),
}


def used(level):
    return sorted(set(WHERE[level][0] + WHERE[level][1]))


def factor_copies(level, plane, refs, buf, sems):
    names = used(level)
    copies = []
    for n in range(4):
        base = refs[len(names) * (n // 2) :]
        choices = [base[names.index(k)] for k in WHERE[level][n % 2]]
        if level == 3:
            choices = [ref.at[FAN] for ref in choices]
        copies.append(fetch(plane, choices, buf.at[n], sems.at[n]))
    return copies


def told_by(plane, level):
    return jnp.bitwise_and(plane - level + 4, 3)


def add_terms(n, at_ref, came, solved, buf, acc_ref):
    terms = dot_t(solved, buf[n, :FAN].reshape(FAN * WIDTH, WIDTH))
    for p in range(FAN):
        acc_ref[at_ref[came, n, p]] += terms[:, p * WIDTH : (p + 1) * WIDTH]


def row_copies(came, refs, rows, sems):
    copies = []
    for r in range(2):
        src = refs[r].at[came, pl.ds((KEEP, SEND)[r], 2 * COLS)]
        copies.append(pltpu.make_async_copy(src, rows.at[pl.ds(2 * COLS * r, 2 * COLS)], sems.at[r]))
        copies[r].start()
    return copies


def rows_of(buf, n, size):
    return buf[n * size : (n + 1) * size]


def inflow_kernel(got_ref, out_ref):
    out_ref[...] = jnp.sum(got_ref[...].astype(F32), axis=0)


def inflow_of(got):
    return pl.pallas_call(
        inflow_kernel,
        in_specs=[VM],
        out_specs=VM,
        out_shape=NODE_F32,
        compiler_params=pltpu.CompilerParams(vmem_limit_bytes=4 * MIB),
        cost_estimate=pl.CostEstimate(flops=MIB, bytes_accessed=MIB, transcendentals=0),
    )(got)


def forward_kernel(level, plane_ref, at_ref, *rest):
    gots, rest = (rest[:1], rest[1:]) if level else ((), rest)
    told, refs, (f_ref, fb_ref, share_ref, rows, rsems, buf, sems, acc_ref) = rest[:2], rest[2:-8], rest[-8:]
    came = told_by(plane_ref[0], level)
    copies_r = row_copies(came, told, rows, rsems)
    copies = factor_copies(level, plane_ref[0], refs, buf, sems)
    acc_ref[...] = jnp.zeros_like(acc_ref)
    for copy in copies_r:
        copy.wait()
    for n in range(4):
        resid = rows_of(rows, n, COLS)
        if level:
            inflow = gots[0][n] if level == 1 else jnp.sum(gots[0][:, n].astype(F32), axis=0)
            resid = (resid.astype(F32) - inflow).astype(BF)
        copies[n].wait()
        f = dot_t(resid, buf[n, FAN])
        solved = f.astype(BF)
        f_ref[n] = f
        fb_ref[n] = solved
        add_terms(n, at_ref, came, solved, buf, acc_ref)
    share_ref[...] = acc_ref[...].astype(BF)


SMALL = [
    pltpu.VMEM((4 * COLS, WIDTH), BF),
    pltpu.SemaphoreType.DMA((2,)),
]
LARGE = [
    pltpu.VMEM((4, PACKED, WIDTH, WIDTH), BF),
    pltpu.SemaphoreType.DMA((4,)),
]
NODE_F32 = jax.ShapeDtypeStruct((4, COLS, WIDTH), F32)
NODE_BF = jax.ShapeDtypeStruct((4, COLS, WIDTH), BF)
COPIES = jax.ShapeDtypeStruct((CHIPS, 4, COLS, WIDTH), BF)


def pick(level, factors):
    return [factors[r][k] for r in range(2) for k in used(level)]


def forward_level(level, plane, at, gots, told, factors):
    blocks = pick(level, factors)
    return pl.pallas_call(
        functools.partial(forward_kernel, level),
        in_specs=[SMEM, SMEM] + [VM] * len(gots) + any_specs(2) + [ANY] * len(blocks),
        out_specs=(VM, VM, VM),
        scratch_shapes=SMALL + LARGE + [pltpu.VMEM((NODES, COLS, WIDTH), F32)],
        out_shape=(NODE_F32, NODE_BF, jax.ShapeDtypeStruct((NODES, COLS, WIDTH), BF)),
        compiler_params=pltpu.CompilerParams(vmem_limit_bytes=LIMIT),
        cost_estimate=pl.CostEstimate(flops=2 * 36 * COLS * WIDTH**2, bytes_accessed=6 * MIB, transcendentals=0),
    )(plane, at, *gots, *told, *blocks)


def top_kernel(plane_ref, got_ref, own_told, other_told, *rest):
    refs, (fb_ref, sol_ref, copies_ref, rows, rsems, invs, sems) = rest[:-7], rest[-7:]
    copies_r = row_copies(told_by(plane_ref[0], 3), (own_told, other_told), rows, rsems)
    copies = factor_copies(3, plane_ref[0], refs, invs, sems)
    for copy in copies_r:
        copy.wait()
    for n in range(4):
        inflow = jnp.sum(got_ref[:, n].astype(F32), axis=0)
        resid = (rows_of(rows, n, COLS).astype(F32) - inflow).astype(BF)
        copies[n].wait()
        inv = invs[n]
        fb = dot_t(resid, inv).astype(BF)
        fb_ref[n] = fb
        sol = dot_n(fb, inv).astype(BF)
        sol_ref[n] = sol
        for k in range(CHIPS):
            copies_ref[k, n] = sol


def top_level(plane, got, told, factors):
    blocks = pick(3, factors)
    return pl.pallas_call(
        top_kernel,
        in_specs=[SMEM, VM] + any_specs(2 + len(blocks)),
        out_specs=(VM, VM, VM),
        scratch_shapes=SMALL + [pltpu.VMEM((4, WIDTH, WIDTH), BF), pltpu.SemaphoreType.DMA((4,))],
        out_shape=(NODE_BF, NODE_BF, COPIES),
        compiler_params=pltpu.CompilerParams(vmem_limit_bytes=8 * MIB),
        cost_estimate=pl.CostEstimate(flops=2 * 8 * COLS * WIDTH**2, bytes_accessed=3 * MIB, transcendentals=0),
    )(plane, got, *told, *blocks)


def backward_kernel(level, plane_ref, at_ref, above_ref, f_ref, *rest):
    count = 2 * len(used(level))
    refs, outs, (buf, sems) = rest[:count], rest[count:-2], rest[-2:]
    copies = factor_copies(level, plane_ref[0], refs, buf, sems)
    came = told_by(plane_ref[0], level)
    for n in range(4):
        picked = jnp.concatenate([above_ref[at_ref[came, n, p]] for p in range(FAN)], axis=1)
        copies[n].wait()
        back = dot_n(picked, buf[n, :FAN].reshape(FAN * WIDTH, WIDTH))
        upper = (f_ref[n] - back).astype(BF)
        sol = dot_n(upper, buf[n, FAN]).astype(BF)
        outs[0][n] = sol
        if level:
            for k in range(CHIPS):
                outs[1][k, n] = sol


def backward_level(level, plane, at, above, f, factors):
    blocks = pick(level, factors)
    out_shape = (NODE_BF, COPIES) if level else (NODE_BF,)
    return pl.pallas_call(
        functools.partial(backward_kernel, level),
        in_specs=[SMEM, SMEM, VM, VM] + any_specs(len(blocks)),
        out_specs=(VM,) * len(out_shape),
        scratch_shapes=LARGE,
        out_shape=out_shape,
        compiler_params=pltpu.CompilerParams(vmem_limit_bytes=LIMIT),
        cost_estimate=pl.CostEstimate(flops=2 * 36 * COLS * WIDTH**2, bytes_accessed=6 * MIB, transcendentals=0),
    )(plane, at, above, f, *blocks)


def last_kernel(core_ref, fx_ref, forward_ref, result_ref):
    core = core_ref[0]
    for k, out_ref in enumerate((forward_ref, result_ref)):
        for j in range(2):
            halves = []
            for half in range(2):
                rel = jnp.bitwise_xor(core, half)
                halves += [fx_ref[z, rel, k, j] for z in range(4)]
            out_ref[j] = jnp.transpose(jnp.concatenate(halves, axis=0).astype(F32))


def last_step(core, fx):
    return pl.pallas_call(
        last_kernel,
        out_shape=(jax.ShapeDtypeStruct((2, WIDTH, WIDTH), F32),) * 2,
        in_specs=[SMEM, VM],
        out_specs=(VM, VM),
        compiler_params=pltpu.CompilerParams(vmem_limit_bytes=8 * MIB),
        cost_estimate=pl.CostEstimate(flops=0, bytes_accessed=2 * 2**20, transcendentals=0),
    )(core, fx)


def swap(value):
    return lax.ppermute(value, "c", [(0, 1), (1, 0)])


def exchange(value):
    return lax.all_to_all(value.reshape(CHIPS, 4, COLS, WIDTH), ("x", "y"), 0, 0, tiled=True)


def on_device(rhs, inverses, blocks, pattern):
    core = lax.axis_index("c").astype(jnp.int32)
    plane = lax.axis_index("z").astype(jnp.int32)
    core1, plane1 = core.reshape(1), plane.reshape(1)
    factor = blocks.reshape(2, FAN, WIDTH, WIDTH)
    inverse = inverses.reshape(2, WIDTH, WIDTH)

    with jax.named_scope("factor_step_1"):
        own_a = join(0, factor, inverse)
        up_1 = lax.ppermute(own_a, "z", UP)
        own_b = join(1, factor, inverse)
        down_1 = lax.ppermute(own_b, "z", DOWN)
        near_a, near_b = swap(own_a), swap(own_b)

    with jax.named_scope("tell_planes"):
        pat = jnp.pad(pattern.reshape(2, FAN).astype(BF), ((0, ROWS - PAT - 2), (0, WIDTH - FAN)))
        message = pack(core1, plane1, rhs.reshape(2, WIDTH, WIDTH), pat)
        told = [message[0]]
        for k in range(1, 4):
            told.append(lax.ppermute(message[k], "z", [(z, (z + k) % 4) for z in range(4)]))
        told = jnp.stack(told)
        up_1, down_1, told = lax.optimization_barrier((up_1, down_1, told))
        told = (told, swap(told))
        targets = jnp.concatenate([t[:, PAT : PAT + 2, :FAN] for t in told], axis=1).astype(jnp.int32)
        targets = jnp.clip(targets, 0, NODES - 1)
        places = (targets % 32) // 2 * 4 + jnp.bitwise_xor(targets % 2, core) * 2 + targets // 32

    with jax.named_scope("factor_step_2"):
        up_2 = lax.ppermute(choose(plane1, 0, own_b, up_1), "z", UP)
        down_2 = lax.ppermute(choose(plane1, 3, down_1, own_a), "z", DOWN)
        up_3 = choose(plane1, 0, up_1, own_b)
        down_3 = choose(plane1, 3, own_a, down_1)
        near = (near_a, near_b, swap(up_1), swap(down_1))
        up_2, down_2, up_3, down_3, told, places, near = lax.optimization_barrier(
            (up_2, down_2, up_3, down_3, told, places, near)
        )
        near += (swap(up_2), swap(down_2))
    with jax.named_scope("factor_step_3"):
        up_3 = lax.ppermute(up_3, "z", UP)
        down_3 = lax.ppermute(down_3, "z", DOWN)

    factors = ([own_a, own_b, up_1, down_1, up_2, down_2], list(near))
    forward = [None] * 3
    solved = [None] * 4
    gots = ()
    for level in range(3):
        with jax.named_scope(f"forward_{level}"):
            forward[level], solved[level], share = forward_level(level, plane1, places, gots, told, factors)
            got = exchange(share)
        if level == 0:
            with jax.named_scope("factor_step_3"):
                up_3, down_3, got = lax.optimization_barrier((up_3, down_3, inflow_of(got)))
                factors[0].extend([up_3, down_3])
                factors[1].extend([swap(up_3), swap(down_3)])
        gots = (got,)
    result = [None] * 4
    with jax.named_scope("top"):
        solved[3], result[3], copies = top_level(plane1, got, told, factors)

    for level in (2, 1, 0):
        with jax.named_scope(f"backward_{level}"):
            above = exchange(copies).reshape(NODES, COLS, WIDTH)
            out = backward_level(level, plane1, places, above, forward[level], factors)
            result[level] = out[0]
            if level > 0:
                copies = out[1]

    with jax.named_scope("to_planes"):
        fx = jnp.stack([jnp.stack(solved), jnp.stack(result)], axis=1).reshape(4, 2, 2, 2, COLS, WIDTH)
        fx = jnp.stack([fx[:, :, 0], swap(fx[:, :, 1])], axis=1)
        fx = lax.all_to_all(fx, "z", 0, 0, tiled=True)
        forward_out, result_out = last_step(core1, fx)
    shape = (1, 2, 1, WIDTH, WIDTH)
    return forward_out.reshape(shape), result_out.reshape(shape)


def solution(mesh):
    wide = Mesh(mesh.devices.reshape(4, 4, 2, 4), ("x", "y", "c", "z"))
    blk = ("x", "y", "c")
    return jax.shard_map(
        on_device,
        mesh=wide,
        in_specs=(
            P("z", None, blk, None, None),
            P("z", None, blk, None, None),
            P("z", None, blk, None, None, None),
            P("z", None, blk, None),
        ),
        out_specs=(P("z", None, blk, None, None), P("z", None, blk, None, None)),
        check_vma=False,
    )
```

time: 260 us -> 245 us (0.942)
  blocking collectives: 105 us -> 130 us
  waiting for transfers between devices: 80.7 us -> 62.9 us
  starting transfers between devices: 31 us -> 15.7 us
  local copies, waits for them, and re-layouts: 16.2 us -> 3.66 us
  Pallas kernels: 24.3 us -> 31.3 us
    all_to_all x2 -> x0, waiting for transfers between devices: 37.6 us -> none  [the longest x1 31.5 us: on_device(): told = lax.all_to_all(message, 'z', 0, 0, tiled=True)]
    all_to_all x5 -> x6, blocking collectives: 91.7 us -> 116 us  [exchange(): lax.all_to_all(value.reshape(CHIPS, 4, COLS, WIDTH), ('x', 'y'), 0, 0, ti...]
    ppermute x6 -> x9, waiting for transfers between devices: 37.7 us -> 56.5 us  [the longest x3 29.5 us: on_device(): lax.ppermute(message[k], 'z', [(z, (z + k) % 4) for z in range(4)])]
    all_to_all x2 -> x0, starting transfers between devices: 11.8 us -> none  [the longest x1 7.09 us: exchange(): lax.all_to_all(value.reshape(CHIPS, 4, COLS, WIDTH), ('x', 'y'), 0, 0, ti...]
    unnamed x57 -> x9, local copies, waits for them, and re-layouts: 13.1 us -> 3.58 us
    pallas_call x1 -> x8, Pallas kernels: 1.01 us -> 6.13 us  [the longest x4 3.11 us: choose(): pl.pallas_call(functools.partial(choose_kernel, chosen), in_specs=[SMEM,...]
    ppermute x6 -> x9, starting transfers between devices: 17.6 us -> 13.4 us  [the longest x1 4.19 us: on_device(): down_1 = lax.ppermute(own_b, 'z', DOWN)]
    squeeze x2 -> x0, local copies, waits for them, and re-layouts: 3.12 us -> none  [the longest x1 3.12 us: on_device(): own_a, own_b = (factor[0], factor[1])]
  transfers between devices with their start and end apart: 17 -> 19, of which waited for: 8 -> 9; matrix products, arithmetic and copies ran while one was open for 0% -> 0% of each run, Pallas kernels for 1% -> 3%
where the time goes in v4:
time: 245 us
  blocking collectives  130 us (53%)
  waiting for transfers between devices  62.9 us (26%)
  Pallas kernels  31.3 us (13%)
  starting transfers between devices  15.7 us (6%)
  local copies, waits for them, and re-layouts  3.66 us (1%)
    all_to_all x6, blocking collectives, exchange(): lax.all_to_all(value.reshape(CHIPS, 4, COLS, WIDTH), ('x', 'y'), 0, 0, ti...  116 us
    ppermute x3, waiting for transfers between devices, on_device(): lax.ppermute(message[k], 'z', [(z, (z + k) % 4) for z in range(4)])  29.5 us
    ppermute x1, waiting for transfers between devices, on_device(): down_2 = lax.ppermute(choose(plane1, 3, down_1, own_a), 'z', DOWN)  23.6 us
    all_to_all x1, blocking collectives, on_device(): fx = lax.all_to_all(fx, 'z', 0, 0, tiled=True)  14 us
    pallas_call x3, Pallas kernels, forward_level(): pl.pallas_call(functools.partial(forward_kernel, level), in_specs=[SMEM,...  12.6 us
    pallas_call x3, Pallas kernels, backward_level(): pl.pallas_call(functools.partial(backward_kernel, level), in_specs=[SMEM,...  11.3 us
    ppermute x10, waiting for transfers between devices, swap(): return lax.ppermute(value, 'c', [(0, 1), (1, 0)])  6.35 us
  transfers between devices with their start and end apart: 19, of which 9 were waited for; matrix products, arithmetic and copies ran while one was open for 0% of the time, Pallas kernels for 3%

profile of v4, /device:TPU:0, one launch (start us, length us, event | category | flops | bytes accessed | tf_op | source)
XLA Modules:
  0.0 244.9 jit_solution(17079666793993888592)
XLA Ops:
  0.6 1.6 copy-done
  2.2 0.9 copy-done.1
  3.2 0.3 factor_step_1.2.here_ref.else_ref.rest_3_.rest_4_.rest_1_
  3.5 4.2 %collective-permute-start.1 = (bf16[9,256,256]{2,1,0:T(8,128)(2,1)S(1)}, bf16[9,256,256]{2,1,0:T(8,128)(2,1)S(1)}, u32[]{:S(2)}, u32[]{:S(2)}) collective-permute-start(bf16[9,256,256]{2,1,0:T(8,128)(2,1)S(1)} %factor_step_1.2.here_ref.else_ref.rest_3_.rest_4_.rest_1_), channel_id=1, source_target_pairs={{0,3},{1,0},{2,1},{3,2},{4,7},{5,4},{6,5},{7,6},{8,11},{9,8},{10,9... | collective-permute-start | bytes 3538952 | tf_op jit(solution)/shard_map/factor_step_1/ppermute | solution.py:355
  7.6 0.3 factor_step_1.3.else_ref.here_ref.rest_2_.rest_3_.rest_0_
  8.0 0.1 collective-permute-start.9
  8.2 1.0 copy-done.2
  9.2 0.1 tell_planes.1
  9.4 3.2 %collective-permute-start.4 = (bf16[144,256]{1,0:T(8,128)(2,1)S(1)}, bf16[144,256]{1,0:T(8,128)(2,1)S(1)}, u32[]{:S(2)}, u32[]{:S(2)}) collective-permute-start(bf16[144,256]{1,0:T(8,128)(2,1)S(1)} %get-tuple-element.77), channel_id=1, source_target_pairs={{0,3},{1,0},{2,1},{3,2},{4,7},{5,4},{6,5},{7,6},{8,11},{9,8},{10,9... | collective-permute-start | bytes 221192 | tf_op jit(solution)/shard_map/tell_planes/ppermute | solution.py:363
  12.5 23.5 %collective-permute-done.4 = bf16[144,256]{1,0:T(8,128)(2,1)S(1)} collective-permute-done((bf16[144,256]{1,0:T(8,128)(2,1)S(1)}, bf16[144,256]{1,0:T(8,128)(2,1)S(1)}, u32[]{:S(2)}, u32[]{:S(2)}) %collective-permute-start.4) | collective-permute-done | bytes 73760 | tf_op jit(solution)/shard_map/tell_planes/ppermute | solution.py:363
  36.0 0.9 collective-permute-done.3
  36.9 5.1 %collective-permute-done.2 = bf16[144,256]{1,0:T(8,128)(2,1)S(1)} collective-permute-done((bf16[144,256]{1,0:T(8,128)(2,1)S(1)}, bf16[144,256]{1,0:T(8,128)(2,1)S(1)}, u32[]{:S(2)}, u32[]{:S(2)}) %collective-permute-start.2) | collective-permute-done | bytes 73760 | tf_op jit(solution)/shard_map/tell_planes/ppermute | solution.py:363
  42.1 0.1 collective-permute-start.7
  42.2 0.5 collective-permute-start.8
  42.7 0.6 factor_step_2.4
  43.3 0.2 collective-permute-start.10
  43.5 0.6 factor_step_2.5
  44.1 2.8 %collective-permute-start.6 = (bf16[9,256,256]{2,1,0:T(8,128)(2,1)S(1)}, bf16[9,256,256]{2,1,0:T(8,128)(2,1)S(1)}, u32[]{:S(2)}, u32[]{:S(2)}) collective-permute-start(bf16[9,256,256]{2,1,0:T(8,128)(2,1)S(1)} %factor_step_2.5), channel_id=1, source_target_pairs={{0,3},{1,0},{2,1},{3,2},{4,7},{5,4},{6,5},{7,6},{8,11},{9,8},{10,9... | collective-permute-start | bytes 3538952 | tf_op jit(solution)/shard_map/factor_step_2/ppermute | solution.py:373
  46.9 0.2 collective-permute-start.11
  47.1 1.3 factor_step_2.6
  48.4 0.6 factor_step_2.7
  49.1 23.6 %collective-permute-done.6.rest_7_.rest_8_.rest_5_ = bf16[9,256,256]{2,1,0:T(8,128)(2,1)S(1)} collective-permute-done((bf16[9,256,256]{2,1,0:T(8,128)(2,1)S(1)}, bf16[9,256,256]{2,1,0:T(8,128)(2,1)S(1)}, u32[]{:S(2)}, u32[]{:S(2)}) %collective-permute-start.6) | collective-permute-done | bytes 1179680 | tf_op jit(solution)/shard_map/factor_step_2/ppermute | solution.py:373
  72.7 3.4 %collective-permute-done.5.rest_6_.rest_7_.rest_4_ = bf16[9,256,256]{2,1,0:T(8,128)(2,1)S(1)} collective-permute-done((bf16[9,256,256]{2,1,0:T(8,128)(2,1)S(1)}, bf16[9,256,256]{2,1,0:T(8,128)(2,1)S(1)}, u32[]{:S(2)}, u32[]{:S(2)}) %collective-permute-start.5) | collective-permute-done | bytes 1179680 | tf_op jit(solution)/shard_map/factor_step_2/ppermute | solution.py:372
  76.1 0.5 collective-permute-start.13
  76.6 3.2 %collective-permute-start.15 = (bf16[9,256,256]{2,1,0:T(8,128)(2,1)S(1)}, bf16[9,256,256]{2,1,0:T(8,128)(2,1)S(1)}, u32[]{:S(2)}, u32[]{:S(2)}) collective-permute-start(bf16[9,256,256]{2,1,0:T(8,128)(2,1)S(1)} %factor_step_2.7), channel_id=1, source_target_pairs={{0,3},{1,0},{2,1},{3,2},{4,7},{5,4},{6,5},{7,6},{8,11},{9,8},{10,9... | collective-permute-start | bytes 3538952 | tf_op jit(solution)/shard_map/factor_step_3/ppermute | solution.py:383
  79.9 0.8 collective-permute-done.13.rest_13_.rest_16_.rest_11_
  80.6 4.0 %forward_0.1 = (f32[4,32,256]{2,1,0:T(8,128)S(1)}, bf16[4,32,256]{2,1,0:T(8,128)(2,1)S(1)}, bf16[64,32,256]{2,1,0:T(8,128)(2,1)S(1)}) custom-call(s32[1]{0:T(128)} %bitcast.1.plane_ref, s32[4,4,8]{2,1,0:T(4,128)S(1)} %fusion.3.at_ref, bf16[4,144,256]{2,1,0:T(8,128)(2,1)S(1)} %pad_maximum_fusion.1.rest_0_.rest_1_.own_told, ...), custom_call_target="tpu_custom_call" | custom-call | flops 150994944 | bytes 6291456 | tf_op jit(solution)/shard_map/forward_0/pallas_call | solution.py:240
  84.6 24.2 %all_to_all.35.got_ref = bf16[16,4,32,256]{3,2,1,0:T(8,128)(2,1)S(1)} all-to-all(bf16[16,4,32,256]{3,2,1,0:T(8,128)(2,1)S(1)} %bitcast.53), channel_id=1, replica_groups=mesh['x'=4,'y'=4,'c'=2,'z'=4] {'x','y'}, dimensions={0} | all-to-all | bytes 2097152 | tf_op jit(solution)/shard_map/forward_0/all_to_all | solution.py:341
  108.9 0.1 factor_step_3.1.rest_0_
  109.0 0.1 collective-permute-start.16
  109.1 0.5 collective-permute-start.17
  109.6 2.3 collective-permute-done.16.rest_17_.rest_10_.rest_14_
  112.0 1.7 collective-permute-done.17.rest_18_.rest_11_.rest_15_
  113.6 4.2 %forward_1.1 = (f32[4,32,256]{2,1,0:T(8,128)S(1)}, bf16[4,32,256]{2,1,0:T(8,128)(2,1)S(1)}, bf16[64,32,256]{2,1,0:T(8,128)(2,1)S(1)}) custom-call(s32[1]{0:T(128)} %bitcast.1.plane_ref, s32[4,4,8]{2,1,0:T(4,128)S(1)} %fusion.3.at_ref, f32[4,32,256]{2,1,0:T(8,128)S(1)} %factor_step_3.1.rest_0_, ...), custom_call_target="tpu_custom_call" | custom-call | flops 150994944 | bytes 6291456 | tf_op jit(solution)/shard_map/forward_1/pallas_call | solution.py:240
  117.9 20.9 %all_to_all.36.rest_0_ = bf16[16,4,32,256]{3,2,1,0:T(8,128)(2,1)S(1)} all-to-all(bf16[16,4,32,256]{3,2,1,0:T(8,128)(2,1)S(1)} %bitcast.51), channel_id=1, replica_groups=mesh['x'=4,'y'=4,'c'=2,'z'=4] {'x','y'}, dimensions={0} | all-to-all | bytes 2097152 | tf_op jit(solution)/shard_map/forward_1/all_to_all | solution.py:341
  138.8 4.5 %forward_2.1 = (f32[4,32,256]{2,1,0:T(8,128)S(1)}, bf16[4,32,256]{2,1,0:T(8,128)(2,1)S(1)}, bf16[64,32,256]{2,1,0:T(8,128)(2,1)S(1)}) custom-call(s32[1]{0:T(128)} %bitcast.1.plane_ref, s32[4,4,8]{2,1,0:T(4,128)S(1)} %fusion.3.at_ref, bf16[16,4,32,256]{3,2,1,0:T(8,128)(2,1)S(1)} %all_to_all.36.rest_0_, ...), custom_call_target="tpu_custom_call" | custom-call | flops 150994944 | bytes 6291456 | tf_op jit(solution)/shard_map/forward_2/pallas_call | solution.py:240
  143.3 19.5 %all_to_all.37.got_ref = bf16[16,4,32,256]{3,2,1,0:T(8,128)(2,1)S(1)} all-to-all(bf16[16,4,32,256]{3,2,1,0:T(8,128)(2,1)S(1)} %bitcast.52), channel_id=1, replica_groups=mesh['x'=4,'y'=4,'c'=2,'z'=4] {'x','y'}, dimensions={0} | all-to-all | bytes 2097152 | tf_op jit(solution)/shard_map/forward_2/all_to_all | solution.py:341
  162.8 2.4 top.1
  165.2 18.3 %all_to_all.38 = bf16[16,4,32,256]{3,2,1,0:T(8,128)(2,1)S(1)} all-to-all(bf16[16,4,32,256]{3,2,1,0:T(8,128)(2,1)S(1)} %get-tuple-element.61), channel_id=1, replica_groups=mesh['x'=4,'y'=4,'c'=2,'z'=4] {'x','y'}, dimensions={0} | all-to-all | bytes 2097152 | tf_op jit(solution)/shard_map/backward_2/all_to_all | solution.py:341
  183.5 3.9 %backward_2.1 = (bf16[4,32,256]{2,1,0:T(8,128)(2,1)S(1)}, bf16[16,4,32,256]{3,2,1,0:T(8,128)(2,1)S(1)}) custom-call(s32[1]{0:T(128)} %bitcast.1.plane_ref, s32[4,4,8]{2,1,0:T(4,128)S(1)} %fusion.3.at_ref, bf16[64,32,256]{2,1,0:T(8,128)(2,1)S(1)} %bitcast.48, f32[4,32,256]{2,1,0:T(8,128)S(1)} %get-tuple-element.62.f_ref, ...), custom_call_target="tpu_custom_call" | custom-call | flops 150994944 | bytes 6291456 | tf_op jit(solution)/shard_map/backward_2/pallas_call | solution.py:303
  187.3 17.1 %all_to_all.39 = bf16[16,4,32,256]{3,2,1,0:T(8,128)(2,1)S(1)} all-to-all(bf16[16,4,32,256]{3,2,1,0:T(8,128)(2,1)S(1)} %get-tuple-element.63), channel_id=1, replica_groups=mesh['x'=4,'y'=4,'c'=2,'z'=4] {'x','y'}, dimensions={0} | all-to-all | bytes 2097152 | tf_op jit(solution)/shard_map/backward_1/all_to_all | solution.py:341
  204.4 3.9 %backward_1.1 = (bf16[4,32,256]{2,1,0:T(8,128)(2,1)S(1)}, bf16[16,4,32,256]{3,2,1,0:T(8,128)(2,1)S(1)}) custom-call(s32[1]{0:T(128)} %bitcast.1.plane_ref, s32[4,4,8]{2,1,0:T(4,128)S(1)} %fusion.3.at_ref, bf16[64,32,256]{2,1,0:T(8,128)(2,1)S(1)} %bitcast.47, f32[4,32,256]{2,1,0:T(8,128)S(1)} %get-tuple-element.64.f_ref, ...), custom_call_target="tpu_custom_call" | custom-call | flops 150994944 | bytes 6291456 | tf_op jit(solution)/shard_map/backward_1/pallas_call | solution.py:303
  208.3 16.2 %all_to_all.40 = bf16[16,4,32,256]{3,2,1,0:T(8,128)(2,1)S(1)} all-to-all(bf16[16,4,32,256]{3,2,1,0:T(8,128)(2,1)S(1)} %get-tuple-element.65), channel_id=1, replica_groups=mesh['x'=4,'y'=4,'c'=2,'z'=4] {'x','y'}, dimensions={0} | all-to-all | bytes 2097152 | tf_op jit(solution)/shard_map/backward_0/all_to_all | solution.py:341
  224.5 3.5 %backward_0.1 = bf16[4,32,256]{2,1,0:T(8,128)(2,1)S(1)} custom-call(s32[1]{0:T(128)} %bitcast.1.plane_ref, s32[4,4,8]{2,1,0:T(4,128)S(1)} %fusion.3.at_ref, bf16[64,32,256]{2,1,0:T(8,128)(2,1)S(1)} %bitcast.46, f32[4,32,256]{2,1,0:T(8,128)S(1)} %get-tuple-element.66.f_ref, bf16[9,256,256]{2,1,0:T(8,128)(2,1)S(1)} %factor_step_1.3.else_ref.here_ref.rest_2_.rest_3_.rest_0_, ...), custom_call_target="tpu_custom_call" | custom-call | flops 150994944 | bytes 6291456 | tf_op jit(solution)/shard_map/backward_0/pallas_call | solution.py:303
  228.1 0.1 collective-permute-start.18
  228.2 1.5 collective-permute-done.18
  229.8 14.0 %all_to_all.41.fx_ref = bf16[4,2,2,2,32,256]{5,4,3,2,1,0:T(8,128)(2,1)S(1)} all-to-all(bf16[4,2,2,2,32,256]{5,4,3,2,1,0:T(8,128)(2,1)S(1)} %pad_maximum_fusion), channel_id=1, replica_groups=mesh['x'=4,'y'=4,'c'=2,'z'=4] {'z'}, dimensions={0} | all-to-all | bytes 1048576 | tf_op jit(solution)/shard_map/to_planes/all_to_all | solution.py:414
  243.8 1.1 to_planes.1
  (32 shorter events, 0.4 us)
Async XLA Ops:
  0.6 1.6 copy-start
  2.2 0.9 copy-start.1
  3.4 4.7 %copy-start.3 = (s32[1,2,1,8]{3,2,1,0:T(1,128)S(1)}, s32[1,2,1,8]{3,2,1,0:T(1,128)}, u32[]{:S(2)}) copy-start(s32[1,2,1,8]{3,2,1,0:T(1,128)} %param.7) | copy-start | bytes 196
  3.5 38.6 %collective-permute-start.1 = (bf16[9,256,256]{2,1,0:T(8,128)(2,1)S(1)}, bf16[9,256,256]{2,1,0:T(8,128)(2,1)S(1)}, u32[]{:S(2)}, u32[]{:S(2)}) collective-permute-start(bf16[9,256,256]{2,1,0:T(8,128)(2,1)S(1)} %factor_step_1.2.here_ref.else_ref.rest_3_.rest_4_.rest_1_), channel_id=1, source_target_pairs={{0,3},{1,0},{2,1},{3,2},{4,7},{5,4},{6,5},{7,6},{8,11},{9,8},{10,9... | collective-permute-start | bytes 3538952 | tf_op jit(solution)/shard_map/factor_step_1/ppermute | solution.py:355
  7.9 34.2 %collective-permute-start = (bf16[9,256,256]{2,1,0:T(8,128)(2,1)S(1)}, bf16[9,256,256]{2,1,0:T(8,128)(2,1)}, u32[]{:S(2)}, u32[]{:S(2)}) collective-permute-start(bf16[9,256,256]{2,1,0:T(8,128)(2,1)S(1)} %factor_step_1.3.else_ref.here_ref.rest_2_.rest_3_.rest_0_), channel_id=1, source_target_pairs={{0,1},{1,2},{2,3},{3,0},{4,5},{5,6},{6,7},{7,4},{8,9},{9,10},{10,1... | collective-permute-start | bytes 3538952 | tf_op jit(solution)/shard_map/factor_step_1/ppermute | solution.py:353
  8.0 38.9 %collective-permute-start.9 = (bf16[9,256,256]{2,1,0:T(8,128)(2,1)S(1)}, bf16[9,256,256]{2,1,0:T(8,128)(2,1)}, u32[]{:S(2)}, u32[]{:S(2)}) collective-permute-start(bf16[9,256,256]{2,1,0:T(8,128)(2,1)S(1)} %factor_step_1.2.here_ref.else_ref.rest_3_.rest_4_.rest_1_), channel_id=1, source_target_pairs={{0,4},{4,0},{1,5},{5,1},{2,6},{6,2},{3,7},{7,3},{8,12},{12,8},{9,1... | collective-permute-start | bytes 3538952 | tf_op jit(solution)/shard_map/factor_step_1/ppermute | solution.py:337
  8.1 1.0 copy-start.2
  9.4 26.7 %collective-permute-start.4 = (bf16[144,256]{1,0:T(8,128)(2,1)S(1)}, bf16[144,256]{1,0:T(8,128)(2,1)S(1)}, u32[]{:S(2)}, u32[]{:S(2)}) collective-permute-start(bf16[144,256]{1,0:T(8,128)(2,1)S(1)} %get-tuple-element.77), channel_id=1, source_target_pairs={{0,3},{1,0},{2,1},{3,2},{4,7},{5,4},{6,5},{7,6},{8,11},{9,8},{10,9... | collective-permute-start | bytes 221192 | tf_op jit(solution)/shard_map/tell_planes/ppermute | solution.py:363
  12.5 24.4 %collective-permute-start.3 = (bf16[144,256]{1,0:T(8,128)(2,1)S(1)}, bf16[144,256]{1,0:T(8,128)(2,1)S(1)}, u32[]{:S(2)}, u32[]{:S(2)}) collective-permute-start(bf16[144,256]{1,0:T(8,128)(2,1)S(1)} %get-tuple-element.78), channel_id=1, source_target_pairs={{0,2},{1,3},{2,0},{3,1},{4,6},{5,7},{6,4},{7,5},{8,10},{9,11},{10,... | collective-permute-start | bytes 221192 | tf_op jit(solution)/shard_map/tell_planes/ppermute | solution.py:363
  36.0 6.0 %collective-permute-start.2 = (bf16[144,256]{1,0:T(8,128)(2,1)S(1)}, bf16[144,256]{1,0:T(8,128)(2,1)S(1)}, u32[]{:S(2)}, u32[]{:S(2)}) collective-permute-start(bf16[144,256]{1,0:T(8,128)(2,1)S(1)} %get-tuple-element.79), channel_id=1, source_target_pairs={{0,1},{1,2},{2,3},{3,0},{4,5},{5,6},{6,7},{7,4},{8,9},{9,10},{10,1... | collective-permute-start | bytes 221192 | tf_op jit(solution)/shard_map/tell_planes/ppermute | solution.py:363
  42.1 4.8 %collective-permute-start.7 = (bf16[4,144,256]{2,1,0:T(8,128)(2,1)S(1)}, bf16[4,144,256]{2,1,0:T(8,128)(2,1)S(1)}, u32[]{:S(2)}, u32[]{:S(2)}) collective-permute-start(bf16[4,144,256]{2,1,0:T(8,128)(2,1)S(1)} %pad_maximum_fusion.1.rest_0_.rest_1_.own_told), channel_id=1, source_target_pairs={{0,4},{4,0},{1,5},{5,1},{2,6},{6,2},{3,7},{7,3},{8,12},{12,8},{9,1... | collective-permute-start | bytes 884744 | tf_op jit(solution)/shard_map/tell_planes/ppermute | solution.py:337
  42.2 6.9 %collective-permute-start.8 = (bf16[9,256,256]{2,1,0:T(8,128)(2,1)S(1)}, bf16[9,256,256]{2,1,0:T(8,128)(2,1)S(1)}, u32[]{:S(2)}, u32[]{:S(2)}) collective-permute-start(bf16[9,256,256]{2,1,0:T(8,128)(2,1)S(1)} %factor_step_1.3.else_ref.here_ref.rest_2_.rest_3_.rest_0_), channel_id=1, source_target_pairs={{0,4},{4,0},{1,5},{5,1},{2,6},{6,2},{3,7},{7,3},{8,12},{12,8},{9,1... | collective-permute-start | bytes 3538952 | tf_op jit(solution)/shard_map/factor_step_1/ppermute | solution.py:337
  43.3 32.8 %collective-permute-start.10 = (bf16[9,256,256]{2,1,0:T(8,128)(2,1)}, bf16[9,256,256]{2,1,0:T(8,128)(2,1)S(1)}, u32[]{:S(2)}, u32[]{:S(2)}) collective-permute-start(bf16[9,256,256]{2,1,0:T(8,128)(2,1)} %collective-permute-done.else_ref.here_ref.rest_4_.rest_5_.rest_2_), channel_id=1, source_target_pairs={{0,4},{4,0},{1,5},{5,1},{2,6},{6,2},{3,7},{7,3},{8,12},{12,8},{9,1... | collective-permute-start | bytes 3538952 | tf_op jit(solution)/shard_map/factor_step_2/ppermute | solution.py:337
  44.1 28.6 %collective-permute-start.6 = (bf16[9,256,256]{2,1,0:T(8,128)(2,1)S(1)}, bf16[9,256,256]{2,1,0:T(8,128)(2,1)S(1)}, u32[]{:S(2)}, u32[]{:S(2)}) collective-permute-start(bf16[9,256,256]{2,1,0:T(8,128)(2,1)S(1)} %factor_step_2.5), channel_id=1, source_target_pairs={{0,3},{1,0},{2,1},{3,2},{4,7},{5,4},{6,5},{7,6},{8,11},{9,8},{10,9... | collective-permute-start | bytes 3538952 | tf_op jit(solution)/shard_map/factor_step_2/ppermute | solution.py:373
  46.9 29.2 %collective-permute-start.5 = (bf16[9,256,256]{2,1,0:T(8,128)(2,1)S(1)}, bf16[9,256,256]{2,1,0:T(8,128)(2,1)S(1)}, u32[]{:S(2)}, u32[]{:S(2)}) collective-permute-start(bf16[9,256,256]{2,1,0:T(8,128)(2,1)S(1)} %factor_step_2.4), channel_id=1, source_target_pairs={{0,1},{1,2},{2,3},{3,0},{4,5},{5,6},{6,7},{7,4},{8,9},{9,10},{10,1... | collective-permute-start | bytes 3538952 | tf_op jit(solution)/shard_map/factor_step_2/ppermute | solution.py:372
  46.9 29.2 %collective-permute-start.11 = (bf16[9,256,256]{2,1,0:T(8,128)(2,1)S(1)}, bf16[9,256,256]{2,1,0:T(8,128)(2,1)S(1)}, u32[]{:S(2)}, u32[]{:S(2)}) collective-permute-start(bf16[9,256,256]{2,1,0:T(8,128)(2,1)S(1)} %collective-permute-done.1.here_ref.else_ref.rest_5_.rest_6_.rest_3_), channel_id=1, source_target_pairs={{0,4},{4,0},{1,5},{5,1},{2,6},{6,2},{3,7},{7,3},{8,12},{12,8},{9,1... | collective-permute-start | bytes 3538952 | tf_op jit(solution)/shard_map/factor_step_2/ppermute | solution.py:337
  76.1 3.8 %collective-permute-start.12 = (bf16[9,256,256]{2,1,0:T(8,128)(2,1)S(1)}, bf16[9,256,256]{2,1,0:T(8,128)(2,1)S(1)}, u32[]{:S(2)}, u32[]{:S(2)}) collective-permute-start(bf16[9,256,256]{2,1,0:T(8,128)(2,1)S(1)} %collective-permute-done.5.rest_6_.rest_7_.rest_4_), channel_id=1, source_target_pairs={{0,4},{4,0},{1,5},{5,1},{2,6},{6,2},{3,7},{7,3},{8,12},{12,8},{9,1... | collective-permute-start | bytes 3538952 | tf_op jit(solution)/shard_map/factor_step_2/ppermute | solution.py:337
  76.1 4.5 %collective-permute-start.13 = (bf16[9,256,256]{2,1,0:T(8,128)(2,1)S(1)}, bf16[9,256,256]{2,1,0:T(8,128)(2,1)S(1)}, u32[]{:S(2)}, u32[]{:S(2)}) collective-permute-start(bf16[9,256,256]{2,1,0:T(8,128)(2,1)S(1)} %collective-permute-done.6.rest_7_.rest_8_.rest_5_), channel_id=1, source_target_pairs={{0,4},{4,0},{1,5},{5,1},{2,6},{6,2},{3,7},{7,3},{8,12},{12,8},{9,1... | collective-permute-start | bytes 3538952 | tf_op jit(solution)/shard_map/factor_step_2/ppermute | solution.py:337
  76.6 32.4 %collective-permute-start.14 = (bf16[9,256,256]{2,1,0:T(8,128)(2,1)S(1)}, bf16[9,256,256]{2,1,0:T(8,128)(2,1)S(1)}, u32[]{:S(2)}, u32[]{:S(2)}) collective-permute-start(bf16[9,256,256]{2,1,0:T(8,128)(2,1)S(1)} %factor_step_2.6), channel_id=1, source_target_pairs={{0,1},{1,2},{2,3},{3,0},{4,5},{5,6},{6,7},{7,4},{8,9},{9,10},{10,1... | collective-permute-start | bytes 3538952 | tf_op jit(solution)/shard_map/factor_step_3/ppermute | solution.py:382
  76.6 32.4 %collective-permute-start.15 = (bf16[9,256,256]{2,1,0:T(8,128)(2,1)S(1)}, bf16[9,256,256]{2,1,0:T(8,128)(2,1)S(1)}, u32[]{:S(2)}, u32[]{:S(2)}) collective-permute-start(bf16[9,256,256]{2,1,0:T(8,128)(2,1)S(1)} %factor_step_2.7), channel_id=1, source_target_pairs={{0,3},{1,0},{2,1},{3,2},{4,7},{5,4},{6,5},{7,6},{8,11},{9,8},{10,9... | collective-permute-start | bytes 3538952 | tf_op jit(solution)/shard_map/factor_step_3/ppermute | solution.py:383
  109.0 2.9 %collective-permute-start.16 = (bf16[9,256,256]{2,1,0:T(8,128)(2,1)S(1)}, bf16[9,256,256]{2,1,0:T(8,128)(2,1)S(1)}, u32[]{:S(2)}, u32[]{:S(2)}) collective-permute-start(bf16[9,256,256]{2,1,0:T(8,128)(2,1)S(1)} %collective-permute-done.14.rest_9_.rest_4_.rest_6_), channel_id=1, source_target_pairs={{0,4},{4,0},{1,5},{5,1},{2,6},{6,2},{3,7},{7,3},{8,12},{12,8},{9,1... | collective-permute-start | bytes 3538952 | tf_op jit(solution)/shard_map/factor_step_3/ppermute | solution.py:337
  109.1 4.5 %collective-permute-start.17 = (bf16[9,256,256]{2,1,0:T(8,128)(2,1)S(1)}, bf16[9,256,256]{2,1,0:T(8,128)(2,1)S(1)}, u32[]{:S(2)}, u32[]{:S(2)}) collective-permute-start(bf16[9,256,256]{2,1,0:T(8,128)(2,1)S(1)} %collective-permute-done.15.rest_10_.rest_5_.rest_7_), channel_id=1, source_target_pairs={{0,4},{4,0},{1,5},{5,1},{2,6},{6,2},{3,7},{7,3},{8,12},{12,8},{9,1... | collective-permute-start | bytes 3538952 | tf_op jit(solution)/shard_map/factor_step_3/ppermute | solution.py:337
  228.1 1.6 collective-permute-start.18

commit v5 on v4

--- a/solution.py
+++ b/solution.py
@@ -123,16 +123,6 @@
     )(plane, here, otherwise)
 
 
-def fetch(plane, choices, dst, sem):
-    for z, src in enumerate(choices):
-
-        @pl.when(plane == z)
-        def _():
-            pltpu.make_async_copy(src, dst, sem).start()
-
-    return pltpu.make_async_copy(choices[0], dst, sem)
-
-
 WHERE = {
     0: ([0, 2, 4, 5], [1, 4, 5, 3]),
     1: ([5, 0, 2, 4], [3, 1, 6, 7]),
@@ -147,14 +137,19 @@
 
 def factor_copies(level, plane, refs, buf, sems):
     names = used(level)
-    copies = []
-    for n in range(4):
-        base = refs[len(names) * (n // 2) :]
-        choices = [base[names.index(k)] for k in WHERE[level][n % 2]]
-        if level == 3:
-            choices = [ref.at[FAN] for ref in choices]
-        copies.append(fetch(plane, choices, buf.at[n], sems.at[n]))
-    return copies
+
+    def copy(n, z):
+        src = refs[len(names) * (n // 2) + names.index(WHERE[level][n % 2][z])]
+        return pltpu.make_async_copy(src.at[FAN] if level == 3 else src, buf.at[n], sems.at[n])
+
+    for z in range(4):
+
+        @pl.when(plane == z)
+        def _():
+            for n in range(4):
+                copy(n, z).start()
+
+    return [copy(n, 0) for n in range(4)]
 
 
 def told_by(plane, level):
@@ -204,6 +199,7 @@
     acc_ref[...] = jnp.zeros_like(acc_ref)
     for copy in copies_r:
         copy.wait()
+    solved = []
     for n in range(4):
         resid = rows_of(rows, n, COLS)
         if level:
@@ -211,10 +207,11 @@
             resid = (resid.astype(F32) - inflow).astype(BF)
         copies[n].wait()
         f = dot_t(resid, buf[n, FAN])
-        solved = f.astype(BF)
         f_ref[n] = f
-        fb_ref[n] = solved
-        add_terms(n, at_ref, came, solved, buf, acc_ref)
+        solved.append(f.astype(BF))
+        fb_ref[n] = solved[n]
+    for n in range(4):
+        add_terms(n, at_ref, came, solved[n], buf, acc_ref)
     share_ref[...] = acc_ref[...].astype(BF)
 
 
@@ -285,12 +282,14 @@
     refs, outs, (buf, sems) = rest[:count], rest[count:-2], rest[-2:]
     copies = factor_copies(level, plane_ref[0], refs, buf, sems)
     came = told_by(plane_ref[0], level)
+    uppers = []
     for n in range(4):
         picked = jnp.concatenate([above_ref[at_ref[came, n, p]] for p in range(FAN)], axis=1)
         copies[n].wait()
         back = dot_n(picked, buf[n, :FAN].reshape(FAN * WIDTH, WIDTH))
-        upper = (f_ref[n] - back).astype(BF)
-        sol = dot_n(upper, buf[n, FAN]).astype(BF)
+        uppers.append((f_ref[n] - back).astype(BF))
+    for n in range(4):
+        sol = dot_n(uppers[n], buf[n, FAN]).astype(BF)
         outs[0][n] = sol
         if level:
             for k in range(CHIPS):
@@ -348,21 +347,22 @@
     factor = blocks.reshape(2, FAN, WIDTH, WIDTH)
     inverse = inverses.reshape(2, WIDTH, WIDTH)
 
-    with jax.named_scope("factor_step_1"):
-        own_a = join(0, factor, inverse)
-        up_1 = lax.ppermute(own_a, "z", UP)
-        own_b = join(1, factor, inverse)
-        down_1 = lax.ppermute(own_b, "z", DOWN)
-        near_a, near_b = swap(own_a), swap(own_b)
-
     with jax.named_scope("tell_planes"):
         pat = jnp.pad(pattern.reshape(2, FAN).astype(BF), ((0, ROWS - PAT - 2), (0, WIDTH - FAN)))
         message = pack(core1, plane1, rhs.reshape(2, WIDTH, WIDTH), pat)
         told = [message[0]]
         for k in range(1, 4):
             told.append(lax.ppermute(message[k], "z", [(z, (z + k) % 4) for z in range(4)]))
+
+    with jax.named_scope("factor_step_1"):
+        own_a, own_b = join(0, factor, inverse), join(1, factor, inverse)
+        own_a, own_b, told = lax.optimization_barrier((own_a, own_b, told))
+        up_1 = lax.ppermute(own_a, "z", UP)
+        down_1 = lax.ppermute(own_b, "z", DOWN)
+        near_a, near_b = swap(own_a), swap(own_b)
+
+    with jax.named_scope("tell_planes"):
         told = jnp.stack(told)
-        up_1, down_1, told = lax.optimization_barrier((up_1, down_1, told))
         told = (told, swap(told))
         targets = jnp.concatenate([t[:, PAT : PAT + 2, :FAN] for t in told], axis=1).astype(jnp.int32)
         targets = jnp.clip(targets, 0, NODES - 1)

time: 245 us -> 237 us (0.967)
  waiting for transfers between devices: 62.9 us -> 57.7 us
    ppermute x3, waiting for transfers between devices: 29.5 us -> 3.08 us  [on_device(): lax.ppermute(message[k], 'z', [(z, (z + k) % 4) for z in range(4)])]
    ppermute x1, waiting for transfers between devices: 0.01 us -> 23.8 us  [on_device(): down_1 = lax.ppermute(own_b, 'z', DOWN)]
    ppermute x1, starting transfers between devices: 4.19 us -> 0.85 us  [on_device(): down_1 = lax.ppermute(own_b, 'z', DOWN)]
    ppermute x1, waiting for transfers between devices: 23.6 us -> 20.8 us  [on_device(): down_2 = lax.ppermute(choose(plane1, 3, down_1, own_a), 'z', DOWN)]
where the time goes in v5:
time: 237 us
  blocking collectives  130 us (55%)
  waiting for transfers between devices  57.7 us (24%)
  Pallas kernels  29.2 us (12%)
  starting transfers between devices  15.4 us (6%)
  local copies, waits for them, and re-layouts  2.71 us (1%)
    all_to_all x6, blocking collectives, exchange(): lax.all_to_all(value.reshape(CHIPS, 4, COLS, WIDTH), ('x', 'y'), 0, 0, ti...  116 us
    ppermute x1, waiting for transfers between devices, on_device(): down_1 = lax.ppermute(own_b, 'z', DOWN)  23.8 us
    ppermute x1, waiting for transfers between devices, on_device(): down_2 = lax.ppermute(choose(plane1, 3, down_1, own_a), 'z', DOWN)  20.8 us
    all_to_all x1, blocking collectives, on_device(): fx = lax.all_to_all(fx, 'z', 0, 0, tiled=True)  14 us
    pallas_call x3, Pallas kernels, forward_level(): pl.pallas_call(functools.partial(forward_kernel, level), in_specs=[SMEM,...  12.3 us
    pallas_call x3, Pallas kernels, backward_level(): pl.pallas_call(functools.partial(backward_kernel, level), in_specs=[SMEM,...  10.3 us
    ppermute x10, waiting for transfers between devices, swap(): return lax.ppermute(value, 'c', [(0, 1), (1, 0)])  6.35 us
    ppermute x3, starting transfers between devices, on_device(): lax.ppermute(message[k], 'z', [(z, (z + k) % 4) for z in range(4)])  5.45 us
  transfers between devices with their start and end apart: 19, of which 9 were waited for; matrix products, arithmetic and copies ran while one was open for 0% of the time, Pallas kernels for 3%

profile of v5, /device:TPU:0, one launch (start us, length us, event | category | flops | bytes accessed | tf_op | source)
XLA Modules:
  0.0 237.0 jit_solution(5993374208860960614)
XLA Ops:
  0.6 0.7 convert_element_type.11
  1.4 1.0 copy-done.2
  2.4 0.1 tell_planes.1
  2.6 4.2 %collective-permute-start.2 = (bf16[144,256]{1,0:T(8,128)(2,1)S(1)}, bf16[144,256]{1,0:T(8,128)(2,1)S(1)}, u32[]{:S(2)}, u32[]{:S(2)}) collective-permute-start(bf16[144,256]{1,0:T(8,128)(2,1)S(1)} %get-tuple-element.82), channel_id=1, source_target_pairs={{0,3},{1,0},{2,1},{3,2},{4,7},{5,4},{6,5},{7,6},{8,11},{9,8},{10,9... | collective-permute-start | bytes 221192 | tf_op jit(solution)/shard_map/tell_planes/ppermute | solution.py:355
  6.8 1.3 collective-permute-start
  8.1 1.6 copy-done
  9.6 0.3 factor_step_1.3.here_ref.else_ref.rest_3_.rest_4_.rest_1_
  9.9 0.3 factor_step_1.2.else_ref.here_ref.rest_2_.rest_3_.rest_0_
  10.2 2.6 %collective-permute-done.1 = bf16[144,256]{1,0:T(8,128)(2,1)S(1)} collective-permute-done((bf16[144,256]{1,0:T(8,128)(2,1)S(1)}, bf16[144,256]{1,0:T(8,128)(2,1)S(1)}, u32[]{:S(2)}, u32[]{:S(2)}) %collective-permute-start.1) | collective-permute-done | bytes 73760 | tf_op jit(solution)/shard_map/tell_planes/ppermute | solution.py:355
  12.9 0.4 collective-permute-done
  13.3 0.9 collective-permute-start.5
  14.2 1.2 collective-permute-start.3
  15.4 0.6 collective-permute-start.7
  16.0 0.1 collective-permute-start.8
  16.1 23.8 %collective-permute-done.5.here_ref.else_ref.rest_5_.rest_6_.rest_3_ = bf16[9,256,256]{2,1,0:T(8,128)(2,1)S(1)} collective-permute-done((bf16[9,256,256]{2,1,0:T(8,128)(2,1)S(1)}, bf16[9,256,256]{2,1,0:T(8,128)(2,1)S(1)}, u32[]{:S(2)}, u32[]{:S(2)}) %collective-permute-start.5) | collective-permute-done | bytes 1179680 | tf_op jit(solution)/shard_map/factor_step_1/ppermute | solution.py:361
  39.8 0.6 factor_step_2.5
  40.5 2.1 collective-permute-start.6
  42.6 0.6 factor_step_2.4
  43.3 0.1 collective-permute-start.11
  43.4 0.5 collective-permute-start.10
  44.0 0.6 factor_step_2.7
  44.6 0.6 factor_step_2.6
  45.3 20.8 %collective-permute-done.6.rest_7_.rest_8_.rest_5_ = bf16[9,256,256]{2,1,0:T(8,128)(2,1)S(1)} collective-permute-done((bf16[9,256,256]{2,1,0:T(8,128)(2,1)S(1)}, bf16[9,256,256]{2,1,0:T(8,128)(2,1)S(1)}, u32[]{:S(2)}, u32[]{:S(2)}) %collective-permute-start.6) | collective-permute-done | bytes 1179680 | tf_op jit(solution)/shard_map/factor_step_2/ppermute | solution.py:373
  66.1 3.7 %collective-permute-done.4.rest_6_.rest_7_.rest_4_ = bf16[9,256,256]{2,1,0:T(8,128)(2,1)S(1)} collective-permute-done((bf16[9,256,256]{2,1,0:T(8,128)(2,1)S(1)}, bf16[9,256,256]{2,1,0:T(8,128)(2,1)S(1)}, u32[]{:S(2)}, u32[]{:S(2)}) %collective-permute-start.4) | collective-permute-done | bytes 1179680 | tf_op jit(solution)/shard_map/factor_step_2/ppermute | solution.py:372
  69.8 0.5 collective-permute-start.13
  70.3 3.2 %collective-permute-start.15 = (bf16[9,256,256]{2,1,0:T(8,128)(2,1)S(1)}, bf16[9,256,256]{2,1,0:T(8,128)(2,1)S(1)}, u32[]{:S(2)}, u32[]{:S(2)}) collective-permute-start(bf16[9,256,256]{2,1,0:T(8,128)(2,1)S(1)} %factor_step_2.7), channel_id=1, source_target_pairs={{0,3},{1,0},{2,1},{3,2},{4,7},{5,4},{6,5},{7,6},{8,11},{9,8},{10,9... | collective-permute-start | bytes 3538952 | tf_op jit(solution)/shard_map/factor_step_3/ppermute | solution.py:383
  73.6 0.8 collective-permute-done.13.rest_13_.rest_16_.rest_11_
  74.4 4.0 %forward_0.1 = (f32[4,32,256]{2,1,0:T(8,128)S(1)}, bf16[4,32,256]{2,1,0:T(8,128)(2,1)S(1)}, bf16[64,32,256]{2,1,0:T(8,128)(2,1)S(1)}) custom-call(s32[1]{0:T(128)} %bitcast.1.plane_ref, s32[4,4,8]{2,1,0:T(4,128)S(1)} %fusion.3.at_ref, bf16[4,144,256]{2,1,0:T(8,128)(2,1)S(1)} %pad_maximum_fusion.1.rest_0_.rest_1_.own_told, ...), custom_call_target="tpu_custom_call" | custom-call | flops 150994944 | bytes 6291456 | tf_op jit(solution)/shard_map/forward_0/pallas_call | solution.py:237
  78.4 24.2 %all_to_all.35.got_ref = bf16[16,4,32,256]{3,2,1,0:T(8,128)(2,1)S(1)} all-to-all(bf16[16,4,32,256]{3,2,1,0:T(8,128)(2,1)S(1)} %bitcast.56), channel_id=1, replica_groups=mesh['x'=4,'y'=4,'c'=2,'z'=4] {'x','y'}, dimensions={0} | all-to-all | bytes 2097152 | tf_op jit(solution)/shard_map/forward_0/all_to_all | solution.py:340
  102.6 0.1 factor_step_3.1.rest_0_
  102.8 0.1 collective-permute-start.16
  102.9 0.5 collective-permute-start.17
  103.4 2.3 collective-permute-done.16.rest_17_.rest_10_.rest_14_
  105.7 1.7 collective-permute-done.17.rest_18_.rest_11_.rest_15_
  107.4 4.0 %forward_1.1 = (f32[4,32,256]{2,1,0:T(8,128)S(1)}, bf16[4,32,256]{2,1,0:T(8,128)(2,1)S(1)}, bf16[64,32,256]{2,1,0:T(8,128)(2,1)S(1)}) custom-call(s32[1]{0:T(128)} %bitcast.1.plane_ref, s32[4,4,8]{2,1,0:T(4,128)S(1)} %fusion.3.at_ref, f32[4,32,256]{2,1,0:T(8,128)S(1)} %factor_step_3.1.rest_0_, ...), custom_call_target="tpu_custom_call" | custom-call | flops 150994944 | bytes 6291456 | tf_op jit(solution)/shard_map/forward_1/pallas_call | solution.py:237
  111.4 20.8 %all_to_all.36.rest_0_ = bf16[16,4,32,256]{3,2,1,0:T(8,128)(2,1)S(1)} all-to-all(bf16[16,4,32,256]{3,2,1,0:T(8,128)(2,1)S(1)} %bitcast.54), channel_id=1, replica_groups=mesh['x'=4,'y'=4,'c'=2,'z'=4] {'x','y'}, dimensions={0} | all-to-all | bytes 2097152 | tf_op jit(solution)/shard_map/forward_1/all_to_all | solution.py:340
  132.2 4.3 %forward_2.1 = (f32[4,32,256]{2,1,0:T(8,128)S(1)}, bf16[4,32,256]{2,1,0:T(8,128)(2,1)S(1)}, bf16[64,32,256]{2,1,0:T(8,128)(2,1)S(1)}) custom-call(s32[1]{0:T(128)} %bitcast.1.plane_ref, s32[4,4,8]{2,1,0:T(4,128)S(1)} %fusion.3.at_ref, bf16[16,4,32,256]{3,2,1,0:T(8,128)(2,1)S(1)} %all_to_all.36.rest_0_, ...), custom_call_target="tpu_custom_call" | custom-call | flops 150994944 | bytes 6291456 | tf_op jit(solution)/shard_map/forward_2/pallas_call | solution.py:237
  136.5 19.5 %all_to_all.37.got_ref = bf16[16,4,32,256]{3,2,1,0:T(8,128)(2,1)S(1)} all-to-all(bf16[16,4,32,256]{3,2,1,0:T(8,128)(2,1)S(1)} %bitcast.55), channel_id=1, replica_groups=mesh['x'=4,'y'=4,'c'=2,'z'=4] {'x','y'}, dimensions={0} | all-to-all | bytes 2097152 | tf_op jit(solution)/shard_map/forward_2/all_to_all | solution.py:340
  156.0 2.2 top.1
  158.3 18.3 %all_to_all.38 = bf16[16,4,32,256]{3,2,1,0:T(8,128)(2,1)S(1)} all-to-all(bf16[16,4,32,256]{3,2,1,0:T(8,128)(2,1)S(1)} %get-tuple-element.67), channel_id=1, replica_groups=mesh['x'=4,'y'=4,'c'=2,'z'=4] {'x','y'}, dimensions={0} | all-to-all | bytes 2097152 | tf_op jit(solution)/shard_map/backward_2/all_to_all | solution.py:340
  176.6 3.4 %backward_2.1 = (bf16[4,32,256]{2,1,0:T(8,128)(2,1)S(1)}, bf16[16,4,32,256]{3,2,1,0:T(8,128)(2,1)S(1)}) custom-call(s32[1]{0:T(128)} %bitcast.1.plane_ref, s32[4,4,8]{2,1,0:T(4,128)S(1)} %fusion.3.at_ref, bf16[64,32,256]{2,1,0:T(8,128)(2,1)S(1)} %bitcast.51, f32[4,32,256]{2,1,0:T(8,128)S(1)} %get-tuple-element.68.f_ref, ...), custom_call_target="tpu_custom_call" | custom-call | flops 150994944 | bytes 6291456 | tf_op jit(solution)/shard_map/backward_2/pallas_call | solution.py:302
  180.0 17.1 %all_to_all.39 = bf16[16,4,32,256]{3,2,1,0:T(8,128)(2,1)S(1)} all-to-all(bf16[16,4,32,256]{3,2,1,0:T(8,128)(2,1)S(1)} %get-tuple-element.69), channel_id=1, replica_groups=mesh['x'=4,'y'=4,'c'=2,'z'=4] {'x','y'}, dimensions={0} | all-to-all | bytes 2097152 | tf_op jit(solution)/shard_map/backward_1/all_to_all | solution.py:340
  197.1 3.4 %backward_1.1 = (bf16[4,32,256]{2,1,0:T(8,128)(2,1)S(1)}, bf16[16,4,32,256]{3,2,1,0:T(8,128)(2,1)S(1)}) custom-call(s32[1]{0:T(128)} %bitcast.1.plane_ref, s32[4,4,8]{2,1,0:T(4,128)S(1)} %fusion.3.at_ref, bf16[64,32,256]{2,1,0:T(8,128)(2,1)S(1)} %bitcast.50, f32[4,32,256]{2,1,0:T(8,128)S(1)} %get-tuple-element.70.f_ref, ...), custom_call_target="tpu_custom_call" | custom-call | flops 150994944 | bytes 6291456 | tf_op jit(solution)/shard_map/backward_1/pallas_call | solution.py:302
  200.5 16.2 %all_to_all.40 = bf16[16,4,32,256]{3,2,1,0:T(8,128)(2,1)S(1)} all-to-all(bf16[16,4,32,256]{3,2,1,0:T(8,128)(2,1)S(1)} %get-tuple-element.71), channel_id=1, replica_groups=mesh['x'=4,'y'=4,'c'=2,'z'=4] {'x','y'}, dimensions={0} | all-to-all | bytes 2097152 | tf_op jit(solution)/shard_map/backward_0/all_to_all | solution.py:340
  216.7 3.4 %backward_0.1 = bf16[4,32,256]{2,1,0:T(8,128)(2,1)S(1)} custom-call(s32[1]{0:T(128)} %bitcast.1.plane_ref, s32[4,4,8]{2,1,0:T(4,128)S(1)} %fusion.3.at_ref, bf16[64,32,256]{2,1,0:T(8,128)(2,1)S(1)} %bitcast.49, f32[4,32,256]{2,1,0:T(8,128)S(1)} %get-tuple-element.72.f_ref, bf16[9,256,256]{2,1,0:T(8,128)(2,1)S(1)} %factor_step_1.2.else_ref.here_ref.rest_2_.rest_3_.rest_0_, ...), custom_call_target="tpu_custom_call" | custom-call | flops 150994944 | bytes 6291456 | tf_op jit(solution)/shard_map/backward_0/pallas_call | solution.py:302
  220.3 1.5 collective-permute-done.18
  221.9 14.0 %all_to_all.41.fx_ref = bf16[4,2,2,2,32,256]{5,4,3,2,1,0:T(8,128)(2,1)S(1)} all-to-all(bf16[4,2,2,2,32,256]{5,4,3,2,1,0:T(8,128)(2,1)S(1)} %pad_maximum_fusion), channel_id=1, replica_groups=mesh['x'=4,'y'=4,'c'=2,'z'=4] {'z'}, dimensions={0} | all-to-all | bytes 1048576 | tf_op jit(solution)/shard_map/to_planes/all_to_all | solution.py:414
  235.9 1.1 to_planes.1
  (30 shorter events, 0.5 us)
Async XLA Ops:
  0.6 7.4 %copy-start.1 = (bf16[1,2,1,256,256]{4,3,2,1,0:T(8,128)(2,1)S(1)}, bf16[1,2,1,256,256]{4,3,2,1,0:T(8,128)(2,1)}, u32[]{:S(2)}) copy-start(bf16[1,2,1,256,256]{4,3,2,1,0:T(8,128)(2,1)} %param.5) | copy-start | bytes 786436
  1.4 1.0 copy-start.2
  2.6 7.6 %collective-permute-start.2 = (bf16[144,256]{1,0:T(8,128)(2,1)S(1)}, bf16[144,256]{1,0:T(8,128)(2,1)S(1)}, u32[]{:S(2)}, u32[]{:S(2)}) collective-permute-start(bf16[144,256]{1,0:T(8,128)(2,1)S(1)} %get-tuple-element.82), channel_id=1, source_target_pairs={{0,3},{1,0},{2,1},{3,2},{4,7},{5,4},{6,5},{7,6},{8,11},{9,8},{10,9... | collective-permute-start | bytes 221192 | tf_op jit(solution)/shard_map/tell_planes/ppermute | solution.py:355
  6.8 6.1 %collective-permute-start.1 = (bf16[144,256]{1,0:T(8,128)(2,1)S(1)}, bf16[144,256]{1,0:T(8,128)(2,1)S(1)}, u32[]{:S(2)}, u32[]{:S(2)}) collective-permute-start(bf16[144,256]{1,0:T(8,128)(2,1)S(1)} %get-tuple-element.83), channel_id=1, source_target_pairs={{0,2},{1,3},{2,0},{3,1},{4,6},{5,7},{6,4},{7,5},{8,10},{9,11},{10,... | collective-permute-start | bytes 221192 | tf_op jit(solution)/shard_map/tell_planes/ppermute | solution.py:355
  6.8 6.5 %collective-permute-start = (bf16[144,256]{1,0:T(8,128)(2,1)S(1)}, bf16[144,256]{1,0:T(8,128)(2,1)S(1)}, u32[]{:S(2)}, u32[]{:S(2)}) collective-permute-start(bf16[144,256]{1,0:T(8,128)(2,1)S(1)} %get-tuple-element.84), channel_id=1, source_target_pairs={{0,1},{1,2},{2,3},{3,0},{4,5},{5,6},{6,7},{7,4},{8,9},{9,10},{10,1... | collective-permute-start | bytes 221192 | tf_op jit(solution)/shard_map/tell_planes/ppermute | solution.py:355
  8.1 1.6 copy-start
  13.3 26.5 %collective-permute-start.5 = (bf16[9,256,256]{2,1,0:T(8,128)(2,1)S(1)}, bf16[9,256,256]{2,1,0:T(8,128)(2,1)S(1)}, u32[]{:S(2)}, u32[]{:S(2)}) collective-permute-start(bf16[9,256,256]{2,1,0:T(8,128)(2,1)S(1)} %factor_step_1.3.here_ref.else_ref.rest_3_.rest_4_.rest_1_), channel_id=1, source_target_pairs={{0,3},{1,0},{2,1},{3,2},{4,7},{5,4},{6,5},{7,6},{8,11},{9,8},{10,9... | collective-permute-start | bytes 3538952 | tf_op jit(solution)/shard_map/factor_step_1/ppermute | solution.py:361
  14.2 28.4 %collective-permute-start.3 = (bf16[9,256,256]{2,1,0:T(8,128)(2,1)S(1)}, bf16[9,256,256]{2,1,0:T(8,128)(2,1)S(1)}, u32[]{:S(2)}, u32[]{:S(2)}) collective-permute-start(bf16[9,256,256]{2,1,0:T(8,128)(2,1)S(1)} %factor_step_1.2.else_ref.here_ref.rest_2_.rest_3_.rest_0_), channel_id=1, source_target_pairs={{0,1},{1,2},{2,3},{3,0},{4,5},{5,6},{6,7},{7,4},{8,9},{9,10},{10,1... | collective-permute-start | bytes 3538952 | tf_op jit(solution)/shard_map/factor_step_1/ppermute | solution.py:360
  15.3 28.1 %collective-permute-start.9 = (bf16[9,256,256]{2,1,0:T(8,128)(2,1)S(1)}, bf16[9,256,256]{2,1,0:T(8,128)(2,1)S(1)}, u32[]{:S(2)}, u32[]{:S(2)}) collective-permute-start(bf16[9,256,256]{2,1,0:T(8,128)(2,1)S(1)} %factor_step_1.3.here_ref.else_ref.rest_3_.rest_4_.rest_1_), channel_id=1, source_target_pairs={{0,4},{4,0},{1,5},{5,1},{2,6},{6,2},{3,7},{7,3},{8,12},{12,8},{9,1... | collective-permute-start | bytes 3538952 | tf_op jit(solution)/shard_map/factor_step_1/ppermute | solution.py:336
  15.4 27.9 %collective-permute-start.7 = (bf16[4,144,256]{2,1,0:T(8,128)(2,1)S(1)}, bf16[4,144,256]{2,1,0:T(8,128)(2,1)S(1)}, u32[]{:S(2)}, u32[]{:S(2)}) collective-permute-start(bf16[4,144,256]{2,1,0:T(8,128)(2,1)S(1)} %pad_maximum_fusion.1.rest_0_.rest_1_.own_told), channel_id=1, source_target_pairs={{0,4},{4,0},{1,5},{5,1},{2,6},{6,2},{3,7},{7,3},{8,12},{12,8},{9,1... | collective-permute-start | bytes 884744 | tf_op jit(solution)/shard_map/tell_planes/ppermute | solution.py:336
  16.0 29.3 %collective-permute-start.8 = (bf16[9,256,256]{2,1,0:T(8,128)(2,1)S(1)}, bf16[9,256,256]{2,1,0:T(8,128)(2,1)S(1)}, u32[]{:S(2)}, u32[]{:S(2)}) collective-permute-start(bf16[9,256,256]{2,1,0:T(8,128)(2,1)S(1)} %factor_step_1.2.else_ref.here_ref.rest_2_.rest_3_.rest_0_), channel_id=1, source_target_pairs={{0,4},{4,0},{1,5},{5,1},{2,6},{6,2},{3,7},{7,3},{8,12},{12,8},{9,1... | collective-permute-start | bytes 3538952 | tf_op jit(solution)/shard_map/factor_step_1/ppermute | solution.py:336
  40.5 25.7 %collective-permute-start.6 = (bf16[9,256,256]{2,1,0:T(8,128)(2,1)S(1)}, bf16[9,256,256]{2,1,0:T(8,128)(2,1)S(1)}, u32[]{:S(2)}, u32[]{:S(2)}) collective-permute-start(bf16[9,256,256]{2,1,0:T(8,128)(2,1)S(1)} %factor_step_2.5), channel_id=1, source_target_pairs={{0,3},{1,0},{2,1},{3,2},{4,7},{5,4},{6,5},{7,6},{8,11},{9,8},{10,9... | collective-permute-start | bytes 3538952 | tf_op jit(solution)/shard_map/factor_step_2/ppermute | solution.py:373
  43.2 26.6 %collective-permute-start.4 = (bf16[9,256,256]{2,1,0:T(8,128)(2,1)S(1)}, bf16[9,256,256]{2,1,0:T(8,128)(2,1)S(1)}, u32[]{:S(2)}, u32[]{:S(2)}) collective-permute-start(bf16[9,256,256]{2,1,0:T(8,128)(2,1)S(1)} %factor_step_2.4), channel_id=1, source_target_pairs={{0,1},{1,2},{2,3},{3,0},{4,5},{5,6},{6,7},{7,4},{8,9},{9,10},{10,1... | collective-permute-start | bytes 3538952 | tf_op jit(solution)/shard_map/factor_step_2/ppermute | solution.py:372
  43.3 22.8 %collective-permute-start.11 = (bf16[9,256,256]{2,1,0:T(8,128)(2,1)S(1)}, bf16[9,256,256]{2,1,0:T(8,128)(2,1)S(1)}, u32[]{:S(2)}, u32[]{:S(2)}) collective-permute-start(bf16[9,256,256]{2,1,0:T(8,128)(2,1)S(1)} %collective-permute-done.5.here_ref.else_ref.rest_5_.rest_6_.rest_3_), channel_id=1, source_target_pairs={{0,4},{4,0},{1,5},{5,1},{2,6},{6,2},{3,7},{7,3},{8,12},{12,8},{9,1... | collective-permute-start | bytes 3538952 | tf_op jit(solution)/shard_map/factor_step_2/ppermute | solution.py:336
  43.4 26.4 %collective-permute-start.10 = (bf16[9,256,256]{2,1,0:T(8,128)(2,1)S(1)}, bf16[9,256,256]{2,1,0:T(8,128)(2,1)S(1)}, u32[]{:S(2)}, u32[]{:S(2)}) collective-permute-start(bf16[9,256,256]{2,1,0:T(8,128)(2,1)S(1)} %collective-permute-done.3.else_ref.here_ref.rest_4_.rest_5_.rest_2_), channel_id=1, source_target_pairs={{0,4},{4,0},{1,5},{5,1},{2,6},{6,2},{3,7},{7,3},{8,12},{12,8},{9,1... | collective-permute-start | bytes 3538952 | tf_op jit(solution)/shard_map/factor_step_2/ppermute | solution.py:336
  69.8 3.8 %collective-permute-start.12 = (bf16[9,256,256]{2,1,0:T(8,128)(2,1)S(1)}, bf16[9,256,256]{2,1,0:T(8,128)(2,1)S(1)}, u32[]{:S(2)}, u32[]{:S(2)}) collective-permute-start(bf16[9,256,256]{2,1,0:T(8,128)(2,1)S(1)} %collective-permute-done.4.rest_6_.rest_7_.rest_4_), channel_id=1, source_target_pairs={{0,4},{4,0},{1,5},{5,1},{2,6},{6,2},{3,7},{7,3},{8,12},{12,8},{9,1... | collective-permute-start | bytes 3538952 | tf_op jit(solution)/shard_map/factor_step_2/ppermute | solution.py:336
  69.8 4.5 %collective-permute-start.13 = (bf16[9,256,256]{2,1,0:T(8,128)(2,1)S(1)}, bf16[9,256,256]{2,1,0:T(8,128)(2,1)S(1)}, u32[]{:S(2)}, u32[]{:S(2)}) collective-permute-start(bf16[9,256,256]{2,1,0:T(8,128)(2,1)S(1)} %collective-permute-done.6.rest_7_.rest_8_.rest_5_), channel_id=1, source_target_pairs={{0,4},{4,0},{1,5},{5,1},{2,6},{6,2},{3,7},{7,3},{8,12},{12,8},{9,1... | collective-permute-start | bytes 3538952 | tf_op jit(solution)/shard_map/factor_step_2/ppermute | solution.py:336
  70.3 32.4 %collective-permute-start.14 = (bf16[9,256,256]{2,1,0:T(8,128)(2,1)S(1)}, bf16[9,256,256]{2,1,0:T(8,128)(2,1)S(1)}, u32[]{:S(2)}, u32[]{:S(2)}) collective-permute-start(bf16[9,256,256]{2,1,0:T(8,128)(2,1)S(1)} %factor_step_2.6), channel_id=1, source_target_pairs={{0,1},{1,2},{2,3},{3,0},{4,5},{5,6},{6,7},{7,4},{8,9},{9,10},{10,1... | collective-permute-start | bytes 3538952 | tf_op jit(solution)/shard_map/factor_step_3/ppermute | solution.py:382
  70.3 32.4 %collective-permute-start.15 = (bf16[9,256,256]{2,1,0:T(8,128)(2,1)S(1)}, bf16[9,256,256]{2,1,0:T(8,128)(2,1)S(1)}, u32[]{:S(2)}, u32[]{:S(2)}) collective-permute-start(bf16[9,256,256]{2,1,0:T(8,128)(2,1)S(1)} %factor_step_2.7), channel_id=1, source_target_pairs={{0,3},{1,0},{2,1},{3,2},{4,7},{5,4},{6,5},{7,6},{8,11},{9,8},{10,9... | collective-permute-start | bytes 3538952 | tf_op jit(solution)/shard_map/factor_step_3/ppermute | solution.py:383
  102.8 2.9 %collective-permute-start.16 = (bf16[9,256,256]{2,1,0:T(8,128)(2,1)S(1)}, bf16[9,256,256]{2,1,0:T(8,128)(2,1)S(1)}, u32[]{:S(2)}, u32[]{:S(2)}) collective-permute-start(bf16[9,256,256]{2,1,0:T(8,128)(2,1)S(1)} %collective-permute-done.14.rest_9_.rest_4_.rest_6_), channel_id=1, source_target_pairs={{0,4},{4,0},{1,5},{5,1},{2,6},{6,2},{3,7},{7,3},{8,12},{12,8},{9,1... | collective-permute-start | bytes 3538952 | tf_op jit(solution)/shard_map/factor_step_3/ppermute | solution.py:336
  102.9 4.5 %collective-permute-start.17 = (bf16[9,256,256]{2,1,0:T(8,128)(2,1)S(1)}, bf16[9,256,256]{2,1,0:T(8,128)(2,1)S(1)}, u32[]{:S(2)}, u32[]{:S(2)}) collective-permute-start(bf16[9,256,256]{2,1,0:T(8,128)(2,1)S(1)} %collective-permute-done.15.rest_10_.rest_5_.rest_7_), channel_id=1, source_target_pairs={{0,4},{4,0},{1,5},{5,1},{2,6},{6,2},{3,7},{7,3},{8,12},{12,8},{9,1... | collective-permute-start | bytes 3538952 | tf_op jit(solution)/shard_map/factor_step_3/ppermute | solution.py:336
  220.2 1.6 collective-permute-start.18

commit v6 on v5

--- a/solution.py
+++ b/solution.py
@@ -37,10 +37,16 @@
 KEEP, SEND, PAT, ROWS = 0, 64, 128, 144
 
 
-def pack_kernel(core_ref, plane_ref, rhs_ref, pat_ref, out_ref):
+def pack_kernel(core_ref, plane_ref, pat_ref, rhs_ref, out_ref):
     core, plane = core_ref[0], plane_ref[0]
+    row = lax.broadcasted_iota(jnp.int32, (ROWS - PAT, WIDTH), 0)
+    col = lax.broadcasted_iota(jnp.int32, (ROWS - PAT, WIDTH), 1)
+    pat = jnp.zeros((ROWS - PAT, WIDTH), F32)
+    for j in range(2):
+        for p in range(FAN):
+            pat = jnp.where((row == j) & (col == p), pat_ref[j, p].astype(F32), pat)
     for k in range(4):
-        out_ref[k, PAT:ROWS] = pat_ref[...]
+        out_ref[k, PAT:ROWS] = pat.astype(BF)
     for j in range(2):
         rt = jnp.transpose(rhs_ref[j]).astype(BF)
         for half in range(2):
@@ -50,15 +56,15 @@
                 out_ref[jnp.bitwise_and(z - plane + 4, 3), pl.ds(at, COLS)] = rt[first : first + COLS]
 
 
-def pack(core, plane, rhs, pat):
+def pack(core, plane, pat, rhs):
     return pl.pallas_call(
         pack_kernel,
         out_shape=jax.ShapeDtypeStruct((4, ROWS, WIDTH), BF),
-        in_specs=[SMEM, SMEM, VM, VM],
+        in_specs=[SMEM, SMEM, SMEM, VM],
         out_specs=VM,
         compiler_params=pltpu.CompilerParams(vmem_limit_bytes=8 * MIB),
         cost_estimate=pl.CostEstimate(flops=0, bytes_accessed=2 * MIB, transcendentals=0),
-    )(core, plane, rhs, pat)
+    )(core, plane, pat, rhs)
 
 
 ANY = pl.BlockSpec(memory_space=pl.ANY)
@@ -135,7 +141,7 @@
     return sorted(set(WHERE[level][0] + WHERE[level][1]))
 
 
-def factor_copies(level, plane, refs, buf, sems):
+def factor_copies(level, plane, refs, buf, sems, nodes=(0, 1, 2, 3)):
     names = used(level)
 
     def copy(n, z):
@@ -146,28 +152,28 @@
 
         @pl.when(plane == z)
         def _():
-            for n in range(4):
+            for n in nodes:
                 copy(n, z).start()
 
-    return [copy(n, 0) for n in range(4)]
+    return {n: copy(n, 0) for n in nodes}
 
 
 def told_by(plane, level):
     return jnp.bitwise_and(plane - level + 4, 3)
 
 
-def add_terms(n, at_ref, came, solved, buf, acc_ref):
-    terms = dot_t(solved, buf[n, :FAN].reshape(FAN * WIDTH, WIDTH))
+def add_terms(n, at_ref, came, solved, block, acc_ref):
+    terms = dot_t(solved, block[:FAN].reshape(FAN * WIDTH, WIDTH))
     for p in range(FAN):
         acc_ref[at_ref[came, n, p]] += terms[:, p * WIDTH : (p + 1) * WIDTH]
 
 
-def row_copies(came, refs, rows, sems):
+def row_copies(came, refs, rows, sems, cores=(0, 1)):
     copies = []
-    for r in range(2):
+    for r in cores:
         src = refs[r].at[came, pl.ds((KEEP, SEND)[r], 2 * COLS)]
         copies.append(pltpu.make_async_copy(src, rows.at[pl.ds(2 * COLS * r, 2 * COLS)], sems.at[r]))
-        copies[r].start()
+        copies[-1].start()
     return copies
 
 
@@ -190,29 +196,44 @@
     )(got)
 
 
-def forward_kernel(level, plane_ref, at_ref, *rest):
+def forward_kernel(level, part, core_ref, plane_ref, at_ref, *rest):
     gots, rest = (rest[:1], rest[1:]) if level else ((), rest)
-    told, refs, (f_ref, fb_ref, share_ref, rows, rsems, buf, sems, acc_ref) = rest[:2], rest[2:-8], rest[-8:]
+    before, rest = (rest[:3], rest[3:]) if part == 1 else ((), rest)
+    told, refs, (f_ref, fb_ref, out_ref, rows, rsems, buf, sems, acc_ref) = rest[:2], rest[2:-8], rest[-8:]
     came = told_by(plane_ref[0], level)
     copies_r = row_copies(came, told, rows, rsems)
-    copies = factor_copies(level, plane_ref[0], refs, buf, sems)
-    acc_ref[...] = jnp.zeros_like(acc_ref)
+
+    def run(nodes):
+        copies = factor_copies(level, plane_ref[0], refs, buf, sems, nodes)
+        solved = {}
+        for n in nodes:
+            resid = rows_of(rows, n, COLS)
+            if level:
+                inflow = gots[0][n] if level == 1 else jnp.sum(gots[0][:, n].astype(F32), axis=0)
+                resid = (resid.astype(F32) - inflow).astype(BF)
+            copies[n].wait()
+            f = dot_t(resid, buf[n, FAN])
+            f_ref[n] = f
+            solved[n] = f.astype(BF)
+            fb_ref[n] = solved[n]
+        for n in nodes:
+            add_terms(n, at_ref, came, solved[n], buf.at[n], acc_ref)
+
+    if part == 1:
+        f_ref[...], fb_ref[...], acc_ref[...] = before[0][...], before[1][...], before[2][...]
+    else:
+        acc_ref[...] = jnp.zeros_like(acc_ref)
     for copy in copies_r:
         copy.wait()
-    solved = []
-    for n in range(4):
-        resid = rows_of(rows, n, COLS)
-        if level:
-            inflow = gots[0][n] if level == 1 else jnp.sum(gots[0][:, n].astype(F32), axis=0)
-            resid = (resid.astype(F32) - inflow).astype(BF)
-        copies[n].wait()
-        f = dot_t(resid, buf[n, FAN])
-        f_ref[n] = f
-        solved.append(f.astype(BF))
-        fb_ref[n] = solved[n]
-    for n in range(4):
-        add_terms(n, at_ref, came, solved[n], buf, acc_ref)
-    share_ref[...] = acc_ref[...].astype(BF)
+    if part is None:
+        run((0, 1, 2, 3))
+    elif part == 0:
+        f_ref[...], fb_ref[...] = jnp.zeros_like(f_ref), jnp.zeros_like(fb_ref)
+        pl.when(core_ref[0] == 1)(lambda: run((0, 1, 2)))
+    else:
+        pl.when(core_ref[0] == 1)(lambda: run((3,)))
+        pl.when(core_ref[0] == 0)(lambda: run((0, 1, 2, 3)))
+    out_ref[...] = acc_ref[...].astype(out_ref.dtype)
 
 
 SMALL = [
@@ -232,17 +253,27 @@
     return [factors[r][k] for r in range(2) for k in used(level)]
 
 
-def forward_level(level, plane, at, gots, told, factors):
-    blocks = pick(level, factors)
-    return pl.pallas_call(
-        functools.partial(forward_kernel, level),
-        in_specs=[SMEM, SMEM] + [VM] * len(gots) + any_specs(2) + [ANY] * len(blocks),
+def forward_part(level, part, here, at, gots, before, told, blocks):
+    last = jax.ShapeDtypeStruct((NODES, COLS, WIDTH), F32 if part == 0 else BF)
+    return pl.pallas_call(
+        functools.partial(forward_kernel, level, part),
+        in_specs=[SMEM] * 3 + [VM] * (len(gots) + len(before)) + any_specs(2 + len(blocks)),
         out_specs=(VM, VM, VM),
         scratch_shapes=SMALL + LARGE + [pltpu.VMEM((NODES, COLS, WIDTH), F32)],
-        out_shape=(NODE_F32, NODE_BF, jax.ShapeDtypeStruct((NODES, COLS, WIDTH), BF)),
+        out_shape=(NODE_F32, NODE_BF, last),
         compiler_params=pltpu.CompilerParams(vmem_limit_bytes=LIMIT),
         cost_estimate=pl.CostEstimate(flops=2 * 36 * COLS * WIDTH**2, bytes_accessed=6 * MIB, transcendentals=0),
-    )(plane, at, *gots, *told, *blocks)
+    )(*here, at, *gots, *before, *told, *blocks)
+
+
+def forward_level(level, here, at, gots, told, factors):
+    return forward_part(level, None, here, at, gots, (), told, pick(level, factors))
+
+
+def forward_halves(level, here, at, gots, told, factors):
+    early = [factors[0][k] for k in used(level)] + [factors[1][k] for k in used(level) if k < 6]
+    before = forward_part(level, 0, here, at, gots, (), told, early)
+    return forward_part(level, 1, here, at, gots, before, told, pick(level, factors))
 
 
 def top_kernel(plane_ref, got_ref, own_told, other_told, *rest):
@@ -348,8 +379,7 @@
     inverse = inverses.reshape(2, WIDTH, WIDTH)
 
     with jax.named_scope("tell_planes"):
-        pat = jnp.pad(pattern.reshape(2, FAN).astype(BF), ((0, ROWS - PAT - 2), (0, WIDTH - FAN)))
-        message = pack(core1, plane1, rhs.reshape(2, WIDTH, WIDTH), pat)
+        message = pack(core1, plane1, pattern.reshape(2, FAN), rhs.reshape(2, WIDTH, WIDTH))
         told = [message[0]]
         for k in range(1, 4):
             told.append(lax.ppermute(message[k], "z", [(z, (z + k) % 4) for z in range(4)]))
@@ -388,7 +418,8 @@
     gots = ()
     for level in range(3):
         with jax.named_scope(f"forward_{level}"):
-            forward[level], solved[level], share = forward_level(level, plane1, places, gots, told, factors)
+            solve = forward_halves if level == 1 else forward_level
+            forward[level], solved[level], share = solve(level, (core1, plane1), places, gots, told, factors)
             got = exchange(share)
         if level == 0:
             with jax.named_scope("factor_step_3"):

time: 237 us -> 231 us (0.975)
  blocking collectives: 130 us -> 123 us
    all_to_all x6, blocking collectives: 116 us -> 109 us  [exchange(): lax.all_to_all(value.reshape(CHIPS, 4, COLS, WIDTH), ('x', 'y'), 0, 0, ti...]
    pallas_call x3 -> x4, Pallas kernels: 12.3 us -> 13.2 us  [forward_part(): pl.pallas_call(functools.partial(forward_kernel, level, part), in_specs=[...]
  transfers between devices with their start and end apart: 19 -> 19, of which waited for: 9 -> 9; matrix products, arithmetic and copies ran while one was open for 0% -> 0% of each run, Pallas kernels for 3% -> 4%
where the time goes in v6:
time: 231 us; the launch traced here: 230 us
  blocking collectives  123 us (53%)
  waiting for transfers between devices  56.6 us (25%)
  Pallas kernels  30.7 us (13%)
  starting transfers between devices  15.4 us (7%)
  local copies, waits for them, and re-layouts  3.42 us (1%)
    all_to_all x6, blocking collectives, exchange(): lax.all_to_all(value.reshape(CHIPS, 4, COLS, WIDTH), ('x', 'y'), 0, 0, ti...  109 us
    ppermute x1, waiting for transfers between devices, on_device(): down_1 = lax.ppermute(own_b, 'z', DOWN)  23.8 us
    ppermute x1, waiting for transfers between devices, on_device(): down_2 = lax.ppermute(choose(plane1, 3, down_1, own_a), 'z', DOWN)  20.8 us
    all_to_all x1, blocking collectives, on_device(): fx = lax.all_to_all(fx, 'z', 0, 0, tiled=True)  13.9 us
    pallas_call x4, Pallas kernels, forward_part(): pl.pallas_call(functools.partial(forward_kernel, level, part), in_specs=[...  13.2 us
    pallas_call x3, Pallas kernels, backward_level(): pl.pallas_call(functools.partial(backward_kernel, level), in_specs=[SMEM,...  10.3 us
    ppermute x3, starting transfers between devices, on_device(): lax.ppermute(message[k], 'z', [(z, (z + k) % 4) for z in range(4)])  5.45 us
    ppermute x10, waiting for transfers between devices, swap(): return lax.ppermute(value, 'c', [(0, 1), (1, 0)])  5.24 us
  transfers between devices with their start and end apart: 19, of which 9 were waited for; matrix products, arithmetic and copies ran while one was open for 0% of the time, Pallas kernels for 4%

profile of v6, /device:TPU:0, one launch (start us, length us, event | category | flops | bytes accessed | tf_op | source)
XLA Modules:
  0.0 230.1 jit_solution(5213675301617055170)
XLA Ops:
  0.7 1.1 copy-done.2
  1.7 0.7 copy-done.3
  2.4 0.7 tell_planes.1
  3.1 4.2 %collective-permute-start.2 = (bf16[144,256]{1,0:T(8,128)(2,1)S(1)}, bf16[144,256]{1,0:T(8,128)(2,1)S(1)}, u32[]{:S(2)}, u32[]{:S(2)}) collective-permute-start(bf16[144,256]{1,0:T(8,128)(2,1)S(1)} %get-tuple-element.88), channel_id=1, source_target_pairs={{0,3},{1,0},{2,1},{3,2},{4,7},{5,4},{6,5},{7,6},{8,11},{9,8},{10,9... | collective-permute-start | bytes 221192 | tf_op jit(solution)/shard_map/tell_planes/ppermute | solution.py:385
  7.3 1.3 collective-permute-start
  8.6 1.6 copy-done
  10.2 0.3 factor_step_1.3.here_ref.else_ref.rest_3_.rest_4_.rest_7_.rest_1_
  10.4 0.3 factor_step_1.2.else_ref.here_ref.rest_2_.rest_3_.rest_6_.rest_0_
  10.8 2.6 %collective-permute-done.1 = bf16[144,256]{1,0:T(8,128)(2,1)S(1)} collective-permute-done((bf16[144,256]{1,0:T(8,128)(2,1)S(1)}, bf16[144,256]{1,0:T(8,128)(2,1)S(1)}, u32[]{:S(2)}, u32[]{:S(2)}) %collective-permute-start.1) | collective-permute-done | bytes 73760 | tf_op jit(solution)/shard_map/tell_planes/ppermute | solution.py:385
  13.4 0.4 collective-permute-done
  13.8 0.9 collective-permute-start.5
  14.7 1.2 collective-permute-start.3
  15.9 0.6 collective-permute-start.7
  16.5 0.1 collective-permute-start.8
  16.6 23.8 %collective-permute-done.5.here_ref.else_ref.rest_5_.rest_6_.rest_9_.rest_3_ = bf16[9,256,256]{2,1,0:T(8,128)(2,1)S(1)} collective-permute-done((bf16[9,256,256]{2,1,0:T(8,128)(2,1)S(1)}, bf16[9,256,256]{2,1,0:T(8,128)(2,1)S(1)}, u32[]{:S(2)}, u32[]{:S(2)}) %collective-permute-start.5) | collective-permute-done | bytes 1179680 | tf_op jit(solution)/shard_map/factor_step_1/ppermute | solution.py:391
  40.4 0.6 factor_step_2.5
  41.0 2.1 collective-permute-start.6
  43.1 0.6 factor_step_2.4
  43.9 0.1 collective-permute-start.11
  44.0 0.5 collective-permute-start.10
  44.5 0.6 factor_step_2.7
  45.2 0.6 factor_step_2.6
  45.8 20.8 %collective-permute-done.6.rest_7_.rest_8_.rest_11_.rest_5_ = bf16[9,256,256]{2,1,0:T(8,128)(2,1)S(1)} collective-permute-done((bf16[9,256,256]{2,1,0:T(8,128)(2,1)S(1)}, bf16[9,256,256]{2,1,0:T(8,128)(2,1)S(1)}, u32[]{:S(2)}, u32[]{:S(2)}) %collective-permute-start.6) | collective-permute-done | bytes 1179680 | tf_op jit(solution)/shard_map/factor_step_2/ppermute | solution.py:403
  66.7 3.7 %collective-permute-done.4.rest_6_.rest_7_.rest_10_.rest_4_ = bf16[9,256,256]{2,1,0:T(8,128)(2,1)S(1)} collective-permute-done((bf16[9,256,256]{2,1,0:T(8,128)(2,1)S(1)}, bf16[9,256,256]{2,1,0:T(8,128)(2,1)S(1)}, u32[]{:S(2)}, u32[]{:S(2)}) %collective-permute-start.4) | collective-permute-done | bytes 1179680 | tf_op jit(solution)/shard_map/factor_step_2/ppermute | solution.py:402
  70.4 0.5 collective-permute-start.13
  70.9 3.2 %collective-permute-start.15 = (bf16[9,256,256]{2,1,0:T(8,128)(2,1)S(1)}, bf16[9,256,256]{2,1,0:T(8,128)(2,1)S(1)}, u32[]{:S(2)}, u32[]{:S(2)}) collective-permute-start(bf16[9,256,256]{2,1,0:T(8,128)(2,1)S(1)} %factor_step_2.7), channel_id=1, source_target_pairs={{0,3},{1,0},{2,1},{3,2},{4,7},{5,4},{6,5},{7,6},{8,11},{9,8},{10,9... | collective-permute-start | bytes 3538952 | tf_op jit(solution)/shard_map/factor_step_3/ppermute | solution.py:413
  74.1 0.8 collective-permute-done.13.rest_13_.rest_16_.rest_19_.rest_11_
  74.9 4.0 %forward_0.1 = (f32[4,32,256]{2,1,0:T(8,128)S(1)}, bf16[4,32,256]{2,1,0:T(8,128)(2,1)S(1)}, bf16[64,32,256]{2,1,0:T(8,128)(2,1)S(1)}) custom-call(s32[1]{0:T(128)} %bitcast.core_ref, s32[1]{0:T(128)} %bitcast.1.plane_ref, s32[4,4,8]{2,1,0:T(4,128)S(1)} %fusion.3.at_ref, bf16[4,144,256]{2,1,0:T(8,128)(2,1)S(1)} %pad_maximum_fusion.1.rest_0_.rest_1_.rest_4_.own_told, ...), custom_call_target="tpu_custom_call" | custom-call | flops 150994944 | bytes 6291456 | tf_op jit(solution)/shard_map/forward_0/pallas_call | solution.py:258
  78.9 24.2 %all_to_all.35.got_ref = bf16[16,4,32,256]{3,2,1,0:T(8,128)(2,1)S(1)} all-to-all(bf16[16,4,32,256]{3,2,1,0:T(8,128)(2,1)S(1)} %bitcast.54), channel_id=1, replica_groups=mesh['x'=4,'y'=4,'c'=2,'z'=4] {'x','y'}, dimensions={0} | all-to-all | bytes 2097152 | tf_op jit(solution)/shard_map/forward_0/all_to_all | solution.py:371
  103.1 0.1 factor_step_3.1.rest_0_
  103.4 0.5 collective-permute-start.17
  103.9 1.1 forward_1.2
  105.0 1.2 collective-permute-done.16.rest_20_.rest_17_.rest_10_.rest_14_
  106.2 1.7 collective-permute-done.17.rest_21_.rest_18_.rest_11_.rest_15_
  107.9 4.0 %forward_1.3 = (f32[4,32,256]{2,1,0:T(8,128)S(1)}, bf16[4,32,256]{2,1,0:T(8,128)(2,1)S(1)}, bf16[64,32,256]{2,1,0:T(8,128)(2,1)S(1)}) custom-call(s32[1]{0:T(128)} %bitcast.core_ref, s32[1]{0:T(128)} %bitcast.1.plane_ref, s32[4,4,8]{2,1,0:T(4,128)S(1)} %fusion.3.at_ref, f32[4,32,256]{2,1,0:T(8,128)S(1)} %factor_step_3.1.rest_0_, ...), custom_call_target="tpu_custom_call" | custom-call | flops 150994944 | bytes 6291456 | tf_op jit(solution)/shard_map/forward_1/pallas_call | solution.py:258
  112.0 18.9 %all_to_all.36.rest_0_ = bf16[16,4,32,256]{3,2,1,0:T(8,128)(2,1)S(1)} all-to-all(bf16[16,4,32,256]{3,2,1,0:T(8,128)(2,1)S(1)} %bitcast.52), channel_id=1, replica_groups=mesh['x'=4,'y'=4,'c'=2,'z'=4] {'x','y'}, dimensions={0} | all-to-all | bytes 2097152 | tf_op jit(solution)/shard_map/forward_1/all_to_all | solution.py:371
  130.9 4.1 %forward_2.1 = (f32[4,32,256]{2,1,0:T(8,128)S(1)}, bf16[4,32,256]{2,1,0:T(8,128)(2,1)S(1)}, bf16[64,32,256]{2,1,0:T(8,128)(2,1)S(1)}) custom-call(s32[1]{0:T(128)} %bitcast.core_ref, s32[1]{0:T(128)} %bitcast.1.plane_ref, s32[4,4,8]{2,1,0:T(4,128)S(1)} %fusion.3.at_ref, bf16[16,4,32,256]{3,2,1,0:T(8,128)(2,1)S(1)} %all_to_all.36.rest_0_, ...), custom_call_target="tpu_custom_call" | custom-call | flops 150994944 | bytes 6291456 | tf_op jit(solution)/shard_map/forward_2/pallas_call | solution.py:258
  135.0 17.3 %all_to_all.37.got_ref = bf16[16,4,32,256]{3,2,1,0:T(8,128)(2,1)S(1)} all-to-all(bf16[16,4,32,256]{3,2,1,0:T(8,128)(2,1)S(1)} %bitcast.53), channel_id=1, replica_groups=mesh['x'=4,'y'=4,'c'=2,'z'=4] {'x','y'}, dimensions={0} | all-to-all | bytes 2097152 | tf_op jit(solution)/shard_map/forward_2/all_to_all | solution.py:371
  152.3 2.2 top.1
  154.5 16.2 %all_to_all.38 = bf16[16,4,32,256]{3,2,1,0:T(8,128)(2,1)S(1)} all-to-all(bf16[16,4,32,256]{3,2,1,0:T(8,128)(2,1)S(1)} %get-tuple-element.73), channel_id=1, replica_groups=mesh['x'=4,'y'=4,'c'=2,'z'=4] {'x','y'}, dimensions={0} | all-to-all | bytes 2097152 | tf_op jit(solution)/shard_map/backward_2/all_to_all | solution.py:371
  170.7 3.4 %backward_2.1 = (bf16[4,32,256]{2,1,0:T(8,128)(2,1)S(1)}, bf16[16,4,32,256]{3,2,1,0:T(8,128)(2,1)S(1)}) custom-call(s32[1]{0:T(128)} %bitcast.1.plane_ref, s32[4,4,8]{2,1,0:T(4,128)S(1)} %fusion.3.at_ref, bf16[64,32,256]{2,1,0:T(8,128)(2,1)S(1)} %bitcast.49, f32[4,32,256]{2,1,0:T(8,128)S(1)} %get-tuple-element.74.f_ref, ...), custom_call_target="tpu_custom_call" | custom-call | flops 150994944 | bytes 6291456 | tf_op jit(solution)/shard_map/backward_2/pallas_call | solution.py:333
  174.2 16.2 %all_to_all.39 = bf16[16,4,32,256]{3,2,1,0:T(8,128)(2,1)S(1)} all-to-all(bf16[16,4,32,256]{3,2,1,0:T(8,128)(2,1)S(1)} %get-tuple-element.75), channel_id=1, replica_groups=mesh['x'=4,'y'=4,'c'=2,'z'=4] {'x','y'}, dimensions={0} | all-to-all | bytes 2097152 | tf_op jit(solution)/shard_map/backward_1/all_to_all | solution.py:371
  190.3 3.4 %backward_1.1 = (bf16[4,32,256]{2,1,0:T(8,128)(2,1)S(1)}, bf16[16,4,32,256]{3,2,1,0:T(8,128)(2,1)S(1)}) custom-call(s32[1]{0:T(128)} %bitcast.1.plane_ref, s32[4,4,8]{2,1,0:T(4,128)S(1)} %fusion.3.at_ref, bf16[64,32,256]{2,1,0:T(8,128)(2,1)S(1)} %bitcast.48, f32[4,32,256]{2,1,0:T(8,128)S(1)} %get-tuple-element.76.f_ref, ...), custom_call_target="tpu_custom_call" | custom-call | flops 150994944 | bytes 6291456 | tf_op jit(solution)/shard_map/backward_1/pallas_call | solution.py:333
  193.8 16.2 %all_to_all.40 = bf16[16,4,32,256]{3,2,1,0:T(8,128)(2,1)S(1)} all-to-all(bf16[16,4,32,256]{3,2,1,0:T(8,128)(2,1)S(1)} %get-tuple-element.77), channel_id=1, replica_groups=mesh['x'=4,'y'=4,'c'=2,'z'=4] {'x','y'}, dimensions={0} | all-to-all | bytes 2097152 | tf_op jit(solution)/shard_map/backward_0/all_to_all | solution.py:371
  209.9 3.4 %backward_0.1 = bf16[4,32,256]{2,1,0:T(8,128)(2,1)S(1)} custom-call(s32[1]{0:T(128)} %bitcast.1.plane_ref, s32[4,4,8]{2,1,0:T(4,128)S(1)} %fusion.3.at_ref, bf16[64,32,256]{2,1,0:T(8,128)(2,1)S(1)} %bitcast.47, f32[4,32,256]{2,1,0:T(8,128)S(1)} %get-tuple-element.78.f_ref, ...), custom_call_target="tpu_custom_call" | custom-call | flops 150994944 | bytes 6291456 | tf_op jit(solution)/shard_map/backward_0/pallas_call | solution.py:333
  213.5 1.5 collective-permute-done.18
  215.1 13.9 %all_to_all.41.fx_ref = bf16[4,2,2,2,32,256]{5,4,3,2,1,0:T(8,128)(2,1)S(1)} all-to-all(bf16[4,2,2,2,32,256]{5,4,3,2,1,0:T(8,128)(2,1)S(1)} %pad_maximum_fusion), channel_id=1, replica_groups=mesh['x'=4,'y'=4,'c'=2,'z'=4] {'z'}, dimensions={0} | all-to-all | bytes 1048576 | tf_op jit(solution)/shard_map/to_planes/all_to_all | solution.py:445
  229.0 1.1 to_planes.1
  (30 shorter events, 0.6 us)
Async XLA Ops:
  0.6 8.0 %copy-start.1 = (bf16[1,2,1,256,256]{4,3,2,1,0:T(8,128)(2,1)S(1)}, bf16[1,2,1,256,256]{4,3,2,1,0:T(8,128)(2,1)}, u32[]{:S(2)}) copy-start(bf16[1,2,1,256,256]{4,3,2,1,0:T(8,128)(2,1)} %param.5) | copy-start | bytes 786436
  0.6 1.1 copy-start.2
  1.7 0.7 copy-start.3
  3.1 7.6 %collective-permute-start.2 = (bf16[144,256]{1,0:T(8,128)(2,1)S(1)}, bf16[144,256]{1,0:T(8,128)(2,1)S(1)}, u32[]{:S(2)}, u32[]{:S(2)}) collective-permute-start(bf16[144,256]{1,0:T(8,128)(2,1)S(1)} %get-tuple-element.88), channel_id=1, source_target_pairs={{0,3},{1,0},{2,1},{3,2},{4,7},{5,4},{6,5},{7,6},{8,11},{9,8},{10,9... | collective-permute-start | bytes 221192 | tf_op jit(solution)/shard_map/tell_planes/ppermute | solution.py:385
  7.3 6.1 %collective-permute-start.1 = (bf16[144,256]{1,0:T(8,128)(2,1)S(1)}, bf16[144,256]{1,0:T(8,128)(2,1)S(1)}, u32[]{:S(2)}, u32[]{:S(2)}) collective-permute-start(bf16[144,256]{1,0:T(8,128)(2,1)S(1)} %get-tuple-element.89), channel_id=1, source_target_pairs={{0,2},{1,3},{2,0},{3,1},{4,6},{5,7},{6,4},{7,5},{8,10},{9,11},{10,... | collective-permute-start | bytes 221192 | tf_op jit(solution)/shard_map/tell_planes/ppermute | solution.py:385
  7.3 6.5 %collective-permute-start = (bf16[144,256]{1,0:T(8,128)(2,1)S(1)}, bf16[144,256]{1,0:T(8,128)(2,1)S(1)}, u32[]{:S(2)}, u32[]{:S(2)}) collective-permute-start(bf16[144,256]{1,0:T(8,128)(2,1)S(1)} %get-tuple-element.90), channel_id=1, source_target_pairs={{0,1},{1,2},{2,3},{3,0},{4,5},{5,6},{6,7},{7,4},{8,9},{9,10},{10,1... | collective-permute-start | bytes 221192 | tf_op jit(solution)/shard_map/tell_planes/ppermute | solution.py:385
  8.6 1.6 copy-start
  13.8 26.5 %collective-permute-start.5 = (bf16[9,256,256]{2,1,0:T(8,128)(2,1)S(1)}, bf16[9,256,256]{2,1,0:T(8,128)(2,1)S(1)}, u32[]{:S(2)}, u32[]{:S(2)}) collective-permute-start(bf16[9,256,256]{2,1,0:T(8,128)(2,1)S(1)} %factor_step_1.3.here_ref.else_ref.rest_3_.rest_4_.rest_7_.rest_1_), channel_id=1, source_target_pairs={{0,3},{1,0},{2,1},{3,2},{4,7},{5,4},{6,5},{7,6},{8,11},{9,8},{10,9... | collective-permute-start | bytes 3538952 | tf_op jit(solution)/shard_map/factor_step_1/ppermute | solution.py:391
  14.7 28.4 %collective-permute-start.3 = (bf16[9,256,256]{2,1,0:T(8,128)(2,1)S(1)}, bf16[9,256,256]{2,1,0:T(8,128)(2,1)S(1)}, u32[]{:S(2)}, u32[]{:S(2)}) collective-permute-start(bf16[9,256,256]{2,1,0:T(8,128)(2,1)S(1)} %factor_step_1.2.else_ref.here_ref.rest_2_.rest_3_.rest_6_.rest_0_), channel_id=1, source_target_pairs={{0,1},{1,2},{2,3},{3,0},{4,5},{5,6},{6,7},{7,4},{8,9},{9,10},{10,1... | collective-permute-start | bytes 3538952 | tf_op jit(solution)/shard_map/factor_step_1/ppermute | solution.py:390
  15.9 28.1 %collective-permute-start.9 = (bf16[9,256,256]{2,1,0:T(8,128)(2,1)S(1)}, bf16[9,256,256]{2,1,0:T(8,128)(2,1)S(1)}, u32[]{:S(2)}, u32[]{:S(2)}) collective-permute-start(bf16[9,256,256]{2,1,0:T(8,128)(2,1)S(1)} %factor_step_1.3.here_ref.else_ref.rest_3_.rest_4_.rest_7_.rest_1_), channel_id=1, source_target_pairs={{0,4},{4,0},{1,5},{5,1},{2,6},{6,2},{3,7},{7,3},{8,12},{12,8},{9,1... | collective-permute-start | bytes 3538952 | tf_op jit(solution)/shard_map/factor_step_1/ppermute | solution.py:367
  15.9 27.9 %collective-permute-start.7 = (bf16[4,144,256]{2,1,0:T(8,128)(2,1)S(1)}, bf16[4,144,256]{2,1,0:T(8,128)(2,1)S(1)}, u32[]{:S(2)}, u32[]{:S(2)}) collective-permute-start(bf16[4,144,256]{2,1,0:T(8,128)(2,1)S(1)} %pad_maximum_fusion.1.rest_0_.rest_1_.rest_4_.own_told), channel_id=1, source_target_pairs={{0,4},{4,0},{1,5},{5,1},{2,6},{6,2},{3,7},{7,3},{8,12},{12,8},{9,1... | collective-permute-start | bytes 884744 | tf_op jit(solution)/shard_map/tell_planes/ppermute | solution.py:367
  16.5 29.3 %collective-permute-start.8 = (bf16[9,256,256]{2,1,0:T(8,128)(2,1)S(1)}, bf16[9,256,256]{2,1,0:T(8,128)(2,1)S(1)}, u32[]{:S(2)}, u32[]{:S(2)}) collective-permute-start(bf16[9,256,256]{2,1,0:T(8,128)(2,1)S(1)} %factor_step_1.2.else_ref.here_ref.rest_2_.rest_3_.rest_6_.rest_0_), channel_id=1, source_target_pairs={{0,4},{4,0},{1,5},{5,1},{2,6},{6,2},{3,7},{7,3},{8,12},{12,8},{9,1... | collective-permute-start | bytes 3538952 | tf_op jit(solution)/shard_map/factor_step_1/ppermute | solution.py:367
  41.0 25.7 %collective-permute-start.6 = (bf16[9,256,256]{2,1,0:T(8,128)(2,1)S(1)}, bf16[9,256,256]{2,1,0:T(8,128)(2,1)S(1)}, u32[]{:S(2)}, u32[]{:S(2)}) collective-permute-start(bf16[9,256,256]{2,1,0:T(8,128)(2,1)S(1)} %factor_step_2.5), channel_id=1, source_target_pairs={{0,3},{1,0},{2,1},{3,2},{4,7},{5,4},{6,5},{7,6},{8,11},{9,8},{10,9... | collective-permute-start | bytes 3538952 | tf_op jit(solution)/shard_map/factor_step_2/ppermute | solution.py:403
  43.8 26.6 %collective-permute-start.4 = (bf16[9,256,256]{2,1,0:T(8,128)(2,1)S(1)}, bf16[9,256,256]{2,1,0:T(8,128)(2,1)S(1)}, u32[]{:S(2)}, u32[]{:S(2)}) collective-permute-start(bf16[9,256,256]{2,1,0:T(8,128)(2,1)S(1)} %factor_step_2.4), channel_id=1, source_target_pairs={{0,1},{1,2},{2,3},{3,0},{4,5},{5,6},{6,7},{7,4},{8,9},{9,10},{10,1... | collective-permute-start | bytes 3538952 | tf_op jit(solution)/shard_map/factor_step_2/ppermute | solution.py:402
  43.9 22.8 %collective-permute-start.11 = (bf16[9,256,256]{2,1,0:T(8,128)(2,1)S(1)}, bf16[9,256,256]{2,1,0:T(8,128)(2,1)S(1)}, u32[]{:S(2)}, u32[]{:S(2)}) collective-permute-start(bf16[9,256,256]{2,1,0:T(8,128)(2,1)S(1)} %collective-permute-done.5.here_ref.else_ref.rest_5_.rest_6_.rest_9_.rest_3_), channel_id=1, source_target_pairs={{0,4},{4,0},{1,5},{5,1},{2,6},{6,2},{3,7},{7,3},{8,12},{12,8},{9,1... | collective-permute-start | bytes 3538952 | tf_op jit(solution)/shard_map/factor_step_2/ppermute | solution.py:367
  44.0 26.4 %collective-permute-start.10 = (bf16[9,256,256]{2,1,0:T(8,128)(2,1)S(1)}, bf16[9,256,256]{2,1,0:T(8,128)(2,1)S(1)}, u32[]{:S(2)}, u32[]{:S(2)}) collective-permute-start(bf16[9,256,256]{2,1,0:T(8,128)(2,1)S(1)} %collective-permute-done.3.else_ref.here_ref.rest_4_.rest_5_.rest_8_.rest_2_), channel_id=1, source_target_pairs={{0,4},{4,0},{1,5},{5,1},{2,6},{6,2},{3,7},{7,3},{8,12},{12,8},{9,1... | collective-permute-start | bytes 3538952 | tf_op jit(solution)/shard_map/factor_step_2/ppermute | solution.py:367
  70.4 3.8 %collective-permute-start.12 = (bf16[9,256,256]{2,1,0:T(8,128)(2,1)S(1)}, bf16[9,256,256]{2,1,0:T(8,128)(2,1)S(1)}, u32[]{:S(2)}, u32[]{:S(2)}) collective-permute-start(bf16[9,256,256]{2,1,0:T(8,128)(2,1)S(1)} %collective-permute-done.4.rest_6_.rest_7_.rest_10_.rest_4_), channel_id=1, source_target_pairs={{0,4},{4,0},{1,5},{5,1},{2,6},{6,2},{3,7},{7,3},{8,12},{12,8},{9,1... | collective-permute-start | bytes 3538952 | tf_op jit(solution)/shard_map/factor_step_2/ppermute | solution.py:367
  70.4 4.5 %collective-permute-start.13 = (bf16[9,256,256]{2,1,0:T(8,128)(2,1)S(1)}, bf16[9,256,256]{2,1,0:T(8,128)(2,1)S(1)}, u32[]{:S(2)}, u32[]{:S(2)}) collective-permute-start(bf16[9,256,256]{2,1,0:T(8,128)(2,1)S(1)} %collective-permute-done.6.rest_7_.rest_8_.rest_11_.rest_5_), channel_id=1, source_target_pairs={{0,4},{4,0},{1,5},{5,1},{2,6},{6,2},{3,7},{7,3},{8,12},{12,8},{9,1... | collective-permute-start | bytes 3538952 | tf_op jit(solution)/shard_map/factor_step_2/ppermute | solution.py:367
  70.9 32.4 %collective-permute-start.14 = (bf16[9,256,256]{2,1,0:T(8,128)(2,1)S(1)}, bf16[9,256,256]{2,1,0:T(8,128)(2,1)S(1)}, u32[]{:S(2)}, u32[]{:S(2)}) collective-permute-start(bf16[9,256,256]{2,1,0:T(8,128)(2,1)S(1)} %factor_step_2.6), channel_id=1, source_target_pairs={{0,1},{1,2},{2,3},{3,0},{4,5},{5,6},{6,7},{7,4},{8,9},{9,10},{10,1... | collective-permute-start | bytes 3538952 | tf_op jit(solution)/shard_map/factor_step_3/ppermute | solution.py:412
  70.9 32.4 %collective-permute-start.15 = (bf16[9,256,256]{2,1,0:T(8,128)(2,1)S(1)}, bf16[9,256,256]{2,1,0:T(8,128)(2,1)S(1)}, u32[]{:S(2)}, u32[]{:S(2)}) collective-permute-start(bf16[9,256,256]{2,1,0:T(8,128)(2,1)S(1)} %factor_step_2.7), channel_id=1, source_target_pairs={{0,3},{1,0},{2,1},{3,2},{4,7},{5,4},{6,5},{7,6},{8,11},{9,8},{10,9... | collective-permute-start | bytes 3538952 | tf_op jit(solution)/shard_map/factor_step_3/ppermute | solution.py:413
  103.3 2.9 %collective-permute-start.16 = (bf16[9,256,256]{2,1,0:T(8,128)(2,1)S(1)}, bf16[9,256,256]{2,1,0:T(8,128)(2,1)S(1)}, u32[]{:S(2)}, u32[]{:S(2)}) collective-permute-start(bf16[9,256,256]{2,1,0:T(8,128)(2,1)S(1)} %collective-permute-done.14.rest_9_.rest_12_.rest_4_.rest_6_), channel_id=1, source_target_pairs={{0,4},{4,0},{1,5},{5,1},{2,6},{6,2},{3,7},{7,3},{8,12},{12,8},{9,1... | collective-permute-start | bytes 3538952 | tf_op jit(solution)/shard_map/factor_step_3/ppermute | solution.py:367
  103.4 4.5 %collective-permute-start.17 = (bf16[9,256,256]{2,1,0:T(8,128)(2,1)S(1)}, bf16[9,256,256]{2,1,0:T(8,128)(2,1)S(1)}, u32[]{:S(2)}, u32[]{:S(2)}) collective-permute-start(bf16[9,256,256]{2,1,0:T(8,128)(2,1)S(1)} %collective-permute-done.15.rest_10_.rest_13_.rest_5_.rest_7_), channel_id=1, source_target_pairs={{0,4},{4,0},{1,5},{5,1},{2,6},{6,2},{3,7},{7,3},{8,12},{12,8},{9,1... | collective-permute-start | bytes 3538952 | tf_op jit(solution)/shard_map/factor_step_3/ppermute | solution.py:367
  213.4 1.6 collective-permute-start.18

commit v7 on v6

--- a/solution.py
+++ b/solution.py
@@ -141,21 +141,9 @@
     return sorted(set(WHERE[level][0] + WHERE[level][1]))
 
 
-def factor_copies(level, plane, refs, buf, sems, nodes=(0, 1, 2, 3)):
-    names = used(level)
-
-    def copy(n, z):
-        src = refs[len(names) * (n // 2) + names.index(WHERE[level][n % 2][z])]
-        return pltpu.make_async_copy(src.at[FAN] if level == 3 else src, buf.at[n], sems.at[n])
-
+def on_plane(plane, run):
     for z in range(4):
-
-        @pl.when(plane == z)
-        def _():
-            for n in nodes:
-                copy(n, z).start()
-
-    return {n: copy(n, 0) for n in nodes}
+        pl.when(plane == z)(functools.partial(run, z))
 
 
 def told_by(plane, level):
@@ -168,17 +156,8 @@
         acc_ref[at_ref[came, n, p]] += terms[:, p * WIDTH : (p + 1) * WIDTH]
 
 
-def row_copies(came, refs, rows, sems, cores=(0, 1)):
-    copies = []
-    for r in cores:
-        src = refs[r].at[came, pl.ds((KEEP, SEND)[r], 2 * COLS)]
-        copies.append(pltpu.make_async_copy(src, rows.at[pl.ds(2 * COLS * r, 2 * COLS)], sems.at[r]))
-        copies[-1].start()
-    return copies
-
-
-def rows_of(buf, n, size):
-    return buf[n * size : (n + 1) * size]
+def rows_of(told, came, n):
+    return told[n // 2][came, pl.ds((KEEP, SEND)[n // 2] + n % 2 * COLS, COLS)]
 
 
 def inflow_kernel(got_ref, out_ref):
@@ -198,52 +177,81 @@
 
 def forward_kernel(level, part, core_ref, plane_ref, at_ref, *rest):
     gots, rest = (rest[:1], rest[1:]) if level else ((), rest)
-    before, rest = (rest[:3], rest[3:]) if part == 1 else ((), rest)
-    told, refs, (f_ref, fb_ref, out_ref, rows, rsems, buf, sems, acc_ref) = rest[:2], rest[2:-8], rest[-8:]
+    before, rest = (rest[:4], rest[4:]) if part == 1 else ((), rest)
+    outs = {None: 4, 0: 5, 1: 6}[part]
+    told, refs, (f_ref, fb_ref, share_ref, *extra) = rest[:2], rest[2:-outs], rest[-outs:]
+    acc_ref = extra[1 if part == 0 else 0]
+    names = used(level)
     came = told_by(plane_ref[0], level)
-    copies_r = row_copies(came, told, rows, rsems)
-
-    def run(nodes):
-        copies = factor_copies(level, plane_ref[0], refs, buf, sems, nodes)
+
+    def block(n, z):
+        return refs[len(names) * (n // 2) + names.index(WHERE[level][n % 2][z])]
+
+    def add(nodes, z, block=block):
         solved = {}
         for n in nodes:
-            resid = rows_of(rows, n, COLS)
+            resid = rows_of(told, came, n)
             if level:
                 inflow = gots[0][n] if level == 1 else jnp.sum(gots[0][:, n].astype(F32), axis=0)
                 resid = (resid.astype(F32) - inflow).astype(BF)
-            copies[n].wait()
-            f = dot_t(resid, buf[n, FAN])
+            f = dot_t(resid, block(n, z)[FAN])
             f_ref[n] = f
             solved[n] = f.astype(BF)
             fb_ref[n] = solved[n]
         for n in nodes:
-            add_terms(n, at_ref, came, solved[n], buf.at[n], acc_ref)
-
-    if part == 1:
-        f_ref[...], fb_ref[...], acc_ref[...] = before[0][...], before[1][...], before[2][...]
-    else:
+            add_terms(n, at_ref, came, solved[n], block(n, z), acc_ref)
+
+    def run(nodes):
         acc_ref[...] = jnp.zeros_like(acc_ref)
-    for copy in copies_r:
-        copy.wait()
+        on_plane(plane_ref[0], functools.partial(add, nodes))
+        share_ref[...] = acc_ref[...].astype(BF)
+
+    def finish(n):
+        f_ref[:n], fb_ref[:n] = before[0][:n], before[1][:n]
+        targets = [at_ref[came, n, p] for p in range(FAN)]
+        for t in targets:
+            acc_ref[t] = before[3][t]
+        on_plane(plane_ref[0], functools.partial(add, (n,)))
+        for t in targets:
+            share_ref[t] = acc_ref[t].astype(BF)
+
+    def staged():
+        buf, sems = extra[1:]
+
+        def copy(n, z):
+            return pltpu.make_async_copy(block(n, z), buf.at[n], sems.at[n])
+
+        def start(z):
+            for n in range(4):
+                copy(n, z).start()
+
+        on_plane(plane_ref[0], start)
+        acc_ref[...] = jnp.zeros_like(acc_ref)
+        for n in range(4):
+            copy(n, 0).wait()
+        add((0, 1, 2, 3), 0, lambda n, z: buf.at[n])
+        share_ref[...] = acc_ref[...].astype(BF)
+
     if part is None:
         run((0, 1, 2, 3))
-    elif part == 0:
-        f_ref[...], fb_ref[...] = jnp.zeros_like(f_ref), jnp.zeros_like(fb_ref)
-        pl.when(core_ref[0] == 1)(lambda: run((0, 1, 2)))
-    else:
-        pl.when(core_ref[0] == 1)(lambda: run((3,)))
-        pl.when(core_ref[0] == 0)(lambda: run((0, 1, 2, 3)))
-    out_ref[...] = acc_ref[...].astype(out_ref.dtype)
-
-
-SMALL = [
-    pltpu.VMEM((4 * COLS, WIDTH), BF),
-    pltpu.SemaphoreType.DMA((2,)),
-]
-LARGE = [
-    pltpu.VMEM((4, PACKED, WIDTH, WIDTH), BF),
-    pltpu.SemaphoreType.DMA((4,)),
-]
+        return
+
+    @pl.when(core_ref[0] == 1)
+    def _():
+        if part == 0:
+            run((0, 1, 2))
+            extra[0][...] = acc_ref[...]
+        else:
+            finish(3)
+
+    if part == 1:
+
+        @pl.when(core_ref[0] == 0)
+        def _():
+            staged()
+
+
+STAGE = [pltpu.VMEM((4, PACKED, WIDTH, WIDTH), BF), pltpu.SemaphoreType.DMA((4,))]
 NODE_F32 = jax.ShapeDtypeStruct((4, COLS, WIDTH), F32)
 NODE_BF = jax.ShapeDtypeStruct((4, COLS, WIDTH), BF)
 COPIES = jax.ShapeDtypeStruct((CHIPS, 4, COLS, WIDTH), BF)
@@ -254,13 +262,17 @@
 
 
 def forward_part(level, part, here, at, gots, before, told, blocks):
-    last = jax.ShapeDtypeStruct((NODES, COLS, WIDTH), F32 if part == 0 else BF)
+    shares = jax.ShapeDtypeStruct((NODES, COLS, WIDTH), BF)
+    out_shape = (NODE_F32, NODE_BF, shares)
+    if part == 0:
+        out_shape += (jax.ShapeDtypeStruct((NODES, COLS, WIDTH), F32),)
     return pl.pallas_call(
         functools.partial(forward_kernel, level, part),
-        in_specs=[SMEM] * 3 + [VM] * (len(gots) + len(before)) + any_specs(2 + len(blocks)),
-        out_specs=(VM, VM, VM),
-        scratch_shapes=SMALL + LARGE + [pltpu.VMEM((NODES, COLS, WIDTH), F32)],
-        out_shape=(NODE_F32, NODE_BF, last),
+        in_specs=[SMEM] * 3 + [VM] * (len(gots) + len(before) + 2 + len(blocks)),
+        out_specs=(VM,) * len(out_shape),
+        scratch_shapes=[pltpu.VMEM((NODES, COLS, WIDTH), F32)] + (STAGE if part == 1 else []),
+        out_shape=out_shape,
+        input_output_aliases={3 + len(gots) + 2: 2} if part == 1 else {},
         compiler_params=pltpu.CompilerParams(vmem_limit_bytes=LIMIT),
         cost_estimate=pl.CostEstimate(flops=2 * 36 * COLS * WIDTH**2, bytes_accessed=6 * MIB, transcendentals=0),
     )(*here, at, *gots, *before, *told, *blocks)
@@ -277,54 +289,61 @@
 
 
 def top_kernel(plane_ref, got_ref, own_told, other_told, *rest):
-    refs, (fb_ref, sol_ref, copies_ref, rows, rsems, invs, sems) = rest[:-7], rest[-7:]
-    copies_r = row_copies(told_by(plane_ref[0], 3), (own_told, other_told), rows, rsems)
-    copies = factor_copies(3, plane_ref[0], refs, invs, sems)
-    for copy in copies_r:
-        copy.wait()
+    refs, (fb_ref, sol_ref, copies_ref) = rest[:-3], rest[-3:]
+    names = used(3)
+    came = told_by(plane_ref[0], 3)
+    resids = []
     for n in range(4):
         inflow = jnp.sum(got_ref[:, n].astype(F32), axis=0)
-        resid = (rows_of(rows, n, COLS).astype(F32) - inflow).astype(BF)
-        copies[n].wait()
-        inv = invs[n]
-        fb = dot_t(resid, inv).astype(BF)
-        fb_ref[n] = fb
-        sol = dot_n(fb, inv).astype(BF)
-        sol_ref[n] = sol
-        for k in range(CHIPS):
-            copies_ref[k, n] = sol
+        resids.append((rows_of((own_told, other_told), came, n).astype(F32) - inflow).astype(BF))
+
+    def run(z):
+        invs = [refs[len(names) * (n // 2) + names.index(WHERE[3][n % 2][z])].at[FAN] for n in range(4)]
+        solved = []
+        for n in range(4):
+            solved.append(dot_t(resids[n], invs[n][...]).astype(BF))
+            fb_ref[n] = solved[n]
+        for n in range(4):
+            sol = dot_n(solved[n], invs[n][...]).astype(BF)
+            sol_ref[n] = sol
+            for k in range(CHIPS):
+                copies_ref[k, n] = sol
+
+    on_plane(plane_ref[0], run)
 
 
 def top_level(plane, got, told, factors):
     blocks = pick(3, factors)
     return pl.pallas_call(
         top_kernel,
-        in_specs=[SMEM, VM] + any_specs(2 + len(blocks)),
+        in_specs=[SMEM] + [VM] * (3 + len(blocks)),
         out_specs=(VM, VM, VM),
-        scratch_shapes=SMALL + [pltpu.VMEM((4, WIDTH, WIDTH), BF), pltpu.SemaphoreType.DMA((4,))],
         out_shape=(NODE_BF, NODE_BF, COPIES),
-        compiler_params=pltpu.CompilerParams(vmem_limit_bytes=8 * MIB),
+        compiler_params=pltpu.CompilerParams(vmem_limit_bytes=LIMIT),
         cost_estimate=pl.CostEstimate(flops=2 * 8 * COLS * WIDTH**2, bytes_accessed=3 * MIB, transcendentals=0),
     )(plane, got, *told, *blocks)
 
 
 def backward_kernel(level, plane_ref, at_ref, above_ref, f_ref, *rest):
-    count = 2 * len(used(level))
-    refs, outs, (buf, sems) = rest[:count], rest[count:-2], rest[-2:]
-    copies = factor_copies(level, plane_ref[0], refs, buf, sems)
+    names = used(level)
+    refs, outs = rest[: 2 * len(names)], rest[2 * len(names) :]
     came = told_by(plane_ref[0], level)
-    uppers = []
-    for n in range(4):
-        picked = jnp.concatenate([above_ref[at_ref[came, n, p]] for p in range(FAN)], axis=1)
-        copies[n].wait()
-        back = dot_n(picked, buf[n, :FAN].reshape(FAN * WIDTH, WIDTH))
-        uppers.append((f_ref[n] - back).astype(BF))
-    for n in range(4):
-        sol = dot_n(uppers[n], buf[n, FAN]).astype(BF)
-        outs[0][n] = sol
-        if level:
-            for k in range(CHIPS):
-                outs[1][k, n] = sol
+
+    def run(z):
+        blocks = [refs[len(names) * (n // 2) + names.index(WHERE[level][n % 2][z])] for n in range(4)]
+        uppers = []
+        for n in range(4):
+            picked = jnp.concatenate([above_ref[at_ref[came, n, p]] for p in range(FAN)], axis=1)
+            back = dot_n(picked, blocks[n][:FAN].reshape(FAN * WIDTH, WIDTH))
+            uppers.append((f_ref[n] - back).astype(BF))
+        for n in range(4):
+            sol = dot_n(uppers[n], blocks[n][FAN]).astype(BF)
+            outs[0][n] = sol
+            if level:
+                for k in range(CHIPS):
+                    outs[1][k, n] = sol
+
+    on_plane(plane_ref[0], run)
 
 
 def backward_level(level, plane, at, above, f, factors):
@@ -332,35 +351,33 @@
     out_shape = (NODE_BF, COPIES) if level else (NODE_BF,)
     return pl.pallas_call(
         functools.partial(backward_kernel, level),
-        in_specs=[SMEM, SMEM, VM, VM] + any_specs(len(blocks)),
+        in_specs=[SMEM, SMEM] + [VM] * (2 + len(blocks)),
         out_specs=(VM,) * len(out_shape),
-        scratch_shapes=LARGE,
         out_shape=out_shape,
         compiler_params=pltpu.CompilerParams(vmem_limit_bytes=LIMIT),
         cost_estimate=pl.CostEstimate(flops=2 * 36 * COLS * WIDTH**2, bytes_accessed=6 * MIB, transcendentals=0),
     )(plane, at, above, f, *blocks)
 
 
-def last_kernel(core_ref, fx_ref, forward_ref, result_ref):
+def last_kernel(core_ref, own_ref, other_ref, forward_ref, result_ref):
     core = core_ref[0]
     for k, out_ref in enumerate((forward_ref, result_ref)):
         for j in range(2):
-            halves = []
-            for half in range(2):
-                rel = jnp.bitwise_xor(core, half)
-                halves += [fx_ref[z, rel, k, j] for z in range(4)]
-            out_ref[j] = jnp.transpose(jnp.concatenate(halves, axis=0).astype(F32))
-
-
-def last_step(core, fx):
+            own = jnp.concatenate([own_ref[z, k, 0, j] for z in range(4)], axis=0).astype(F32)
+            other = jnp.concatenate([other_ref[z, k, 1, j] for z in range(4)], axis=0).astype(F32)
+            low, high = jnp.where(core == 0, own, other), jnp.where(core == 0, other, own)
+            out_ref[j] = jnp.transpose(jnp.concatenate([low, high], axis=0))
+
+
+def last_step(core, own, other):
     return pl.pallas_call(
         last_kernel,
         out_shape=(jax.ShapeDtypeStruct((2, WIDTH, WIDTH), F32),) * 2,
-        in_specs=[SMEM, VM],
+        in_specs=[SMEM, VM, VM],
         out_specs=(VM, VM),
         compiler_params=pltpu.CompilerParams(vmem_limit_bytes=8 * MIB),
-        cost_estimate=pl.CostEstimate(flops=0, bytes_accessed=2 * 2**20, transcendentals=0),
-    )(core, fx)
+        cost_estimate=pl.CostEstimate(flops=0, bytes_accessed=2 * MIB, transcendentals=0),
+    )(core, own, other)
 
 
 def swap(value):
@@ -441,9 +458,8 @@
 
     with jax.named_scope("to_planes"):
         fx = jnp.stack([jnp.stack(solved), jnp.stack(result)], axis=1).reshape(4, 2, 2, 2, COLS, WIDTH)
-        fx = jnp.stack([fx[:, :, 0], swap(fx[:, :, 1])], axis=1)
         fx = lax.all_to_all(fx, "z", 0, 0, tiled=True)
-        forward_out, result_out = last_step(core1, fx)
+        forward_out, result_out = last_step(core1, fx, swap(fx))
     shape = (1, 2, 1, WIDTH, WIDTH)
     return forward_out.reshape(shape), result_out.reshape(shape)
 

time: 231 us -> 221 us (0.957)
  Pallas kernels: 30.7 us -> 19.9 us
    pallas_call x3, Pallas kernels: 10.3 us -> 5.22 us  [backward_level(): pl.pallas_call(functools.partial(backward_kernel, level), in_specs=[SMEM,...]
    pallas_call x4, Pallas kernels: 13.2 us -> 9.04 us  [forward_part(): pl.pallas_call(functools.partial(forward_kernel, level, part), in_specs=[...]
  transfers between devices with their start and end apart: 19 -> 19, of which waited for: 9 -> 9; matrix products, arithmetic and copies ran while one was open for 0% -> 0% of each run, Pallas kernels for 4% -> 3%
where the time goes in v7:
time: 221 us; the launch traced here: 219 us
  blocking collectives  123 us (56%)
  waiting for transfers between devices  57.3 us (26%)
  Pallas kernels  19.9 us (9%)
  starting transfers between devices  15.3 us (7%)
  local copies, waits for them, and re-layouts  3.38 us (2%)
    all_to_all x6, blocking collectives, exchange(): lax.all_to_all(value.reshape(CHIPS, 4, COLS, WIDTH), ('x', 'y'), 0, 0, ti...  110 us
    ppermute x1, waiting for transfers between devices, on_device(): down_1 = lax.ppermute(own_b, 'z', DOWN)  23.8 us
    ppermute x1, waiting for transfers between devices, on_device(): down_2 = lax.ppermute(choose(plane1, 3, down_1, own_a), 'z', DOWN)  20.8 us
    all_to_all x1, blocking collectives, on_device(): fx = lax.all_to_all(fx, 'z', 0, 0, tiled=True)  12.2 us
    pallas_call x4, Pallas kernels, forward_part(): pl.pallas_call(functools.partial(forward_kernel, level, part), in_specs=[...  9.04 us
    ppermute x10, waiting for transfers between devices, swap(): return lax.ppermute(value, 'c', [(0, 1), (1, 0)])  5.87 us
    ppermute x3, starting transfers between devices, on_device(): lax.ppermute(message[k], 'z', [(z, (z + k) % 4) for z in range(4)])  5.45 us
    pallas_call x3, Pallas kernels, backward_level(): pl.pallas_call(functools.partial(backward_kernel, level), in_specs=[SMEM,...  5.22 us
  transfers between devices with their start and end apart: 19, of which 9 were waited for; matrix products, arithmetic and copies ran while one was open for 0% of the time, Pallas kernels for 3%

profile of v7, /device:TPU:0, one launch (start us, length us, event | category | flops | bytes accessed | tf_op | source)
XLA Modules:
  0.0 219.4 jit_solution(11761158985562626952)
XLA Ops:
  0.7 1.1 copy-done.2
  1.7 0.7 copy-done.3
  2.4 0.7 tell_planes.1
  3.1 4.2 %collective-permute-start.2 = (bf16[144,256]{1,0:T(8,128)(2,1)S(1)}, bf16[144,256]{1,0:T(8,128)(2,1)S(1)}, u32[]{:S(2)}, u32[]{:S(2)}) collective-permute-start(bf16[144,256]{1,0:T(8,128)(2,1)S(1)} %get-tuple-element.88), channel_id=1, source_target_pairs={{0,3},{1,0},{2,1},{3,2},{4,7},{5,4},{6,5},{7,6},{8,11},{9,8},{10,9... | collective-permute-start | bytes 221192 | tf_op jit(solution)/shard_map/tell_planes/ppermute | solution.py:402
  7.3 1.3 collective-permute-start
  8.6 1.6 copy-done
  10.2 0.3 factor_step_1.3.here_ref.else_ref.rest_3_.rest_4_.rest_8_.rest_1_
  10.4 0.3 factor_step_1.2.else_ref.here_ref.rest_2_.rest_3_.rest_7_.rest_0_
  10.8 2.6 %collective-permute-done.1 = bf16[144,256]{1,0:T(8,128)(2,1)S(1)} collective-permute-done((bf16[144,256]{1,0:T(8,128)(2,1)S(1)}, bf16[144,256]{1,0:T(8,128)(2,1)S(1)}, u32[]{:S(2)}, u32[]{:S(2)}) %collective-permute-start.1) | collective-permute-done | bytes 73760 | tf_op jit(solution)/shard_map/tell_planes/ppermute | solution.py:402
  13.4 0.4 collective-permute-done
  13.8 0.9 collective-permute-start.5
  14.7 1.2 collective-permute-start.3
  15.9 0.6 collective-permute-start.7
  16.5 0.1 collective-permute-start.8
  16.6 23.8 %collective-permute-done.5.here_ref.else_ref.rest_5_.rest_6_.rest_10_.rest_3_ = bf16[9,256,256]{2,1,0:T(8,128)(2,1)S(1)} collective-permute-done((bf16[9,256,256]{2,1,0:T(8,128)(2,1)S(1)}, bf16[9,256,256]{2,1,0:T(8,128)(2,1)S(1)}, u32[]{:S(2)}, u32[]{:S(2)}) %collective-permute-start.5) | collective-permute-done | bytes 1179680 | tf_op jit(solution)/shard_map/factor_step_1/ppermute | solution.py:408
  40.4 0.6 factor_step_2.5
  41.0 2.1 collective-permute-start.6
  43.1 0.6 factor_step_2.4
  43.9 0.1 collective-permute-start.11
  44.0 0.5 collective-permute-start.10
  44.5 0.6 factor_step_2.7
  45.2 0.6 factor_step_2.6
  45.8 20.8 %collective-permute-done.6.rest_7_.rest_8_.rest_12_.rest_5_ = bf16[9,256,256]{2,1,0:T(8,128)(2,1)S(1)} collective-permute-done((bf16[9,256,256]{2,1,0:T(8,128)(2,1)S(1)}, bf16[9,256,256]{2,1,0:T(8,128)(2,1)S(1)}, u32[]{:S(2)}, u32[]{:S(2)}) %collective-permute-start.6) | collective-permute-done | bytes 1179680 | tf_op jit(solution)/shard_map/factor_step_2/ppermute | solution.py:420
  66.7 3.7 %collective-permute-done.4.rest_6_.rest_7_.rest_11_.rest_4_ = bf16[9,256,256]{2,1,0:T(8,128)(2,1)S(1)} collective-permute-done((bf16[9,256,256]{2,1,0:T(8,128)(2,1)S(1)}, bf16[9,256,256]{2,1,0:T(8,128)(2,1)S(1)}, u32[]{:S(2)}, u32[]{:S(2)}) %collective-permute-start.4) | collective-permute-done | bytes 1179680 | tf_op jit(solution)/shard_map/factor_step_2/ppermute | solution.py:419
  70.4 0.5 collective-permute-start.13
  70.9 3.2 %collective-permute-start.15 = (bf16[9,256,256]{2,1,0:T(8,128)(2,1)S(1)}, bf16[9,256,256]{2,1,0:T(8,128)(2,1)S(1)}, u32[]{:S(2)}, u32[]{:S(2)}) collective-permute-start(bf16[9,256,256]{2,1,0:T(8,128)(2,1)S(1)} %factor_step_2.7), channel_id=1, source_target_pairs={{0,3},{1,0},{2,1},{3,2},{4,7},{5,4},{6,5},{7,6},{8,11},{9,8},{10,9... | collective-permute-start | bytes 3538952 | tf_op jit(solution)/shard_map/factor_step_3/ppermute | solution.py:430
  74.1 0.8 collective-permute-done.13.rest_13_.rest_16_.rest_20_.rest_11_
  74.9 2.2 %forward_0.1 = (f32[4,32,256]{2,1,0:T(8,128)S(1)}, bf16[4,32,256]{2,1,0:T(8,128)(2,1)S(1)}, bf16[64,32,256]{2,1,0:T(8,128)(2,1)S(1)}) custom-call(s32[1]{0:T(128)} %bitcast.core_ref, s32[1]{0:T(128)} %bitcast.1.plane_ref, s32[4,4,8]{2,1,0:T(4,128)S(1)} %fusion.3.at_ref, bf16[4,144,256]{2,1,0:T(8,128)(2,1)S(1)} %pad_maximum_fusion.rest_0_.rest_1_.rest_5_.own_told, ...), custom_call_target="tpu_custom_call" | custom-call | flops 150994944 | bytes 6291456 | tf_op jit(solution)/shard_map/forward_0/pallas_call | solution.py:269
  77.1 24.2 %all_to_all.35.got_ref = bf16[16,4,32,256]{3,2,1,0:T(8,128)(2,1)S(1)} all-to-all(bf16[16,4,32,256]{3,2,1,0:T(8,128)(2,1)S(1)} %bitcast.47), channel_id=1, replica_groups=mesh['x'=4,'y'=4,'c'=2,'z'=4] {'x','y'}, dimensions={0} | all-to-all | bytes 2097152 | tf_op jit(solution)/shard_map/forward_0/all_to_all | solution.py:388
  101.4 0.1 factor_step_3.1.rest_0_
  101.6 0.5 collective-permute-start.17
  102.1 0.9 forward_1.2
  103.0 1.5 collective-permute-done.16.rest_21_.rest_17_.rest_10_.rest_14_
  104.5 1.7 collective-permute-done.17.rest_22_.rest_18_.rest_11_.rest_15_
  106.2 3.6 %forward_1.3 = (f32[4,32,256]{2,1,0:T(8,128)S(1)}, bf16[4,32,256]{2,1,0:T(8,128)(2,1)S(1)}, bf16[64,32,256]{2,1,0:T(8,128)(2,1)S(1)}) custom-call(s32[1]{0:T(128)} %bitcast.core_ref, s32[1]{0:T(128)} %bitcast.1.plane_ref, s32[4,4,8]{2,1,0:T(4,128)S(1)} %fusion.3.at_ref, f32[4,32,256]{2,1,0:T(8,128)S(1)} %factor_step_3.1.rest_0_, ...), custom_call_target="tpu_custom_call", output_to_operand_aliasing={{2}: (6, {})} | custom-call | flops 150994944 | bytes 6291456 | tf_op jit(solution)/shard_map/forward_1/pallas_call | solution.py:269
  109.7 20.4 %all_to_all.36.rest_0_ = bf16[16,4,32,256]{3,2,1,0:T(8,128)(2,1)S(1)} all-to-all(bf16[16,4,32,256]{3,2,1,0:T(8,128)(2,1)S(1)} %bitcast.41), channel_id=1, replica_groups=mesh['x'=4,'y'=4,'c'=2,'z'=4] {'x','y'}, dimensions={0} | all-to-all | bytes 2097152 | tf_op jit(solution)/shard_map/forward_1/all_to_all | solution.py:388
  130.1 2.4 %forward_2.1 = (f32[4,32,256]{2,1,0:T(8,128)S(1)}, bf16[4,32,256]{2,1,0:T(8,128)(2,1)S(1)}, bf16[64,32,256]{2,1,0:T(8,128)(2,1)S(1)}) custom-call(s32[1]{0:T(128)} %bitcast.core_ref, s32[1]{0:T(128)} %bitcast.1.plane_ref, s32[4,4,8]{2,1,0:T(4,128)S(1)} %fusion.3.at_ref, bf16[16,4,32,256]{3,2,1,0:T(8,128)(2,1)S(1)} %all_to_all.36.rest_0_, ...), custom_call_target="tpu_custom_call" | custom-call | flops 150994944 | bytes 6291456 | tf_op jit(solution)/shard_map/forward_2/pallas_call | solution.py:269
  132.5 17.3 %all_to_all.37.got_ref = bf16[16,4,32,256]{3,2,1,0:T(8,128)(2,1)S(1)} all-to-all(bf16[16,4,32,256]{3,2,1,0:T(8,128)(2,1)S(1)} %bitcast.46), channel_id=1, replica_groups=mesh['x'=4,'y'=4,'c'=2,'z'=4] {'x','y'}, dimensions={0} | all-to-all | bytes 2097152 | tf_op jit(solution)/shard_map/forward_2/all_to_all | solution.py:388
  149.8 0.6 top.1
  150.4 16.2 %all_to_all.38 = bf16[16,4,32,256]{3,2,1,0:T(8,128)(2,1)S(1)} all-to-all(bf16[16,4,32,256]{3,2,1,0:T(8,128)(2,1)S(1)} %get-tuple-element.75), channel_id=1, replica_groups=mesh['x'=4,'y'=4,'c'=2,'z'=4] {'x','y'}, dimensions={0} | all-to-all | bytes 2097152 | tf_op jit(solution)/shard_map/backward_2/all_to_all | solution.py:388
  166.6 1.7 backward_2.1
  168.3 16.2 %all_to_all.39 = bf16[16,4,32,256]{3,2,1,0:T(8,128)(2,1)S(1)} all-to-all(bf16[16,4,32,256]{3,2,1,0:T(8,128)(2,1)S(1)} %get-tuple-element.77), channel_id=1, replica_groups=mesh['x'=4,'y'=4,'c'=2,'z'=4] {'x','y'}, dimensions={0} | all-to-all | bytes 2097152 | tf_op jit(solution)/shard_map/backward_1/all_to_all | solution.py:388
  184.4 1.9 backward_1.1
  186.4 16.2 %all_to_all.40 = bf16[16,4,32,256]{3,2,1,0:T(8,128)(2,1)S(1)} all-to-all(bf16[16,4,32,256]{3,2,1,0:T(8,128)(2,1)S(1)} %get-tuple-element.79), channel_id=1, replica_groups=mesh['x'=4,'y'=4,'c'=2,'z'=4] {'x','y'}, dimensions={0} | all-to-all | bytes 2097152 | tf_op jit(solution)/shard_map/backward_0/all_to_all | solution.py:388
  202.5 1.6 backward_0.1
  204.2 12.2 %all_to_all.41.own_ref = bf16[4,2,2,2,32,256]{5,4,3,2,1,0:T(8,128)(2,1)S(1)} all-to-all(bf16[4,2,2,2,32,256]{5,4,3,2,1,0:T(8,128)(2,1)S(1)} %maximum_maximum_fusion), channel_id=1, replica_groups=mesh['x'=4,'y'=4,'c'=2,'z'=4] {'z'}, dimensions={0} | all-to-all | bytes 1048576 | tf_op jit(solution)/shard_map/to_planes/all_to_all | solution.py:461
  216.4 1.9 collective-permute-done.18.other_ref
  218.3 1.1 to_planes.1
  (28 shorter events, 0.4 us)
Async XLA Ops:
  0.6 8.0 %copy-start.1 = (bf16[1,2,1,256,256]{4,3,2,1,0:T(8,128)(2,1)S(1)}, bf16[1,2,1,256,256]{4,3,2,1,0:T(8,128)(2,1)}, u32[]{:S(2)}) copy-start(bf16[1,2,1,256,256]{4,3,2,1,0:T(8,128)(2,1)} %param.5) | copy-start | bytes 786436
  0.6 1.1 copy-start.2
  1.7 0.7 copy-start.3
  3.1 7.6 %collective-permute-start.2 = (bf16[144,256]{1,0:T(8,128)(2,1)S(1)}, bf16[144,256]{1,0:T(8,128)(2,1)S(1)}, u32[]{:S(2)}, u32[]{:S(2)}) collective-permute-start(bf16[144,256]{1,0:T(8,128)(2,1)S(1)} %get-tuple-element.88), channel_id=1, source_target_pairs={{0,3},{1,0},{2,1},{3,2},{4,7},{5,4},{6,5},{7,6},{8,11},{9,8},{10,9... | collective-permute-start | bytes 221192 | tf_op jit(solution)/shard_map/tell_planes/ppermute | solution.py:402
  7.3 6.1 %collective-permute-start.1 = (bf16[144,256]{1,0:T(8,128)(2,1)S(1)}, bf16[144,256]{1,0:T(8,128)(2,1)S(1)}, u32[]{:S(2)}, u32[]{:S(2)}) collective-permute-start(bf16[144,256]{1,0:T(8,128)(2,1)S(1)} %get-tuple-element.89), channel_id=1, source_target_pairs={{0,2},{1,3},{2,0},{3,1},{4,6},{5,7},{6,4},{7,5},{8,10},{9,11},{10,... | collective-permute-start | bytes 221192 | tf_op jit(solution)/shard_map/tell_planes/ppermute | solution.py:402
  7.3 6.5 %collective-permute-start = (bf16[144,256]{1,0:T(8,128)(2,1)S(1)}, bf16[144,256]{1,0:T(8,128)(2,1)S(1)}, u32[]{:S(2)}, u32[]{:S(2)}) collective-permute-start(bf16[144,256]{1,0:T(8,128)(2,1)S(1)} %get-tuple-element.90), channel_id=1, source_target_pairs={{0,1},{1,2},{2,3},{3,0},{4,5},{5,6},{6,7},{7,4},{8,9},{9,10},{10,1... | collective-permute-start | bytes 221192 | tf_op jit(solution)/shard_map/tell_planes/ppermute | solution.py:402
  8.6 1.6 copy-start
  13.8 26.5 %collective-permute-start.5 = (bf16[9,256,256]{2,1,0:T(8,128)(2,1)S(1)}, bf16[9,256,256]{2,1,0:T(8,128)(2,1)S(1)}, u32[]{:S(2)}, u32[]{:S(2)}) collective-permute-start(bf16[9,256,256]{2,1,0:T(8,128)(2,1)S(1)} %factor_step_1.3.here_ref.else_ref.rest_3_.rest_4_.rest_8_.rest_1_), channel_id=1, source_target_pairs={{0,3},{1,0},{2,1},{3,2},{4,7},{5,4},{6,5},{7,6},{8,11},{9,8},{10,9... | collective-permute-start | bytes 3538952 | tf_op jit(solution)/shard_map/factor_step_1/ppermute | solution.py:408
  14.7 28.4 %collective-permute-start.3 = (bf16[9,256,256]{2,1,0:T(8,128)(2,1)S(1)}, bf16[9,256,256]{2,1,0:T(8,128)(2,1)S(1)}, u32[]{:S(2)}, u32[]{:S(2)}) collective-permute-start(bf16[9,256,256]{2,1,0:T(8,128)(2,1)S(1)} %factor_step_1.2.else_ref.here_ref.rest_2_.rest_3_.rest_7_.rest_0_), channel_id=1, source_target_pairs={{0,1},{1,2},{2,3},{3,0},{4,5},{5,6},{6,7},{7,4},{8,9},{9,10},{10,1... | collective-permute-start | bytes 3538952 | tf_op jit(solution)/shard_map/factor_step_1/ppermute | solution.py:407
  15.9 28.1 %collective-permute-start.9 = (bf16[9,256,256]{2,1,0:T(8,128)(2,1)S(1)}, bf16[9,256,256]{2,1,0:T(8,128)(2,1)S(1)}, u32[]{:S(2)}, u32[]{:S(2)}) collective-permute-start(bf16[9,256,256]{2,1,0:T(8,128)(2,1)S(1)} %factor_step_1.3.here_ref.else_ref.rest_3_.rest_4_.rest_8_.rest_1_), channel_id=1, source_target_pairs={{0,4},{4,0},{1,5},{5,1},{2,6},{6,2},{3,7},{7,3},{8,12},{12,8},{9,1... | collective-permute-start | bytes 3538952 | tf_op jit(solution)/shard_map/factor_step_1/ppermute | solution.py:384
  15.9 27.9 %collective-permute-start.7 = (bf16[4,144,256]{2,1,0:T(8,128)(2,1)S(1)}, bf16[4,144,256]{2,1,0:T(8,128)(2,1)S(1)}, u32[]{:S(2)}, u32[]{:S(2)}) collective-permute-start(bf16[4,144,256]{2,1,0:T(8,128)(2,1)S(1)} %pad_maximum_fusion.rest_0_.rest_1_.rest_5_.own_told), channel_id=1, source_target_pairs={{0,4},{4,0},{1,5},{5,1},{2,6},{6,2},{3,7},{7,3},{8,12},{12,8},{9,1... | collective-permute-start | bytes 884744 | tf_op jit(solution)/shard_map/tell_planes/ppermute | solution.py:384
  16.5 29.3 %collective-permute-start.8 = (bf16[9,256,256]{2,1,0:T(8,128)(2,1)S(1)}, bf16[9,256,256]{2,1,0:T(8,128)(2,1)S(1)}, u32[]{:S(2)}, u32[]{:S(2)}) collective-permute-start(bf16[9,256,256]{2,1,0:T(8,128)(2,1)S(1)} %factor_step_1.2.else_ref.here_ref.rest_2_.rest_3_.rest_7_.rest_0_), channel_id=1, source_target_pairs={{0,4},{4,0},{1,5},{5,1},{2,6},{6,2},{3,7},{7,3},{8,12},{12,8},{9,1... | collective-permute-start | bytes 3538952 | tf_op jit(solution)/shard_map/factor_step_1/ppermute | solution.py:384
  41.0 25.7 %collective-permute-start.6 = (bf16[9,256,256]{2,1,0:T(8,128)(2,1)S(1)}, bf16[9,256,256]{2,1,0:T(8,128)(2,1)S(1)}, u32[]{:S(2)}, u32[]{:S(2)}) collective-permute-start(bf16[9,256,256]{2,1,0:T(8,128)(2,1)S(1)} %factor_step_2.5), channel_id=1, source_target_pairs={{0,3},{1,0},{2,1},{3,2},{4,7},{5,4},{6,5},{7,6},{8,11},{9,8},{10,9... | collective-permute-start | bytes 3538952 | tf_op jit(solution)/shard_map/factor_step_2/ppermute | solution.py:420
  43.8 26.6 %collective-permute-start.4 = (bf16[9,256,256]{2,1,0:T(8,128)(2,1)S(1)}, bf16[9,256,256]{2,1,0:T(8,128)(2,1)S(1)}, u32[]{:S(2)}, u32[]{:S(2)}) collective-permute-start(bf16[9,256,256]{2,1,0:T(8,128)(2,1)S(1)} %factor_step_2.4), channel_id=1, source_target_pairs={{0,1},{1,2},{2,3},{3,0},{4,5},{5,6},{6,7},{7,4},{8,9},{9,10},{10,1... | collective-permute-start | bytes 3538952 | tf_op jit(solution)/shard_map/factor_step_2/ppermute | solution.py:419
  43.9 22.8 %collective-permute-start.11 = (bf16[9,256,256]{2,1,0:T(8,128)(2,1)S(1)}, bf16[9,256,256]{2,1,0:T(8,128)(2,1)S(1)}, u32[]{:S(2)}, u32[]{:S(2)}) collective-permute-start(bf16[9,256,256]{2,1,0:T(8,128)(2,1)S(1)} %collective-permute-done.5.here_ref.else_ref.rest_5_.rest_6_.rest_10_.rest_3_), channel_id=1, source_target_pairs={{0,4},{4,0},{1,5},{5,1},{2,6},{6,2},{3,7},{7,3},{8,12},{12,8},{9,1... | collective-permute-start | bytes 3538952 | tf_op jit(solution)/shard_map/factor_step_2/ppermute | solution.py:384
  44.0 26.4 %collective-permute-start.10 = (bf16[9,256,256]{2,1,0:T(8,128)(2,1)S(1)}, bf16[9,256,256]{2,1,0:T(8,128)(2,1)S(1)}, u32[]{:S(2)}, u32[]{:S(2)}) collective-permute-start(bf16[9,256,256]{2,1,0:T(8,128)(2,1)S(1)} %collective-permute-done.3.else_ref.here_ref.rest_4_.rest_5_.rest_9_.rest_2_), channel_id=1, source_target_pairs={{0,4},{4,0},{1,5},{5,1},{2,6},{6,2},{3,7},{7,3},{8,12},{12,8},{9,1... | collective-permute-start | bytes 3538952 | tf_op jit(solution)/shard_map/factor_step_2/ppermute | solution.py:384
  70.4 3.8 %collective-permute-start.12 = (bf16[9,256,256]{2,1,0:T(8,128)(2,1)S(1)}, bf16[9,256,256]{2,1,0:T(8,128)(2,1)S(1)}, u32[]{:S(2)}, u32[]{:S(2)}) collective-permute-start(bf16[9,256,256]{2,1,0:T(8,128)(2,1)S(1)} %collective-permute-done.4.rest_6_.rest_7_.rest_11_.rest_4_), channel_id=1, source_target_pairs={{0,4},{4,0},{1,5},{5,1},{2,6},{6,2},{3,7},{7,3},{8,12},{12,8},{9,1... | collective-permute-start | bytes 3538952 | tf_op jit(solution)/shard_map/factor_step_2/ppermute | solution.py:384
  70.4 4.5 %collective-permute-start.13 = (bf16[9,256,256]{2,1,0:T(8,128)(2,1)S(1)}, bf16[9,256,256]{2,1,0:T(8,128)(2,1)S(1)}, u32[]{:S(2)}, u32[]{:S(2)}) collective-permute-start(bf16[9,256,256]{2,1,0:T(8,128)(2,1)S(1)} %collective-permute-done.6.rest_7_.rest_8_.rest_12_.rest_5_), channel_id=1, source_target_pairs={{0,4},{4,0},{1,5},{5,1},{2,6},{6,2},{3,7},{7,3},{8,12},{12,8},{9,1... | collective-permute-start | bytes 3538952 | tf_op jit(solution)/shard_map/factor_step_2/ppermute | solution.py:384
  70.9 30.7 %collective-permute-start.14 = (bf16[9,256,256]{2,1,0:T(8,128)(2,1)S(1)}, bf16[9,256,256]{2,1,0:T(8,128)(2,1)S(1)}, u32[]{:S(2)}, u32[]{:S(2)}) collective-permute-start(bf16[9,256,256]{2,1,0:T(8,128)(2,1)S(1)} %factor_step_2.6), channel_id=1, source_target_pairs={{0,1},{1,2},{2,3},{3,0},{4,5},{5,6},{6,7},{7,4},{8,9},{9,10},{10,1... | collective-permute-start | bytes 3538952 | tf_op jit(solution)/shard_map/factor_step_3/ppermute | solution.py:429
  70.9 30.7 %collective-permute-start.15 = (bf16[9,256,256]{2,1,0:T(8,128)(2,1)S(1)}, bf16[9,256,256]{2,1,0:T(8,128)(2,1)S(1)}, u32[]{:S(2)}, u32[]{:S(2)}) collective-permute-start(bf16[9,256,256]{2,1,0:T(8,128)(2,1)S(1)} %factor_step_2.7), channel_id=1, source_target_pairs={{0,3},{1,0},{2,1},{3,2},{4,7},{5,4},{6,5},{7,6},{8,11},{9,8},{10,9... | collective-permute-start | bytes 3538952 | tf_op jit(solution)/shard_map/factor_step_3/ppermute | solution.py:430
  101.6 2.9 %collective-permute-start.16 = (bf16[9,256,256]{2,1,0:T(8,128)(2,1)S(1)}, bf16[9,256,256]{2,1,0:T(8,128)(2,1)S(1)}, u32[]{:S(2)}, u32[]{:S(2)}) collective-permute-start(bf16[9,256,256]{2,1,0:T(8,128)(2,1)S(1)} %collective-permute-done.14.rest_9_.rest_13_.rest_4_.rest_6_), channel_id=1, source_target_pairs={{0,4},{4,0},{1,5},{5,1},{2,6},{6,2},{3,7},{7,3},{8,12},{12,8},{9,1... | collective-permute-start | bytes 3538952 | tf_op jit(solution)/shard_map/factor_step_3/ppermute | solution.py:384
  101.6 4.5 %collective-permute-start.17 = (bf16[9,256,256]{2,1,0:T(8,128)(2,1)S(1)}, bf16[9,256,256]{2,1,0:T(8,128)(2,1)S(1)}, u32[]{:S(2)}, u32[]{:S(2)}) collective-permute-start(bf16[9,256,256]{2,1,0:T(8,128)(2,1)S(1)} %collective-permute-done.15.rest_10_.rest_14_.rest_5_.rest_7_), channel_id=1, source_target_pairs={{0,4},{4,0},{1,5},{5,1},{2,6},{6,2},{3,7},{7,3},{8,12},{12,8},{9,1... | collective-permute-start | bytes 3538952 | tf_op jit(solution)/shard_map/factor_step_3/ppermute | solution.py:384
  216.4 1.9 collective-permute-start.18

commit v8 on v7

--- a/solution.py
+++ b/solution.py
@@ -385,7 +385,7 @@
 
 
 def exchange(value):
-    return lax.all_to_all(value.reshape(CHIPS, 4, COLS, WIDTH), ("x", "y"), 0, 0, tiled=True)
+    return lax.all_to_all(value.reshape(CHIPS, 4, COLS, WIDTH), ("y", "x"), 0, 0, tiled=True)
 
 
 def on_device(rhs, inverses, blocks, pattern):
@@ -413,7 +413,8 @@
         told = (told, swap(told))
         targets = jnp.concatenate([t[:, PAT : PAT + 2, :FAN] for t in told], axis=1).astype(jnp.int32)
         targets = jnp.clip(targets, 0, NODES - 1)
-        places = (targets % 32) // 2 * 4 + jnp.bitwise_xor(targets % 2, core) * 2 + targets // 32
+        chip = targets % 8 // 2 * 4 + targets % 32 // 8
+        places = chip * 4 + jnp.bitwise_xor(targets % 2, core) * 2 + targets // 32
 
     with jax.named_scope("factor_step_2"):
         up_2 = lax.ppermute(choose(plane1, 0, own_b, up_1), "z", UP)

time: 221 us -> 220 us (level)
  no operation moved by 1% of the time
where the time goes in v8:
time: 220 us; the launch traced here: 219 us
  blocking collectives  122 us (55%)
  waiting for transfers between devices  57.3 us (26%)
  Pallas kernels  19.9 us (9%)
  starting transfers between devices  15.3 us (7%)
  local copies, waits for them, and re-layouts  3.38 us (2%)
    all_to_all x6, blocking collectives, exchange(): lax.all_to_all(value.reshape(CHIPS, 4, COLS, WIDTH), ('y', 'x'), 0, 0, ti...  110 us
    ppermute x1, waiting for transfers between devices, on_device(): down_1 = lax.ppermute(own_b, 'z', DOWN)  23.8 us
    ppermute x1, waiting for transfers between devices, on_device(): down_2 = lax.ppermute(choose(plane1, 3, down_1, own_a), 'z', DOWN)  20.8 us
    all_to_all x1, blocking collectives, on_device(): fx = lax.all_to_all(fx, 'z', 0, 0, tiled=True)  12.2 us
    pallas_call x4, Pallas kernels, forward_part(): pl.pallas_call(functools.partial(forward_kernel, level, part), in_specs=[...  9.04 us
    ppermute x10, waiting for transfers between devices, swap(): return lax.ppermute(value, 'c', [(0, 1), (1, 0)])  5.87 us
    ppermute x3, starting transfers between devices, on_device(): lax.ppermute(message[k], 'z', [(z, (z + k) % 4) for z in range(4)])  5.45 us
    pallas_call x3, Pallas kernels, backward_level(): pl.pallas_call(functools.partial(backward_kernel, level), in_specs=[SMEM,...  5.22 us
  transfers between devices with their start and end apart: 19, of which 9 were waited for; matrix products, arithmetic and copies ran while one was open for 0% of the time, Pallas kernels for 3%

profile of v8, /device:TPU:0, one launch (start us, length us, event | category | flops | bytes accessed | tf_op | source)
XLA Modules:
  0.0 218.7 jit_solution(14755573198182358794)
XLA Ops:
  0.7 1.1 copy-done.2
  1.7 0.7 copy-done.3
  2.4 0.7 tell_planes.1
  3.1 4.2 %collective-permute-start.2 = (bf16[144,256]{1,0:T(8,128)(2,1)S(1)}, bf16[144,256]{1,0:T(8,128)(2,1)S(1)}, u32[]{:S(2)}, u32[]{:S(2)}) collective-permute-start(bf16[144,256]{1,0:T(8,128)(2,1)S(1)} %get-tuple-element.88), channel_id=1, source_target_pairs={{0,3},{1,0},{2,1},{3,2},{4,7},{5,4},{6,5},{7,6},{8,11},{9,8},{10,9... | collective-permute-start | bytes 221192 | tf_op jit(solution)/shard_map/tell_planes/ppermute | solution.py:402
  7.3 1.3 collective-permute-start
  8.6 1.6 copy-done
  10.2 0.3 factor_step_1.3.here_ref.else_ref.rest_3_.rest_4_.rest_8_.rest_1_
  10.4 0.3 factor_step_1.2.else_ref.here_ref.rest_2_.rest_3_.rest_7_.rest_0_
  10.8 2.6 %collective-permute-done.1 = bf16[144,256]{1,0:T(8,128)(2,1)S(1)} collective-permute-done((bf16[144,256]{1,0:T(8,128)(2,1)S(1)}, bf16[144,256]{1,0:T(8,128)(2,1)S(1)}, u32[]{:S(2)}, u32[]{:S(2)}) %collective-permute-start.1) | collective-permute-done | bytes 73760 | tf_op jit(solution)/shard_map/tell_planes/ppermute | solution.py:402
  13.4 0.4 collective-permute-done
  13.8 0.9 collective-permute-start.5
  14.7 1.2 collective-permute-start.3
  15.9 0.6 collective-permute-start.7
  16.5 0.1 collective-permute-start.8
  16.6 23.8 %collective-permute-done.5.here_ref.else_ref.rest_5_.rest_6_.rest_10_.rest_3_ = bf16[9,256,256]{2,1,0:T(8,128)(2,1)S(1)} collective-permute-done((bf16[9,256,256]{2,1,0:T(8,128)(2,1)S(1)}, bf16[9,256,256]{2,1,0:T(8,128)(2,1)S(1)}, u32[]{:S(2)}, u32[]{:S(2)}) %collective-permute-start.5) | collective-permute-done | bytes 1179680 | tf_op jit(solution)/shard_map/factor_step_1/ppermute | solution.py:408
  40.4 0.6 factor_step_2.5
  41.0 2.1 collective-permute-start.6
  43.1 0.6 factor_step_2.4
  43.9 0.1 collective-permute-start.11
  44.0 0.5 collective-permute-start.10
  44.5 0.6 factor_step_2.7
  45.2 0.6 factor_step_2.6
  45.8 20.8 %collective-permute-done.6.rest_7_.rest_8_.rest_12_.rest_5_ = bf16[9,256,256]{2,1,0:T(8,128)(2,1)S(1)} collective-permute-done((bf16[9,256,256]{2,1,0:T(8,128)(2,1)S(1)}, bf16[9,256,256]{2,1,0:T(8,128)(2,1)S(1)}, u32[]{:S(2)}, u32[]{:S(2)}) %collective-permute-start.6) | collective-permute-done | bytes 1179680 | tf_op jit(solution)/shard_map/factor_step_2/ppermute | solution.py:421
  66.7 3.7 %collective-permute-done.4.rest_6_.rest_7_.rest_11_.rest_4_ = bf16[9,256,256]{2,1,0:T(8,128)(2,1)S(1)} collective-permute-done((bf16[9,256,256]{2,1,0:T(8,128)(2,1)S(1)}, bf16[9,256,256]{2,1,0:T(8,128)(2,1)S(1)}, u32[]{:S(2)}, u32[]{:S(2)}) %collective-permute-start.4) | collective-permute-done | bytes 1179680 | tf_op jit(solution)/shard_map/factor_step_2/ppermute | solution.py:420
  70.4 0.5 collective-permute-start.13
  70.9 3.2 %collective-permute-start.15 = (bf16[9,256,256]{2,1,0:T(8,128)(2,1)S(1)}, bf16[9,256,256]{2,1,0:T(8,128)(2,1)S(1)}, u32[]{:S(2)}, u32[]{:S(2)}) collective-permute-start(bf16[9,256,256]{2,1,0:T(8,128)(2,1)S(1)} %factor_step_2.7), channel_id=1, source_target_pairs={{0,3},{1,0},{2,1},{3,2},{4,7},{5,4},{6,5},{7,6},{8,11},{9,8},{10,9... | collective-permute-start | bytes 3538952 | tf_op jit(solution)/shard_map/factor_step_3/ppermute | solution.py:431
  74.1 0.8 collective-permute-done.13.rest_13_.rest_16_.rest_20_.rest_11_
  74.9 2.2 %forward_0.1 = (f32[4,32,256]{2,1,0:T(8,128)S(1)}, bf16[4,32,256]{2,1,0:T(8,128)(2,1)S(1)}, bf16[64,32,256]{2,1,0:T(8,128)(2,1)S(1)}) custom-call(s32[1]{0:T(128)} %bitcast.core_ref, s32[1]{0:T(128)} %bitcast.1.plane_ref, s32[4,4,8]{2,1,0:T(4,128)S(1)} %fusion.5.at_ref, bf16[4,144,256]{2,1,0:T(8,128)(2,1)S(1)} %pad_maximum_fusion.rest_0_.rest_1_.rest_5_.own_told, ...), custom_call_target="tpu_custom_call" | custom-call | flops 150994944 | bytes 6291456 | tf_op jit(solution)/shard_map/forward_0/pallas_call | solution.py:269
  77.1 24.3 %all_to_all.35.got_ref = bf16[16,4,32,256]{3,2,1,0:T(8,128)(2,1)S(1)} all-to-all(bf16[16,4,32,256]{3,2,1,0:T(8,128)(2,1)S(1)} %bitcast.47), channel_id=1, replica_groups=mesh['x'=4,'y'=4,'c'=2,'z'=4] {'y','x'}, dimensions={0} | all-to-all | bytes 2097152 | tf_op jit(solution)/shard_map/forward_0/all_to_all | solution.py:388
  101.4 0.1 factor_step_3.1.rest_0_
  101.7 0.5 collective-permute-start.17
  102.2 0.9 forward_1.2
  103.1 1.5 collective-permute-done.16.rest_21_.rest_17_.rest_10_.rest_14_
  104.5 1.7 collective-permute-done.17.rest_22_.rest_18_.rest_11_.rest_15_
  106.2 3.6 %forward_1.3 = (f32[4,32,256]{2,1,0:T(8,128)S(1)}, bf16[4,32,256]{2,1,0:T(8,128)(2,1)S(1)}, bf16[64,32,256]{2,1,0:T(8,128)(2,1)S(1)}) custom-call(s32[1]{0:T(128)} %bitcast.core_ref, s32[1]{0:T(128)} %bitcast.1.plane_ref, s32[4,4,8]{2,1,0:T(4,128)S(1)} %fusion.5.at_ref, f32[4,32,256]{2,1,0:T(8,128)S(1)} %factor_step_3.1.rest_0_, ...), custom_call_target="tpu_custom_call", output_to_operand_aliasing={{2}: (6, {})} | custom-call | flops 150994944 | bytes 6291456 | tf_op jit(solution)/shard_map/forward_1/pallas_call | solution.py:269
  109.8 20.5 %all_to_all.36.rest_0_ = bf16[16,4,32,256]{3,2,1,0:T(8,128)(2,1)S(1)} all-to-all(bf16[16,4,32,256]{3,2,1,0:T(8,128)(2,1)S(1)} %bitcast.41), channel_id=1, replica_groups=mesh['x'=4,'y'=4,'c'=2,'z'=4] {'y','x'}, dimensions={0} | all-to-all | bytes 2097152 | tf_op jit(solution)/shard_map/forward_1/all_to_all | solution.py:388
  130.2 2.4 %forward_2.1 = (f32[4,32,256]{2,1,0:T(8,128)S(1)}, bf16[4,32,256]{2,1,0:T(8,128)(2,1)S(1)}, bf16[64,32,256]{2,1,0:T(8,128)(2,1)S(1)}) custom-call(s32[1]{0:T(128)} %bitcast.core_ref, s32[1]{0:T(128)} %bitcast.1.plane_ref, s32[4,4,8]{2,1,0:T(4,128)S(1)} %fusion.5.at_ref, bf16[16,4,32,256]{3,2,1,0:T(8,128)(2,1)S(1)} %all_to_all.36.rest_0_, ...), custom_call_target="tpu_custom_call" | custom-call | flops 150994944 | bytes 6291456 | tf_op jit(solution)/shard_map/forward_2/pallas_call | solution.py:269
  132.6 17.0 %all_to_all.37.got_ref = bf16[16,4,32,256]{3,2,1,0:T(8,128)(2,1)S(1)} all-to-all(bf16[16,4,32,256]{3,2,1,0:T(8,128)(2,1)S(1)} %bitcast.46), channel_id=1, replica_groups=mesh['x'=4,'y'=4,'c'=2,'z'=4] {'y','x'}, dimensions={0} | all-to-all | bytes 2097152 | tf_op jit(solution)/shard_map/forward_2/all_to_all | solution.py:388
  149.6 0.6 top.1
  150.2 16.2 %all_to_all.38 = bf16[16,4,32,256]{3,2,1,0:T(8,128)(2,1)S(1)} all-to-all(bf16[16,4,32,256]{3,2,1,0:T(8,128)(2,1)S(1)} %get-tuple-element.75), channel_id=1, replica_groups=mesh['x'=4,'y'=4,'c'=2,'z'=4] {'y','x'}, dimensions={0} | all-to-all | bytes 2097152 | tf_op jit(solution)/shard_map/backward_2/all_to_all | solution.py:388
  166.4 1.7 backward_2.1
  168.1 15.9 %all_to_all.39 = bf16[16,4,32,256]{3,2,1,0:T(8,128)(2,1)S(1)} all-to-all(bf16[16,4,32,256]{3,2,1,0:T(8,128)(2,1)S(1)} %get-tuple-element.77), channel_id=1, replica_groups=mesh['x'=4,'y'=4,'c'=2,'z'=4] {'y','x'}, dimensions={0} | all-to-all | bytes 2097152 | tf_op jit(solution)/shard_map/backward_1/all_to_all | solution.py:388
  183.9 1.9 backward_1.1
  185.9 15.9 %all_to_all.40 = bf16[16,4,32,256]{3,2,1,0:T(8,128)(2,1)S(1)} all-to-all(bf16[16,4,32,256]{3,2,1,0:T(8,128)(2,1)S(1)} %get-tuple-element.79), channel_id=1, replica_groups=mesh['x'=4,'y'=4,'c'=2,'z'=4] {'y','x'}, dimensions={0} | all-to-all | bytes 2097152 | tf_op jit(solution)/shard_map/backward_0/all_to_all | solution.py:388
  201.8 1.6 backward_0.1
  203.5 12.2 %all_to_all.41.own_ref = bf16[4,2,2,2,32,256]{5,4,3,2,1,0:T(8,128)(2,1)S(1)} all-to-all(bf16[4,2,2,2,32,256]{5,4,3,2,1,0:T(8,128)(2,1)S(1)} %maximum_maximum_fusion), channel_id=1, replica_groups=mesh['x'=4,'y'=4,'c'=2,'z'=4] {'z'}, dimensions={0} | all-to-all | bytes 1048576 | tf_op jit(solution)/shard_map/to_planes/all_to_all | solution.py:462
  215.7 1.9 collective-permute-done.18.other_ref
  217.6 1.1 to_planes.1
  (28 shorter events, 0.4 us)
Async XLA Ops:
  0.6 8.0 %copy-start.1 = (bf16[1,2,1,256,256]{4,3,2,1,0:T(8,128)(2,1)S(1)}, bf16[1,2,1,256,256]{4,3,2,1,0:T(8,128)(2,1)}, u32[]{:S(2)}) copy-start(bf16[1,2,1,256,256]{4,3,2,1,0:T(8,128)(2,1)} %param.5) | copy-start | bytes 786436
  0.6 1.1 copy-start.2
  1.7 0.7 copy-start.3
  3.1 7.6 %collective-permute-start.2 = (bf16[144,256]{1,0:T(8,128)(2,1)S(1)}, bf16[144,256]{1,0:T(8,128)(2,1)S(1)}, u32[]{:S(2)}, u32[]{:S(2)}) collective-permute-start(bf16[144,256]{1,0:T(8,128)(2,1)S(1)} %get-tuple-element.88), channel_id=1, source_target_pairs={{0,3},{1,0},{2,1},{3,2},{4,7},{5,4},{6,5},{7,6},{8,11},{9,8},{10,9... | collective-permute-start | bytes 221192 | tf_op jit(solution)/shard_map/tell_planes/ppermute | solution.py:402
  7.3 6.1 %collective-permute-start.1 = (bf16[144,256]{1,0:T(8,128)(2,1)S(1)}, bf16[144,256]{1,0:T(8,128)(2,1)S(1)}, u32[]{:S(2)}, u32[]{:S(2)}) collective-permute-start(bf16[144,256]{1,0:T(8,128)(2,1)S(1)} %get-tuple-element.89), channel_id=1, source_target_pairs={{0,2},{1,3},{2,0},{3,1},{4,6},{5,7},{6,4},{7,5},{8,10},{9,11},{10,... | collective-permute-start | bytes 221192 | tf_op jit(solution)/shard_map/tell_planes/ppermute | solution.py:402
  7.3 6.5 %collective-permute-start = (bf16[144,256]{1,0:T(8,128)(2,1)S(1)}, bf16[144,256]{1,0:T(8,128)(2,1)S(1)}, u32[]{:S(2)}, u32[]{:S(2)}) collective-permute-start(bf16[144,256]{1,0:T(8,128)(2,1)S(1)} %get-tuple-element.90), channel_id=1, source_target_pairs={{0,1},{1,2},{2,3},{3,0},{4,5},{5,6},{6,7},{7,4},{8,9},{9,10},{10,1... | collective-permute-start | bytes 221192 | tf_op jit(solution)/shard_map/tell_planes/ppermute | solution.py:402
  8.6 1.6 copy-start
  13.8 26.5 %collective-permute-start.5 = (bf16[9,256,256]{2,1,0:T(8,128)(2,1)S(1)}, bf16[9,256,256]{2,1,0:T(8,128)(2,1)S(1)}, u32[]{:S(2)}, u32[]{:S(2)}) collective-permute-start(bf16[9,256,256]{2,1,0:T(8,128)(2,1)S(1)} %factor_step_1.3.here_ref.else_ref.rest_3_.rest_4_.rest_8_.rest_1_), channel_id=1, source_target_pairs={{0,3},{1,0},{2,1},{3,2},{4,7},{5,4},{6,5},{7,6},{8,11},{9,8},{10,9... | collective-permute-start | bytes 3538952 | tf_op jit(solution)/shard_map/factor_step_1/ppermute | solution.py:408
  14.7 28.4 %collective-permute-start.3 = (bf16[9,256,256]{2,1,0:T(8,128)(2,1)S(1)}, bf16[9,256,256]{2,1,0:T(8,128)(2,1)S(1)}, u32[]{:S(2)}, u32[]{:S(2)}) collective-permute-start(bf16[9,256,256]{2,1,0:T(8,128)(2,1)S(1)} %factor_step_1.2.else_ref.here_ref.rest_2_.rest_3_.rest_7_.rest_0_), channel_id=1, source_target_pairs={{0,1},{1,2},{2,3},{3,0},{4,5},{5,6},{6,7},{7,4},{8,9},{9,10},{10,1... | collective-permute-start | bytes 3538952 | tf_op jit(solution)/shard_map/factor_step_1/ppermute | solution.py:407
  15.9 28.1 %collective-permute-start.9 = (bf16[9,256,256]{2,1,0:T(8,128)(2,1)S(1)}, bf16[9,256,256]{2,1,0:T(8,128)(2,1)S(1)}, u32[]{:S(2)}, u32[]{:S(2)}) collective-permute-start(bf16[9,256,256]{2,1,0:T(8,128)(2,1)S(1)} %factor_step_1.3.here_ref.else_ref.rest_3_.rest_4_.rest_8_.rest_1_), channel_id=1, source_target_pairs={{0,4},{4,0},{1,5},{5,1},{2,6},{6,2},{3,7},{7,3},{8,12},{12,8},{9,1... | collective-permute-start | bytes 3538952 | tf_op jit(solution)/shard_map/factor_step_1/ppermute | solution.py:384
  15.9 27.9 %collective-permute-start.7 = (bf16[4,144,256]{2,1,0:T(8,128)(2,1)S(1)}, bf16[4,144,256]{2,1,0:T(8,128)(2,1)S(1)}, u32[]{:S(2)}, u32[]{:S(2)}) collective-permute-start(bf16[4,144,256]{2,1,0:T(8,128)(2,1)S(1)} %pad_maximum_fusion.rest_0_.rest_1_.rest_5_.own_told), channel_id=1, source_target_pairs={{0,4},{4,0},{1,5},{5,1},{2,6},{6,2},{3,7},{7,3},{8,12},{12,8},{9,1... | collective-permute-start | bytes 884744 | tf_op jit(solution)/shard_map/tell_planes/ppermute | solution.py:384
  16.5 29.3 %collective-permute-start.8 = (bf16[9,256,256]{2,1,0:T(8,128)(2,1)S(1)}, bf16[9,256,256]{2,1,0:T(8,128)(2,1)S(1)}, u32[]{:S(2)}, u32[]{:S(2)}) collective-permute-start(bf16[9,256,256]{2,1,0:T(8,128)(2,1)S(1)} %factor_step_1.2.else_ref.here_ref.rest_2_.rest_3_.rest_7_.rest_0_), channel_id=1, source_target_pairs={{0,4},{4,0},{1,5},{5,1},{2,6},{6,2},{3,7},{7,3},{8,12},{12,8},{9,1... | collective-permute-start | bytes 3538952 | tf_op jit(solution)/shard_map/factor_step_1/ppermute | solution.py:384
  41.0 25.7 %collective-permute-start.6 = (bf16[9,256,256]{2,1,0:T(8,128)(2,1)S(1)}, bf16[9,256,256]{2,1,0:T(8,128)(2,1)S(1)}, u32[]{:S(2)}, u32[]{:S(2)}) collective-permute-start(bf16[9,256,256]{2,1,0:T(8,128)(2,1)S(1)} %factor_step_2.5), channel_id=1, source_target_pairs={{0,3},{1,0},{2,1},{3,2},{4,7},{5,4},{6,5},{7,6},{8,11},{9,8},{10,9... | collective-permute-start | bytes 3538952 | tf_op jit(solution)/shard_map/factor_step_2/ppermute | solution.py:421
  43.8 26.6 %collective-permute-start.4 = (bf16[9,256,256]{2,1,0:T(8,128)(2,1)S(1)}, bf16[9,256,256]{2,1,0:T(8,128)(2,1)S(1)}, u32[]{:S(2)}, u32[]{:S(2)}) collective-permute-start(bf16[9,256,256]{2,1,0:T(8,128)(2,1)S(1)} %factor_step_2.4), channel_id=1, source_target_pairs={{0,1},{1,2},{2,3},{3,0},{4,5},{5,6},{6,7},{7,4},{8,9},{9,10},{10,1... | collective-permute-start | bytes 3538952 | tf_op jit(solution)/shard_map/factor_step_2/ppermute | solution.py:420
  43.9 22.8 %collective-permute-start.11 = (bf16[9,256,256]{2,1,0:T(8,128)(2,1)S(1)}, bf16[9,256,256]{2,1,0:T(8,128)(2,1)S(1)}, u32[]{:S(2)}, u32[]{:S(2)}) collective-permute-start(bf16[9,256,256]{2,1,0:T(8,128)(2,1)S(1)} %collective-permute-done.5.here_ref.else_ref.rest_5_.rest_6_.rest_10_.rest_3_), channel_id=1, source_target_pairs={{0,4},{4,0},{1,5},{5,1},{2,6},{6,2},{3,7},{7,3},{8,12},{12,8},{9,1... | collective-permute-start | bytes 3538952 | tf_op jit(solution)/shard_map/factor_step_2/ppermute | solution.py:384
  44.0 26.4 %collective-permute-start.10 = (bf16[9,256,256]{2,1,0:T(8,128)(2,1)S(1)}, bf16[9,256,256]{2,1,0:T(8,128)(2,1)S(1)}, u32[]{:S(2)}, u32[]{:S(2)}) collective-permute-start(bf16[9,256,256]{2,1,0:T(8,128)(2,1)S(1)} %collective-permute-done.3.else_ref.here_ref.rest_4_.rest_5_.rest_9_.rest_2_), channel_id=1, source_target_pairs={{0,4},{4,0},{1,5},{5,1},{2,6},{6,2},{3,7},{7,3},{8,12},{12,8},{9,1... | collective-permute-start | bytes 3538952 | tf_op jit(solution)/shard_map/factor_step_2/ppermute | solution.py:384
  70.4 3.8 %collective-permute-start.12 = (bf16[9,256,256]{2,1,0:T(8,128)(2,1)S(1)}, bf16[9,256,256]{2,1,0:T(8,128)(2,1)S(1)}, u32[]{:S(2)}, u32[]{:S(2)}) collective-permute-start(bf16[9,256,256]{2,1,0:T(8,128)(2,1)S(1)} %collective-permute-done.4.rest_6_.rest_7_.rest_11_.rest_4_), channel_id=1, source_target_pairs={{0,4},{4,0},{1,5},{5,1},{2,6},{6,2},{3,7},{7,3},{8,12},{12,8},{9,1... | collective-permute-start | bytes 3538952 | tf_op jit(solution)/shard_map/factor_step_2/ppermute | solution.py:384
  70.4 4.5 %collective-permute-start.13 = (bf16[9,256,256]{2,1,0:T(8,128)(2,1)S(1)}, bf16[9,256,256]{2,1,0:T(8,128)(2,1)S(1)}, u32[]{:S(2)}, u32[]{:S(2)}) collective-permute-start(bf16[9,256,256]{2,1,0:T(8,128)(2,1)S(1)} %collective-permute-done.6.rest_7_.rest_8_.rest_12_.rest_5_), channel_id=1, source_target_pairs={{0,4},{4,0},{1,5},{5,1},{2,6},{6,2},{3,7},{7,3},{8,12},{12,8},{9,1... | collective-permute-start | bytes 3538952 | tf_op jit(solution)/shard_map/factor_step_2/ppermute | solution.py:384
  70.9 30.7 %collective-permute-start.14 = (bf16[9,256,256]{2,1,0:T(8,128)(2,1)S(1)}, bf16[9,256,256]{2,1,0:T(8,128)(2,1)S(1)}, u32[]{:S(2)}, u32[]{:S(2)}) collective-permute-start(bf16[9,256,256]{2,1,0:T(8,128)(2,1)S(1)} %factor_step_2.6), channel_id=1, source_target_pairs={{0,1},{1,2},{2,3},{3,0},{4,5},{5,6},{6,7},{7,4},{8,9},{9,10},{10,1... | collective-permute-start | bytes 3538952 | tf_op jit(solution)/shard_map/factor_step_3/ppermute | solution.py:430
  70.9 30.7 %collective-permute-start.15 = (bf16[9,256,256]{2,1,0:T(8,128)(2,1)S(1)}, bf16[9,256,256]{2,1,0:T(8,128)(2,1)S(1)}, u32[]{:S(2)}, u32[]{:S(2)}) collective-permute-start(bf16[9,256,256]{2,1,0:T(8,128)(2,1)S(1)} %factor_step_2.7), channel_id=1, source_target_pairs={{0,3},{1,0},{2,1},{3,2},{4,7},{5,4},{6,5},{7,6},{8,11},{9,8},{10,9... | collective-permute-start | bytes 3538952 | tf_op jit(solution)/shard_map/factor_step_3/ppermute | solution.py:431
  101.6 2.9 %collective-permute-start.16 = (bf16[9,256,256]{2,1,0:T(8,128)(2,1)S(1)}, bf16[9,256,256]{2,1,0:T(8,128)(2,1)S(1)}, u32[]{:S(2)}, u32[]{:S(2)}) collective-permute-start(bf16[9,256,256]{2,1,0:T(8,128)(2,1)S(1)} %collective-permute-done.14.rest_9_.rest_13_.rest_4_.rest_6_), channel_id=1, source_target_pairs={{0,4},{4,0},{1,5},{5,1},{2,6},{6,2},{3,7},{7,3},{8,12},{12,8},{9,1... | collective-permute-start | bytes 3538952 | tf_op jit(solution)/shard_map/factor_step_3/ppermute | solution.py:384
  101.7 4.5 %collective-permute-start.17 = (bf16[9,256,256]{2,1,0:T(8,128)(2,1)S(1)}, bf16[9,256,256]{2,1,0:T(8,128)(2,1)S(1)}, u32[]{:S(2)}, u32[]{:S(2)}) collective-permute-start(bf16[9,256,256]{2,1,0:T(8,128)(2,1)S(1)} %collective-permute-done.15.rest_10_.rest_14_.rest_5_.rest_7_), channel_id=1, source_target_pairs={{0,4},{4,0},{1,5},{5,1},{2,6},{6,2},{3,7},{7,3},{8,12},{12,8},{9,1... | collective-permute-start | bytes 3538952 | tf_op jit(solution)/shard_map/factor_step_3/ppermute | solution.py:384
  215.7 1.9 collective-permute-start.18

commit v9 on v8

--- a/solution.py
+++ b/solution.py
@@ -364,7 +364,7 @@
     for k, out_ref in enumerate((forward_ref, result_ref)):
         for j in range(2):
             own = jnp.concatenate([own_ref[z, k, 0, j] for z in range(4)], axis=0).astype(F32)
-            other = jnp.concatenate([other_ref[z, k, 1, j] for z in range(4)], axis=0).astype(F32)
+            other = jnp.concatenate([other_ref[z, k, j] for z in range(4)], axis=0).astype(F32)
             low, high = jnp.where(core == 0, own, other), jnp.where(core == 0, other, own)
             out_ref[j] = jnp.transpose(jnp.concatenate([low, high], axis=0))
 
@@ -460,7 +460,7 @@
     with jax.named_scope("to_planes"):
         fx = jnp.stack([jnp.stack(solved), jnp.stack(result)], axis=1).reshape(4, 2, 2, 2, COLS, WIDTH)
         fx = lax.all_to_all(fx, "z", 0, 0, tiled=True)
-        forward_out, result_out = last_step(core1, fx, swap(fx))
+        forward_out, result_out = last_step(core1, fx, swap(fx[:, :, 1]))
     shape = (1, 2, 1, WIDTH, WIDTH)
     return forward_out.reshape(shape), result_out.reshape(shape)
 

time: 220 us -> 220 us (level)
  no operation moved by 1% of the time
where the time goes in v9:
time: 220 us; the launch traced here: 218 us
  blocking collectives  122 us (55%)
  waiting for transfers between devices  56.8 us (26%)
  Pallas kernels  19.9 us (9%)
  starting transfers between devices  15.4 us (7%)
  local copies, waits for them, and re-layouts  3.44 us (2%)
    all_to_all x6, blocking collectives, exchange(): lax.all_to_all(value.reshape(CHIPS, 4, COLS, WIDTH), ('y', 'x'), 0, 0, ti...  110 us
    ppermute x1, waiting for transfers between devices, on_device(): down_1 = lax.ppermute(own_b, 'z', DOWN)  23.8 us
    ppermute x1, waiting for transfers between devices, on_device(): down_2 = lax.ppermute(choose(plane1, 3, down_1, own_a), 'z', DOWN)  20.8 us
    all_to_all x1, blocking collectives, on_device(): fx = lax.all_to_all(fx, 'z', 0, 0, tiled=True)  12.2 us
    pallas_call x4, Pallas kernels, forward_part(): pl.pallas_call(functools.partial(forward_kernel, level, part), in_specs=[...  9.05 us
    ppermute x3, starting transfers between devices, on_device(): lax.ppermute(message[k], 'z', [(z, (z + k) % 4) for z in range(4)])  5.45 us
    ppermute x10, waiting for transfers between devices, swap(): return lax.ppermute(value, 'c', [(0, 1), (1, 0)])  5.43 us
    pallas_call x3, Pallas kernels, backward_level(): pl.pallas_call(functools.partial(backward_kernel, level), in_specs=[SMEM,...  5.22 us
  transfers between devices with their start and end apart: 19, of which 9 were waited for; matrix products, arithmetic and copies ran while one was open for 0% of the time, Pallas kernels for 3%

profile of v9, /device:TPU:0, one launch (start us, length us, event | category | flops | bytes accessed | tf_op | source)
XLA Modules:
  0.0 218.4 jit_solution(18362821499920414063)
XLA Ops:
  0.7 1.1 copy-done.2
  1.7 0.7 copy-done.3
  2.4 0.7 tell_planes.1
  3.1 4.2 %collective-permute-start.2 = (bf16[144,256]{1,0:T(8,128)(2,1)S(1)}, bf16[144,256]{1,0:T(8,128)(2,1)S(1)}, u32[]{:S(2)}, u32[]{:S(2)}) collective-permute-start(bf16[144,256]{1,0:T(8,128)(2,1)S(1)} %get-tuple-element.90), channel_id=1, source_target_pairs={{0,3},{1,0},{2,1},{3,2},{4,7},{5,4},{6,5},{7,6},{8,11},{9,8},{10,9... | collective-permute-start | bytes 221192 | tf_op jit(solution)/shard_map/tell_planes/ppermute | solution.py:402
  7.3 1.3 collective-permute-start
  8.6 1.6 copy-done
  10.2 0.3 factor_step_1.3.here_ref.else_ref.rest_3_.rest_4_.rest_8_.rest_1_
  10.4 0.3 factor_step_1.2.else_ref.here_ref.rest_2_.rest_3_.rest_7_.rest_0_
  10.8 2.6 %collective-permute-done.1 = bf16[144,256]{1,0:T(8,128)(2,1)S(1)} collective-permute-done((bf16[144,256]{1,0:T(8,128)(2,1)S(1)}, bf16[144,256]{1,0:T(8,128)(2,1)S(1)}, u32[]{:S(2)}, u32[]{:S(2)}) %collective-permute-start.1) | collective-permute-done | bytes 73760 | tf_op jit(solution)/shard_map/tell_planes/ppermute | solution.py:402
  13.4 0.4 collective-permute-done
  13.8 0.9 collective-permute-start.5
  14.7 1.2 collective-permute-start.3
  15.9 0.6 collective-permute-start.7
  16.5 0.1 collective-permute-start.8
  16.6 23.8 %collective-permute-done.5.here_ref.else_ref.rest_5_.rest_6_.rest_10_.rest_3_ = bf16[9,256,256]{2,1,0:T(8,128)(2,1)S(1)} collective-permute-done((bf16[9,256,256]{2,1,0:T(8,128)(2,1)S(1)}, bf16[9,256,256]{2,1,0:T(8,128)(2,1)S(1)}, u32[]{:S(2)}, u32[]{:S(2)}) %collective-permute-start.5) | collective-permute-done | bytes 1179680 | tf_op jit(solution)/shard_map/factor_step_1/ppermute | solution.py:408
  40.4 0.6 factor_step_2.5
  41.0 2.1 collective-permute-start.6
  43.1 0.6 factor_step_2.4
  43.9 0.1 collective-permute-start.11
  44.0 0.5 collective-permute-start.10
  44.5 0.6 factor_step_2.7
  45.2 0.6 factor_step_2.6
  45.8 20.8 %collective-permute-done.6.rest_7_.rest_8_.rest_12_.rest_5_ = bf16[9,256,256]{2,1,0:T(8,128)(2,1)S(1)} collective-permute-done((bf16[9,256,256]{2,1,0:T(8,128)(2,1)S(1)}, bf16[9,256,256]{2,1,0:T(8,128)(2,1)S(1)}, u32[]{:S(2)}, u32[]{:S(2)}) %collective-permute-start.6) | collective-permute-done | bytes 1179680 | tf_op jit(solution)/shard_map/factor_step_2/ppermute | solution.py:421
  66.7 3.7 %collective-permute-done.4.rest_6_.rest_7_.rest_11_.rest_4_ = bf16[9,256,256]{2,1,0:T(8,128)(2,1)S(1)} collective-permute-done((bf16[9,256,256]{2,1,0:T(8,128)(2,1)S(1)}, bf16[9,256,256]{2,1,0:T(8,128)(2,1)S(1)}, u32[]{:S(2)}, u32[]{:S(2)}) %collective-permute-start.4) | collective-permute-done | bytes 1179680 | tf_op jit(solution)/shard_map/factor_step_2/ppermute | solution.py:420
  70.4 0.5 collective-permute-start.13
  70.9 3.2 %collective-permute-start.15 = (bf16[9,256,256]{2,1,0:T(8,128)(2,1)S(1)}, bf16[9,256,256]{2,1,0:T(8,128)(2,1)S(1)}, u32[]{:S(2)}, u32[]{:S(2)}) collective-permute-start(bf16[9,256,256]{2,1,0:T(8,128)(2,1)S(1)} %factor_step_2.7), channel_id=1, source_target_pairs={{0,3},{1,0},{2,1},{3,2},{4,7},{5,4},{6,5},{7,6},{8,11},{9,8},{10,9... | collective-permute-start | bytes 3538952 | tf_op jit(solution)/shard_map/factor_step_3/ppermute | solution.py:431
  74.1 0.8 collective-permute-done.13.rest_13_.rest_16_.rest_20_.rest_11_
  74.9 2.2 %forward_0.1 = (f32[4,32,256]{2,1,0:T(8,128)S(1)}, bf16[4,32,256]{2,1,0:T(8,128)(2,1)S(1)}, bf16[64,32,256]{2,1,0:T(8,128)(2,1)S(1)}) custom-call(s32[1]{0:T(128)} %bitcast.core_ref, s32[1]{0:T(128)} %bitcast.1.plane_ref, s32[4,4,8]{2,1,0:T(4,128)S(1)} %fusion.5.at_ref, bf16[4,144,256]{2,1,0:T(8,128)(2,1)S(1)} %pad_maximum_fusion.rest_0_.rest_1_.rest_5_.own_told, ...), custom_call_target="tpu_custom_call" | custom-call | flops 150994944 | bytes 6291456 | tf_op jit(solution)/shard_map/forward_0/pallas_call | solution.py:269
  77.1 24.3 %all_to_all.35.got_ref = bf16[16,4,32,256]{3,2,1,0:T(8,128)(2,1)S(1)} all-to-all(bf16[16,4,32,256]{3,2,1,0:T(8,128)(2,1)S(1)} %bitcast.67), channel_id=1, replica_groups=mesh['x'=4,'y'=4,'c'=2,'z'=4] {'y','x'}, dimensions={0} | all-to-all | bytes 2097152 | tf_op jit(solution)/shard_map/forward_0/all_to_all | solution.py:388
  101.4 0.1 factor_step_3.1.rest_0_
  101.7 0.5 collective-permute-start.17
  102.2 0.9 forward_1.2
  103.1 1.5 collective-permute-done.16.rest_21_.rest_17_.rest_10_.rest_14_
  104.5 1.7 collective-permute-done.17.rest_22_.rest_18_.rest_11_.rest_15_
  106.2 3.6 %forward_1.3 = (f32[4,32,256]{2,1,0:T(8,128)S(1)}, bf16[4,32,256]{2,1,0:T(8,128)(2,1)S(1)}, bf16[64,32,256]{2,1,0:T(8,128)(2,1)S(1)}) custom-call(s32[1]{0:T(128)} %bitcast.core_ref, s32[1]{0:T(128)} %bitcast.1.plane_ref, s32[4,4,8]{2,1,0:T(4,128)S(1)} %fusion.5.at_ref, f32[4,32,256]{2,1,0:T(8,128)S(1)} %factor_step_3.1.rest_0_, ...), custom_call_target="tpu_custom_call", output_to_operand_aliasing={{2}: (6, {})} | custom-call | flops 150994944 | bytes 6291456 | tf_op jit(solution)/shard_map/forward_1/pallas_call | solution.py:269
  109.8 20.5 %all_to_all.36.rest_0_ = bf16[16,4,32,256]{3,2,1,0:T(8,128)(2,1)S(1)} all-to-all(bf16[16,4,32,256]{3,2,1,0:T(8,128)(2,1)S(1)} %bitcast.61), channel_id=1, replica_groups=mesh['x'=4,'y'=4,'c'=2,'z'=4] {'y','x'}, dimensions={0} | all-to-all | bytes 2097152 | tf_op jit(solution)/shard_map/forward_1/all_to_all | solution.py:388
  130.2 2.4 %forward_2.1 = (f32[4,32,256]{2,1,0:T(8,128)S(1)}, bf16[4,32,256]{2,1,0:T(8,128)(2,1)S(1)}, bf16[64,32,256]{2,1,0:T(8,128)(2,1)S(1)}) custom-call(s32[1]{0:T(128)} %bitcast.core_ref, s32[1]{0:T(128)} %bitcast.1.plane_ref, s32[4,4,8]{2,1,0:T(4,128)S(1)} %fusion.5.at_ref, bf16[16,4,32,256]{3,2,1,0:T(8,128)(2,1)S(1)} %all_to_all.36.rest_0_, ...), custom_call_target="tpu_custom_call" | custom-call | flops 150994944 | bytes 6291456 | tf_op jit(solution)/shard_map/forward_2/pallas_call | solution.py:269
  132.6 17.0 %all_to_all.37.got_ref = bf16[16,4,32,256]{3,2,1,0:T(8,128)(2,1)S(1)} all-to-all(bf16[16,4,32,256]{3,2,1,0:T(8,128)(2,1)S(1)} %bitcast.66), channel_id=1, replica_groups=mesh['x'=4,'y'=4,'c'=2,'z'=4] {'y','x'}, dimensions={0} | all-to-all | bytes 2097152 | tf_op jit(solution)/shard_map/forward_2/all_to_all | solution.py:388
  149.6 0.6 top.1
  150.2 16.2 %all_to_all.38 = bf16[16,4,32,256]{3,2,1,0:T(8,128)(2,1)S(1)} all-to-all(bf16[16,4,32,256]{3,2,1,0:T(8,128)(2,1)S(1)} %get-tuple-element.75), channel_id=1, replica_groups=mesh['x'=4,'y'=4,'c'=2,'z'=4] {'y','x'}, dimensions={0} | all-to-all | bytes 2097152 | tf_op jit(solution)/shard_map/backward_2/all_to_all | solution.py:388
  166.4 1.7 backward_2.1
  168.1 15.9 %all_to_all.39 = bf16[16,4,32,256]{3,2,1,0:T(8,128)(2,1)S(1)} all-to-all(bf16[16,4,32,256]{3,2,1,0:T(8,128)(2,1)S(1)} %get-tuple-element.77), channel_id=1, replica_groups=mesh['x'=4,'y'=4,'c'=2,'z'=4] {'y','x'}, dimensions={0} | all-to-all | bytes 2097152 | tf_op jit(solution)/shard_map/backward_1/all_to_all | solution.py:388
  183.9 1.9 backward_1.1
  185.9 15.9 %all_to_all.40 = bf16[16,4,32,256]{3,2,1,0:T(8,128)(2,1)S(1)} all-to-all(bf16[16,4,32,256]{3,2,1,0:T(8,128)(2,1)S(1)} %get-tuple-element.79), channel_id=1, replica_groups=mesh['x'=4,'y'=4,'c'=2,'z'=4] {'y','x'}, dimensions={0} | all-to-all | bytes 2097152 | tf_op jit(solution)/shard_map/backward_0/all_to_all | solution.py:388
  201.8 1.6 backward_0.1
  203.5 12.2 %all_to_all.41 = bf16[4,2,2,2,32,256]{5,4,3,1,2,0:T(8,128)(2,1)S(1)} all-to-all(bf16[4,2,2,2,32,256]{5,4,3,1,2,0:T(8,128)(2,1)S(1)} %maximum_maximum_fusion), channel_id=1, replica_groups=mesh['x'=4,'y'=4,'c'=2,'z'=4] {'z'}, dimensions={0} | all-to-all | bytes 1048576 | tf_op jit(solution)/shard_map/to_planes/all_to_all | solution.py:462
  215.8 1.5 collective-permute-done.18.other_ref
  217.3 1.1 to_planes.1
  (30 shorter events, 0.6 us)
Async XLA Ops:
  0.6 8.0 %copy-start.1 = (bf16[1,2,1,256,256]{4,3,2,1,0:T(8,128)(2,1)S(1)}, bf16[1,2,1,256,256]{4,3,2,1,0:T(8,128)(2,1)}, u32[]{:S(2)}) copy-start(bf16[1,2,1,256,256]{4,3,2,1,0:T(8,128)(2,1)} %param.5) | copy-start | bytes 786436
  0.6 1.1 copy-start.2
  1.7 0.7 copy-start.3
  3.1 7.6 %collective-permute-start.2 = (bf16[144,256]{1,0:T(8,128)(2,1)S(1)}, bf16[144,256]{1,0:T(8,128)(2,1)S(1)}, u32[]{:S(2)}, u32[]{:S(2)}) collective-permute-start(bf16[144,256]{1,0:T(8,128)(2,1)S(1)} %get-tuple-element.90), channel_id=1, source_target_pairs={{0,3},{1,0},{2,1},{3,2},{4,7},{5,4},{6,5},{7,6},{8,11},{9,8},{10,9... | collective-permute-start | bytes 221192 | tf_op jit(solution)/shard_map/tell_planes/ppermute | solution.py:402
  7.3 6.1 %collective-permute-start.1 = (bf16[144,256]{1,0:T(8,128)(2,1)S(1)}, bf16[144,256]{1,0:T(8,128)(2,1)S(1)}, u32[]{:S(2)}, u32[]{:S(2)}) collective-permute-start(bf16[144,256]{1,0:T(8,128)(2,1)S(1)} %get-tuple-element.91), channel_id=1, source_target_pairs={{0,2},{1,3},{2,0},{3,1},{4,6},{5,7},{6,4},{7,5},{8,10},{9,11},{10,... | collective-permute-start | bytes 221192 | tf_op jit(solution)/shard_map/tell_planes/ppermute | solution.py:402
  7.3 6.5 %collective-permute-start = (bf16[144,256]{1,0:T(8,128)(2,1)S(1)}, bf16[144,256]{1,0:T(8,128)(2,1)S(1)}, u32[]{:S(2)}, u32[]{:S(2)}) collective-permute-start(bf16[144,256]{1,0:T(8,128)(2,1)S(1)} %get-tuple-element.92), channel_id=1, source_target_pairs={{0,1},{1,2},{2,3},{3,0},{4,5},{5,6},{6,7},{7,4},{8,9},{9,10},{10,1... | collective-permute-start | bytes 221192 | tf_op jit(solution)/shard_map/tell_planes/ppermute | solution.py:402
  8.6 1.6 copy-start
  13.8 26.5 %collective-permute-start.5 = (bf16[9,256,256]{2,1,0:T(8,128)(2,1)S(1)}, bf16[9,256,256]{2,1,0:T(8,128)(2,1)S(1)}, u32[]{:S(2)}, u32[]{:S(2)}) collective-permute-start(bf16[9,256,256]{2,1,0:T(8,128)(2,1)S(1)} %factor_step_1.3.here_ref.else_ref.rest_3_.rest_4_.rest_8_.rest_1_), channel_id=1, source_target_pairs={{0,3},{1,0},{2,1},{3,2},{4,7},{5,4},{6,5},{7,6},{8,11},{9,8},{10,9... | collective-permute-start | bytes 3538952 | tf_op jit(solution)/shard_map/factor_step_1/ppermute | solution.py:408
  14.7 28.4 %collective-permute-start.3 = (bf16[9,256,256]{2,1,0:T(8,128)(2,1)S(1)}, bf16[9,256,256]{2,1,0:T(8,128)(2,1)S(1)}, u32[]{:S(2)}, u32[]{:S(2)}) collective-permute-start(bf16[9,256,256]{2,1,0:T(8,128)(2,1)S(1)} %factor_step_1.2.else_ref.here_ref.rest_2_.rest_3_.rest_7_.rest_0_), channel_id=1, source_target_pairs={{0,1},{1,2},{2,3},{3,0},{4,5},{5,6},{6,7},{7,4},{8,9},{9,10},{10,1... | collective-permute-start | bytes 3538952 | tf_op jit(solution)/shard_map/factor_step_1/ppermute | solution.py:407
  15.9 28.1 %collective-permute-start.9 = (bf16[9,256,256]{2,1,0:T(8,128)(2,1)S(1)}, bf16[9,256,256]{2,1,0:T(8,128)(2,1)S(1)}, u32[]{:S(2)}, u32[]{:S(2)}) collective-permute-start(bf16[9,256,256]{2,1,0:T(8,128)(2,1)S(1)} %factor_step_1.3.here_ref.else_ref.rest_3_.rest_4_.rest_8_.rest_1_), channel_id=1, source_target_pairs={{0,4},{4,0},{1,5},{5,1},{2,6},{6,2},{3,7},{7,3},{8,12},{12,8},{9,1... | collective-permute-start | bytes 3538952 | tf_op jit(solution)/shard_map/factor_step_1/ppermute | solution.py:384
  15.9 27.9 %collective-permute-start.7 = (bf16[4,144,256]{2,1,0:T(8,128)(2,1)S(1)}, bf16[4,144,256]{2,1,0:T(8,128)(2,1)S(1)}, u32[]{:S(2)}, u32[]{:S(2)}) collective-permute-start(bf16[4,144,256]{2,1,0:T(8,128)(2,1)S(1)} %pad_maximum_fusion.rest_0_.rest_1_.rest_5_.own_told), channel_id=1, source_target_pairs={{0,4},{4,0},{1,5},{5,1},{2,6},{6,2},{3,7},{7,3},{8,12},{12,8},{9,1... | collective-permute-start | bytes 884744 | tf_op jit(solution)/shard_map/tell_planes/ppermute | solution.py:384
  16.5 29.3 %collective-permute-start.8 = (bf16[9,256,256]{2,1,0:T(8,128)(2,1)S(1)}, bf16[9,256,256]{2,1,0:T(8,128)(2,1)S(1)}, u32[]{:S(2)}, u32[]{:S(2)}) collective-permute-start(bf16[9,256,256]{2,1,0:T(8,128)(2,1)S(1)} %factor_step_1.2.else_ref.here_ref.rest_2_.rest_3_.rest_7_.rest_0_), channel_id=1, source_target_pairs={{0,4},{4,0},{1,5},{5,1},{2,6},{6,2},{3,7},{7,3},{8,12},{12,8},{9,1... | collective-permute-start | bytes 3538952 | tf_op jit(solution)/shard_map/factor_step_1/ppermute | solution.py:384
  41.0 25.7 %collective-permute-start.6 = (bf16[9,256,256]{2,1,0:T(8,128)(2,1)S(1)}, bf16[9,256,256]{2,1,0:T(8,128)(2,1)S(1)}, u32[]{:S(2)}, u32[]{:S(2)}) collective-permute-start(bf16[9,256,256]{2,1,0:T(8,128)(2,1)S(1)} %factor_step_2.5), channel_id=1, source_target_pairs={{0,3},{1,0},{2,1},{3,2},{4,7},{5,4},{6,5},{7,6},{8,11},{9,8},{10,9... | collective-permute-start | bytes 3538952 | tf_op jit(solution)/shard_map/factor_step_2/ppermute | solution.py:421
  43.8 26.6 %collective-permute-start.4 = (bf16[9,256,256]{2,1,0:T(8,128)(2,1)S(1)}, bf16[9,256,256]{2,1,0:T(8,128)(2,1)S(1)}, u32[]{:S(2)}, u32[]{:S(2)}) collective-permute-start(bf16[9,256,256]{2,1,0:T(8,128)(2,1)S(1)} %factor_step_2.4), channel_id=1, source_target_pairs={{0,1},{1,2},{2,3},{3,0},{4,5},{5,6},{6,7},{7,4},{8,9},{9,10},{10,1... | collective-permute-start | bytes 3538952 | tf_op jit(solution)/shard_map/factor_step_2/ppermute | solution.py:420
  43.9 22.8 %collective-permute-start.11 = (bf16[9,256,256]{2,1,0:T(8,128)(2,1)S(1)}, bf16[9,256,256]{2,1,0:T(8,128)(2,1)S(1)}, u32[]{:S(2)}, u32[]{:S(2)}) collective-permute-start(bf16[9,256,256]{2,1,0:T(8,128)(2,1)S(1)} %collective-permute-done.5.here_ref.else_ref.rest_5_.rest_6_.rest_10_.rest_3_), channel_id=1, source_target_pairs={{0,4},{4,0},{1,5},{5,1},{2,6},{6,2},{3,7},{7,3},{8,12},{12,8},{9,1... | collective-permute-start | bytes 3538952 | tf_op jit(solution)/shard_map/factor_step_2/ppermute | solution.py:384
  44.0 26.4 %collective-permute-start.10 = (bf16[9,256,256]{2,1,0:T(8,128)(2,1)S(1)}, bf16[9,256,256]{2,1,0:T(8,128)(2,1)S(1)}, u32[]{:S(2)}, u32[]{:S(2)}) collective-permute-start(bf16[9,256,256]{2,1,0:T(8,128)(2,1)S(1)} %collective-permute-done.3.else_ref.here_ref.rest_4_.rest_5_.rest_9_.rest_2_), channel_id=1, source_target_pairs={{0,4},{4,0},{1,5},{5,1},{2,6},{6,2},{3,7},{7,3},{8,12},{12,8},{9,1... | collective-permute-start | bytes 3538952 | tf_op jit(solution)/shard_map/factor_step_2/ppermute | solution.py:384
  70.4 3.8 %collective-permute-start.12 = (bf16[9,256,256]{2,1,0:T(8,128)(2,1)S(1)}, bf16[9,256,256]{2,1,0:T(8,128)(2,1)S(1)}, u32[]{:S(2)}, u32[]{:S(2)}) collective-permute-start(bf16[9,256,256]{2,1,0:T(8,128)(2,1)S(1)} %collective-permute-done.4.rest_6_.rest_7_.rest_11_.rest_4_), channel_id=1, source_target_pairs={{0,4},{4,0},{1,5},{5,1},{2,6},{6,2},{3,7},{7,3},{8,12},{12,8},{9,1... | collective-permute-start | bytes 3538952 | tf_op jit(solution)/shard_map/factor_step_2/ppermute | solution.py:384
  70.4 4.5 %collective-permute-start.13 = (bf16[9,256,256]{2,1,0:T(8,128)(2,1)S(1)}, bf16[9,256,256]{2,1,0:T(8,128)(2,1)S(1)}, u32[]{:S(2)}, u32[]{:S(2)}) collective-permute-start(bf16[9,256,256]{2,1,0:T(8,128)(2,1)S(1)} %collective-permute-done.6.rest_7_.rest_8_.rest_12_.rest_5_), channel_id=1, source_target_pairs={{0,4},{4,0},{1,5},{5,1},{2,6},{6,2},{3,7},{7,3},{8,12},{12,8},{9,1... | collective-permute-start | bytes 3538952 | tf_op jit(solution)/shard_map/factor_step_2/ppermute | solution.py:384
  70.9 30.7 %collective-permute-start.14 = (bf16[9,256,256]{2,1,0:T(8,128)(2,1)S(1)}, bf16[9,256,256]{2,1,0:T(8,128)(2,1)S(1)}, u32[]{:S(2)}, u32[]{:S(2)}) collective-permute-start(bf16[9,256,256]{2,1,0:T(8,128)(2,1)S(1)} %factor_step_2.6), channel_id=1, source_target_pairs={{0,1},{1,2},{2,3},{3,0},{4,5},{5,6},{6,7},{7,4},{8,9},{9,10},{10,1... | collective-permute-start | bytes 3538952 | tf_op jit(solution)/shard_map/factor_step_3/ppermute | solution.py:430
  70.9 30.7 %collective-permute-start.15 = (bf16[9,256,256]{2,1,0:T(8,128)(2,1)S(1)}, bf16[9,256,256]{2,1,0:T(8,128)(2,1)S(1)}, u32[]{:S(2)}, u32[]{:S(2)}) collective-permute-start(bf16[9,256,256]{2,1,0:T(8,128)(2,1)S(1)} %factor_step_2.7), channel_id=1, source_target_pairs={{0,3},{1,0},{2,1},{3,2},{4,7},{5,4},{6,5},{7,6},{8,11},{9,8},{10,9... | collective-permute-start | bytes 3538952 | tf_op jit(solution)/shard_map/factor_step_3/ppermute | solution.py:431
  101.6 2.9 %collective-permute-start.16 = (bf16[9,256,256]{2,1,0:T(8,128)(2,1)S(1)}, bf16[9,256,256]{2,1,0:T(8,128)(2,1)S(1)}, u32[]{:S(2)}, u32[]{:S(2)}) collective-permute-start(bf16[9,256,256]{2,1,0:T(8,128)(2,1)S(1)} %collective-permute-done.14.rest_9_.rest_13_.rest_4_.rest_6_), channel_id=1, source_target_pairs={{0,4},{4,0},{1,5},{5,1},{2,6},{6,2},{3,7},{7,3},{8,12},{12,8},{9,1... | collective-permute-start | bytes 3538952 | tf_op jit(solution)/shard_map/factor_step_3/ppermute | solution.py:384
  101.7 4.5 %collective-permute-start.17 = (bf16[9,256,256]{2,1,0:T(8,128)(2,1)S(1)}, bf16[9,256,256]{2,1,0:T(8,128)(2,1)S(1)}, u32[]{:S(2)}, u32[]{:S(2)}) collective-permute-start(bf16[9,256,256]{2,1,0:T(8,128)(2,1)S(1)} %collective-permute-done.15.rest_10_.rest_14_.rest_5_.rest_7_), channel_id=1, source_target_pairs={{0,4},{4,0},{1,5},{5,1},{2,6},{6,2},{3,7},{7,3},{8,12},{12,8},{9,1... | collective-permute-start | bytes 3538952 | tf_op jit(solution)/shard_map/factor_step_3/ppermute | solution.py:384
  215.7 1.6 collective-permute-start.18

commit v10 on v8

--- a/solution.py
+++ b/solution.py
@@ -226,9 +226,9 @@
                 copy(n, z).start()
 
         on_plane(plane_ref[0], start)
-        acc_ref[...] = jnp.zeros_like(acc_ref)
         for n in range(4):
             copy(n, 0).wait()
+        acc_ref[...] = jnp.zeros_like(acc_ref)
         add((0, 1, 2, 3), 0, lambda n, z: buf.at[n])
         share_ref[...] = acc_ref[...].astype(BF)
 

time: 220 us -> 220 us (level)
  no operation moved by 1% of the time
where the time goes in v10:
time: 220 us; the launch traced here: 219 us
  blocking collectives  122 us (55%)
  waiting for transfers between devices  57.3 us (26%)
  Pallas kernels  19.8 us (9%)
  starting transfers between devices  15.3 us (7%)
  local copies, waits for them, and re-layouts  3.38 us (2%)
    all_to_all x6, blocking collectives, exchange(): lax.all_to_all(value.reshape(CHIPS, 4, COLS, WIDTH), ('y', 'x'), 0, 0, ti...  110 us
    ppermute x1, waiting for transfers between devices, on_device(): down_1 = lax.ppermute(own_b, 'z', DOWN)  23.8 us
    ppermute x1, waiting for transfers between devices, on_device(): down_2 = lax.ppermute(choose(plane1, 3, down_1, own_a), 'z', DOWN)  20.8 us
    all_to_all x1, blocking collectives, on_device(): fx = lax.all_to_all(fx, 'z', 0, 0, tiled=True)  12.2 us
    pallas_call x4, Pallas kernels, forward_part(): pl.pallas_call(functools.partial(forward_kernel, level, part), in_specs=[...  8.94 us
    ppermute x10, waiting for transfers between devices, swap(): return lax.ppermute(value, 'c', [(0, 1), (1, 0)])  5.87 us
    ppermute x3, starting transfers between devices, on_device(): lax.ppermute(message[k], 'z', [(z, (z + k) % 4) for z in range(4)])  5.45 us
    pallas_call x3, Pallas kernels, backward_level(): pl.pallas_call(functools.partial(backward_kernel, level), in_specs=[SMEM,...  5.22 us
  transfers between devices with their start and end apart: 19, of which 9 were waited for; matrix products, arithmetic and copies ran while one was open for 0% of the time, Pallas kernels for 3%

profile of v10, /device:TPU:0, one launch (start us, length us, event | category | flops | bytes accessed | tf_op | source)
XLA Modules:
  0.0 218.9 jit_solution(14210229589635748459)
XLA Ops:
  0.7 1.1 copy-done.2
  1.7 0.7 copy-done.3
  2.4 0.7 tell_planes.1
  3.1 4.2 %collective-permute-start.2 = (bf16[144,256]{1,0:T(8,128)(2,1)S(1)}, bf16[144,256]{1,0:T(8,128)(2,1)S(1)}, u32[]{:S(2)}, u32[]{:S(2)}) collective-permute-start(bf16[144,256]{1,0:T(8,128)(2,1)S(1)} %get-tuple-element.88), channel_id=1, source_target_pairs={{0,3},{1,0},{2,1},{3,2},{4,7},{5,4},{6,5},{7,6},{8,11},{9,8},{10,9... | collective-permute-start | bytes 221192 | tf_op jit(solution)/shard_map/tell_planes/ppermute | solution.py:402
  7.3 1.3 collective-permute-start
  8.6 1.6 copy-done
  10.2 0.3 factor_step_1.3.here_ref.else_ref.rest_3_.rest_4_.rest_8_.rest_1_
  10.4 0.3 factor_step_1.2.else_ref.here_ref.rest_2_.rest_3_.rest_7_.rest_0_
  10.8 2.6 %collective-permute-done.1 = bf16[144,256]{1,0:T(8,128)(2,1)S(1)} collective-permute-done((bf16[144,256]{1,0:T(8,128)(2,1)S(1)}, bf16[144,256]{1,0:T(8,128)(2,1)S(1)}, u32[]{:S(2)}, u32[]{:S(2)}) %collective-permute-start.1) | collective-permute-done | bytes 73760 | tf_op jit(solution)/shard_map/tell_planes/ppermute | solution.py:402
  13.4 0.4 collective-permute-done
  13.8 0.9 collective-permute-start.5
  14.7 1.2 collective-permute-start.3
  15.9 0.6 collective-permute-start.7
  16.5 0.1 collective-permute-start.8
  16.6 23.8 %collective-permute-done.5.here_ref.else_ref.rest_5_.rest_6_.rest_10_.rest_3_ = bf16[9,256,256]{2,1,0:T(8,128)(2,1)S(1)} collective-permute-done((bf16[9,256,256]{2,1,0:T(8,128)(2,1)S(1)}, bf16[9,256,256]{2,1,0:T(8,128)(2,1)S(1)}, u32[]{:S(2)}, u32[]{:S(2)}) %collective-permute-start.5) | collective-permute-done | bytes 1179680 | tf_op jit(solution)/shard_map/factor_step_1/ppermute | solution.py:408
  40.4 0.6 factor_step_2.5
  41.0 2.1 collective-permute-start.6
  43.1 0.6 factor_step_2.4
  43.9 0.1 collective-permute-start.11
  44.0 0.5 collective-permute-start.10
  44.5 0.6 factor_step_2.7
  45.2 0.6 factor_step_2.6
  45.8 20.8 %collective-permute-done.6.rest_7_.rest_8_.rest_12_.rest_5_ = bf16[9,256,256]{2,1,0:T(8,128)(2,1)S(1)} collective-permute-done((bf16[9,256,256]{2,1,0:T(8,128)(2,1)S(1)}, bf16[9,256,256]{2,1,0:T(8,128)(2,1)S(1)}, u32[]{:S(2)}, u32[]{:S(2)}) %collective-permute-start.6) | collective-permute-done | bytes 1179680 | tf_op jit(solution)/shard_map/factor_step_2/ppermute | solution.py:421
  66.7 3.7 %collective-permute-done.4.rest_6_.rest_7_.rest_11_.rest_4_ = bf16[9,256,256]{2,1,0:T(8,128)(2,1)S(1)} collective-permute-done((bf16[9,256,256]{2,1,0:T(8,128)(2,1)S(1)}, bf16[9,256,256]{2,1,0:T(8,128)(2,1)S(1)}, u32[]{:S(2)}, u32[]{:S(2)}) %collective-permute-start.4) | collective-permute-done | bytes 1179680 | tf_op jit(solution)/shard_map/factor_step_2/ppermute | solution.py:420
  70.4 0.5 collective-permute-start.13
  70.9 3.2 %collective-permute-start.15 = (bf16[9,256,256]{2,1,0:T(8,128)(2,1)S(1)}, bf16[9,256,256]{2,1,0:T(8,128)(2,1)S(1)}, u32[]{:S(2)}, u32[]{:S(2)}) collective-permute-start(bf16[9,256,256]{2,1,0:T(8,128)(2,1)S(1)} %factor_step_2.7), channel_id=1, source_target_pairs={{0,3},{1,0},{2,1},{3,2},{4,7},{5,4},{6,5},{7,6},{8,11},{9,8},{10,9... | collective-permute-start | bytes 3538952 | tf_op jit(solution)/shard_map/factor_step_3/ppermute | solution.py:431
  74.1 0.8 collective-permute-done.13.rest_13_.rest_16_.rest_20_.rest_11_
  74.9 2.2 %forward_0.1 = (f32[4,32,256]{2,1,0:T(8,128)S(1)}, bf16[4,32,256]{2,1,0:T(8,128)(2,1)S(1)}, bf16[64,32,256]{2,1,0:T(8,128)(2,1)S(1)}) custom-call(s32[1]{0:T(128)} %bitcast.core_ref, s32[1]{0:T(128)} %bitcast.1.plane_ref, s32[4,4,8]{2,1,0:T(4,128)S(1)} %fusion.5.at_ref, bf16[4,144,256]{2,1,0:T(8,128)(2,1)S(1)} %pad_maximum_fusion.rest_0_.rest_1_.rest_5_.own_told, ...), custom_call_target="tpu_custom_call" | custom-call | flops 150994944 | bytes 6291456 | tf_op jit(solution)/shard_map/forward_0/pallas_call | solution.py:269
  77.2 24.3 %all_to_all.35.got_ref = bf16[16,4,32,256]{3,2,1,0:T(8,128)(2,1)S(1)} all-to-all(bf16[16,4,32,256]{3,2,1,0:T(8,128)(2,1)S(1)} %bitcast.47), channel_id=1, replica_groups=mesh['x'=4,'y'=4,'c'=2,'z'=4] {'y','x'}, dimensions={0} | all-to-all | bytes 2097152 | tf_op jit(solution)/shard_map/forward_0/all_to_all | solution.py:388
  101.4 0.1 factor_step_3.1.rest_0_
  101.7 0.5 collective-permute-start.17
  102.2 0.9 forward_1.2
  103.1 1.5 collective-permute-done.16.rest_21_.rest_17_.rest_10_.rest_14_
  104.5 1.7 collective-permute-done.17.rest_22_.rest_18_.rest_11_.rest_15_
  106.2 3.5 %forward_1.3 = (f32[4,32,256]{2,1,0:T(8,128)S(1)}, bf16[4,32,256]{2,1,0:T(8,128)(2,1)S(1)}, bf16[64,32,256]{2,1,0:T(8,128)(2,1)S(1)}) custom-call(s32[1]{0:T(128)} %bitcast.core_ref, s32[1]{0:T(128)} %bitcast.1.plane_ref, s32[4,4,8]{2,1,0:T(4,128)S(1)} %fusion.5.at_ref, f32[4,32,256]{2,1,0:T(8,128)S(1)} %factor_step_3.1.rest_0_, ...), custom_call_target="tpu_custom_call", output_to_operand_aliasing={{2}: (6, {})} | custom-call | flops 150994944 | bytes 6291456 | tf_op jit(solution)/shard_map/forward_1/pallas_call | solution.py:269
  109.7 20.6 %all_to_all.36.rest_0_ = bf16[16,4,32,256]{3,2,1,0:T(8,128)(2,1)S(1)} all-to-all(bf16[16,4,32,256]{3,2,1,0:T(8,128)(2,1)S(1)} %bitcast.41), channel_id=1, replica_groups=mesh['x'=4,'y'=4,'c'=2,'z'=4] {'y','x'}, dimensions={0} | all-to-all | bytes 2097152 | tf_op jit(solution)/shard_map/forward_1/all_to_all | solution.py:388
  130.2 2.4 %forward_2.1 = (f32[4,32,256]{2,1,0:T(8,128)S(1)}, bf16[4,32,256]{2,1,0:T(8,128)(2,1)S(1)}, bf16[64,32,256]{2,1,0:T(8,128)(2,1)S(1)}) custom-call(s32[1]{0:T(128)} %bitcast.core_ref, s32[1]{0:T(128)} %bitcast.1.plane_ref, s32[4,4,8]{2,1,0:T(4,128)S(1)} %fusion.5.at_ref, bf16[16,4,32,256]{3,2,1,0:T(8,128)(2,1)S(1)} %all_to_all.36.rest_0_, ...), custom_call_target="tpu_custom_call" | custom-call | flops 150994944 | bytes 6291456 | tf_op jit(solution)/shard_map/forward_2/pallas_call | solution.py:269
  132.6 17.1 %all_to_all.37.got_ref = bf16[16,4,32,256]{3,2,1,0:T(8,128)(2,1)S(1)} all-to-all(bf16[16,4,32,256]{3,2,1,0:T(8,128)(2,1)S(1)} %bitcast.46), channel_id=1, replica_groups=mesh['x'=4,'y'=4,'c'=2,'z'=4] {'y','x'}, dimensions={0} | all-to-all | bytes 2097152 | tf_op jit(solution)/shard_map/forward_2/all_to_all | solution.py:388
  149.7 0.6 top.1
  150.3 16.3 %all_to_all.38 = bf16[16,4,32,256]{3,2,1,0:T(8,128)(2,1)S(1)} all-to-all(bf16[16,4,32,256]{3,2,1,0:T(8,128)(2,1)S(1)} %get-tuple-element.75), channel_id=1, replica_groups=mesh['x'=4,'y'=4,'c'=2,'z'=4] {'y','x'}, dimensions={0} | all-to-all | bytes 2097152 | tf_op jit(solution)/shard_map/backward_2/all_to_all | solution.py:388
  166.6 1.7 backward_2.1
  168.3 15.8 %all_to_all.39 = bf16[16,4,32,256]{3,2,1,0:T(8,128)(2,1)S(1)} all-to-all(bf16[16,4,32,256]{3,2,1,0:T(8,128)(2,1)S(1)} %get-tuple-element.77), channel_id=1, replica_groups=mesh['x'=4,'y'=4,'c'=2,'z'=4] {'y','x'}, dimensions={0} | all-to-all | bytes 2097152 | tf_op jit(solution)/shard_map/backward_1/all_to_all | solution.py:388
  184.2 1.9 backward_1.1
  186.1 16.0 %all_to_all.40 = bf16[16,4,32,256]{3,2,1,0:T(8,128)(2,1)S(1)} all-to-all(bf16[16,4,32,256]{3,2,1,0:T(8,128)(2,1)S(1)} %get-tuple-element.79), channel_id=1, replica_groups=mesh['x'=4,'y'=4,'c'=2,'z'=4] {'y','x'}, dimensions={0} | all-to-all | bytes 2097152 | tf_op jit(solution)/shard_map/backward_0/all_to_all | solution.py:388
  202.0 1.6 backward_0.1
  203.7 12.2 %all_to_all.41.own_ref = bf16[4,2,2,2,32,256]{5,4,3,2,1,0:T(8,128)(2,1)S(1)} all-to-all(bf16[4,2,2,2,32,256]{5,4,3,2,1,0:T(8,128)(2,1)S(1)} %maximum_maximum_fusion), channel_id=1, replica_groups=mesh['x'=4,'y'=4,'c'=2,'z'=4] {'z'}, dimensions={0} | all-to-all | bytes 1048576 | tf_op jit(solution)/shard_map/to_planes/all_to_all | solution.py:462
  215.9 1.9 collective-permute-done.18.other_ref
  217.8 1.1 to_planes.1
  (28 shorter events, 0.4 us)
Async XLA Ops:
  0.6 8.0 %copy-start.1 = (bf16[1,2,1,256,256]{4,3,2,1,0:T(8,128)(2,1)S(1)}, bf16[1,2,1,256,256]{4,3,2,1,0:T(8,128)(2,1)}, u32[]{:S(2)}) copy-start(bf16[1,2,1,256,256]{4,3,2,1,0:T(8,128)(2,1)} %param.5) | copy-start | bytes 786436
  0.6 1.1 copy-start.2
  1.7 0.7 copy-start.3
  3.1 7.6 %collective-permute-start.2 = (bf16[144,256]{1,0:T(8,128)(2,1)S(1)}, bf16[144,256]{1,0:T(8,128)(2,1)S(1)}, u32[]{:S(2)}, u32[]{:S(2)}) collective-permute-start(bf16[144,256]{1,0:T(8,128)(2,1)S(1)} %get-tuple-element.88), channel_id=1, source_target_pairs={{0,3},{1,0},{2,1},{3,2},{4,7},{5,4},{6,5},{7,6},{8,11},{9,8},{10,9... | collective-permute-start | bytes 221192 | tf_op jit(solution)/shard_map/tell_planes/ppermute | solution.py:402
  7.3 6.1 %collective-permute-start.1 = (bf16[144,256]{1,0:T(8,128)(2,1)S(1)}, bf16[144,256]{1,0:T(8,128)(2,1)S(1)}, u32[]{:S(2)}, u32[]{:S(2)}) collective-permute-start(bf16[144,256]{1,0:T(8,128)(2,1)S(1)} %get-tuple-element.89), channel_id=1, source_target_pairs={{0,2},{1,3},{2,0},{3,1},{4,6},{5,7},{6,4},{7,5},{8,10},{9,11},{10,... | collective-permute-start | bytes 221192 | tf_op jit(solution)/shard_map/tell_planes/ppermute | solution.py:402
  7.3 6.5 %collective-permute-start = (bf16[144,256]{1,0:T(8,128)(2,1)S(1)}, bf16[144,256]{1,0:T(8,128)(2,1)S(1)}, u32[]{:S(2)}, u32[]{:S(2)}) collective-permute-start(bf16[144,256]{1,0:T(8,128)(2,1)S(1)} %get-tuple-element.90), channel_id=1, source_target_pairs={{0,1},{1,2},{2,3},{3,0},{4,5},{5,6},{6,7},{7,4},{8,9},{9,10},{10,1... | collective-permute-start | bytes 221192 | tf_op jit(solution)/shard_map/tell_planes/ppermute | solution.py:402
  8.6 1.6 copy-start
  13.8 26.5 %collective-permute-start.5 = (bf16[9,256,256]{2,1,0:T(8,128)(2,1)S(1)}, bf16[9,256,256]{2,1,0:T(8,128)(2,1)S(1)}, u32[]{:S(2)}, u32[]{:S(2)}) collective-permute-start(bf16[9,256,256]{2,1,0:T(8,128)(2,1)S(1)} %factor_step_1.3.here_ref.else_ref.rest_3_.rest_4_.rest_8_.rest_1_), channel_id=1, source_target_pairs={{0,3},{1,0},{2,1},{3,2},{4,7},{5,4},{6,5},{7,6},{8,11},{9,8},{10,9... | collective-permute-start | bytes 3538952 | tf_op jit(solution)/shard_map/factor_step_1/ppermute | solution.py:408
  14.7 28.4 %collective-permute-start.3 = (bf16[9,256,256]{2,1,0:T(8,128)(2,1)S(1)}, bf16[9,256,256]{2,1,0:T(8,128)(2,1)S(1)}, u32[]{:S(2)}, u32[]{:S(2)}) collective-permute-start(bf16[9,256,256]{2,1,0:T(8,128)(2,1)S(1)} %factor_step_1.2.else_ref.here_ref.rest_2_.rest_3_.rest_7_.rest_0_), channel_id=1, source_target_pairs={{0,1},{1,2},{2,3},{3,0},{4,5},{5,6},{6,7},{7,4},{8,9},{9,10},{10,1... | collective-permute-start | bytes 3538952 | tf_op jit(solution)/shard_map/factor_step_1/ppermute | solution.py:407
  15.9 28.1 %collective-permute-start.9 = (bf16[9,256,256]{2,1,0:T(8,128)(2,1)S(1)}, bf16[9,256,256]{2,1,0:T(8,128)(2,1)S(1)}, u32[]{:S(2)}, u32[]{:S(2)}) collective-permute-start(bf16[9,256,256]{2,1,0:T(8,128)(2,1)S(1)} %factor_step_1.3.here_ref.else_ref.rest_3_.rest_4_.rest_8_.rest_1_), channel_id=1, source_target_pairs={{0,4},{4,0},{1,5},{5,1},{2,6},{6,2},{3,7},{7,3},{8,12},{12,8},{9,1... | collective-permute-start | bytes 3538952 | tf_op jit(solution)/shard_map/factor_step_1/ppermute | solution.py:384
  15.9 27.9 %collective-permute-start.7 = (bf16[4,144,256]{2,1,0:T(8,128)(2,1)S(1)}, bf16[4,144,256]{2,1,0:T(8,128)(2,1)S(1)}, u32[]{:S(2)}, u32[]{:S(2)}) collective-permute-start(bf16[4,144,256]{2,1,0:T(8,128)(2,1)S(1)} %pad_maximum_fusion.rest_0_.rest_1_.rest_5_.own_told), channel_id=1, source_target_pairs={{0,4},{4,0},{1,5},{5,1},{2,6},{6,2},{3,7},{7,3},{8,12},{12,8},{9,1... | collective-permute-start | bytes 884744 | tf_op jit(solution)/shard_map/tell_planes/ppermute | solution.py:384
  16.5 29.3 %collective-permute-start.8 = (bf16[9,256,256]{2,1,0:T(8,128)(2,1)S(1)}, bf16[9,256,256]{2,1,0:T(8,128)(2,1)S(1)}, u32[]{:S(2)}, u32[]{:S(2)}) collective-permute-start(bf16[9,256,256]{2,1,0:T(8,128)(2,1)S(1)} %factor_step_1.2.else_ref.here_ref.rest_2_.rest_3_.rest_7_.rest_0_), channel_id=1, source_target_pairs={{0,4},{4,0},{1,5},{5,1},{2,6},{6,2},{3,7},{7,3},{8,12},{12,8},{9,1... | collective-permute-start | bytes 3538952 | tf_op jit(solution)/shard_map/factor_step_1/ppermute | solution.py:384
  41.0 25.7 %collective-permute-start.6 = (bf16[9,256,256]{2,1,0:T(8,128)(2,1)S(1)}, bf16[9,256,256]{2,1,0:T(8,128)(2,1)S(1)}, u32[]{:S(2)}, u32[]{:S(2)}) collective-permute-start(bf16[9,256,256]{2,1,0:T(8,128)(2,1)S(1)} %factor_step_2.5), channel_id=1, source_target_pairs={{0,3},{1,0},{2,1},{3,2},{4,7},{5,4},{6,5},{7,6},{8,11},{9,8},{10,9... | collective-permute-start | bytes 3538952 | tf_op jit(solution)/shard_map/factor_step_2/ppermute | solution.py:421
  43.8 26.6 %collective-permute-start.4 = (bf16[9,256,256]{2,1,0:T(8,128)(2,1)S(1)}, bf16[9,256,256]{2,1,0:T(8,128)(2,1)S(1)}, u32[]{:S(2)}, u32[]{:S(2)}) collective-permute-start(bf16[9,256,256]{2,1,0:T(8,128)(2,1)S(1)} %factor_step_2.4), channel_id=1, source_target_pairs={{0,1},{1,2},{2,3},{3,0},{4,5},{5,6},{6,7},{7,4},{8,9},{9,10},{10,1... | collective-permute-start | bytes 3538952 | tf_op jit(solution)/shard_map/factor_step_2/ppermute | solution.py:420
  43.9 22.8 %collective-permute-start.11 = (bf16[9,256,256]{2,1,0:T(8,128)(2,1)S(1)}, bf16[9,256,256]{2,1,0:T(8,128)(2,1)S(1)}, u32[]{:S(2)}, u32[]{:S(2)}) collective-permute-start(bf16[9,256,256]{2,1,0:T(8,128)(2,1)S(1)} %collective-permute-done.5.here_ref.else_ref.rest_5_.rest_6_.rest_10_.rest_3_), channel_id=1, source_target_pairs={{0,4},{4,0},{1,5},{5,1},{2,6},{6,2},{3,7},{7,3},{8,12},{12,8},{9,1... | collective-permute-start | bytes 3538952 | tf_op jit(solution)/shard_map/factor_step_2/ppermute | solution.py:384
  44.0 26.4 %collective-permute-start.10 = (bf16[9,256,256]{2,1,0:T(8,128)(2,1)S(1)}, bf16[9,256,256]{2,1,0:T(8,128)(2,1)S(1)}, u32[]{:S(2)}, u32[]{:S(2)}) collective-permute-start(bf16[9,256,256]{2,1,0:T(8,128)(2,1)S(1)} %collective-permute-done.3.else_ref.here_ref.rest_4_.rest_5_.rest_9_.rest_2_), channel_id=1, source_target_pairs={{0,4},{4,0},{1,5},{5,1},{2,6},{6,2},{3,7},{7,3},{8,12},{12,8},{9,1... | collective-permute-start | bytes 3538952 | tf_op jit(solution)/shard_map/factor_step_2/ppermute | solution.py:384
  70.4 3.8 %collective-permute-start.12 = (bf16[9,256,256]{2,1,0:T(8,128)(2,1)S(1)}, bf16[9,256,256]{2,1,0:T(8,128)(2,1)S(1)}, u32[]{:S(2)}, u32[]{:S(2)}) collective-permute-start(bf16[9,256,256]{2,1,0:T(8,128)(2,1)S(1)} %collective-permute-done.4.rest_6_.rest_7_.rest_11_.rest_4_), channel_id=1, source_target_pairs={{0,4},{4,0},{1,5},{5,1},{2,6},{6,2},{3,7},{7,3},{8,12},{12,8},{9,1... | collective-permute-start | bytes 3538952 | tf_op jit(solution)/shard_map/factor_step_2/ppermute | solution.py:384
  70.4 4.5 %collective-permute-start.13 = (bf16[9,256,256]{2,1,0:T(8,128)(2,1)S(1)}, bf16[9,256,256]{2,1,0:T(8,128)(2,1)S(1)}, u32[]{:S(2)}, u32[]{:S(2)}) collective-permute-start(bf16[9,256,256]{2,1,0:T(8,128)(2,1)S(1)} %collective-permute-done.6.rest_7_.rest_8_.rest_12_.rest_5_), channel_id=1, source_target_pairs={{0,4},{4,0},{1,5},{5,1},{2,6},{6,2},{3,7},{7,3},{8,12},{12,8},{9,1... | collective-permute-start | bytes 3538952 | tf_op jit(solution)/shard_map/factor_step_2/ppermute | solution.py:384
  70.9 30.7 %collective-permute-start.14 = (bf16[9,256,256]{2,1,0:T(8,128)(2,1)S(1)}, bf16[9,256,256]{2,1,0:T(8,128)(2,1)S(1)}, u32[]{:S(2)}, u32[]{:S(2)}) collective-permute-start(bf16[9,256,256]{2,1,0:T(8,128)(2,1)S(1)} %factor_step_2.6), channel_id=1, source_target_pairs={{0,1},{1,2},{2,3},{3,0},{4,5},{5,6},{6,7},{7,4},{8,9},{9,10},{10,1... | collective-permute-start | bytes 3538952 | tf_op jit(solution)/shard_map/factor_step_3/ppermute | solution.py:430
  70.9 30.7 %collective-permute-start.15 = (bf16[9,256,256]{2,1,0:T(8,128)(2,1)S(1)}, bf16[9,256,256]{2,1,0:T(8,128)(2,1)S(1)}, u32[]{:S(2)}, u32[]{:S(2)}) collective-permute-start(bf16[9,256,256]{2,1,0:T(8,128)(2,1)S(1)} %factor_step_2.7), channel_id=1, source_target_pairs={{0,3},{1,0},{2,1},{3,2},{4,7},{5,4},{6,5},{7,6},{8,11},{9,8},{10,9... | collective-permute-start | bytes 3538952 | tf_op jit(solution)/shard_map/factor_step_3/ppermute | solution.py:431
  101.6 2.9 %collective-permute-start.16 = (bf16[9,256,256]{2,1,0:T(8,128)(2,1)S(1)}, bf16[9,256,256]{2,1,0:T(8,128)(2,1)S(1)}, u32[]{:S(2)}, u32[]{:S(2)}) collective-permute-start(bf16[9,256,256]{2,1,0:T(8,128)(2,1)S(1)} %collective-permute-done.14.rest_9_.rest_13_.rest_4_.rest_6_), channel_id=1, source_target_pairs={{0,4},{4,0},{1,5},{5,1},{2,6},{6,2},{3,7},{7,3},{8,12},{12,8},{9,1... | collective-permute-start | bytes 3538952 | tf_op jit(solution)/shard_map/factor_step_3/ppermute | solution.py:384
  101.7 4.5 %collective-permute-start.17 = (bf16[9,256,256]{2,1,0:T(8,128)(2,1)S(1)}, bf16[9,256,256]{2,1,0:T(8,128)(2,1)S(1)}, u32[]{:S(2)}, u32[]{:S(2)}) collective-permute-start(bf16[9,256,256]{2,1,0:T(8,128)(2,1)S(1)} %collective-permute-done.15.rest_10_.rest_14_.rest_5_.rest_7_), channel_id=1, source_target_pairs={{0,4},{4,0},{1,5},{5,1},{2,6},{6,2},{3,7},{7,3},{8,12},{12,8},{9,1... | collective-permute-start | bytes 3538952 | tf_op jit(solution)/shard_map/factor_step_3/ppermute | solution.py:384
  215.9 1.9 collective-permute-start.18
